TPU v7x, 32 devices: a whole 2x2x4 slice. The times are simulated.
32 devices in a mesh: dp: 16 (over z, x, core), tensor: 2 (over y).
Axes of the slice: x: 2, y: 2, z: 4, core: 2. Of those that a mesh axis runs over, the one named last changes fastest.
Arguments:
- grads: bfloat16 [16, 24, 128, 4096], P('dp', None, None, 'tensor'), may hold values from -6 to 6
- owner: int32 [24], replicated, may hold values from 0 to 15, as said below
- momentum: float32 [16, 2, 128, 4096], P('dp', None, None, 'tensor'), may hold values from -6 to 6, as said below
Outputs:
- update: bfloat16 [24, 128, 4096], P(None, None, 'tensor')
- new_momentum: float32 [16, 2, 128, 4096], P('dp', None, None, 'tensor')
Inputs may be any that keep to these rules, and one draw needn't show every extreme that they name: Every owner holds at least one matrix and no owner holds more than 2; some owner holds exactly 2. Slot s of owner p holds the momentum of the matrix of slot_rank s among those that owner p holds; slots beyond an owner's count hold values that are carried over.
All inputs are finite; a program needn't handle non-finite values.
Results may differ from a plain program's by a relative error of at most 0.03.
Values may be sent and summed in bfloat16 or wider, within the bound.
No kernel may reach another device: no remote copies, remote signals or barrier semaphores. Data moves between devices by JAX's collectives and lax.ppermute only.
A program may use at most 128 MiB of HBM per device.

v0:
```python
import math

import jax
import jax.numpy as jnp
from jax import lax
from jax.sharding import PartitionSpec as P

R = 128
D = 4096
ITERS = 5


COEF_A = 3.4445
COEF_B = -4.775
COEF_C = 2.0315
EPSILON = 1e-07
DECAY = 0.95


def next_polynomial(gram):
    gram = lax.optimization_barrier(gram)
    square = jnp.einsum("srt,stu->sru", gram, gram, preferred_element_type=jnp.float32)
    return (COEF_B * gram.astype(jnp.float32) + COEF_C * square).astype(jnp.bfloat16)


def apply_polynomial(polynomial, iterate):
    return COEF_A * iterate.astype(jnp.float32) + jnp.einsum(
        "srt,std->srd", polynomial, iterate, preferred_element_type=jnp.float32
    )


def orthogonalize_gathered(rounded, local_cols, factor):
    gathered = lax.all_gather(rounded, "tensor", axis=2, tiled=True)
    squares = jnp.sum(jnp.square(gathered.astype(jnp.float32)), axis=(1, 2))
    iterate = (gathered.astype(jnp.float32) / (jnp.sqrt(squares)[:, None, None] + EPSILON)).astype(
        jnp.bfloat16
    )
    start = lax.axis_index("tensor") * local_cols
    following = None
    for step in range(ITERS):
        gram = jnp.einsum(
            "srd,std->srt", iterate, iterate, preferred_element_type=jnp.float32
        ).astype(jnp.bfloat16)
        polynomial = next_polynomial(gram)
        if step + 1 < ITERS:
            iterate = apply_polynomial(polynomial, iterate).astype(jnp.bfloat16)
        else:
            own_cols = lax.dynamic_slice_in_dim(iterate, start, local_cols, 2)
            following = apply_polynomial(polynomial, own_cols)
    return (factor * following).astype(jnp.bfloat16)


def per_device(grads, owner, momentum):
    owner_count = lax.axis_size("dp")
    myself = lax.axis_index("dp")
    matrices = owner.shape[0]
    slot_count = momentum.shape[1]
    head_rows = grads.shape[2]
    local_cols = grads.shape[3]
    factor = 0.2 * math.sqrt(max(R, D))
    positions = jnp.arange(matrices, dtype=jnp.int32)
    same_owner = owner[:, None] == owner[None, :]
    earlier = positions[None, :] < positions[:, None]
    slot_rank = jnp.sum((same_owner & earlier).astype(jnp.int32), axis=1)
    owner_ids = jnp.arange(owner_count, dtype=jnp.int32)
    slot_ids = jnp.arange(slot_count, dtype=jnp.int32)
    matches = (owner[None, None, :] == owner_ids[:, None, None]) & (
        slot_rank[None, None, :] == slot_ids[None, :, None]
    )
    filled = jnp.any(matches, axis=2)
    source = jnp.sum(jnp.where(matches, positions[None, None, :], 0), axis=2)
    gradient = grads[0]
    zero_float = jnp.zeros((), jnp.float32)
    packed = jnp.take(gradient, source.reshape(-1), axis=0).astype(jnp.float32)
    packed = jnp.where(filled.reshape(-1)[:, None, None], packed, zero_float)
    summed = lax.psum_scatter(
        packed.reshape(owner_count, slot_count, head_rows, local_cols).astype(jnp.bfloat16),
        "dp",
        scatter_dimension=0,
        tiled=True,
    ).astype(jnp.float32)
    mean_grad = summed[0] / owner_count
    previous = momentum[0]
    following = DECAY * previous + mean_grad
    held_here = lax.dynamic_index_in_dim(filled, myself, 0, keepdims=False)
    new_momentum = jnp.where(held_here[:, None, None], following, previous)[None]
    rounded = (mean_grad + DECAY * following).astype(jnp.bfloat16)
    result = orthogonalize_gathered(rounded, local_cols, factor)
    everything = lax.all_gather(result, "dp", axis=0, tiled=True)
    update = jnp.take(everything, owner * slot_count + slot_rank, axis=0)
    return (update, new_momentum)


def solution(mesh):
    in_specs = (P("dp", None, None, "tensor"), P(), P("dp", None, None, "tensor"))
    out_specs = (P(None, None, "tensor"), P("dp", None, None, "tensor"))
    return jax.shard_map(
        per_device, mesh=mesh, in_specs=in_specs, out_specs=out_specs, check_vma=False
    )
```

profile of v0, /device:TPU:0, one launch (start us, length us, event | category | flops | bytes accessed | tf_op | source)
XLA Modules:
  0.0 434.5 jit_solution(14414858799945735916)
XLA Ops:
  7.2 0.9 convert_reduce_fusion
  8.1 0.7 iota_compare_fusion.1
  8.8 0.1 fusion.42
  8.9 0.1 copy.7
  9.0 0.1 and_reduce_fusion
  9.1 0.1 reshape.111
  9.2 0.1 copy.6
  9.3 0.1 copy.5
  9.4 11.8 %gather_fusion = bf16[32,128,2048]{2,1,0:T(8,128)(2,1)} fusion(bf16[24,128,2048]{2,1,0:T(8,128)(2,1)} %bitcast.39, s32[1024]{0:T(1024)S(1)} %pad_clamp_fusion.1), kind=kCustom, calls=%fused_computation | custom fusion | bytes 33554560 | tf_op jit(solution)/shard_map/jit(_take)/gather | solution.py:74
  21.2 15.6 %select_convert_fusion = bf16[16,2,128,2048]{3,2,1,0:T(8,128)(2,1)} fusion(bf16[16,2,128,2048]{3,2,1,0:T(8,128)(2,1)} %bitcast.38, pred[16,2]{1,0:T(8,128)(4,1)S(1)} %copy.6, pred[16,2]{1,0:T(8,128)(4,1)S(1)} %copy.5), kind=kLoop, calls=%fused_computation.2 | loop fusion | flops 33554432 | bytes 33554496 | tf_op jit(solution)/shard_map/convert_element_type | solution.py:77
  36.8 0.0 all-gather.3.cloned.1.call-start
  36.9 181.4 %reduce-scatter.2.cloned.1.call-done = bf16[1,2,128,2048]{3,2,1,0:T(8,128)(2,1)} async-done(((bf16[16,2,128,2048]{3,2,1,0:T(8,128)(2,1)}), bf16[1,2,128,2048]{3,2,1,0:T(8,128)(2,1)}) %reduce-scatter.2.cloned.1.call-update) | async-done | bytes 1048592 | tf_op jit(solution)/shard_map/reduce_scatter | solution.py:76
  218.2 2.6 fusion.10
  220.9 0.0 all-gather.5.cloned.1.call-start
  221.0 32.2 %all-gather.3.cloned.1.call-done = bf16[2,128,4096]{2,1,0:T(8,128)(2,1)} async-done(((bf16[2,128,2048]{2,1,0:T(8,128)(2,1)}), bf16[2,128,4096]{2,1,0:T(8,128)(2,1)}) %all-gather.3.cloned.1.call-update) | async-done | bytes 2097168 | tf_op jit(solution)/shard_map/all_gather | solution.py:33
  253.2 2.4 fusion.4
  255.6 0.5 fusion.5
  256.1 0.7 convolution_convert_fusion.4
  256.8 2.2 fusion
  259.0 3.1 convolution_convert_fusion.3
  262.1 2.2 fusion.1
  264.3 3.1 convolution_convert_fusion.2
  267.4 2.2 fusion.2
  269.7 2.9 convolution_convert_fusion.1
  272.6 3.1 fusion.3
  275.7 0.7 convolution_convert_fusion
  276.5 1.7 fusion.7
  278.2 0.2 dynamic-slice_reduce_fusion
  278.4 3.4 add_select_fusion
  281.8 123.4 %all-gather.5.cloned.1.call-done = bf16[32,128,2048]{2,1,0:T(8,128)(2,1)} async-done(((bf16[2,128,2048]{2,1,0:T(8,128)(2,1)}), bf16[32,128,2048]{2,1,0:T(8,128)(2,1)}) %all-gather.5.cloned.1.call-update) | async-done | bytes 16777232 | tf_op jit(solution)/shard_map/all_gather | solution.py:89
  405.2 12.0 %gather_fusion.1 = bf16[24,128,2048]{2,1,0:T(8,128)(2,1)} fusion(bf16[32,128,2048]{2,1,0:T(8,128)(2,1)} %all-gather.5.cloned.1.call-done, s32[1024]{0:T(1024)S(1)} %pad_clamp_fusion), kind=kCustom, calls=%fused_computation.1 | custom fusion | bytes 25165920 | tf_op jit(solution)/shard_map/jit(_take)/gather | solution.py:90
  417.2 10.8 %broadcast_select_fusion = bf16[24,128,2048]{2,1,0:T(8,128)(2,1)} fusion(bf16[24,128,2048]{2,1,0:T(8,128)(2,1)} %gather_fusion.1, pred[24]{0:T(512)(128)(4,1)S(1)} %get-tuple-element.2), kind=kLoop, calls=%fused_computation.3 | loop fusion | flops 6291456 | bytes 25165848 | tf_op jit(solution)/shard_map/jit(_take)/select_n | solution.py:90
  (23 shorter events, 0.2 us)
Async XLA Ops:
  7.2 211.1 %reduce-scatter.2.cloned.1.call-start = ((), (), s32[]{:S(2)}) async-start(), calls=%async_computation.1 | async-start | bytes 17825792 | tf_op jit(solution)/shard_map/reduce_scatter | solution.py:76
  36.8 181.4 %copy-start.2 = (f32[1,2,128,2048]{3,2,1,0:T(8,128)S(1)}, f32[1,2,128,2048]{3,2,1,0:T(8,128)}, u32[]{:S(2)}) copy-start(f32[1,2,128,2048]{3,2,1,0:T(8,128)} %param.5) | copy-start | bytes 6291460
  36.8 216.4 %all-gather.3.cloned.1.call-start = ((), (), s32[]{:S(2)}) async-start(), calls=%async_computation.2 | async-start | bytes 3145728 | tf_op jit(solution)/shard_map/all_gather | solution.py:33
  220.9 184.3 %all-gather.5.cloned.1.call-start = ((), (), s32[]{:S(2)}) async-start(), calls=%async_computation.3 | async-start | bytes 17825792 | tf_op jit(solution)/shard_map/all_gather | solution.py:89
  253.2 2.4 copy-start.3
  259.0 3.1 copy-start
  264.3 3.1 copy-start.1
  276.4 1.9 copy-start.5
  276.5 1.9 copy-start.4
Sparse Core Ops, SparseCore 0:
  36.9 181.2 reduce-scatter.1
  221.0 32.1 all-gather.2
  278.3 126.8 all-gather.4
where the time goes:
time: 435 us; the launch traced here: 434 us
  waiting for transfers between devices  337 us (77%)
  other arithmetic  37.1 us (9%)
  local copies, waits for them, and re-layouts  24.3 us (6%)
  matrix products  22 us (5%)
  between operations  13.9 us (3%)
    reduce_scatter x1, waiting for transfers between devices, per_device(): lax.psum_scatter(packed.reshape(owner_count, slot_count, head_rows, local...  181 us
    all_gather x1, waiting for transfers between devices, per_device(): everything = lax.all_gather(result, 'dp', axis=0, tiled=True)  123 us
    all_gather x1, waiting for transfers between devices, orthogonalize_gathered(): gathered = lax.all_gather(rounded, 'tensor', axis=2, tiled=True)  32.2 us
    convert_element_type x1, other arithmetic, per_device(): packed.reshape(owner_count, slot_count, head_rows, local_cols)  15.6 us
    gather x1, local copies, waits for them, and re-layouts, per_device(): update = jnp.take(everything, owner * slot_count + slot_rank, axis=0)  12 us
    gather x1, local copies, waits for them, and re-layouts, per_device(): packed = jnp.take(gradient, source.reshape(-1), axis=0).astype(jnp.float32)  11.8 us
    dot_general x5, matrix products, apply_polynomial(): jnp.einsum('srt,std->srd', polynomial, iterate, preferred_element_type=jn...  11.5 us
    select_n x1, other arithmetic, per_device(): update = jnp.take(everything, owner * slot_count + slot_rank, axis=0)  10.8 us
  transfers between devices with their start and end apart: 3, of which 3 were waited for; matrix products, arithmetic and copies ran while one was open for 1% of the time, Pallas kernels for 0%

commit v1 on v0

v1 whole, which is shorter than its diff:
```python
import functools
import math

import jax
import jax.numpy as jnp
from jax import lax
from jax.experimental import pallas as pl
from jax.experimental.pallas import tpu as pltpu
from jax.sharding import PartitionSpec as P

R = 128
D = 4096
ITERS = 5

COEF_A = 3.4445
COEF_B = -4.775
COEF_C = 2.0315
EPSILON = 1e-07
DECAY = 0.95

CORES = 2
PAIR = 2
VMEM_BYTES = 48 * 1024 * 1024


def copy_blocks(count, first, rows, idx_ref, src_ref, out_ref, sem):
    def copy(i):
        return pltpu.make_async_copy(
            src_ref.at[idx_ref[i], pl.ds(first, rows)], out_ref.at[i], sem.at[i]
        )

    def start(i, _):
        copy(i).start()
        return 0

    def wait(i, _):
        copy(i).wait()
        return 0

    lax.fori_loop(0, count, start, 0)
    lax.fori_loop(0, count, wait, 0)


def take_blocks(src, idx, first, rows):
    count = idx.shape[0]
    cols = src.shape[2]
    size = count * rows * cols * src.dtype.itemsize
    return pl.pallas_call(
        functools.partial(copy_blocks, count, first, rows),
        out_shape=jax.ShapeDtypeStruct((count, rows, cols), src.dtype),
        in_specs=[
            pl.BlockSpec(memory_space=pltpu.SMEM),
            pl.BlockSpec(memory_space=pl.ANY),
        ],
        out_specs=pl.BlockSpec(memory_space=pl.ANY),
        scratch_shapes=[pltpu.SemaphoreType.DMA((count,))],
        cost_estimate=pl.CostEstimate(flops=0, bytes_accessed=2 * size, transcendentals=0),
    )(idx, src)


def sum_blocks(count, first, rows, outs, idx_ref, src_ref, other_ref, *rest):
    out_refs = rest[:outs]
    mine, sums, sem_mine, sem_other, sem_out = rest[outs:]
    each = count // outs

    def copies(i):
        return (
            pltpu.make_async_copy(
                src_ref.at[idx_ref[i], pl.ds(first, rows)], mine.at[i], sem_mine.at[i]
            ),
            pltpu.make_async_copy(other_ref.at[i], sums.at[i], sem_other.at[i]),
        )

    def start(i, _):
        for c in copies(i):
            c.start()
        return 0

    lax.fori_loop(0, count, start, 0)
    for part, out_ref in enumerate(out_refs):

        def leave(i, part=part, out_ref=out_ref):
            return pltpu.make_async_copy(
                sums.at[part * each + i], out_ref.at[i], sem_out.at[part * each + i]
            )

        def body(i, _, part=part, leave=leave):
            at = part * each + i
            for c in copies(at):
                c.wait()
            sums[at] = sums[at] + mine[at]
            leave(i).start()
            return 0

        lax.fori_loop(0, each, body, 0)
    for part, out_ref in enumerate(out_refs):

        def finish(i, _, part=part, out_ref=out_ref):
            pltpu.make_async_copy(
                sums.at[part * each + i], out_ref.at[i], sem_out.at[part * each + i]
            ).wait()
            return 0

        lax.fori_loop(0, each, finish, 0)


def add_taken(src, idx, first, rows, other, outs):
    count = idx.shape[0]
    cols = src.shape[2]
    size = count * rows * cols * src.dtype.itemsize
    each = jax.ShapeDtypeStruct((count // outs, rows, cols), src.dtype)
    return pl.pallas_call(
        functools.partial(sum_blocks, count, first, rows, outs),
        out_shape=[each] * outs,
        in_specs=[
            pl.BlockSpec(memory_space=pltpu.SMEM),
            pl.BlockSpec(memory_space=pl.ANY),
            pl.BlockSpec(memory_space=pl.ANY),
        ],
        out_specs=[pl.BlockSpec(memory_space=pl.ANY)] * outs,
        scratch_shapes=[
            pltpu.VMEM((count, rows, cols), src.dtype),
            pltpu.VMEM((count, rows, cols), src.dtype),
            pltpu.SemaphoreType.DMA((count,)),
            pltpu.SemaphoreType.DMA((count,)),
            pltpu.SemaphoreType.DMA((count,)),
        ],
        compiler_params=pltpu.CompilerParams(vmem_limit_bytes=VMEM_BYTES),
        cost_estimate=pl.CostEstimate(
            flops=size // 2, bytes_accessed=3 * size, transcendentals=0
        ),
    )(idx, src, other)


def momentum_kernel(scale, sizes, held_ref, momentum_ref, *rest):
    part_refs = rest[: sum(sizes)]
    next_ref, rounded_ref, gram_ref = rest[sum(sizes) :]
    held = held_ref[pl.program_id(0)] > 0
    first, used = 0, 0
    for size in sizes:
        total = None
        for ref in part_refs[used : used + size]:
            term = ref[0].astype(jnp.float32)
            total = term if total is None else total + term
        rows = total.shape[0]
        here = pl.ds(first, rows)
        mean = total * scale
        previous = momentum_ref[0, here]
        following = DECAY * previous + mean
        next_ref[0, here] = jnp.where(held, following, previous)
        rounded_ref[0, here] = (mean + DECAY * following).astype(jnp.bfloat16)
        first += rows
        used += size
    rounded = rounded_ref[0]
    gram_ref[0] = lax.dot_general(
        rounded, rounded, (((1,), (1,)), ((), ())), preferred_element_type=jnp.float32
    )


def momentum_step(held, momentum, parts, owner_count):
    slots, rows, cols = momentum.shape
    flat = [a for part in parts for a in part]
    return pl.pallas_call(
        functools.partial(
            momentum_kernel, 1.0 / owner_count, [len(part) for part in parts]
        ),
        grid=(slots,),
        out_shape=[
            jax.ShapeDtypeStruct((slots, rows, cols), jnp.float32),
            jax.ShapeDtypeStruct((slots, rows, cols), jnp.bfloat16),
            jax.ShapeDtypeStruct((slots, rows, rows), jnp.float32),
        ],
        in_specs=[
            pl.BlockSpec(memory_space=pltpu.SMEM),
            pl.BlockSpec((1, rows, cols), lambda s: (s, 0, 0)),
        ]
        + [pl.BlockSpec((1,) + a.shape[1:], lambda s: (s, 0, 0)) for a in flat],
        out_specs=[
            pl.BlockSpec((1, rows, cols), lambda s: (s, 0, 0)),
            pl.BlockSpec((1, rows, cols), lambda s: (s, 0, 0)),
            pl.BlockSpec((1, rows, rows), lambda s: (s, 0, 0)),
        ],
        compiler_params=pltpu.CompilerParams(vmem_limit_bytes=VMEM_BYTES),
        cost_estimate=pl.CostEstimate(
            flops=2 * slots * rows * rows * cols,
            bytes_accessed=slots * rows * cols * 16,
            transcendentals=0,
        ),
    )(held, momentum, *flat)


def exact(a, b):
    return jnp.dot(
        a, b, preferred_element_type=jnp.float32, precision=lax.Precision.HIGHEST
    )


def orthogonalize_kernel(factor, slots, grams, *refs):
    gram_refs = refs[:grams]
    rounded_ref, out_ref = refs[grams:]
    rows = rounded_ref.shape[1]
    row_ids = lax.broadcasted_iota(jnp.int32, (rows, rows), 0)
    col_ids = lax.broadcasted_iota(jnp.int32, (rows, rows), 1)
    diagonal = row_ids == col_ids
    held = []
    for s in range(slots):
        gram = gram_refs[0][s]
        for ref in gram_refs[1:]:
            gram = gram + ref[s]
        squares = jnp.sum(
            jnp.sum(jnp.where(diagonal, gram, 0.0), axis=0, keepdims=True),
            axis=1,
            keepdims=True,
        )
        inverse = 1.0 / (jnp.sqrt(squares) + EPSILON)
        held.append([gram * inverse * inverse, None, inverse])
    for step in range(ITERS):
        squared = [exact(h[0], h[0]) for h in held]
        factors = [
            COEF_B * h[0] + COEF_C * q + jnp.where(diagonal, COEF_A, 0.0)
            for h, q in zip(held, squared)
        ]
        for h, m in zip(held, factors):
            h[1] = m if h[1] is None else exact(m, h[1])
        if step + 1 < ITERS:
            once = [exact(m, h[0]) for h, m in zip(held, factors)]
            for h, m, o in zip(held, factors, once):
                h[0] = exact(m, o)
    for s, h in enumerate(held):
        whole = h[1] * (factor * h[2])
        high = whole.astype(jnp.bfloat16)
        low = (whole - high.astype(jnp.float32)).astype(jnp.bfloat16)
        rounded = rounded_ref[s]
        out_ref[s] = (
            jnp.dot(high, rounded, preferred_element_type=jnp.float32)
            + jnp.dot(low, rounded, preferred_element_type=jnp.float32)
        ).astype(jnp.bfloat16)


def orthogonalize(grams, rounded, factor):
    slots, rows, cols = rounded.shape
    return pl.pallas_call(
        functools.partial(orthogonalize_kernel, factor, slots, len(grams)),
        out_shape=jax.ShapeDtypeStruct(rounded.shape, jnp.bfloat16),
        in_specs=[pl.BlockSpec(memory_space=pltpu.VMEM)] * (len(grams) + 1),
        out_specs=pl.BlockSpec(memory_space=pltpu.VMEM),
        compiler_params=pltpu.CompilerParams(vmem_limit_bytes=VMEM_BYTES),
        cost_estimate=pl.CostEstimate(
            flops=slots * (4 * rows * rows * cols + 20 * 12 * rows * rows * rows),
            bytes_accessed=slots * rows * cols * 4,
            transcendentals=0,
        ),
    )(*grams, rounded)


class Place:
    def __init__(self):
        self.count = lax.axis_size("dp")
        self.depth = self.count // (PAIR * CORES)
        me = lax.axis_index("dp")
        self.core = me % CORES
        self.x = (me // CORES) % PAIR
        self.z = me // (CORES * PAIR)

    def pairs(self, move):
        found = []
        for z in range(self.depth):
            for x in range(PAIR):
                for core in range(CORES):
                    to = move(z, x, core)
                    if to is not None:
                        a, b, c = to
                        found.append(
                            (
                                (z * PAIR + x) * CORES + core,
                                (a * PAIR + b) * CORES + c,
                            )
                        )
        return found

    def swap_cores(self, value):
        return lax.ppermute(value, "dp", self.pairs(lambda z, x, c: (z, x, 1 - c)))

    def swap_x(self, value):
        return lax.ppermute(value, "dp", self.pairs(lambda z, x, c: (z, 1 - x, c)))

    def shift_z(self, value, step, sources):
        return lax.ppermute(
            value,
            "dp",
            self.pairs(lambda z, x, c: (z + step, x, c) if z in sources else None),
        )


def chain_sum(place, blocks):
    depth = place.depth

    def own(at):
        return lax.dynamic_index_in_dim(blocks, jnp.clip(at, 0, depth - 1), 0, False)

    up, down = blocks[depth - 1], blocks[0]
    for t in range(1, depth):
        up = place.shift_z(up, 1, range(0, t))
        down = place.shift_z(down, -1, range(depth - t, depth))
        if t + 1 < depth:
            up = up + own(depth - 1 - t + place.z)
            down = down + own(t - (depth - 1) + place.z)
    return up, down, own(place.z)


def reduce_to_owners(place, gradient, source, slot_count, shares):
    cols = gradient.shape[2]
    core_first = jnp.take(source, place.core, axis=2)
    other_core = jnp.take(source, 1 - place.core, axis=2)

    def ordered(table, x_first):
        if not x_first:
            return table.reshape(-1)
        away = jnp.take(table, 1 - place.x, axis=1)
        home = jnp.take(table, place.x, axis=1)
        return jnp.concatenate([away.reshape(-1), home.reshape(-1)])

    first = 0
    received = []
    for rows, x_first in shares:
        sent = take_blocks(gradient, ordered(other_core, x_first), first, rows)
        received.append((first, rows, x_first, place.swap_cores(sent)))
        first += rows
    results = []
    for first, rows, x_first, other in received:
        mine = ordered(core_first, x_first)
        if x_first:
            away, home = add_taken(gradient, mine, first, rows, other, 2)
            blocks = home + place.swap_x(away)
            blocks = blocks.reshape(place.depth, slot_count, rows, cols)
            results.append(chain_sum(place, blocks))
        else:
            (blocks,) = add_taken(gradient, mine, first, rows, other, 1)
            blocks = blocks.reshape(place.depth, PAIR, slot_count, rows, cols)
            up, down, own = chain_sum(place, blocks)
            both = up + down + own
            away = lax.dynamic_index_in_dim(both, 1 - place.x, 0, False)
            home = lax.dynamic_index_in_dim(both, place.x, 0, False)
            got = place.swap_x(away)
            results.append((home, got))
    return results


def per_device(grads, owner, momentum):
    place = Place()
    owner_count = place.count
    matrices = owner.shape[0]
    slot_count = momentum.shape[1]
    head_rows = grads.shape[2]
    factor = 0.2 * math.sqrt(max(R, D))
    positions = jnp.arange(matrices, dtype=jnp.int32)
    same_owner = owner[:, None] == owner[None, :]
    earlier = positions[None, :] < positions[:, None]
    slot_rank = jnp.sum((same_owner & earlier).astype(jnp.int32), axis=1)
    spot = owner * slot_count + slot_rank
    spots = jnp.arange(owner_count * slot_count, dtype=jnp.int32)
    matches = spot[None, :] == spots[:, None]
    filled = jnp.any(matches, axis=1).astype(jnp.int32)
    source = jnp.sum(jnp.where(matches, positions[None, :], 0), axis=1)
    source = source.reshape(place.depth, PAIR, CORES, slot_count)
    held = lax.dynamic_slice_in_dim(
        filled, lax.axis_index("dp") * slot_count, slot_count, 0
    )

    cut = head_rows * 5 // 8
    shares = ((cut, True), (head_rows - cut, False))
    parts = reduce_to_owners(place, grads[0], source, slot_count, shares)
    new_momentum, rounded, gram = momentum_step(held, momentum[0], parts, owner_count)

    width = lax.axis_size("tensor")
    grams = [gram]
    for _ in range(width - 1):
        grams.append(
            lax.ppermute(
                grams[-1], "tensor", [(i, (i + 1) % width) for i in range(width)]
            )
        )
    result = orthogonalize(grams, rounded, factor)
    everything = lax.all_gather(result, "dp", axis=0, tiled=True)
    update = take_blocks(everything, spot, 0, head_rows)
    return (update, new_momentum[None])


def solution(mesh):
    in_specs = (P("dp", None, None, "tensor"), P(), P("dp", None, None, "tensor"))
    out_specs = (P(None, None, "tensor"), P("dp", None, None, "tensor"))
    return jax.shard_map(
        per_device, mesh=mesh, in_specs=in_specs, out_specs=out_specs, check_vma=False
    )
```

time: 435 us -> 957 us (2.20)
  Pallas kernels: 0 us -> 663 us
  waiting for transfers between devices: 337 us -> 209 us
  starting transfers between devices: 0.12 us -> 43.5 us
  matrix products: 22 us -> 0 us
  other arithmetic: 37.1 us -> 18.6 us
  local copies, waits for them, and re-layouts: 24.3 us -> 8.65 us
    pallas_call x0 -> x7, Pallas kernels: none -> 663 us  [the longest x3 641 us: take_blocks(): pl.pallas_call(functools.partial(copy_blocks, count, first, rows), out_sh...]
    reduce_scatter x1 -> x0, waiting for transfers between devices: 181 us -> none  [per_device(): lax.psum_scatter(packed.reshape(owner_count, slot_count, head_rows, local...]
    ppermute x0 -> x17, waiting for transfers between devices: none -> 81.1 us  [the longest x2 48.3 us: swap_x(): return lax.ppermute(value, 'dp', self.pairs(lambda z, x, c: (z, 1 - x, c)))]
    ppermute x0 -> x17, starting transfers between devices: none -> 43.5 us  [the longest x12 36.5 us: shift_z(): lax.ppermute(value, 'dp', self.pairs(lambda z, x, c: (z + step, x, c) if...]
    all_gather x1 -> x0, waiting for transfers between devices: 32.2 us -> none  [orthogonalize_gathered(): gathered = lax.all_gather(rounded, 'tensor', axis=2, tiled=True)]
    gather x2 -> x0, local copies, waits for them, and re-layouts: 23.8 us -> none  [the longest x1 12 us: per_device(): update = jnp.take(everything, owner * slot_count + slot_rank, axis=0)]
    dot_general x10 -> x0, matrix products: 22 us -> none  [the longest x5 11.5 us: apply_polynomial(): jnp.einsum('srt,std->srd', polynomial, iterate, preferred_element_type=jn...]
    convert_element_type x3 -> x1, other arithmetic: 18.7 us -> 0.01 us  [per_device(): filled = jnp.any(matches, axis=1).astype(jnp.int32)]
  transfers between devices with their start and end apart: 3 -> 18, of which waited for: 3 -> 9; matrix products, arithmetic and copies ran while one was open for 1% -> 2% of each run, Pallas kernels for 0% -> 12%
where the time goes in v1:
time: 957 us
  Pallas kernels  663 us (69%)
  waiting for transfers between devices  209 us (22%)
  starting transfers between devices  43.5 us (5%)
  other arithmetic  18.6 us (2%)
  between operations  14.3 us (1%)
    pallas_call x3, Pallas kernels, take_blocks(): pl.pallas_call(functools.partial(copy_blocks, count, first, rows), out_sh...  641 us
    all_gather x1, waiting for transfers between devices, per_device(): everything = lax.all_gather(result, 'dp', axis=0, tiled=True)  128 us
    ppermute x2, waiting for transfers between devices, swap_x(): return lax.ppermute(value, 'dp', self.pairs(lambda z, x, c: (z, 1 - x, c)))  48.3 us
    ppermute x12, starting transfers between devices, shift_z(): lax.ppermute(value, 'dp', self.pairs(lambda z, x, c: (z + step, x, c) if...  36.5 us
    ppermute x12, waiting for transfers between devices, shift_z(): lax.ppermute(value, 'dp', self.pairs(lambda z, x, c: (z + step, x, c) if...  29.4 us
  transfers between devices with their start and end apart: 18, of which 9 were waited for; matrix products, arithmetic and copies ran while one was open for 2% of the time, Pallas kernels for 12%

profile of v1, /device:TPU:0, one launch (start us, length us, event | category | flops | bytes accessed | tf_op | source)
XLA Modules:
  0.0 956.6 jit_solution(9166231062983281811)
XLA Ops:
  10.2 160.7 %shard_map.50 = bf16[16,80,2048]{2,1,0:T(8,128)(2,1)} custom-call(s32[16]{0:T(128)} %pad_add_fusion.1.idx_ref, bf16[24,128,2048]{2,1,0:T(8,128)(2,1)} %bitcast.51), custom_call_target="tpu_custom_call" | custom-call | bytes 10485760 | tf_op jit(solution)/shard_map/pallas_call | solution.py:48
  172.1 97.2 %shard_map.52 = bf16[16,48,2048]{2,1,0:T(8,128)(2,1)} custom-call(s32[16]{0:T(128)} %reshape.51.idx_ref, bf16[24,128,2048]{2,1,0:T(8,128)(2,1)} %bitcast.52), custom_call_target="tpu_custom_call" | custom-call | bytes 6291456 | tf_op jit(solution)/shard_map/pallas_call | solution.py:48
  269.9 6.7 shard_map.51
  278.0 3.1 collective-permute-start.1
  281.2 6.6 shard_map.53
  289.1 4.4 collective-permute-start.9
  293.5 1.5 collective-permute-start.12
  295.0 43.6 %collective-permute-done.1 = bf16[8,80,2048]{2,1,0:T(8,128)(2,1)} collective-permute-done((bf16[8,80,2048]{2,1,0:T(8,128)(2,1)}, bf16[8,80,2048]{2,1,0:T(8,128)(2,1)}, u32[]{:S(2)}, u32[]{:S(2)}) %collective-permute-start.1) | collective-permute-done | bytes 2621472 | tf_op jit(solution)/shard_map/ppermute | solution.py:285
  338.6 3.6 add.94
  345.0 4.3 collective-permute-start.2
  349.3 2.7 bitcast_add_fusion.2
  352.0 1.6 collective-permute-start.13
  353.6 2.2 collective-permute-start.10
  355.8 8.2 collective-permute-done.2
  364.0 2.9 bitcast_add_fusion.6
  368.3 5.0 collective-permute-start.3
  373.4 7.5 collective-permute-done.10
  380.8 2.7 bitcast_add_fusion.1
  384.8 6.0 collective-permute-start.11
  390.8 4.1 collective-permute-done.3
  394.9 2.9 bitcast_add_fusion.5
  399.0 5.9 collective-permute-start.4
  404.9 6.8 collective-permute-done.11
  413.3 1.8 collective-permute-start.15
  416.4 4.7 collective-permute-done.15.rest_4_
  421.1 2.8 collective-permute-done.4.rest_0_
  423.9 1.6 copy-done.1
  425.5 3.1 shard_map.54
  430.1 3.4 collective-permute-done.16.refs_1_
  433.6 5.4 shard_map.55
  439.0 127.6 %all-gather.2.cloned.1.call-done.src_ref = bf16[32,128,2048]{2,1,0:T(8,128)(2,1)} async-done(((bf16[2,128,2048]{2,1,0:T(8,128)(2,1)}), bf16[32,128,2048]{2,1,0:T(8,128)(2,1)}) %all-gather.2.cloned.1.call-update) | async-done | bytes 16777232 | tf_op jit(solution)/shard_map/all_gather | solution.py:384
  566.6 383.2 %shard_map.56 = bf16[24,128,2048]{2,1,0:T(8,128)(2,1)} custom-call(s32[24]{0:T(128)} %copy-done.3, bf16[32,128,2048]{2,1,0:T(8,128)(2,1)} %all-gather.2.cloned.1.call-done.src_ref), custom_call_target="tpu_custom_call" | custom-call | bytes 25165824 | tf_op jit(solution)/shard_map/pallas_call | solution.py:48
  (53 shorter events, 18.8 us)
Async XLA Ops:
  7.2 559.4 %all-gather.2.cloned.1.call-start = ((), (), s32[]{:S(2)}) async-start(), calls=%async_computation | async-start | bytes 17825792 | tf_op jit(solution)/shard_map/all_gather | solution.py:384
  8.9 406.2 %copy-start.3 = (s32[24]{0:T(128)}, s32[24]{0:T(128)S(1)}, u32[]{:S(2)}) copy-start(s32[24]{0:T(128)S(1)} %multiply_add_fusion.idx_ref) | copy-start | bytes 292
  171.0 98.9 %collective-permute-start = (bf16[16,80,2048]{2,1,0:T(8,128)(2,1)}, bf16[16,80,2048]{2,1,0:T(8,128)(2,1)}, u32[]{:S(2)}, u32[]{:S(2)}) collective-permute-start(bf16[16,80,2048]{2,1,0:T(8,128)(2,1)} %shard_map.50), channel_id=1, source_target_pairs={{0,2},{2,0},{4,6},{6,4},{8,10},{10,8},{12,14},{14,12},{16,18},{18,... | collective-permute-start | bytes 15728648 | tf_op jit(solution)/shard_map/ppermute | solution.py:282
  269.3 11.9 %collective-permute-start.8 = (bf16[16,48,2048]{2,1,0:T(8,128)(2,1)}, bf16[16,48,2048]{2,1,0:T(8,128)(2,1)}, u32[]{:S(2)}, u32[]{:S(2)}) collective-permute-start(bf16[16,48,2048]{2,1,0:T(8,128)(2,1)} %shard_map.52), channel_id=1, source_target_pairs={{0,2},{2,0},{4,6},{6,4},{8,10},{10,8},{12,14},{14,12},{16,18},{18,... | collective-permute-start | bytes 9437192 | tf_op jit(solution)/shard_map/ppermute | solution.py:282
  276.5 1.5 copy-start
  278.0 60.5 %collective-permute-start.1 = (bf16[8,80,2048]{2,1,0:T(8,128)(2,1)}, bf16[8,80,2048]{2,1,0:T(8,128)(2,1)}, u32[]{:S(2)}, u32[]{:S(2)}) collective-permute-start(bf16[8,80,2048]{2,1,0:T(8,128)(2,1)} %get-tuple-element.10), channel_id=1, source_target_pairs={{0,4},{2,6},{4,0},{6,2},{8,12},{10,14},{12,8},{14,10},{16,20},{18,... | collective-permute-start | bytes 7864328 | tf_op jit(solution)/shard_map/ppermute | solution.py:285
  289.1 60.3 %collective-permute-start.9 = (bf16[2,2,48,2048]{3,2,1,0:T(8,128)(2,1)}, bf16[2,2,48,2048]{3,2,1,0:T(8,128)(2,1)}, u32[]{:S(2)}, u32[]{:S(2)}) collective-permute-start(bf16[2,2,48,2048]{3,2,1,0:T(8,128)(2,1)} %bitcast.16), channel_id=1, source_target_pairs={{0,8},{2,10},{4,12},{6,14},{1,9},{3,11},{5,13},{7,15}} | collective-permute-start | bytes 2359304 | tf_op jit(solution)/shard_map/ppermute | solution.py:288
  293.5 55.9 %collective-permute-start.12 = (bf16[2,2,48,2048]{3,2,1,0:T(8,128)(2,1)}, bf16[2,2,48,2048]{3,2,1,0:T(8,128)(2,1)}, u32[]{:S(2)}, u32[]{:S(2)}) collective-permute-start(bf16[2,2,48,2048]{3,2,1,0:T(8,128)(2,1)} %bitcast.20), channel_id=1, source_target_pairs={{24,16},{26,18},{28,20},{30,22},{25,17},{27,19},{29,21},{31,23}} | collective-permute-start | bytes 2359304 | tf_op jit(solution)/shard_map/ppermute | solution.py:288
  342.1 9.9 %copy-start.2 = (bf16[8,80,2048]{2,1,0:T(8,128)(2,1)}, bf16[8,80,2048]{2,1,0:T(8,128)(2,1)S(1)}, u32[]{:S(2)}) copy-start(bf16[8,80,2048]{2,1,0:T(8,128)(2,1)S(1)} %add.94) | copy-start | bytes 7864324
  343.5 12.3 %collective-permute-start.5 = (bf16[2,80,2048]{2,1,0:T(8,128)(2,1)}, bf16[2,80,2048]{2,1,0:T(8,128)(2,1)}, u32[]{:S(2)}, u32[]{:S(2)}) collective-permute-start(bf16[2,80,2048]{2,1,0:T(8,128)(2,1)} %get-tuple-element.46), channel_id=1, source_target_pairs={{24,16},{26,18},{28,20},{30,22},{25,17},{27,19},{29,21},{31,23}} | collective-permute-start | bytes 1966088 | tf_op jit(solution)/shard_map/ppermute | solution.py:288
  345.0 19.0 %collective-permute-start.2 = (bf16[2,80,2048]{2,1,0:T(8,128)(2,1)}, bf16[2,80,2048]{2,1,0:T(8,128)(2,1)}, u32[]{:S(2)}, u32[]{:S(2)}) collective-permute-start(bf16[2,80,2048]{2,1,0:T(8,128)(2,1)} %get-tuple-element.47), channel_id=1, source_target_pairs={{0,8},{2,10},{4,12},{6,14},{1,9},{3,11},{5,13},{7,15}} | collective-permute-start | bytes 1966088 | tf_op jit(solution)/shard_map/ppermute | solution.py:288
  352.0 21.3 %collective-permute-start.13 = (bf16[2,2,48,2048]{3,2,1,0:T(8,128)(2,1)}, bf16[2,2,48,2048]{3,2,1,0:T(8,128)(2,1)}, u32[]{:S(2)}, u32[]{:S(2)}) collective-permute-start(bf16[2,2,48,2048]{3,2,1,0:T(8,128)(2,1)} %get-tuple-element.38), channel_id=1, source_target_pairs={{16,8},{18,10},{20,12},{22,14},{24,16},{26,18},{28,20},{30,22},{17... | collective-permute-start | bytes 2359304 | tf_op jit(solution)/shard_map/ppermute | solution.py:288
  353.6 27.2 %collective-permute-start.10 = (bf16[2,2,48,2048]{3,2,1,0:T(8,128)(2,1)}, bf16[2,2,48,2048]{3,2,1,0:T(8,128)(2,1)}, u32[]{:S(2)}, u32[]{:S(2)}) collective-permute-start(bf16[2,2,48,2048]{3,2,1,0:T(8,128)(2,1)} %get-tuple-element.39), channel_id=1, source_target_pairs={{0,8},{2,10},{4,12},{6,14},{8,16},{10,18},{12,20},{14,22},{1,9},{3... | collective-permute-start | bytes 2359304 | tf_op jit(solution)/shard_map/ppermute | solution.py:288
  366.8 23.9 %collective-permute-start.6 = (bf16[2,80,2048]{2,1,0:T(8,128)(2,1)}, bf16[2,80,2048]{2,1,0:T(8,128)(2,1)}, u32[]{:S(2)}, u32[]{:S(2)}) collective-permute-start(bf16[2,80,2048]{2,1,0:T(8,128)(2,1)} %get-tuple-element.44), channel_id=1, source_target_pairs={{16,8},{18,10},{20,12},{22,14},{24,16},{26,18},{28,20},{30,22},{17... | collective-permute-start | bytes 1966088 | tf_op jit(solution)/shard_map/ppermute | solution.py:288
  368.3 26.5 %collective-permute-start.3 = (bf16[2,80,2048]{2,1,0:T(8,128)(2,1)}, bf16[2,80,2048]{2,1,0:T(8,128)(2,1)}, u32[]{:S(2)}, u32[]{:S(2)}) collective-permute-start(bf16[2,80,2048]{2,1,0:T(8,128)(2,1)} %get-tuple-element.45), channel_id=1, source_target_pairs={{0,8},{2,10},{4,12},{6,14},{8,16},{10,18},{12,20},{14,22},{1,9},{3... | collective-permute-start | bytes 1966088 | tf_op jit(solution)/shard_map/ppermute | solution.py:288
  383.5 21.4 %collective-permute-start.14 = (bf16[2,2,48,2048]{3,2,1,0:T(8,128)(2,1)}, bf16[2,2,48,2048]{3,2,1,0:T(8,128)(2,1)}, u32[]{:S(2)}, u32[]{:S(2)}) collective-permute-start(bf16[2,2,48,2048]{3,2,1,0:T(8,128)(2,1)} %get-tuple-element.36), channel_id=1, source_target_pairs={{8,0},{10,2},{12,4},{14,6},{16,8},{18,10},{20,12},{22,14},{24,16},... | collective-permute-start | bytes 2359304 | tf_op jit(solution)/shard_map/ppermute | solution.py:288
  384.8 26.9 %collective-permute-start.11 = (bf16[2,2,48,2048]{3,2,1,0:T(8,128)(2,1)}, bf16[2,2,48,2048]{3,2,1,0:T(8,128)(2,1)}, u32[]{:S(2)}, u32[]{:S(2)}) collective-permute-start(bf16[2,2,48,2048]{3,2,1,0:T(8,128)(2,1)} %get-tuple-element.37), channel_id=1, source_target_pairs={{0,8},{2,10},{4,12},{6,14},{8,16},{10,18},{12,20},{14,22},{16,24},... | collective-permute-start | bytes 2359304 | tf_op jit(solution)/shard_map/ppermute | solution.py:288
  397.7 23.4 %collective-permute-start.7 = (bf16[2,80,2048]{2,1,0:T(8,128)(2,1)}, bf16[2,80,2048]{2,1,0:T(8,128)(2,1)}, u32[]{:S(2)}, u32[]{:S(2)}) collective-permute-start(bf16[2,80,2048]{2,1,0:T(8,128)(2,1)} %get-tuple-element.42), channel_id=1, source_target_pairs={{8,0},{10,2},{12,4},{14,6},{16,8},{18,10},{20,12},{22,14},{24,16},... | collective-permute-start | bytes 1966088 | tf_op jit(solution)/shard_map/ppermute | solution.py:288
  399.0 24.9 %collective-permute-start.4 = (bf16[2,80,2048]{2,1,0:T(8,128)(2,1)}, bf16[2,80,2048]{2,1,0:T(8,128)(2,1)}, u32[]{:S(2)}, u32[]{:S(2)}) collective-permute-start(bf16[2,80,2048]{2,1,0:T(8,128)(2,1)} %get-tuple-element.43), channel_id=1, source_target_pairs={{0,8},{2,10},{4,12},{6,14},{8,16},{10,18},{12,20},{14,22},{16,24},... | collective-permute-start | bytes 1966088 | tf_op jit(solution)/shard_map/ppermute | solution.py:288
  413.3 7.8 collective-permute-start.15
  423.9 1.6 copy-start.1
  428.6 5.0 collective-permute-start.16
Sparse Core Ops, SparseCore 0:
  439.1 127.3 all-gather.1

commit v2 on v1

--- a/solution.py
+++ b/solution.py
@@ -23,113 +23,90 @@
 VMEM_BYTES = 48 * 1024 * 1024
 
 
-def copy_blocks(count, first, rows, idx_ref, src_ref, out_ref, sem):
-    def copy(i):
+def combine_kernel(plans, arrays, table_ref, *refs):
+    sources = refs[:arrays]
+    outs = refs[len(refs) - 3 * len(plans) : len(refs) - 2 * len(plans)]
+    held = refs[len(refs) - 2 * len(plans) : len(refs) - len(plans)]
+    sems = refs[len(refs) - len(plans) :]
+
+    def load(p, t, i):
+        count, rows, terms = plans[p]
+        at, first, offset = terms[t]
         return pltpu.make_async_copy(
-            src_ref.at[idx_ref[i], pl.ds(first, rows)], out_ref.at[i], sem.at[i]
-        )
-
-    def start(i, _):
-        copy(i).start()
-        return 0
-
-    def wait(i, _):
-        copy(i).wait()
-        return 0
-
-    lax.fori_loop(0, count, start, 0)
-    lax.fori_loop(0, count, wait, 0)
-
-
-def take_blocks(src, idx, first, rows):
-    count = idx.shape[0]
-    cols = src.shape[2]
-    size = count * rows * cols * src.dtype.itemsize
+            sources[at].at[table_ref[offset + i], pl.ds(first, rows)],
+            held[p].at[t, i],
+            sems[p].at[t, i],
+        )
+
+    def leave(p, i):
+        return pltpu.make_async_copy(
+            held[p].at[0, i], outs[p].at[i], sems[p].at[len(plans[p][2]), i]
+        )
+
+    for p, (count, _, terms) in enumerate(plans):
+
+        @pl.loop(0, count)
+        def _(i, p=p, terms=terms):
+            for t in range(len(terms)):
+                load(p, t, i).start()
+
+    for p, (count, _, terms) in enumerate(plans):
+
+        @pl.loop(0, count)
+        def _(i, p=p, terms=terms):
+            for t in range(len(terms)):
+                load(p, t, i).wait()
+            if len(terms) > 1:
+                total = held[p][0, i].astype(jnp.float32)
+                for t in range(1, len(terms)):
+                    total = total + held[p][t, i].astype(jnp.float32)
+                held[p][0, i] = total.astype(held[p].dtype)
+            leave(p, i).start()
+
+    for p, (count, _, _) in enumerate(plans):
+
+        @pl.loop(0, count)
+        def _(i, p=p):
+            leave(p, i).wait()
+
+
+def combine(after, *wanted):
+    arrays, tables, plans, offset, size = [], [], [], 0, 0
+    for rows, terms in wanted:
+        found = []
+        for array, items, first in terms:
+            places = [i for i, a in enumerate(arrays) if a is array]
+            if not places:
+                arrays.append(array)
+                places = [len(arrays) - 1]
+            found.append((places[0], first, offset))
+            tables.append(jnp.asarray(items, jnp.int32).reshape(-1))
+            offset += tables[-1].shape[0]
+        count = tables[-1].shape[0]
+        plans.append((count, rows, tuple(found)))
+        size += (len(found) + 1) * count * rows
+    cols, kind = arrays[0].shape[2], arrays[0].dtype
+    size *= cols * kind.itemsize
     return pl.pallas_call(
-        functools.partial(copy_blocks, count, first, rows),
-        out_shape=jax.ShapeDtypeStruct((count, rows, cols), src.dtype),
-        in_specs=[
-            pl.BlockSpec(memory_space=pltpu.SMEM),
-            pl.BlockSpec(memory_space=pl.ANY),
+        functools.partial(combine_kernel, tuple(plans), len(arrays)),
+        out_shape=[
+            jax.ShapeDtypeStruct((count, rows, cols), kind) for count, rows, _ in plans
         ],
-        out_specs=pl.BlockSpec(memory_space=pl.ANY),
-        scratch_shapes=[pltpu.SemaphoreType.DMA((count,))],
-        cost_estimate=pl.CostEstimate(flops=0, bytes_accessed=2 * size, transcendentals=0),
-    )(idx, src)
-
-
-def sum_blocks(count, first, rows, outs, idx_ref, src_ref, other_ref, *rest):
-    out_refs = rest[:outs]
-    mine, sums, sem_mine, sem_other, sem_out = rest[outs:]
-    each = count // outs
-
-    def copies(i):
-        return (
-            pltpu.make_async_copy(
-                src_ref.at[idx_ref[i], pl.ds(first, rows)], mine.at[i], sem_mine.at[i]
-            ),
-            pltpu.make_async_copy(other_ref.at[i], sums.at[i], sem_other.at[i]),
-        )
-
-    def start(i, _):
-        for c in copies(i):
-            c.start()
-        return 0
-
-    lax.fori_loop(0, count, start, 0)
-    for part, out_ref in enumerate(out_refs):
-
-        def leave(i, part=part, out_ref=out_ref):
-            return pltpu.make_async_copy(
-                sums.at[part * each + i], out_ref.at[i], sem_out.at[part * each + i]
-            )
-
-        def body(i, _, part=part, leave=leave):
-            at = part * each + i
-            for c in copies(at):
-                c.wait()
-            sums[at] = sums[at] + mine[at]
-            leave(i).start()
-            return 0
-
-        lax.fori_loop(0, each, body, 0)
-    for part, out_ref in enumerate(out_refs):
-
-        def finish(i, _, part=part, out_ref=out_ref):
-            pltpu.make_async_copy(
-                sums.at[part * each + i], out_ref.at[i], sem_out.at[part * each + i]
-            ).wait()
-            return 0
-
-        lax.fori_loop(0, each, finish, 0)
-
-
-def add_taken(src, idx, first, rows, other, outs):
-    count = idx.shape[0]
-    cols = src.shape[2]
-    size = count * rows * cols * src.dtype.itemsize
-    each = jax.ShapeDtypeStruct((count // outs, rows, cols), src.dtype)
-    return pl.pallas_call(
-        functools.partial(sum_blocks, count, first, rows, outs),
-        out_shape=[each] * outs,
-        in_specs=[
-            pl.BlockSpec(memory_space=pltpu.SMEM),
-            pl.BlockSpec(memory_space=pl.ANY),
-            pl.BlockSpec(memory_space=pl.ANY),
-        ],
-        out_specs=[pl.BlockSpec(memory_space=pl.ANY)] * outs,
+        in_specs=[pl.BlockSpec(memory_space=pltpu.SMEM)]
+        + [pl.BlockSpec(memory_space=pl.ANY)] * (len(arrays) + len(after)),
+        out_specs=[pl.BlockSpec(memory_space=pl.ANY)] * len(plans),
         scratch_shapes=[
-            pltpu.VMEM((count, rows, cols), src.dtype),
-            pltpu.VMEM((count, rows, cols), src.dtype),
-            pltpu.SemaphoreType.DMA((count,)),
-            pltpu.SemaphoreType.DMA((count,)),
-            pltpu.SemaphoreType.DMA((count,)),
+            pltpu.VMEM((len(terms), count, rows, cols), kind)
+            for count, rows, terms in plans
+        ]
+        + [
+            pltpu.SemaphoreType.DMA((len(terms) + 1, count)) for count, _, terms in plans
         ],
         compiler_params=pltpu.CompilerParams(vmem_limit_bytes=VMEM_BYTES),
         cost_estimate=pl.CostEstimate(
-            flops=size // 2, bytes_accessed=3 * size, transcendentals=0
+            flops=size // 4, bytes_accessed=size, transcendentals=0
         ),
-    )(idx, src, other)
+    )(jnp.concatenate(tables), *arrays, *after)
 
 
 def momentum_kernel(scale, sizes, held_ref, momentum_ref, *rest):
@@ -292,58 +269,132 @@
         )
 
 
-def chain_sum(place, blocks):
-    depth = place.depth
-
-    def own(at):
-        return lax.dynamic_index_in_dim(blocks, jnp.clip(at, 0, depth - 1), 0, False)
-
-    up, down = blocks[depth - 1], blocks[0]
-    for t in range(1, depth):
-        up = place.shift_z(up, 1, range(0, t))
-        down = place.shift_z(down, -1, range(depth - t, depth))
-        if t + 1 < depth:
-            up = up + own(depth - 1 - t + place.z)
-            down = down + own(t - (depth - 1) + place.z)
-    return up, down, own(place.z)
-
-
-def reduce_to_owners(place, gradient, source, slot_count, shares):
-    cols = gradient.shape[2]
-    core_first = jnp.take(source, place.core, axis=2)
-    other_core = jnp.take(source, 1 - place.core, axis=2)
-
-    def ordered(table, x_first):
-        if not x_first:
+class Flow:
+    def __init__(self, place, gradient, source, slots, first, rows, x_first):
+        self.place, self.gradient, self.slots = place, gradient, slots
+        self.first, self.rows, self.x_first = first, rows, x_first
+        self.mine = jnp.take(source, place.core, axis=2)
+        self.theirs = jnp.take(source, 1 - place.core, axis=2)
+        self.group = slots if x_first else slots * PAIR
+        self.step = 0
+
+    def ordered(self, table):
+        if not self.x_first:
             return table.reshape(-1)
-        away = jnp.take(table, 1 - place.x, axis=1)
-        home = jnp.take(table, place.x, axis=1)
+        away = jnp.take(table, 1 - self.place.x, axis=1)
+        home = jnp.take(table, self.place.x, axis=1)
         return jnp.concatenate([away.reshape(-1), home.reshape(-1)])
 
-    first = 0
-    received = []
-    for rows, x_first in shares:
-        sent = take_blocks(gradient, ordered(other_core, x_first), first, rows)
-        received.append((first, rows, x_first, place.swap_cores(sent)))
-        first += rows
-    results = []
-    for first, rows, x_first, other in received:
-        mine = ordered(core_first, x_first)
-        if x_first:
-            away, home = add_taken(gradient, mine, first, rows, other, 2)
-            blocks = home + place.swap_x(away)
-            blocks = blocks.reshape(place.depth, slot_count, rows, cols)
-            results.append(chain_sum(place, blocks))
-        else:
-            (blocks,) = add_taken(gradient, mine, first, rows, other, 1)
-            blocks = blocks.reshape(place.depth, PAIR, slot_count, rows, cols)
-            up, down, own = chain_sum(place, blocks)
-            both = up + down + own
-            away = lax.dynamic_index_in_dim(both, 1 - place.x, 0, False)
-            home = lax.dynamic_index_in_dim(both, place.x, 0, False)
-            got = place.swap_x(away)
-            results.append((home, got))
-    return results
+    def block(self, at):
+        at = jnp.clip(at, 0, self.place.depth - 1)
+        return at * self.group + jnp.arange(self.group, dtype=jnp.int32)
+
+    def every(self, array):
+        return jnp.arange(array.shape[0], dtype=jnp.int32)
+
+    def pack(self, after):
+        term = (self.gradient, self.ordered(self.theirs), self.first)
+        (sent,) = combine(after, (self.rows, [term]))
+        self.got = self.place.swap_cores(sent)
+        return [sent]
+
+    def add_core(self, after):
+        items = self.ordered(self.mine)
+        count = items.shape[0]
+        half = count // 2
+        ids = jnp.arange(count, dtype=jnp.int32)
+
+        def part(a, b):
+            return (
+                self.rows,
+                [(self.gradient, items[a:b], self.first), (self.got, ids[a:b], 0)],
+            )
+
+        if self.x_first:
+            away, self.home = combine(after, part(0, half), part(half, count))
+            self.got = self.place.swap_x(away)
+            return [away]
+        (self.blocks,) = combine(after, part(0, count))
+        self.send_first()
+        return [self.blocks]
+
+    def send_first(self):
+        depth, group = self.place.depth, self.group
+        self.up = self.blocks[(depth - 1) * group :]
+        self.down = self.blocks[:group]
+        self.send()
+
+    def send(self):
+        self.step += 1
+        t, depth = self.step, self.place.depth
+        self.up = self.place.shift_z(self.up, 1, range(0, t))
+        self.down = self.place.shift_z(self.down, -1, range(depth - t, depth))
+
+    def add_x(self, after):
+        ids = self.every(self.home)
+        (self.blocks,) = combine(
+            after, (self.rows, [(self.home, ids, 0), (self.got, ids, 0)])
+        )
+        self.send_first()
+        return [self.blocks]
+
+    def add_z(self, after):
+        t, z, depth = self.step, self.place.z, self.place.depth
+        ids = jnp.arange(self.group, dtype=jnp.int32)
+        self.up, self.down = combine(
+            after,
+            (self.rows, [(self.up, ids, 0), (self.blocks, self.block(depth - 1 - t + z), 0)]),
+            (self.rows, [(self.down, ids, 0), (self.blocks, self.block(t - depth + 1 + z), 0)]),
+        )
+        made = [self.up]
+        self.send()
+        return made
+
+    def last_z(self, after):
+        slots, x = self.slots, self.place.x
+        ids = jnp.arange(slots, dtype=jnp.int32)
+
+        def part(x):
+            return (
+                self.rows,
+                [
+                    (self.up, x * slots + ids, 0),
+                    (self.down, x * slots + ids, 0),
+                    (self.blocks, self.block(self.place.z)[: slots] + x * slots, 0),
+                ],
+            )
+
+        away, self.home = combine(after, part(1 - x), part(x))
+        self.got = self.place.swap_x(away)
+        return [away]
+
+    def sums(self):
+        if not self.x_first:
+            return [self.home, self.got]
+        rows, cols = self.blocks.shape[1:]
+        own = self.blocks.reshape(self.place.depth, self.slots, rows, cols)
+        own = lax.dynamic_index_in_dim(own, self.place.z, 0, False)
+        return [self.up, self.down, own]
+
+
+def reduce_to_owners(place, gradient, source, slots):
+    rows = gradient.shape[1]
+    unit = rows // 8
+    make = functools.partial(Flow, place, gradient, source, slots)
+    b = make(0, 3 * unit, False)
+    a = make(3 * unit, 3 * unit, True)
+    c = make(6 * unit, 2 * unit, True)
+    order = [b.pack, a.pack, c.pack, b.add_core, a.add_core]
+    steps = place.depth - 2
+    order += [b.add_z] * steps
+    order += [c.add_core, a.add_x, b.last_z]
+    order += [a.add_z] * steps
+    order += [c.add_x]
+    order += [c.add_z] * steps
+    after = []
+    for work in order:
+        after = work(after)
+    return [flow.sums() for flow in (b, a, c)]
 
 
 def per_device(grads, owner, momentum):
@@ -367,9 +418,7 @@
         filled, lax.axis_index("dp") * slot_count, slot_count, 0
     )
 
-    cut = head_rows * 5 // 8
-    shares = ((cut, True), (head_rows - cut, False))
-    parts = reduce_to_owners(place, grads[0], source, slot_count, shares)
+    parts = reduce_to_owners(place, grads[0], source, slot_count)
     new_momentum, rounded, gram = momentum_step(held, momentum[0], parts, owner_count)
 
     width = lax.axis_size("tensor")
@@ -382,7 +431,7 @@
         )
     result = orthogonalize(grams, rounded, factor)
     everything = lax.all_gather(result, "dp", axis=0, tiled=True)
-    update = take_blocks(everything, spot, 0, head_rows)
+    (update,) = combine([], (head_rows, [(everything, spot, 0)]))
     return (update, new_momentum[None])
 
 

time: 957 us -> 338 us (0.35)
  Pallas kernels: 663 us -> 85.5 us
  waiting for transfers between devices: 209 us -> 170 us
  starting transfers between devices: 43.5 us -> 59.9 us
  other arithmetic: 18.6 us -> 2.21 us
    pallas_call x5 -> x16, Pallas kernels: 654 us -> 77.5 us  [combine(): pl.pallas_call(functools.partial(combine_kernel, tuple(plans), len(arrays...]
    ppermute x2 -> x3, waiting for transfers between devices: 48.3 us -> 0.01 us  [swap_x(): return lax.ppermute(value, 'dp', self.pairs(lambda z, x, c: (z, 1 - x, c)))]
    ppermute x12 -> x18, starting transfers between devices: 36.5 us -> 53.8 us  [shift_z(): lax.ppermute(value, 'dp', self.pairs(lambda z, x, c: (z + step, x, c) if...]
    add x6 -> x7, other arithmetic: 16.1 us -> 0.03 us  [the longest x5 0.02 us: block(): return at * self.group + jnp.arange(self.group, dtype=jnp.int32)]
    ppermute x12 -> x18, waiting for transfers between devices: 29.4 us -> 41.1 us  [shift_z(): lax.ppermute(value, 'dp', self.pairs(lambda z, x, c: (z + step, x, c) if...]
  transfers between devices with their start and end apart: 18 -> 26, of which waited for: 9 -> 9; matrix products, arithmetic and copies ran while one was open for 2% -> 1% of each run, Pallas kernels for 12% -> 16%
where the time goes in v2:
time: 338 us; the launch traced here: 337 us
  waiting for transfers between devices  170 us (50%)
  Pallas kernels  85.5 us (25%)
  starting transfers between devices  59.9 us (18%)
  between operations  14.5 us (4%)
  local copies, waits for them, and re-layouts  5.08 us (2%)
    all_gather x1, waiting for transfers between devices, per_device(): everything = lax.all_gather(result, 'dp', axis=0, tiled=True)  125 us
    pallas_call x16, Pallas kernels, combine(): pl.pallas_call(functools.partial(combine_kernel, tuple(plans), len(arrays...  77.5 us
    ppermute x18, starting transfers between devices, shift_z(): lax.ppermute(value, 'dp', self.pairs(lambda z, x, c: (z + step, x, c) if...  53.8 us
    ppermute x18, waiting for transfers between devices, shift_z(): lax.ppermute(value, 'dp', self.pairs(lambda z, x, c: (z + step, x, c) if...  41.1 us
  transfers between devices with their start and end apart: 26, of which 9 were waited for; matrix products, arithmetic and copies ran while one was open for 1% of the time, Pallas kernels for 16%

profile of v2, /device:TPU:0, one launch (start us, length us, event | category | flops | bytes accessed | tf_op | source)
XLA Modules:
  0.0 337.1 jit_solution(1877111528597067610)
XLA Ops:
  9.1 6.0 %shard_map.50.refs_1_ = bf16[16,48,2048]{2,1,0:T(8,128)(2,1)S(1)} custom-call(s32[16]{0:T(128)S(1)} %reshape.42.table_ref, bf16[24,128,2048]{2,1,0:T(8,128)(2,1)} %bitcast.29), custom_call_target="tpu_custom_call" | custom-call | flops 1572864 | bytes 6291456 | tf_op jit(solution)/shard_map/pallas_call | solution.py:90
  16.8 4.1 %shard_map.51.refs_1_ = bf16[16,48,2048]{2,1,0:T(8,128)(2,1)} custom-call(s32[16]{0:T(128)S(1)} %pad_add_fusion.3.table_ref, bf16[24,128,2048]{2,1,0:T(8,128)(2,1)} %bitcast.30, bf16[16,48,2048]{2,1,0:T(8,128)(2,1)} %copy-done.1), custom_call_target="tpu_custom_call" | custom-call | flops 1572864 | bytes 6291456 | tf_op jit(solution)/shard_map/pallas_call | solution.py:90
  21.7 3.5 %shard_map.52.refs_2_ = bf16[16,32,2048]{2,1,0:T(8,128)(2,1)} custom-call(s32[16]{0:T(128)S(1)} %pad_add_fusion.3.table_ref, bf16[24,128,2048]{2,1,0:T(8,128)(2,1)} %bitcast.31, bf16[16,48,2048]{2,1,0:T(8,128)(2,1)} %shard_map.51.refs_1_), custom_call_target="tpu_custom_call" | custom-call | flops 1048576 | bytes 4194304 | tf_op jit(solution)/shard_map/pallas_call | solution.py:90
  26.3 7.0 %shard_map.53.refs_2_.refs_1_ = bf16[16,48,2048]{2,1,0:T(8,128)(2,1)S(1)} custom-call(s32[32]{0:T(128)S(1)} %get-tuple-element.86.table_ref, bf16[24,128,2048]{2,1,0:T(8,128)(2,1)} %bitcast.32, bf16[16,48,2048]{2,1,0:T(8,128)(2,1)} %collective-permute-done.refs_1_, bf16[16,32,2048]{2,1,0:T(8,128)(2,1)} %shard_map.52.refs_2_), custom_call_target="tpu_custom_call" | custom-call | flops 2359296 | bytes 9437184 | tf_op jit(solution)/shard_map/pallas_call | solution.py:90
  35.2 5.5 %collective-permute-start.1 = (bf16[4,48,2048]{2,1,0:T(8,128)(2,1)S(1)}, bf16[4,48,2048]{2,1,0:T(8,128)(2,1)}, u32[]{:S(2)}, u32[]{:S(2)}) collective-permute-start(bf16[4,48,2048]{2,1,0:T(8,128)(2,1)S(1)} %get-tuple-element.69), channel_id=1, source_target_pairs={{0,8},{2,10},{4,12},{6,14},{1,9},{3,11},{5,13},{7,15}} | collective-permute-start | bytes 2359304 | tf_op jit(solution)/shard_map/ppermute | solution.py:265
  40.8 6.7 %shard_map.54 = (bf16[8,48,2048]{2,1,0:T(8,128)(2,1)}, bf16[8,48,2048]{2,1,0:T(8,128)(2,1)S(1)}) custom-call(s32[32]{0:T(128)S(1)} %get-tuple-element.87.table_ref, bf16[24,128,2048]{2,1,0:T(8,128)(2,1)} %bitcast.33, bf16[16,48,2048]{2,1,0:T(8,128)(2,1)} %collective-permute-done.3.refs_1_, bf16[16,48,2048]{2,1,0:T(8,128)(2,1)} %copy-done), custom_call_target="tpu_custom_call" | custom-call | flops 2359296 | bytes 9437184 | tf_op jit(solution)/shard_map/pallas_call | solution.py:90
  49.4 7.5 %collective-permute-done.1.refs_0_ = bf16[4,48,2048]{2,1,0:T(8,128)(2,1)} collective-permute-done((bf16[4,48,2048]{2,1,0:T(8,128)(2,1)S(1)}, bf16[4,48,2048]{2,1,0:T(8,128)(2,1)}, u32[]{:S(2)}, u32[]{:S(2)}) %collective-permute-start.1) | collective-permute-done | bytes 786464 | tf_op jit(solution)/shard_map/ppermute | solution.py:265
  56.9 3.9 %shard_map.55 = (bf16[4,48,2048]{2,1,0:T(8,128)(2,1)S(1)}, bf16[4,48,2048]{2,1,0:T(8,128)(2,1)}) custom-call(s32[16]{0:T(128)S(1)} %get-tuple-element.82.table_ref, bf16[4,48,2048]{2,1,0:T(8,128)(2,1)} %collective-permute-done.1.refs_0_, bf16[16,48,2048]{2,1,0:T(8,128)(2,1)} %copy-done, bf16[4,48,2048]{2,1,0:T(8,128)(2,1)} %collective-permute-done.2.refs_2_, ...), custom_call_target="tpu_custom_call" | custom-call | flops 1179648 | bytes 4718592 | tf_op jit(solution)/shard_map/pallas_call | solution.py:90
  61.5 5.9 %collective-permute-start.4 = (bf16[4,48,2048]{2,1,0:T(8,128)(2,1)S(1)}, bf16[4,48,2048]{2,1,0:T(8,128)(2,1)}, u32[]{:S(2)}, u32[]{:S(2)}) collective-permute-start(bf16[4,48,2048]{2,1,0:T(8,128)(2,1)S(1)} %get-tuple-element.26.refs_3_), channel_id=1, source_target_pairs={{0,8},{2,10},{4,12},{6,14},{8,16},{10,18},{12,20},{14,22},{1,9},{3... | collective-permute-start | bytes 2359304 | tf_op jit(solution)/shard_map/ppermute | solution.py:265
  67.6 15.2 %collective-permute-done.4.refs_0_ = bf16[4,48,2048]{2,1,0:T(8,128)(2,1)} collective-permute-done((bf16[4,48,2048]{2,1,0:T(8,128)(2,1)S(1)}, bf16[4,48,2048]{2,1,0:T(8,128)(2,1)}, u32[]{:S(2)}, u32[]{:S(2)}) %collective-permute-start.4) | collective-permute-done | bytes 786464 | tf_op jit(solution)/shard_map/ppermute | solution.py:265
  82.7 3.6 %shard_map.56 = (bf16[4,48,2048]{2,1,0:T(8,128)(2,1)}, bf16[4,48,2048]{2,1,0:T(8,128)(2,1)}) custom-call(s32[16]{0:T(128)S(1)} %get-tuple-element.83.table_ref, bf16[4,48,2048]{2,1,0:T(8,128)(2,1)} %collective-permute-done.4.refs_0_, bf16[16,48,2048]{2,1,0:T(8,128)(2,1)} %copy-done, bf16[4,48,2048]{2,1,0:T(8,128)(2,1)S(1)} %collective-permute-done.5.refs_2_, ...), custom_call_target="tpu_custom_call" | custom-call | flops 1179648 | bytes 4718592 | tf_op jit(solution)/shard_map/pallas_call | solution.py:90
  87.7 6.2 %collective-permute-start.6 = (bf16[4,48,2048]{2,1,0:T(8,128)(2,1)}, bf16[4,48,2048]{2,1,0:T(8,128)(2,1)}, u32[]{:S(2)}, u32[]{:S(2)}) collective-permute-start(bf16[4,48,2048]{2,1,0:T(8,128)(2,1)} %get-tuple-element.28.refs_2_), channel_id=1, source_target_pairs={{0,8},{2,10},{4,12},{6,14},{8,16},{10,18},{12,20},{14,22},{16,24},... | collective-permute-start | bytes 2359304 | tf_op jit(solution)/shard_map/ppermute | solution.py:265
  93.9 5.0 %shard_map.57 = (bf16[8,32,2048]{2,1,0:T(8,128)(2,1)}, bf16[8,32,2048]{2,1,0:T(8,128)(2,1)S(1)}) custom-call(s32[32]{0:T(128)S(1)} %get-tuple-element.87.table_ref, bf16[24,128,2048]{2,1,0:T(8,128)(2,1)} %bitcast.34, bf16[16,32,2048]{2,1,0:T(8,128)(2,1)} %collective-permute-done.9.refs_1_, bf16[4,48,2048]{2,1,0:T(8,128)(2,1)} %get-tuple-element.28.refs_2_), custom_call_target="tpu_custom_call" | custom-call | flops 1572864 | bytes 6291456 | tf_op jit(solution)/shard_map/pallas_call | solution.py:90
  99.9 7.4 %shard_map.58.refs_3_.refs_1_ = bf16[8,48,2048]{2,1,0:T(8,128)(2,1)S(1)} custom-call(s32[16]{0:T(128)S(1)} %pad_add_fusion.5.table_ref, bf16[8,48,2048]{2,1,0:T(8,128)(2,1)S(1)} %copy-done.4, bf16[8,48,2048]{2,1,0:T(8,128)(2,1)S(1)} %collective-permute-done.8.refs_1_, bf16[8,32,2048]{2,1,0:T(8,128)(2,1)} %get-tuple-element.31.refs_2_), custom_call_target="tpu_custom_call" | custom-call | flops 1179648 | bytes 4718592 | tf_op jit(solution)/shard_map/pallas_call | solution.py:90
  109.0 3.4 collective-permute-start.11
  112.5 3.2 shard_map.59
  118.2 4.0 %shard_map.60 = (bf16[2,48,2048]{2,1,0:T(8,128)(2,1)S(1)}, bf16[2,48,2048]{2,1,0:T(8,128)(2,1)S(1)}) custom-call(s32[8]{0:T(128)S(1)} %get-tuple-element.80.table_ref, bf16[2,48,2048]{2,1,0:T(8,128)(2,1)S(1)} %collective-permute-done.11.refs_0_, bf16[8,48,2048]{2,1,0:T(8,128)(2,1)S(1)} %shard_map.58.refs_3_.refs_1_, ...), custom_call_target="tpu_custom_call" | custom-call | flops 589824 | bytes 2359296 | tf_op jit(solution)/shard_map/pallas_call | solution.py:90
  122.8 4.9 %collective-permute-start.13 = (bf16[2,48,2048]{2,1,0:T(8,128)(2,1)S(1)}, bf16[2,48,2048]{2,1,0:T(8,128)(2,1)S(1)}, u32[]{:S(2)}, u32[]{:S(2)}) collective-permute-start(bf16[2,48,2048]{2,1,0:T(8,128)(2,1)S(1)} %get-tuple-element.34.refs_3_), channel_id=1, source_target_pairs={{0,8},{2,10},{4,12},{6,14},{8,16},{10,18},{12,20},{14,22},{1,9},{3... | collective-permute-start | bytes 1179656 | tf_op jit(solution)/shard_map/ppermute | solution.py:265
  127.8 5.2 %collective-permute-done.13.refs_0_ = bf16[2,48,2048]{2,1,0:T(8,128)(2,1)S(1)} collective-permute-done((bf16[2,48,2048]{2,1,0:T(8,128)(2,1)S(1)}, bf16[2,48,2048]{2,1,0:T(8,128)(2,1)S(1)}, u32[]{:S(2)}, u32[]{:S(2)}) %collective-permute-start.13) | collective-permute-done | bytes 393248 | tf_op jit(solution)/shard_map/ppermute | solution.py:265
  133.0 4.0 %shard_map.61 = (bf16[2,48,2048]{2,1,0:T(8,128)(2,1)S(1)}, bf16[2,48,2048]{2,1,0:T(8,128)(2,1)S(1)}) custom-call(s32[8]{0:T(128)S(1)} %get-tuple-element.81.table_ref, bf16[2,48,2048]{2,1,0:T(8,128)(2,1)S(1)} %collective-permute-done.13.refs_0_, bf16[8,48,2048]{2,1,0:T(8,128)(2,1)S(1)} %shard_map.58.refs_3_.refs_1_, ...), custom_call_target="tpu_custom_call" | custom-call | flops 589824 | bytes 2359296 | tf_op jit(solution)/shard_map/pallas_call | solution.py:90
  137.7 3.9 %shard_map.62.refs_1_.refs_3_ = bf16[8,32,2048]{2,1,0:T(8,128)(2,1)S(1)} custom-call(s32[16]{0:T(128)S(1)} %pad_add_fusion.5.table_ref, bf16[8,32,2048]{2,1,0:T(8,128)(2,1)S(1)} %copy-done.6, bf16[8,32,2048]{2,1,0:T(8,128)(2,1)} %collective-permute-done.17.refs_1_, bf16[2,48,2048]{2,1,0:T(8,128)(2,1)S(1)} %get-tuple-element.36.refs_2_), custom_call_target="tpu_custom_call" | custom-call | flops 786432 | bytes 3145728 | tf_op jit(solution)/shard_map/pallas_call | solution.py:90
  142.4 4.6 %collective-permute-start.18 = (bf16[2,32,2048]{2,1,0:T(8,128)(2,1)S(1)}, bf16[2,32,2048]{2,1,0:T(8,128)(2,1)S(1)}, u32[]{:S(2)}, u32[]{:S(2)}) collective-permute-start(bf16[2,32,2048]{2,1,0:T(8,128)(2,1)S(1)} %get-tuple-element.73), channel_id=1, source_target_pairs={{0,8},{2,10},{4,12},{6,14},{1,9},{3,11},{5,13},{7,15}} | collective-permute-start | bytes 786440 | tf_op jit(solution)/shard_map/ppermute | solution.py:265
  147.0 3.8 %collective-permute-done.18.refs_0_ = bf16[2,32,2048]{2,1,0:T(8,128)(2,1)S(1)} collective-permute-done((bf16[2,32,2048]{2,1,0:T(8,128)(2,1)S(1)}, bf16[2,32,2048]{2,1,0:T(8,128)(2,1)S(1)}, u32[]{:S(2)}, u32[]{:S(2)}) %collective-permute-start.18) | collective-permute-done | bytes 262176 | tf_op jit(solution)/shard_map/ppermute | solution.py:265
  150.8 2.9 shard_map.63
  155.1 5.0 %collective-permute-start.20 = (bf16[2,32,2048]{2,1,0:T(8,128)(2,1)}, bf16[2,32,2048]{2,1,0:T(8,128)(2,1)}, u32[]{:S(2)}, u32[]{:S(2)}) collective-permute-start(bf16[2,32,2048]{2,1,0:T(8,128)(2,1)} %get-tuple-element.39.refs_3_), channel_id=1, source_target_pairs={{0,8},{2,10},{4,12},{6,14},{8,16},{10,18},{12,20},{14,22},{1,9},{3... | collective-permute-start | bytes 786440 | tf_op jit(solution)/shard_map/ppermute | solution.py:265
  161.6 3.9 %collective-permute-start.15 = (bf16[2,48,2048]{2,1,0:T(8,128)(2,1)}, bf16[2,48,2048]{2,1,0:T(8,128)(2,1)S(1)}, u32[]{:S(2)}, u32[]{:S(2)}) collective-permute-start(bf16[2,48,2048]{2,1,0:T(8,128)(2,1)} %copy-done.7), channel_id=1, source_target_pairs={{0,8},{2,10},{4,12},{6,14},{8,16},{10,18},{12,20},{14,22},{16,24},... | collective-permute-start | bytes 1179656 | tf_op jit(solution)/shard_map/ppermute | solution.py:265
  169.2 4.6 %collective-permute-start.22 = (bf16[2,32,2048]{2,1,0:T(8,128)(2,1)S(1)}, bf16[2,32,2048]{2,1,0:T(8,128)(2,1)S(1)}, u32[]{:S(2)}, u32[]{:S(2)}) collective-permute-start(bf16[2,32,2048]{2,1,0:T(8,128)(2,1)S(1)} %get-tuple-element.41), channel_id=1, source_target_pairs={{0,8},{2,10},{4,12},{6,14},{8,16},{10,18},{12,20},{14,22},{16,24},... | collective-permute-start | bytes 786440 | tf_op jit(solution)/shard_map/ppermute | solution.py:265
  177.8 4.2 %collective-permute-done.23.rest_6_ = bf16[2,32,2048]{2,1,0:T(8,128)(2,1)S(1)} collective-permute-done((bf16[2,32,2048]{2,1,0:T(8,128)(2,1)S(1)}, bf16[2,32,2048]{2,1,0:T(8,128)(2,1)S(1)}, u32[]{:S(2)}, u32[]{:S(2)}) %collective-permute-start.23) | collective-permute-done | bytes 262176 | tf_op jit(solution)/shard_map/ppermute | solution.py:265
  186.1 3.4 %collective-permute-done.24.refs_1_ = f32[2,128,128]{2,1,0:T(8,128)S(1)} collective-permute-done((f32[2,128,128]{2,1,0:T(8,128)S(1)}, f32[2,128,128]{2,1,0:T(8,128)S(1)}, u32[]{:S(2)}, u32[]{:S(2)}) %collective-permute-start.24) | collective-permute-done | bytes 131104 | tf_op jit(solution)/shard_map/ppermute | solution.py:428
  189.6 5.4 %shard_map.66 = bf16[2,128,2048]{2,1,0:T(8,128)(2,1)} custom-call(f32[2,128,128]{2,1,0:T(8,128)S(1)} %get-tuple-element.43.refs_0_, f32[2,128,128]{2,1,0:T(8,128)S(1)} %collective-permute-done.24.refs_1_, bf16[2,128,2048]{2,1,0:T(8,128)(2,1)S(1)} %get-tuple-element.44.refs_2_), custom_call_target="tpu_custom_call" | custom-call | flops 1275068416 | bytes 2097152 | tf_op jit(solution)/shard_map/pallas_call | solution.py:219
  195.0 125.3 %all-gather.2.cloned.1.call-done.refs_0_ = bf16[32,128,2048]{2,1,0:T(8,128)(2,1)} async-done(((bf16[2,128,2048]{2,1,0:T(8,128)(2,1)}), bf16[32,128,2048]{2,1,0:T(8,128)(2,1)}) %all-gather.2.cloned.1.call-update) | async-done | bytes 16777232 | tf_op jit(solution)/shard_map/all_gather | solution.py:433
  320.3 10.0 %shard_map.67 = bf16[24,128,2048]{2,1,0:T(8,128)(2,1)} custom-call(s32[24]{0:T(128)S(1)} %multiply_add_fusion.table_ref, bf16[32,128,2048]{2,1,0:T(8,128)(2,1)} %all-gather.2.cloned.1.call-done.refs_0_), custom_call_target="tpu_custom_call" | custom-call | flops 6291456 | bytes 25165824 | tf_op jit(solution)/shard_map/pallas_call | solution.py:90
  (104 shorter events, 33.5 us)
Async XLA Ops:
  7.2 313.1 %all-gather.2.cloned.1.call-start = ((), (), s32[]{:S(2)}) async-start(), calls=%async_computation | async-start | bytes 17825792 | tf_op jit(solution)/shard_map/all_gather | solution.py:433
  15.1 11.2 %collective-permute-start = (bf16[16,48,2048]{2,1,0:T(8,128)(2,1)S(1)}, bf16[16,48,2048]{2,1,0:T(8,128)(2,1)}, u32[]{:S(2)}, u32[]{:S(2)}) collective-permute-start(bf16[16,48,2048]{2,1,0:T(8,128)(2,1)S(1)} %shard_map.50.refs_1_), channel_id=1, source_target_pairs={{0,2},{2,0},{4,6},{6,4},{8,10},{10,8},{12,14},{14,12},{16,18},{18,... | collective-permute-start | bytes 9437192 | tf_op jit(solution)/shard_map/ppermute | solution.py:259
  20.9 19.9 %collective-permute-start.3 = (bf16[16,48,2048]{2,1,0:T(8,128)(2,1)}, bf16[16,48,2048]{2,1,0:T(8,128)(2,1)}, u32[]{:S(2)}, u32[]{:S(2)}) collective-permute-start(bf16[16,48,2048]{2,1,0:T(8,128)(2,1)} %shard_map.51.refs_1_), channel_id=1, source_target_pairs={{0,2},{2,0},{4,6},{6,4},{8,10},{10,8},{12,14},{14,12},{16,18},{18,... | collective-permute-start | bytes 9437192 | tf_op jit(solution)/shard_map/ppermute | solution.py:259
  25.3 68.6 %collective-permute-start.9 = (bf16[16,32,2048]{2,1,0:T(8,128)(2,1)}, bf16[16,32,2048]{2,1,0:T(8,128)(2,1)}, u32[]{:S(2)}, u32[]{:S(2)}) collective-permute-start(bf16[16,32,2048]{2,1,0:T(8,128)(2,1)} %shard_map.52.refs_2_), channel_id=1, source_target_pairs={{0,2},{2,0},{4,6},{6,4},{8,10},{10,8},{12,14},{14,12},{16,18},{18,... | collective-permute-start | bytes 6291464 | tf_op jit(solution)/shard_map/ppermute | solution.py:259
  33.3 7.5 %copy-start = (bf16[16,48,2048]{2,1,0:T(8,128)(2,1)}, bf16[16,48,2048]{2,1,0:T(8,128)(2,1)S(1)}, u32[]{:S(2)}) copy-start(bf16[16,48,2048]{2,1,0:T(8,128)(2,1)S(1)} %shard_map.53.refs_2_.refs_1_) | copy-start | bytes 9437188
  33.5 15.9 %collective-permute-start.2 = (bf16[4,48,2048]{2,1,0:T(8,128)(2,1)S(1)}, bf16[4,48,2048]{2,1,0:T(8,128)(2,1)}, u32[]{:S(2)}, u32[]{:S(2)}) collective-permute-start(bf16[4,48,2048]{2,1,0:T(8,128)(2,1)S(1)} %get-tuple-element.68), channel_id=1, source_target_pairs={{24,16},{26,18},{28,20},{30,22},{25,17},{27,19},{29,21},{31,23}} | collective-permute-start | bytes 2359304 | tf_op jit(solution)/shard_map/ppermute | solution.py:265
  35.2 21.6 %collective-permute-start.1 = (bf16[4,48,2048]{2,1,0:T(8,128)(2,1)S(1)}, bf16[4,48,2048]{2,1,0:T(8,128)(2,1)}, u32[]{:S(2)}, u32[]{:S(2)}) collective-permute-start(bf16[4,48,2048]{2,1,0:T(8,128)(2,1)S(1)} %get-tuple-element.69), channel_id=1, source_target_pairs={{0,8},{2,10},{4,12},{6,14},{1,9},{3,11},{5,13},{7,15}} | collective-permute-start | bytes 2359304 | tf_op jit(solution)/shard_map/ppermute | solution.py:265
  48.6 51.2 %collective-permute-start.8 = (bf16[8,48,2048]{2,1,0:T(8,128)(2,1)}, bf16[8,48,2048]{2,1,0:T(8,128)(2,1)S(1)}, u32[]{:S(2)}, u32[]{:S(2)}) collective-permute-start(bf16[8,48,2048]{2,1,0:T(8,128)(2,1)} %get-tuple-element.25.refs_3_), channel_id=1, source_target_pairs={{0,4},{2,6},{4,0},{6,2},{8,12},{10,14},{12,8},{14,10},{16,20},{18,... | collective-permute-start | bytes 4718600 | tf_op jit(solution)/shard_map/ppermute | solution.py:262
  60.8 6.8 %collective-permute-start.5 = (bf16[4,48,2048]{2,1,0:T(8,128)(2,1)}, bf16[4,48,2048]{2,1,0:T(8,128)(2,1)S(1)}, u32[]{:S(2)}, u32[]{:S(2)}) collective-permute-start(bf16[4,48,2048]{2,1,0:T(8,128)(2,1)} %get-tuple-element.27), channel_id=1, source_target_pairs={{16,8},{18,10},{20,12},{22,14},{24,16},{26,18},{28,20},{30,22},{17... | collective-permute-start | bytes 2359304 | tf_op jit(solution)/shard_map/ppermute | solution.py:265
  61.5 21.2 %collective-permute-start.4 = (bf16[4,48,2048]{2,1,0:T(8,128)(2,1)S(1)}, bf16[4,48,2048]{2,1,0:T(8,128)(2,1)}, u32[]{:S(2)}, u32[]{:S(2)}) collective-permute-start(bf16[4,48,2048]{2,1,0:T(8,128)(2,1)S(1)} %get-tuple-element.26.refs_3_), channel_id=1, source_target_pairs={{0,8},{2,10},{4,12},{6,14},{8,16},{10,18},{12,20},{14,22},{1,9},{3... | collective-permute-start | bytes 2359304 | tf_op jit(solution)/shard_map/ppermute | solution.py:265
  86.4 26.1 %collective-permute-start.7 = (bf16[4,48,2048]{2,1,0:T(8,128)(2,1)}, bf16[4,48,2048]{2,1,0:T(8,128)(2,1)}, u32[]{:S(2)}, u32[]{:S(2)}) collective-permute-start(bf16[4,48,2048]{2,1,0:T(8,128)(2,1)} %get-tuple-element.29), channel_id=1, source_target_pairs={{8,0},{10,2},{12,4},{14,6},{16,8},{18,10},{20,12},{22,14},{24,16},... | collective-permute-start | bytes 2359304 | tf_op jit(solution)/shard_map/ppermute | solution.py:265
  87.7 12.2 %copy-start.4 = (bf16[8,48,2048]{2,1,0:T(8,128)(2,1)S(1)}, bf16[8,48,2048]{2,1,0:T(8,128)(2,1)}, u32[]{:S(2)}) copy-start(bf16[8,48,2048]{2,1,0:T(8,128)(2,1)} %copy-done.3) | copy-start | bytes 4718596
  87.7 24.8 %collective-permute-start.6 = (bf16[4,48,2048]{2,1,0:T(8,128)(2,1)}, bf16[4,48,2048]{2,1,0:T(8,128)(2,1)}, u32[]{:S(2)}, u32[]{:S(2)}) collective-permute-start(bf16[4,48,2048]{2,1,0:T(8,128)(2,1)} %get-tuple-element.28.refs_2_), channel_id=1, source_target_pairs={{0,8},{2,10},{4,12},{6,14},{8,16},{10,18},{12,20},{14,22},{16,24},... | collective-permute-start | bytes 2359304 | tf_op jit(solution)/shard_map/ppermute | solution.py:265
  98.9 8.4 %copy-start.5 = (bf16[8,32,2048]{2,1,0:T(8,128)(2,1)}, bf16[8,32,2048]{2,1,0:T(8,128)(2,1)S(1)}, u32[]{:S(2)}) copy-start(bf16[8,32,2048]{2,1,0:T(8,128)(2,1)S(1)} %get-tuple-element.38.refs_0_) | copy-start | bytes 3145732
  98.9 38.1 %collective-permute-start.17 = (bf16[8,32,2048]{2,1,0:T(8,128)(2,1)}, bf16[8,32,2048]{2,1,0:T(8,128)(2,1)}, u32[]{:S(2)}, u32[]{:S(2)}) collective-permute-start(bf16[8,32,2048]{2,1,0:T(8,128)(2,1)} %get-tuple-element.31.refs_2_), channel_id=1, source_target_pairs={{0,4},{2,6},{4,0},{6,2},{8,12},{10,14},{12,8},{14,10},{16,20},{18,... | collective-permute-start | bytes 3145736 | tf_op jit(solution)/shard_map/ppermute | solution.py:262
  108.3 7.4 %collective-permute-start.12 = (bf16[2,48,2048]{2,1,0:T(8,128)(2,1)}, bf16[2,48,2048]{2,1,0:T(8,128)(2,1)S(1)}, u32[]{:S(2)}, u32[]{:S(2)}) collective-permute-start(bf16[2,48,2048]{2,1,0:T(8,128)(2,1)} %get-tuple-element.70), channel_id=1, source_target_pairs={{24,16},{26,18},{28,20},{30,22},{25,17},{27,19},{29,21},{31,23}} | collective-permute-start | bytes 1179656 | tf_op jit(solution)/shard_map/ppermute | solution.py:265
  109.0 9.2 %collective-permute-start.11 = (bf16[2,48,2048]{2,1,0:T(8,128)(2,1)}, bf16[2,48,2048]{2,1,0:T(8,128)(2,1)S(1)}, u32[]{:S(2)}, u32[]{:S(2)}) collective-permute-start(bf16[2,48,2048]{2,1,0:T(8,128)(2,1)} %get-tuple-element.71), channel_id=1, source_target_pairs={{0,8},{2,10},{4,12},{6,14},{1,9},{3,11},{5,13},{7,15}} | collective-permute-start | bytes 1179656 | tf_op jit(solution)/shard_map/ppermute | solution.py:265
  118.2 19.6 %copy-start.6 = (bf16[8,32,2048]{2,1,0:T(8,128)(2,1)S(1)}, bf16[8,32,2048]{2,1,0:T(8,128)(2,1)}, u32[]{:S(2)}) copy-start(bf16[8,32,2048]{2,1,0:T(8,128)(2,1)} %copy-done.5) | copy-start | bytes 3145732
  122.1 5.6 %collective-permute-start.14 = (bf16[2,48,2048]{2,1,0:T(8,128)(2,1)S(1)}, bf16[2,48,2048]{2,1,0:T(8,128)(2,1)S(1)}, u32[]{:S(2)}, u32[]{:S(2)}) collective-permute-start(bf16[2,48,2048]{2,1,0:T(8,128)(2,1)S(1)} %get-tuple-element.35), channel_id=1, source_target_pairs={{16,8},{18,10},{20,12},{22,14},{24,16},{26,18},{28,20},{30,22},{17... | collective-permute-start | bytes 1179656 | tf_op jit(solution)/shard_map/ppermute | solution.py:265
  122.8 10.2 %collective-permute-start.13 = (bf16[2,48,2048]{2,1,0:T(8,128)(2,1)S(1)}, bf16[2,48,2048]{2,1,0:T(8,128)(2,1)S(1)}, u32[]{:S(2)}, u32[]{:S(2)}) collective-permute-start(bf16[2,48,2048]{2,1,0:T(8,128)(2,1)S(1)} %get-tuple-element.34.refs_3_), channel_id=1, source_target_pairs={{0,8},{2,10},{4,12},{6,14},{8,16},{10,18},{12,20},{14,22},{1,9},{3... | collective-permute-start | bytes 1179656 | tf_op jit(solution)/shard_map/ppermute | solution.py:265
  137.0 4.7 %copy-start.7 = (bf16[2,48,2048]{2,1,0:T(8,128)(2,1)}, bf16[2,48,2048]{2,1,0:T(8,128)(2,1)S(1)}, u32[]{:S(2)}) copy-start(bf16[2,48,2048]{2,1,0:T(8,128)(2,1)S(1)} %get-tuple-element.36.refs_2_) | copy-start | bytes 1179652
  141.7 5.3 %collective-permute-start.19 = (bf16[2,32,2048]{2,1,0:T(8,128)(2,1)S(1)}, bf16[2,32,2048]{2,1,0:T(8,128)(2,1)S(1)}, u32[]{:S(2)}, u32[]{:S(2)}) collective-permute-start(bf16[2,32,2048]{2,1,0:T(8,128)(2,1)S(1)} %get-tuple-element.72), channel_id=1, source_target_pairs={{24,16},{26,18},{28,20},{30,22},{25,17},{27,19},{29,21},{31,23}} | collective-permute-start | bytes 786440 | tf_op jit(solution)/shard_map/ppermute | solution.py:265
  142.4 8.4 %collective-permute-start.18 = (bf16[2,32,2048]{2,1,0:T(8,128)(2,1)S(1)}, bf16[2,32,2048]{2,1,0:T(8,128)(2,1)S(1)}, u32[]{:S(2)}, u32[]{:S(2)}) collective-permute-start(bf16[2,32,2048]{2,1,0:T(8,128)(2,1)S(1)} %get-tuple-element.73), channel_id=1, source_target_pairs={{0,8},{2,10},{4,12},{6,14},{1,9},{3,11},{5,13},{7,15}} | collective-permute-start | bytes 786440 | tf_op jit(solution)/shard_map/ppermute | solution.py:265
  153.7 13.1 %collective-permute-start.21 = (bf16[2,32,2048]{2,1,0:T(8,128)(2,1)}, bf16[2,32,2048]{2,1,0:T(8,128)(2,1)}, u32[]{:S(2)}, u32[]{:S(2)}) collective-permute-start(bf16[2,32,2048]{2,1,0:T(8,128)(2,1)} %get-tuple-element.40), channel_id=1, source_target_pairs={{16,8},{18,10},{20,12},{22,14},{24,16},{26,18},{28,20},{30,22},{17... | collective-permute-start | bytes 786440 | tf_op jit(solution)/shard_map/ppermute | solution.py:265
  155.1 11.7 %collective-permute-start.20 = (bf16[2,32,2048]{2,1,0:T(8,128)(2,1)}, bf16[2,32,2048]{2,1,0:T(8,128)(2,1)}, u32[]{:S(2)}, u32[]{:S(2)}) collective-permute-start(bf16[2,32,2048]{2,1,0:T(8,128)(2,1)} %get-tuple-element.39.refs_3_), channel_id=1, source_target_pairs={{0,8},{2,10},{4,12},{6,14},{8,16},{10,18},{12,20},{14,22},{1,9},{3... | collective-permute-start | bytes 786440 | tf_op jit(solution)/shard_map/ppermute | solution.py:265
  160.2 21.8 %copy-start.2 = (f32[1,2,128,2048]{3,2,1,0:T(8,128)S(1)}, f32[1,2,128,2048]{3,2,1,0:T(8,128)}, u32[]{:S(2)}) copy-start(f32[1,2,128,2048]{3,2,1,0:T(8,128)} %param.9) | copy-start | bytes 6291460
  160.3 14.9 %collective-permute-start.10 = (bf16[2,48,2048]{2,1,0:T(8,128)(2,1)S(1)}, bf16[2,48,2048]{2,1,0:T(8,128)(2,1)S(1)}, u32[]{:S(2)}, u32[]{:S(2)}) collective-permute-start(bf16[2,48,2048]{2,1,0:T(8,128)(2,1)S(1)} %get-tuple-element.33.refs_3_), channel_id=1, source_target_pairs={{0,4},{2,6},{4,0},{6,2},{8,12},{10,14},{12,8},{14,10},{16,20},{18,... | collective-permute-start | bytes 1179656 | tf_op jit(solution)/shard_map/ppermute | solution.py:262
  161.6 16.3 %collective-permute-start.15 = (bf16[2,48,2048]{2,1,0:T(8,128)(2,1)}, bf16[2,48,2048]{2,1,0:T(8,128)(2,1)S(1)}, u32[]{:S(2)}, u32[]{:S(2)}) collective-permute-start(bf16[2,48,2048]{2,1,0:T(8,128)(2,1)} %copy-done.7), channel_id=1, source_target_pairs={{0,8},{2,10},{4,12},{6,14},{8,16},{10,18},{12,20},{14,22},{16,24},... | collective-permute-start | bytes 1179656 | tf_op jit(solution)/shard_map/ppermute | solution.py:265
  165.4 12.4 %collective-permute-start.16 = (bf16[2,48,2048]{2,1,0:T(8,128)(2,1)}, bf16[2,48,2048]{2,1,0:T(8,128)(2,1)S(1)}, u32[]{:S(2)}, u32[]{:S(2)}) collective-permute-start(bf16[2,48,2048]{2,1,0:T(8,128)(2,1)} %copy-done.8), channel_id=1, source_target_pairs={{8,0},{10,2},{12,4},{14,6},{16,8},{18,10},{20,12},{22,14},{24,16},... | collective-permute-start | bytes 1179656 | tf_op jit(solution)/shard_map/ppermute | solution.py:265
  169.2 8.7 %collective-permute-start.22 = (bf16[2,32,2048]{2,1,0:T(8,128)(2,1)S(1)}, bf16[2,32,2048]{2,1,0:T(8,128)(2,1)S(1)}, u32[]{:S(2)}, u32[]{:S(2)}) collective-permute-start(bf16[2,32,2048]{2,1,0:T(8,128)(2,1)S(1)} %get-tuple-element.41), channel_id=1, source_target_pairs={{0,8},{2,10},{4,12},{6,14},{8,16},{10,18},{12,20},{14,22},{16,24},... | collective-permute-start | bytes 786440 | tf_op jit(solution)/shard_map/ppermute | solution.py:265
  173.7 8.3 %collective-permute-start.23 = (bf16[2,32,2048]{2,1,0:T(8,128)(2,1)S(1)}, bf16[2,32,2048]{2,1,0:T(8,128)(2,1)S(1)}, u32[]{:S(2)}, u32[]{:S(2)}) collective-permute-start(bf16[2,32,2048]{2,1,0:T(8,128)(2,1)S(1)} %get-tuple-element.42), channel_id=1, source_target_pairs={{8,0},{10,2},{12,4},{14,6},{16,8},{18,10},{20,12},{22,14},{24,16},... | collective-permute-start | bytes 786440 | tf_op jit(solution)/shard_map/ppermute | solution.py:265
  184.6 5.0 %collective-permute-start.24 = (f32[2,128,128]{2,1,0:T(8,128)S(1)}, f32[2,128,128]{2,1,0:T(8,128)S(1)}, u32[]{:S(2)}, u32[]{:S(2)}) collective-permute-start(f32[2,128,128]{2,1,0:T(8,128)S(1)} %get-tuple-element.43.refs_0_), channel_id=1, source_target_pairs={{0,1},{1,0},{2,3},{3,2},{4,5},{5,4},{6,7},{7,6},{8,9},{9,8},{10,11... | collective-permute-start | bytes 393224 | tf_op jit(solution)/shard_map/ppermute | solution.py:428
  (3 other events, 3.6 us)
Sparse Core Ops, SparseCore 0:
  195.1 125.1 all-gather.1

commit v3 on v0

v3 whole, which is shorter than its diff:
```python
import functools
import math

import jax
import jax.numpy as jnp
import numpy as np
from jax import lax
from jax.experimental import pallas as pl
from jax.experimental.pallas import tpu as pltpu
from jax.sharding import PartitionSpec as P

R = 128
D = 4096
ITERS = 5

COEF_A = 3.4445
COEF_B = -4.775
COEF_C = 2.0315
EPSILON = 1e-07
DECAY = 0.95

CORE_BIT = 1
X_BIT = 2
VMEM_BYTES = 24 * 1024 * 1024
MORE_VMEM_BYTES = 44 * 1024 * 1024


def in_vmem(count=1):
    return [pl.BlockSpec(memory_space=pltpu.VMEM)] * count


def anywhere(count=1):
    return [pl.BlockSpec(memory_space=pl.ANY)] * count


def in_hbm():
    return [pl.BlockSpec(memory_space=pltpu.HBM)]


def in_smem(count=1):
    return [pl.BlockSpec(memory_space=pltpu.SMEM)] * count


def limits(size=VMEM_BYTES):
    return pltpu.CompilerParams(vmem_limit_bytes=size)


def cost(size, flops=0):
    return pl.CostEstimate(flops=flops, bytes_accessed=size, transcendentals=0)


def nbytes(*arrays):
    return sum(math.prod(a.shape) * a.dtype.itemsize for a in arrays)


def pack_kernel(first, ids_ref, src_ref, *rest):
    out_ref, sem = rest[-2:]
    count, rows = out_ref.shape[:2]

    def copy(i):
        return pltpu.make_async_copy(
            src_ref.at[ids_ref[i], pl.ds(first, rows)], out_ref.at[i], sem.at[i]
        )

    @pl.loop(0, count)
    def _(i):
        copy(i).start()

    @pl.loop(0, count)
    def _(i):
        copy(i).wait()


def pack(after, src, ids, first, rows):
    count = ids.shape[0]
    out = jax.ShapeDtypeStruct((count, rows, src.shape[2]), src.dtype)
    return pl.pallas_call(
        functools.partial(pack_kernel, first),
        out_shape=out,
        in_specs=in_smem() + in_hbm() + anywhere(len(after)),
        out_specs=in_vmem()[0],
        scratch_shapes=[pltpu.SemaphoreType.DMA((count,))],
        compiler_params=limits(MORE_VMEM_BYTES),
        cost_estimate=cost(2 * nbytes(out)),
    )(ids, src, *after)


def add_taken_kernel(first, ids_ref, src_ref, got_ref, *rest):
    away_ref, home_ref, mine, sem = rest[-4:]
    count, rows = mine.shape[:2]
    half = count // 2

    def copy(i):
        return pltpu.make_async_copy(
            src_ref.at[ids_ref[i], pl.ds(first, rows)], mine.at[i], sem.at[i]
        )

    @pl.loop(0, count)
    def _(i):
        copy(i).start()

    for start, out_ref in ((0, away_ref), (half, home_ref)):

        @pl.loop(0, half)
        def _(i, start=start, out_ref=out_ref):
            copy(start + i).wait()
            out_ref[i] = got_ref[start + i] + mine[start + i]


def add_taken(after, src, ids, first, got):
    count, rows, cols = got.shape
    half = jax.ShapeDtypeStruct((count // 2, rows, cols), got.dtype)
    return pl.pallas_call(
        functools.partial(add_taken_kernel, first),
        out_shape=[half, half],
        in_specs=in_smem() + in_hbm() + in_vmem() + anywhere(len(after)),
        out_specs=in_vmem(2),
        scratch_shapes=[
            pltpu.VMEM(got.shape, got.dtype),
            pltpu.SemaphoreType.DMA((count,)),
        ],
        compiler_params=limits(MORE_VMEM_BYTES),
        cost_estimate=cost(3 * nbytes(got), nbytes(got) // 2),
    )(ids, src, got, *after)


def add_halves_kernel(home_ref, got_ref, *rest):
    away_out, home_out = rest[-2:]
    half = away_out.shape[0]
    for start, out_ref in ((0, away_out), (half, home_out)):

        @pl.loop(0, half)
        def _(i, start=start, out_ref=out_ref):
            out_ref[i] = home_ref[start + i] + got_ref[start + i]


def add_halves(after, home, got):
    count, rows, cols = got.shape
    half = jax.ShapeDtypeStruct((count // 2, rows, cols), got.dtype)
    return pl.pallas_call(
        add_halves_kernel,
        out_shape=[half, half],
        in_specs=in_vmem(2) + anywhere(len(after)),
        out_specs=in_vmem(2),
        compiler_params=limits(),
        cost_estimate=cost(3 * nbytes(got), nbytes(got) // 2),
    )(home, got, *after)


def spread_kernel(first, pieces, to_ref, *refs):
    piece_refs = refs[:pieces]
    out_ref, sem = refs[-2:]
    slots, rows = piece_refs[0].shape[:2]
    for wait in (False, True):
        for p in range(pieces):
            for s in range(slots):
                to = to_ref[p * slots + s]

                @pl.when(to >= 0)
                def _(p=p, s=s, to=to, wait=wait):
                    copy = pltpu.make_async_copy(
                        piece_refs[p].at[s],
                        out_ref.at[to, pl.ds(first, rows)],
                        sem.at[p, s],
                    )
                    if wait:
                        copy.wait()
                    else:
                        copy.start()


def spread(target, matrices, head_rows, pieces, to, first):
    slots, rows, cols = pieces[0].shape
    out = jax.ShapeDtypeStruct((matrices, head_rows, cols), pieces[0].dtype)
    count = len(pieces)
    more = [] if target is None else [target]
    return pl.pallas_call(
        functools.partial(spread_kernel, first, count),
        out_shape=out,
        in_specs=in_smem() + in_vmem(count) + anywhere(len(more)),
        out_specs=anywhere()[0],
        scratch_shapes=[pltpu.SemaphoreType.DMA((count, slots))],
        input_output_aliases={1 + count: 0} if more else {},
        compiler_params=limits(),
        cost_estimate=cost(2 * nbytes(*pieces)),
    )(to, *pieces, *more)


def momentum_kernel(scale, sizes, held_ref, momentum_ref, *rest):
    part_refs = rest[: sum(sizes)]
    next_ref, rounded_ref, gram_ref = rest[sum(sizes) :]
    held = held_ref[pl.program_id(0)] > 0
    first, used = 0, 0
    for size in sizes:
        total = None
        for ref in part_refs[used : used + size]:
            term = ref[0].astype(jnp.float32)
            total = term if total is None else total + term
        rows = total.shape[0]
        here = pl.ds(first, rows)
        mean = total * scale
        previous = momentum_ref[0, here]
        following = DECAY * previous + mean
        next_ref[0, here] = jnp.where(held, following, previous)
        rounded_ref[0, here] = (mean + DECAY * following).astype(jnp.bfloat16)
        first += rows
        used += size
    rounded = rounded_ref[0]
    gram_ref[0] = lax.dot_general(
        rounded, rounded, (((1,), (1,)), ((), ())), preferred_element_type=jnp.float32
    )


def momentum_step(held, momentum, parts, owner_count):
    slots, rows, cols = momentum.shape
    flat = [a for part in parts for a in part]
    return pl.pallas_call(
        functools.partial(
            momentum_kernel, 1.0 / owner_count, [len(part) for part in parts]
        ),
        grid=(slots,),
        out_shape=[
            jax.ShapeDtypeStruct((slots, rows, cols), jnp.float32),
            jax.ShapeDtypeStruct((slots, rows, cols), jnp.bfloat16),
            jax.ShapeDtypeStruct((slots, rows, rows), jnp.float32),
        ],
        in_specs=[
            pl.BlockSpec(memory_space=pltpu.SMEM),
            pl.BlockSpec((1, rows, cols), lambda s: (s, 0, 0)),
        ]
        + [pl.BlockSpec((1,) + a.shape[1:], lambda s: (s, 0, 0)) for a in flat],
        out_specs=[
            pl.BlockSpec((1, rows, cols), lambda s: (s, 0, 0)),
            pl.BlockSpec((1, rows, cols), lambda s: (s, 0, 0)),
            pl.BlockSpec((1, rows, rows), lambda s: (s, 0, 0)),
        ],
        compiler_params=limits(),
        cost_estimate=pl.CostEstimate(
            flops=2 * slots * rows * rows * cols,
            bytes_accessed=slots * rows * cols * 16,
            transcendentals=0,
        ),
    )(held, momentum, *flat)


def exact(a, b):
    return jnp.dot(
        a, b, preferred_element_type=jnp.float32, precision=lax.Precision.HIGHEST
    )


def orthogonalize_kernel(factor, slots, grams, *refs):
    gram_refs = refs[:grams]
    rounded_ref = refs[grams]
    out_refs = refs[grams + 1 :]
    rows = rounded_ref.shape[1]
    row_ids = lax.broadcasted_iota(jnp.int32, (rows, rows), 0)
    col_ids = lax.broadcasted_iota(jnp.int32, (rows, rows), 1)
    diagonal = row_ids == col_ids
    held = []
    for s in range(slots):
        gram = gram_refs[0][s]
        for ref in gram_refs[1:]:
            gram = gram + ref[s]
        squares = jnp.sum(
            jnp.sum(jnp.where(diagonal, gram, 0.0), axis=0, keepdims=True),
            axis=1,
            keepdims=True,
        )
        inverse = 1.0 / (jnp.sqrt(squares) + EPSILON)
        held.append([gram * inverse * inverse, None, inverse])
    for step in range(ITERS):
        squared = [exact(h[0], h[0]) for h in held]
        factors = [
            COEF_B * h[0] + COEF_C * q + jnp.where(diagonal, COEF_A, 0.0)
            for h, q in zip(held, squared)
        ]
        for h, m in zip(held, factors):
            h[1] = m if h[1] is None else exact(m, h[1])
        if step + 1 < ITERS:
            once = [exact(m, h[0]) for h, m in zip(held, factors)]
            for h, m, o in zip(held, factors, once):
                h[0] = exact(m, o)
    for s, h in enumerate(held):
        whole = h[1] * (factor * h[2])
        high = whole.astype(jnp.bfloat16)
        low = (whole - high.astype(jnp.float32)).astype(jnp.bfloat16)
        rounded = rounded_ref[s]
        result = (
            jnp.dot(high, rounded, preferred_element_type=jnp.float32)
            + jnp.dot(low, rounded, preferred_element_type=jnp.float32)
        ).astype(jnp.bfloat16)
        first = 0
        for out_ref in out_refs:
            out_ref[s] = result[first : first + out_ref.shape[1]]
            first += out_ref.shape[1]


def orthogonalize(grams, rounded, factor, shares):
    slots, rows, cols = rounded.shape
    return pl.pallas_call(
        functools.partial(orthogonalize_kernel, factor, slots, len(grams)),
        out_shape=[
            jax.ShapeDtypeStruct((slots, share, cols), jnp.bfloat16) for share in shares
        ],
        in_specs=in_vmem(len(grams) + 1),
        out_specs=in_vmem(len(shares)),
        compiler_params=limits(),
        cost_estimate=pl.CostEstimate(
            flops=slots * (4 * rows * rows * cols + 20 * 12 * rows * rows * rows),
            bytes_accessed=slots * rows * cols * 4,
            transcendentals=0,
        ),
    )(*grams, rounded)


def swap(value, bit):
    count = lax.axis_size("dp")
    return lax.ppermute(value, "dp", [(i, i ^ bit) for i in range(count)])


def z_bits():
    bits, bit = [], 2 * X_BIT
    while bit < lax.axis_size("dp"):
        bits.append(bit)
        bit *= 2
    return bits


def offsets(bits):
    if not bits:
        return [0]
    rest = offsets(bits[1:])
    return [bits[0] | o for o in rest] + rest


def sum_shares(unit, z):
    return (
        (3 * unit, z + [X_BIT]),
        (2 * unit, [X_BIT] + z),
        (3 * unit, [X_BIT] + z),
    )


def sum_order(depth):
    order = [(0, "pack"), (1, "pack"), (2, "pack"), (0, "add"), (1, "add")]
    order += [(0, "add"), (2, "add"), (1, "add")]
    for _ in range(depth - 1):
        order += [(0, "add"), (1, "add"), (2, "add")]
    return order + [(2, "add")]


class Flow:
    def __init__(self, gradient, by_owner, first, rows, bits):
        self.gradient, self.first, self.rows, self.bits = gradient, first, rows, bits
        me = lax.axis_index("dp")
        order = np.array(offsets(bits), np.int32)
        self.mine = by_owner[me ^ order].reshape(-1)
        self.theirs = by_owner[me ^ CORE_BIT ^ order].reshape(-1)
        self.done = 0

    def pack(self, after):
        sent = pack(after, self.gradient, self.theirs, self.first, self.rows)
        self.got = swap(sent, CORE_BIT)
        return [sent]

    def add(self, after):
        if self.done == 0:
            away, self.home = add_taken(
                after, self.gradient, self.mine, self.first, self.got
            )
        else:
            away, self.home = add_halves(after, self.home, self.got)
        self.got = swap(away, self.bits[self.done])
        self.done += 1
        return [away]


def gather_pieces(own, bits):
    pieces = {0: own}
    for bit in bits:
        for offset in list(pieces):
            pieces[offset | bit] = swap(pieces[offset], bit)
    return pieces


def per_device(grads, owner, momentum):
    owner_count = lax.axis_size("dp")
    me = lax.axis_index("dp")
    matrices = owner.shape[0]
    slot_count = momentum.shape[1]
    head_rows = grads.shape[2]
    factor = 0.2 * math.sqrt(max(R, D))
    positions = jnp.arange(matrices, dtype=jnp.int32)
    same_owner = owner[:, None] == owner[None, :]
    earlier = positions[None, :] < positions[:, None]
    slot_rank = jnp.sum((same_owner & earlier).astype(jnp.int32), axis=1)
    spot = owner * slot_count + slot_rank
    spots = jnp.arange(owner_count * slot_count, dtype=jnp.int32)
    matches = spot[None, :] == spots[:, None]
    filled = jnp.any(matches, axis=1)
    source = jnp.sum(jnp.where(matches, positions[None, :], 0), axis=1)
    by_owner = source.reshape(owner_count, slot_count)
    target = jnp.where(filled, source, -1).reshape(owner_count, slot_count)
    held = (target[me] >= 0).astype(jnp.int32)

    unit = head_rows // 8
    z = z_bits()
    flows, first = [], 0
    for rows, bits in sum_shares(unit, z):
        flows.append(Flow(grads[0], by_owner, first, rows, bits))
        first += rows
    after = []
    for flow, work in sum_order(len(z)):
        after = getattr(flows[flow], work)(after)
    parts = [(flow.home, flow.got) for flow in flows]
    new_momentum, rounded, gram = momentum_step(held, momentum[0], parts, owner_count)

    width = lax.axis_size("tensor")
    grams = [gram]
    for _ in range(width - 1):
        grams.append(
            lax.ppermute(
                grams[-1], "tensor", [(i, (i + 1) % width) for i in range(width)]
            )
        )
    back = z[::-1]
    shares = ((6 * unit, back + [X_BIT]), (2 * unit, back[:1] + [X_BIT] + back[1:]))
    blocks = orthogonalize(grams, rounded, factor, [rows for rows, _ in shares])
    update, first = None, 0
    for (rows, bits), block in zip(shares, blocks):
        pieces = gather_pieces(block, bits)
        names = list(pieces)
        half = len(names) // 2
        for part in (names[:half], names[half:]):
            there = [pieces[o] for o in part] + [swap(pieces[o], CORE_BIT) for o in part]
            places = np.array(part + [o | CORE_BIT for o in part], np.int32)
            to = target[me ^ places].reshape(-1)
            update = spread(update, matrices, head_rows, there, to, first)
        first += rows
    return (update, new_momentum[None])


def solution(mesh):
    in_specs = (P("dp", None, None, "tensor"), P(), P("dp", None, None, "tensor"))
    out_specs = (P(None, None, "tensor"), P("dp", None, None, "tensor"))
    return jax.shard_map(
        per_device, mesh=mesh, in_specs=in_specs, out_specs=out_specs, check_vma=False
    )
```

time: 435 us -> 347 us (0.80)
  waiting for transfers between devices: 337 us -> 236 us
  Pallas kernels: 0 us -> 44.1 us
  starting transfers between devices: 0.12 us -> 33.1 us
  other arithmetic: 37.1 us -> 4.26 us
  matrix products: 22 us -> 0 us
  between operations: 13.9 us -> 1.12 us
    ppermute x0 -> x43, waiting for transfers between devices: none -> 236 us  [the longest x42 233 us: swap(): return lax.ppermute(value, 'dp', [(i, i ^ bit) for i in range(count)])]
    reduce_scatter x1 -> x0, waiting for transfers between devices: 181 us -> none  [per_device(): lax.psum_scatter(packed.reshape(owner_count, slot_count, head_rows, local...]
    all_gather x2 -> x0, waiting for transfers between devices: 156 us -> none  [the longest x1 123 us: per_device(): everything = lax.all_gather(result, 'dp', axis=0, tiled=True)]
    pallas_call x0 -> x18, Pallas kernels: none -> 44.1 us  [the longest x3 11.6 us: add_taken(): pl.pallas_call(functools.partial(add_taken_kernel, first), out_shape=[hal...]
    ppermute x0 -> x43, starting transfers between devices: none -> 33.1 us  [the longest x42 31.5 us: swap(): return lax.ppermute(value, 'dp', [(i, i ^ bit) for i in range(count)])]
    dot_general x10 -> x0, matrix products: 22 us -> none  [the longest x5 11.5 us: apply_polynomial(): jnp.einsum('srt,std->srd', polynomial, iterate, preferred_element_type=jn...]
    unnamed x12 -> x88, local copies, waits for them, and re-layouts: 0.03 us -> 21.3 us
    gather x2 -> x8, local copies, waits for them, and re-layouts: 23.8 us -> 4.45 us  [the longest x4 2.22 us: per_device(): to = target[me ^ places].reshape(-1)]
  transfers between devices with their start and end apart: 3 -> 43, of which waited for: 3 -> 14; matrix products, arithmetic and copies ran while one was open for 1% -> 2% of each run, Pallas kernels for 0% -> 9%
where the time goes in v3:
time: 347 us; the launch traced here: 346 us
  waiting for transfers between devices  236 us (68%)
  Pallas kernels  44.1 us (13%)
  starting transfers between devices  33.1 us (10%)
  local copies, waits for them, and re-layouts  27.2 us (8%)
  other arithmetic  4.26 us (1%)
    ppermute x42, waiting for transfers between devices, swap(): return lax.ppermute(value, 'dp', [(i, i ^ bit) for i in range(count)])  233 us
    ppermute x42, starting transfers between devices, swap(): return lax.ppermute(value, 'dp', [(i, i ^ bit) for i in range(count)])  31.5 us
    unnamed x88, local copies, waits for them, and re-layouts  21.3 us
    pallas_call x3, Pallas kernels, add_taken(): pl.pallas_call(functools.partial(add_taken_kernel, first), out_shape=[hal...  11.6 us
    pallas_call x4, Pallas kernels, spread(): pl.pallas_call(functools.partial(spread_kernel, first, count), out_shape=...  11 us
    pallas_call x3, Pallas kernels, pack(): pl.pallas_call(functools.partial(pack_kernel, first), out_shape=out, in_s...  10.6 us
  transfers between devices with their start and end apart: 43, of which 14 were waited for; matrix products, arithmetic and copies ran while one was open for 2% of the time, Pallas kernels for 9%

profile of v3, /device:TPU:0, one launch (start us, length us, event | category | flops | bytes accessed | tf_op | source)
XLA Modules:
  0.0 346.1 jit_solution(11448765744656119154)
XLA Ops:
  4.8 2.6 shard_map.113.rest_0_
  9.3 3.6 %shard_map.114.rest_0_ = bf16[16,32,2048]{2,1,0:T(8,128)(2,1)} custom-call(s32[16]{0:T(128)S(1)} %reshape.48.ids_ref, bf16[24,128,2048]{2,1,0:T(8,128)(2,1)} %bitcast.7, bf16[16,48,2048]{2,1,0:T(8,128)(2,1)S(1)} %shard_map.113.rest_0_), custom_call_target="tpu_custom_call" | custom-call | bytes 4194304 | tf_op jit(solution)/shard_map/pallas_call | solution.py:77
  12.9 4.3 %shard_map.115.rest_0_ = bf16[16,48,2048]{2,1,0:T(8,128)(2,1)} custom-call(s32[16]{0:T(128)S(1)} %reshape.48.ids_ref, bf16[24,128,2048]{2,1,0:T(8,128)(2,1)} %bitcast.8, bf16[16,32,2048]{2,1,0:T(8,128)(2,1)} %shard_map.114.rest_0_), custom_call_target="tpu_custom_call" | custom-call | bytes 6291456 | tf_op jit(solution)/shard_map/pallas_call | solution.py:77
  18.5 4.2 %shard_map.116 = (bf16[8,48,2048]{2,1,0:T(8,128)(2,1)S(1)}, bf16[8,48,2048]{2,1,0:T(8,128)(2,1)S(1)}) custom-call(s32[16]{0:T(128)S(1)} %reshape.46.ids_ref, bf16[24,128,2048]{2,1,0:T(8,128)(2,1)} %bitcast.9, bf16[16,48,2048]{2,1,0:T(8,128)(2,1)} %collective-permute-done.got_ref, bf16[16,48,2048]{2,1,0:T(8,128)(2,1)} %shard_map.115.rest_0_), custom_call_target="tpu_custom_call" | custom-call | flops 1572864 | bytes 9437184 | tf_op jit(solution)/shard_map/pallas_call | solution.py:113
  22.7 2.5 collective-permute-start.1
  26.3 3.4 shard_map.117
  29.7 2.6 collective-permute-start.4
  32.3 27.9 %collective-permute-done.1.got_ref = bf16[8,48,2048]{2,1,0:T(8,128)(2,1)} collective-permute-done((bf16[8,48,2048]{2,1,0:T(8,128)(2,1)S(1)}, bf16[8,48,2048]{2,1,0:T(8,128)(2,1)}, u32[]{:S(2)}, u32[]{:S(2)}) %collective-permute-start.1) | collective-permute-done | bytes 1572896 | tf_op jit(solution)/shard_map/ppermute | solution.py:319
  61.8 4.0 %shard_map.119 = (bf16[8,48,2048]{2,1,0:T(8,128)(2,1)S(1)}, bf16[8,48,2048]{2,1,0:T(8,128)(2,1)S(1)}) custom-call(s32[16]{0:T(128)S(1)} %reshape.50.ids_ref, bf16[24,128,2048]{2,1,0:T(8,128)(2,1)} %bitcast.11, bf16[16,48,2048]{2,1,0:T(8,128)(2,1)} %collective-permute-done.5.got_ref, bf16[4,48,2048]{2,1,0:T(8,128)(2,1)S(1)} %get-tuple-element.29.rest_0_), custom_call_target="tpu_custom_call" | custom-call | flops 1572864 | bytes 9437184 | tf_op jit(solution)/shard_map/pallas_call | solution.py:113
  65.9 1.8 collective-permute-start.9
  67.6 2.6 collective-permute-start.3
  72.1 32.3 %collective-permute-done.3.got_ref = bf16[4,48,2048]{2,1,0:T(8,128)(2,1)S(1)} collective-permute-done((bf16[4,48,2048]{2,1,0:T(8,128)(2,1)S(1)}, bf16[4,48,2048]{2,1,0:T(8,128)(2,1)S(1)}, u32[]{:S(2)}, u32[]{:S(2)}) %collective-permute-start.3) | collective-permute-done | bytes 786464 | tf_op jit(solution)/shard_map/ppermute | solution.py:319
  107.1 17.4 %collective-permute-done.10.got_ref = bf16[4,48,2048]{2,1,0:T(8,128)(2,1)S(1)} collective-permute-done((bf16[4,48,2048]{2,1,0:T(8,128)(2,1)S(1)}, bf16[4,48,2048]{2,1,0:T(8,128)(2,1)S(1)}, u32[]{:S(2)}, u32[]{:S(2)}) %collective-permute-start.10) | collective-permute-done | bytes 786464 | tf_op jit(solution)/shard_map/ppermute | solution.py:319
  125.3 3.4 collective-permute-start.11
  130.1 27.2 %collective-permute-done.8.rest_3_ = bf16[2,32,2048]{2,1,0:T(8,128)(2,1)S(1)} collective-permute-done((bf16[2,32,2048]{2,1,0:T(8,128)(2,1)}, bf16[2,32,2048]{2,1,0:T(8,128)(2,1)S(1)}, u32[]{:S(2)}, u32[]{:S(2)}) %collective-permute-start.8) | collective-permute-done | bytes 262176 | tf_op jit(solution)/shard_map/ppermute | solution.py:319
  157.3 2.9 shard_map.125
  161.7 3.4 collective-permute-done.12.refs_1_
  165.2 4.4 %shard_map.126 = (bf16[2,96,2048]{2,1,0:T(8,128)(2,1)S(1)}, bf16[2,32,2048]{2,1,0:T(8,128)(2,1)S(1)}) custom-call(f32[2,128,128]{2,1,0:T(8,128)S(1)} %get-tuple-element.43.refs_0_, f32[2,128,128]{2,1,0:T(8,128)S(1)} %collective-permute-done.12.refs_1_, bf16[2,128,2048]{2,1,0:T(8,128)(2,1)S(1)} %get-tuple-element.44.refs_2_), custom_call_target="tpu_custom_call" | custom-call | flops 1275068416 | bytes 2097152 | tf_op jit(solution)/shard_map/pallas_call | solution.py:301
  169.7 2.9 collective-permute-start.14
  174.6 41.5 %collective-permute-done.14.refs_1_ = bf16[2,32,2048]{2,1,0:T(8,128)(2,1)S(1)} collective-permute-done((bf16[2,32,2048]{2,1,0:T(8,128)(2,1)S(1)}, bf16[2,32,2048]{2,1,0:T(8,128)(2,1)S(1)}, u32[]{:S(2)}, u32[]{:S(2)}) %collective-permute-start.14) | collective-permute-done | bytes 262176 | tf_op jit(solution)/shard_map/ppermute | solution.py:319
  217.7 4.9 %collective-permute-done.18.refs_3_ = bf16[2,32,2048]{2,1,0:T(8,128)(2,1)} collective-permute-done((bf16[2,32,2048]{2,1,0:T(8,128)(2,1)S(1)}, bf16[2,32,2048]{2,1,0:T(8,128)(2,1)}, u32[]{:S(2)}, u32[]{:S(2)}) %collective-permute-start.18) | collective-permute-done | bytes 262176 | tf_op jit(solution)/shard_map/ppermute | solution.py:319
  225.3 1.8 collective-permute-start.33
  227.1 16.7 %collective-permute-done.15.refs_1_ = bf16[2,32,2048]{2,1,0:T(8,128)(2,1)} collective-permute-done((bf16[2,32,2048]{2,1,0:T(8,128)(2,1)S(1)}, bf16[2,32,2048]{2,1,0:T(8,128)(2,1)}, u32[]{:S(2)}, u32[]{:S(2)}) %collective-permute-start.15) | collective-permute-done | bytes 262176 | tf_op jit(solution)/shard_map/ppermute | solution.py:319
  244.5 20.8 %collective-permute-done.17.refs_2_ = bf16[2,32,2048]{2,1,0:T(8,128)(2,1)} collective-permute-done((bf16[2,32,2048]{2,1,0:T(8,128)(2,1)S(1)}, bf16[2,32,2048]{2,1,0:T(8,128)(2,1)}, u32[]{:S(2)}, u32[]{:S(2)}) %collective-permute-start.17) | collective-permute-done | bytes 262176 | tf_op jit(solution)/shard_map/ppermute | solution.py:319
  267.8 5.2 %collective-permute-done.19.refs_3_ = bf16[2,32,2048]{2,1,0:T(8,128)(2,1)} collective-permute-done((bf16[2,32,2048]{2,1,0:T(8,128)(2,1)}, bf16[2,32,2048]{2,1,0:T(8,128)(2,1)}, u32[]{:S(2)}, u32[]{:S(2)}) %collective-permute-start.19) | collective-permute-done | bytes 262176 | tf_op jit(solution)/shard_map/ppermute | solution.py:319
  279.1 7.4 %collective-permute-done.30.refs_1_ = bf16[2,96,2048]{2,1,0:T(8,128)(2,1)S(1)} collective-permute-done((bf16[2,96,2048]{2,1,0:T(8,128)(2,1)S(1)}, bf16[2,96,2048]{2,1,0:T(8,128)(2,1)S(1)}, u32[]{:S(2)}, u32[]{:S(2)}) %collective-permute-start.30) | collective-permute-done | bytes 786464 | tf_op jit(solution)/shard_map/ppermute | solution.py:319
  287.4 16.0 %collective-permute-done.32.refs_2_ = bf16[2,96,2048]{2,1,0:T(8,128)(2,1)S(1)} collective-permute-done((bf16[2,96,2048]{2,1,0:T(8,128)(2,1)S(1)}, bf16[2,96,2048]{2,1,0:T(8,128)(2,1)S(1)}, u32[]{:S(2)}, u32[]{:S(2)}) %collective-permute-start.32) | collective-permute-done | bytes 786464 | tf_op jit(solution)/shard_map/ppermute | solution.py:319
  304.3 15.1 %collective-permute-done.34.refs_3_ = bf16[2,96,2048]{2,1,0:T(8,128)(2,1)S(1)} collective-permute-done((bf16[2,96,2048]{2,1,0:T(8,128)(2,1)S(1)}, bf16[2,96,2048]{2,1,0:T(8,128)(2,1)S(1)}, u32[]{:S(2)}, u32[]{:S(2)}) %collective-permute-start.34) | collective-permute-done | bytes 786464 | tf_op jit(solution)/shard_map/ppermute | solution.py:319
  333.5 2.9 shard_map.127.refs_8_
  337.9 3.0 shard_map.128.refs_8_
  340.9 2.4 shard_map.129.refs_8_
  343.3 2.7 shard_map.130
  (195 shorter events, 51.2 us)
Async XLA Ops:
  17.3 44.6 %collective-permute-start.5 = (bf16[16,48,2048]{2,1,0:T(8,128)(2,1)}, bf16[16,48,2048]{2,1,0:T(8,128)(2,1)}, u32[]{:S(2)}, u32[]{:S(2)}) collective-permute-start(bf16[16,48,2048]{2,1,0:T(8,128)(2,1)} %shard_map.115.rest_0_), channel_id=1, source_target_pairs={{0,2},{2,0},{4,6},{6,4},{8,10},{10,8},{12,14},{14,12},{16,18},{18,... | collective-permute-start | bytes 9437192 | tf_op jit(solution)/shard_map/ppermute | solution.py:319
  22.7 37.6 %collective-permute-start.1 = (bf16[8,48,2048]{2,1,0:T(8,128)(2,1)S(1)}, bf16[8,48,2048]{2,1,0:T(8,128)(2,1)}, u32[]{:S(2)}, u32[]{:S(2)}) collective-permute-start(bf16[8,48,2048]{2,1,0:T(8,128)(2,1)S(1)} %get-tuple-element.26.rest_0_), channel_id=1, source_target_pairs={{0,8},{2,10},{4,12},{6,14},{8,0},{10,2},{12,4},{14,6},{16,24},{18,... | collective-permute-start | bytes 4718600 | tf_op jit(solution)/shard_map/ppermute | solution.py:319
  29.7 40.5 %collective-permute-start.4 = (bf16[8,32,2048]{2,1,0:T(8,128)(2,1)S(1)}, bf16[8,32,2048]{2,1,0:T(8,128)(2,1)S(1)}, u32[]{:S(2)}, u32[]{:S(2)}) collective-permute-start(bf16[8,32,2048]{2,1,0:T(8,128)(2,1)S(1)} %get-tuple-element.27.rest_0_), channel_id=1, source_target_pairs={{0,4},{2,6},{4,0},{6,2},{8,12},{10,14},{12,8},{14,10},{16,20},{18,... | collective-permute-start | bytes 3145736 | tf_op jit(solution)/shard_map/ppermute | solution.py:319
  65.9 39.4 %collective-permute-start.9 = (bf16[8,48,2048]{2,1,0:T(8,128)(2,1)S(1)}, bf16[8,48,2048]{2,1,0:T(8,128)(2,1)S(1)}, u32[]{:S(2)}, u32[]{:S(2)}) collective-permute-start(bf16[8,48,2048]{2,1,0:T(8,128)(2,1)S(1)} %get-tuple-element.31.rest_0_), channel_id=1, source_target_pairs={{0,4},{2,6},{4,0},{6,2},{8,12},{10,14},{12,8},{14,10},{16,20},{18,... | collective-permute-start | bytes 4718600 | tf_op jit(solution)/shard_map/ppermute | solution.py:319
  67.6 36.7 %collective-permute-start.3 = (bf16[4,48,2048]{2,1,0:T(8,128)(2,1)S(1)}, bf16[4,48,2048]{2,1,0:T(8,128)(2,1)S(1)}, u32[]{:S(2)}, u32[]{:S(2)}) collective-permute-start(bf16[4,48,2048]{2,1,0:T(8,128)(2,1)S(1)} %get-tuple-element.29.rest_0_), channel_id=1, source_target_pairs={{0,16},{2,18},{4,20},{6,22},{8,24},{10,26},{12,28},{14,30},{16,0},... | collective-permute-start | bytes 2359304 | tf_op jit(solution)/shard_map/ppermute | solution.py:319
  70.4 34.8 %collective-permute-start.7 = (bf16[4,32,2048]{2,1,0:T(8,128)(2,1)S(1)}, bf16[4,32,2048]{2,1,0:T(8,128)(2,1)S(1)}, u32[]{:S(2)}, u32[]{:S(2)}) collective-permute-start(bf16[4,32,2048]{2,1,0:T(8,128)(2,1)S(1)} %get-tuple-element.32.rest_0_), channel_id=1, source_target_pairs={{0,8},{2,10},{4,12},{6,14},{8,0},{10,2},{12,4},{14,6},{16,24},{18,... | collective-permute-start | bytes 1572872 | tf_op jit(solution)/shard_map/ppermute | solution.py:319
  106.0 18.4 %collective-permute-start.10 = (bf16[4,48,2048]{2,1,0:T(8,128)(2,1)S(1)}, bf16[4,48,2048]{2,1,0:T(8,128)(2,1)S(1)}, u32[]{:S(2)}, u32[]{:S(2)}) collective-permute-start(bf16[4,48,2048]{2,1,0:T(8,128)(2,1)S(1)} %get-tuple-element.40.rest_0_), channel_id=1, source_target_pairs={{0,8},{2,10},{4,12},{6,14},{8,0},{10,2},{12,4},{14,6},{16,24},{18,... | collective-permute-start | bytes 2359304 | tf_op jit(solution)/shard_map/ppermute | solution.py:319
  106.7 50.6 %collective-permute-start.6 = (bf16[2,48,2048]{2,1,0:T(8,128)(2,1)}, bf16[2,48,2048]{2,1,0:T(8,128)(2,1)S(1)}, u32[]{:S(2)}, u32[]{:S(2)}) collective-permute-start(bf16[2,48,2048]{2,1,0:T(8,128)(2,1)} %get-tuple-element.34.rest_0_), channel_id=1, source_target_pairs={{0,4},{2,6},{4,0},{6,2},{8,12},{10,14},{12,8},{14,10},{16,20},{18,... | collective-permute-start | bytes 1179656 | tf_op jit(solution)/shard_map/ppermute | solution.py:319
  125.3 32.0 %collective-permute-start.11 = (bf16[2,48,2048]{2,1,0:T(8,128)(2,1)}, bf16[2,48,2048]{2,1,0:T(8,128)(2,1)}, u32[]{:S(2)}, u32[]{:S(2)}) collective-permute-start(bf16[2,48,2048]{2,1,0:T(8,128)(2,1)} %get-tuple-element.42), channel_id=1, source_target_pairs={{0,16},{2,18},{4,20},{6,22},{8,24},{10,26},{12,28},{14,30},{16,0},... | collective-permute-start | bytes 1179656 | tf_op jit(solution)/shard_map/ppermute | solution.py:319
  129.4 27.9 %collective-permute-start.8 = (bf16[2,32,2048]{2,1,0:T(8,128)(2,1)}, bf16[2,32,2048]{2,1,0:T(8,128)(2,1)S(1)}, u32[]{:S(2)}, u32[]{:S(2)}) collective-permute-start(bf16[2,32,2048]{2,1,0:T(8,128)(2,1)} %copy-done.35), channel_id=1, source_target_pairs={{0,16},{2,18},{4,20},{6,22},{8,24},{10,26},{12,28},{14,30},{16,0},... | collective-permute-start | bytes 786440 | tf_op jit(solution)/shard_map/ppermute | solution.py:319
  169.6 55.7 %collective-permute-start.29 = (bf16[2,96,2048]{2,1,0:T(8,128)(2,1)S(1)}, bf16[2,96,2048]{2,1,0:T(8,128)(2,1)S(1)}, u32[]{:S(2)}, u32[]{:S(2)}) collective-permute-start(bf16[2,96,2048]{2,1,0:T(8,128)(2,1)S(1)} %get-tuple-element.46.refs_0_), channel_id=1, source_target_pairs={{0,16},{2,18},{4,20},{6,22},{8,24},{10,26},{12,28},{14,30},{16,0},... | collective-permute-start | bytes 2359304 | tf_op jit(solution)/shard_map/ppermute | solution.py:319
  169.7 46.4 %collective-permute-start.14 = (bf16[2,32,2048]{2,1,0:T(8,128)(2,1)S(1)}, bf16[2,32,2048]{2,1,0:T(8,128)(2,1)S(1)}, u32[]{:S(2)}, u32[]{:S(2)}) collective-permute-start(bf16[2,32,2048]{2,1,0:T(8,128)(2,1)S(1)} %get-tuple-element.45.refs_0_), channel_id=1, source_target_pairs={{0,16},{2,18},{4,20},{6,22},{8,24},{10,26},{12,28},{14,30},{16,0},... | collective-permute-start | bytes 786440 | tf_op jit(solution)/shard_map/ppermute | solution.py:319
  172.6 43.8 %collective-permute-start.16 = (bf16[2,32,2048]{2,1,0:T(8,128)(2,1)S(1)}, bf16[2,32,2048]{2,1,0:T(8,128)(2,1)S(1)}, u32[]{:S(2)}, u32[]{:S(2)}) collective-permute-start(bf16[2,32,2048]{2,1,0:T(8,128)(2,1)S(1)} %get-tuple-element.45.refs_0_), channel_id=1, source_target_pairs={{0,4},{2,6},{4,0},{6,2},{8,12},{10,14},{12,8},{14,10},{16,20},{18,... | collective-permute-start | bytes 786440 | tf_op jit(solution)/shard_map/ppermute | solution.py:319
  173.0 43.5 %collective-permute-start.24 = (bf16[2,32,2048]{2,1,0:T(8,128)(2,1)S(1)}, bf16[2,32,2048]{2,1,0:T(8,128)(2,1)S(1)}, u32[]{:S(2)}, u32[]{:S(2)}) collective-permute-start(bf16[2,32,2048]{2,1,0:T(8,128)(2,1)S(1)} %get-tuple-element.45.refs_0_), channel_id=1, source_target_pairs={{0,2},{2,0},{4,6},{6,4},{8,10},{10,8},{12,14},{14,12},{16,18},{18,... | collective-permute-start | bytes 786440 | tf_op jit(solution)/shard_map/ppermute | solution.py:319
  173.0 44.7 %collective-permute-start.13 = (bf16[2,32,2048]{2,1,0:T(8,128)(2,1)S(1)}, bf16[2,32,2048]{2,1,0:T(8,128)(2,1)}, u32[]{:S(2)}, u32[]{:S(2)}) collective-permute-start(bf16[2,32,2048]{2,1,0:T(8,128)(2,1)S(1)} %get-tuple-element.45.refs_0_), channel_id=1, source_target_pairs={{0,8},{2,10},{4,12},{6,14},{8,0},{10,2},{12,4},{14,6},{16,24},{18,... | collective-permute-start | bytes 786440 | tf_op jit(solution)/shard_map/ppermute | solution.py:319
  217.7 47.9 %collective-permute-start.31 = (bf16[2,96,2048]{2,1,0:T(8,128)(2,1)S(1)}, bf16[2,96,2048]{2,1,0:T(8,128)(2,1)S(1)}, u32[]{:S(2)}, u32[]{:S(2)}) collective-permute-start(bf16[2,96,2048]{2,1,0:T(8,128)(2,1)S(1)} %get-tuple-element.46.refs_0_), channel_id=1, source_target_pairs={{0,8},{2,10},{4,12},{6,14},{8,0},{10,2},{12,4},{14,6},{16,24},{18,... | collective-permute-start | bytes 2359304 | tf_op jit(solution)/shard_map/ppermute | solution.py:319
  222.6 43.0 %collective-permute-start.39 = (bf16[2,96,2048]{2,1,0:T(8,128)(2,1)S(1)}, bf16[2,96,2048]{2,1,0:T(8,128)(2,1)S(1)}, u32[]{:S(2)}, u32[]{:S(2)}) collective-permute-start(bf16[2,96,2048]{2,1,0:T(8,128)(2,1)S(1)} %get-tuple-element.46.refs_0_), channel_id=1, source_target_pairs={{0,2},{2,0},{4,6},{6,4},{8,10},{10,8},{12,14},{14,12},{16,18},{18,... | collective-permute-start | bytes 2359304 | tf_op jit(solution)/shard_map/ppermute | solution.py:319
  223.3 42.8 %collective-permute-start.28 = (bf16[2,96,2048]{2,1,0:T(8,128)(2,1)S(1)}, bf16[2,96,2048]{2,1,0:T(8,128)(2,1)S(1)}, u32[]{:S(2)}, u32[]{:S(2)}) collective-permute-start(bf16[2,96,2048]{2,1,0:T(8,128)(2,1)S(1)} %get-tuple-element.46.refs_0_), channel_id=1, source_target_pairs={{0,4},{2,6},{4,0},{6,2},{8,12},{10,14},{12,8},{14,10},{16,20},{18,... | collective-permute-start | bytes 2359304 | tf_op jit(solution)/shard_map/ppermute | solution.py:319
  224.3 19.5 %collective-permute-start.15 = (bf16[2,32,2048]{2,1,0:T(8,128)(2,1)S(1)}, bf16[2,32,2048]{2,1,0:T(8,128)(2,1)}, u32[]{:S(2)}, u32[]{:S(2)}) collective-permute-start(bf16[2,32,2048]{2,1,0:T(8,128)(2,1)S(1)} %collective-permute-done.14.refs_1_), channel_id=1, source_target_pairs={{0,8},{2,10},{4,12},{6,14},{8,0},{10,2},{12,4},{14,6},{16,24},{18,... | collective-permute-start | bytes 786440 | tf_op jit(solution)/shard_map/ppermute | solution.py:319
  225.3 49.4 %collective-permute-start.33 = (bf16[2,96,2048]{2,1,0:T(8,128)(2,1)S(1)}, bf16[2,96,2048]{2,1,0:T(8,128)(2,1)S(1)}, u32[]{:S(2)}, u32[]{:S(2)}) collective-permute-start(bf16[2,96,2048]{2,1,0:T(8,128)(2,1)S(1)} %collective-permute-done.29.refs_1_), channel_id=1, source_target_pairs={{0,8},{2,10},{4,12},{6,14},{8,0},{10,2},{12,4},{14,6},{16,24},{18,... | collective-permute-start | bytes 2359304 | tf_op jit(solution)/shard_map/ppermute | solution.py:319
  243.8 21.5 %collective-permute-start.17 = (bf16[2,32,2048]{2,1,0:T(8,128)(2,1)S(1)}, bf16[2,32,2048]{2,1,0:T(8,128)(2,1)}, u32[]{:S(2)}, u32[]{:S(2)}) collective-permute-start(bf16[2,32,2048]{2,1,0:T(8,128)(2,1)S(1)} %collective-permute-done.16.refs_2_), channel_id=1, source_target_pairs={{0,8},{2,10},{4,12},{6,14},{8,0},{10,2},{12,4},{14,6},{16,24},{18,... | collective-permute-start | bytes 786440 | tf_op jit(solution)/shard_map/ppermute | solution.py:319
  266.1 20.4 %collective-permute-start.30 = (bf16[2,96,2048]{2,1,0:T(8,128)(2,1)S(1)}, bf16[2,96,2048]{2,1,0:T(8,128)(2,1)S(1)}, u32[]{:S(2)}, u32[]{:S(2)}) collective-permute-start(bf16[2,96,2048]{2,1,0:T(8,128)(2,1)S(1)} %collective-permute-done.29.refs_1_), channel_id=1, source_target_pairs={{0,4},{2,6},{4,0},{6,2},{8,12},{10,14},{12,8},{14,10},{16,20},{18,... | collective-permute-start | bytes 2359304 | tf_op jit(solution)/shard_map/ppermute | solution.py:319
  273.0 30.4 %collective-permute-start.32 = (bf16[2,96,2048]{2,1,0:T(8,128)(2,1)S(1)}, bf16[2,96,2048]{2,1,0:T(8,128)(2,1)S(1)}, u32[]{:S(2)}, u32[]{:S(2)}) collective-permute-start(bf16[2,96,2048]{2,1,0:T(8,128)(2,1)S(1)} %collective-permute-done.31.refs_2_), channel_id=1, source_target_pairs={{0,4},{2,6},{4,0},{6,2},{8,12},{10,14},{12,8},{14,10},{16,20},{18,... | collective-permute-start | bytes 2359304 | tf_op jit(solution)/shard_map/ppermute | solution.py:319
  274.7 44.7 %collective-permute-start.34 = (bf16[2,96,2048]{2,1,0:T(8,128)(2,1)S(1)}, bf16[2,96,2048]{2,1,0:T(8,128)(2,1)S(1)}, u32[]{:S(2)}, u32[]{:S(2)}) collective-permute-start(bf16[2,96,2048]{2,1,0:T(8,128)(2,1)S(1)} %collective-permute-done.33.refs_3_), channel_id=1, source_target_pairs={{0,4},{2,6},{4,0},{6,2},{8,12},{10,14},{12,8},{14,10},{16,20},{18,... | collective-permute-start | bytes 2359304 | tf_op jit(solution)/shard_map/ppermute | solution.py:319
  276.0 44.3 %collective-permute-start.35 = (bf16[2,96,2048]{2,1,0:T(8,128)(2,1)S(1)}, bf16[2,96,2048]{2,1,0:T(8,128)(2,1)S(1)}, u32[]{:S(2)}, u32[]{:S(2)}) collective-permute-start(bf16[2,96,2048]{2,1,0:T(8,128)(2,1)S(1)} %collective-permute-done.28.refs_0_), channel_id=1, source_target_pairs={{0,2},{2,0},{4,6},{6,4},{8,10},{10,8},{12,14},{14,12},{16,18},{18,... | collective-permute-start | bytes 2359304 | tf_op jit(solution)/shard_map/ppermute | solution.py:319
  277.8 43.9 %collective-permute-start.42 = (bf16[2,96,2048]{2,1,0:T(8,128)(2,1)S(1)}, bf16[2,96,2048]{2,1,0:T(8,128)(2,1)S(1)}, u32[]{:S(2)}, u32[]{:S(2)}) collective-permute-start(bf16[2,96,2048]{2,1,0:T(8,128)(2,1)S(1)} %collective-permute-done.33.refs_3_), channel_id=1, source_target_pairs={{0,2},{2,0},{4,6},{6,4},{8,10},{10,8},{12,14},{14,12},{16,18},{18,... | collective-permute-start | bytes 2359304 | tf_op jit(solution)/shard_map/ppermute | solution.py:319
  286.5 36.0 %collective-permute-start.36 = (bf16[2,96,2048]{2,1,0:T(8,128)(2,1)S(1)}, bf16[2,96,2048]{2,1,0:T(8,128)(2,1)S(1)}, u32[]{:S(2)}, u32[]{:S(2)}) collective-permute-start(bf16[2,96,2048]{2,1,0:T(8,128)(2,1)S(1)} %collective-permute-done.30.refs_1_), channel_id=1, source_target_pairs={{0,2},{2,0},{4,6},{6,4},{8,10},{10,8},{12,14},{14,12},{16,18},{18,... | collective-permute-start | bytes 2359304 | tf_op jit(solution)/shard_map/ppermute | solution.py:319
  303.4 20.6 %collective-permute-start.37 = (bf16[2,96,2048]{2,1,0:T(8,128)(2,1)S(1)}, bf16[2,96,2048]{2,1,0:T(8,128)(2,1)S(1)}, u32[]{:S(2)}, u32[]{:S(2)}) collective-permute-start(bf16[2,96,2048]{2,1,0:T(8,128)(2,1)S(1)} %collective-permute-done.32.refs_2_), channel_id=1, source_target_pairs={{0,2},{2,0},{4,6},{6,4},{8,10},{10,8},{12,14},{14,12},{16,18},{18,... | collective-permute-start | bytes 2359304 | tf_op jit(solution)/shard_map/ppermute | solution.py:319
  321.2 22.1 %collective-permute-start.20 = (bf16[2,32,2048]{2,1,0:T(8,128)(2,1)}, bf16[2,32,2048]{2,1,0:T(8,128)(2,1)}, u32[]{:S(2)}, u32[]{:S(2)}) collective-permute-start(bf16[2,32,2048]{2,1,0:T(8,128)(2,1)} %collective-permute-done.13.refs_0_), channel_id=1, source_target_pairs={{0,2},{2,0},{4,6},{6,4},{8,10},{10,8},{12,14},{14,12},{16,18},{18,... | collective-permute-start | bytes 786440 | tf_op jit(solution)/shard_map/ppermute | solution.py:319
  322.6 18.3 %collective-permute-start.27 = (bf16[2,32,2048]{2,1,0:T(8,128)(2,1)}, bf16[2,32,2048]{2,1,0:T(8,128)(2,1)}, u32[]{:S(2)}, u32[]{:S(2)}) collective-permute-start(bf16[2,32,2048]{2,1,0:T(8,128)(2,1)} %collective-permute-done.18.refs_3_), channel_id=1, source_target_pairs={{0,2},{2,0},{4,6},{6,4},{8,10},{10,8},{12,14},{14,12},{16,18},{18,... | collective-permute-start | bytes 786440 | tf_op jit(solution)/shard_map/ppermute | solution.py:319
  323.5 19.8 %collective-permute-start.21 = (bf16[2,32,2048]{2,1,0:T(8,128)(2,1)}, bf16[2,32,2048]{2,1,0:T(8,128)(2,1)}, u32[]{:S(2)}, u32[]{:S(2)}) collective-permute-start(bf16[2,32,2048]{2,1,0:T(8,128)(2,1)} %collective-permute-done.15.refs_1_), channel_id=1, source_target_pairs={{0,2},{2,0},{4,6},{6,4},{8,10},{10,8},{12,14},{14,12},{16,18},{18,... | collective-permute-start | bytes 786440 | tf_op jit(solution)/shard_map/ppermute | solution.py:319
  324.9 18.4 %collective-permute-start.22 = (bf16[2,32,2048]{2,1,0:T(8,128)(2,1)}, bf16[2,32,2048]{2,1,0:T(8,128)(2,1)}, u32[]{:S(2)}, u32[]{:S(2)}) collective-permute-start(bf16[2,32,2048]{2,1,0:T(8,128)(2,1)} %collective-permute-done.17.refs_2_), channel_id=1, source_target_pairs={{0,2},{2,0},{4,6},{6,4},{8,10},{10,8},{12,14},{14,12},{16,18},{18,... | collective-permute-start | bytes 786440 | tf_op jit(solution)/shard_map/ppermute | solution.py:319
  (55 other events, 875.8 us)

commit v4 on v3

v4 whole, which is shorter than its diff:
```python
import functools
import math

import jax
import jax.numpy as jnp
from jax import lax
from jax.experimental import pallas as pl
from jax.experimental.pallas import tpu as pltpu
from jax.sharding import PartitionSpec as P

R = 128
D = 4096
ITERS = 5

COEF_A = 3.4445
COEF_B = -4.775
COEF_C = 2.0315
EPSILON = 1e-07
DECAY = 0.95

CORE_BIT = 1
X_BIT = 2
VMEM_BYTES = 24 * 1024 * 1024
MORE_VMEM_BYTES = 44 * 1024 * 1024


def in_vmem(count=1):
    return [pl.BlockSpec(memory_space=pltpu.VMEM)] * count


def anywhere(count=1):
    return [pl.BlockSpec(memory_space=pl.ANY)] * count


def in_hbm():
    return [pl.BlockSpec(memory_space=pltpu.HBM)]


def in_smem(count=1):
    return [pl.BlockSpec(memory_space=pltpu.SMEM)] * count


def limits(size=VMEM_BYTES):
    return pltpu.CompilerParams(vmem_limit_bytes=size)


def small_cost():
    return pl.CostEstimate(flops=0, bytes_accessed=0, transcendentals=0)


def table_kernel(slots, me_ref, owner_ref, table_ref, used):
    spots, matrices = table_ref.shape[0], owner_ref.shape[0]

    @pl.loop(0, spots)
    def _(i):
        table_ref[i] = -1

    @pl.loop(0, spots // slots)
    def _(i):
        used[i] = 0

    @pl.loop(0, matrices)
    def _(m):
        at = owner_ref[m]
        rank = used[at]
        table_ref[(at ^ me_ref[0]) * slots + rank] = m
        used[at] = rank + 1


def build_table(me, owner, owners, slots):
    return pl.pallas_call(
        functools.partial(table_kernel, slots),
        out_shape=jax.ShapeDtypeStruct((owners * slots,), jnp.int32),
        in_specs=in_smem(2),
        out_specs=in_smem()[0],
        scratch_shapes=[pltpu.SMEM((owners,), jnp.int32)],
        cost_estimate=small_cost(),
    )(me, owner)


def starts(order, slots):
    return [
        (n * slots + s, offset * slots + s)
        for n, offset in enumerate(order)
        for s in range(slots)
    ]


def fetch(table_ref, src_ref, first, order, slots, into, sem):
    rows = into.shape[1]
    for item, place in starts(order, slots):
        matrix = jnp.maximum(table_ref[place], 0)
        pltpu.make_async_copy(
            src_ref.at[matrix, pl.ds(first, rows)], into.at[item], sem.at[item]
        ).start()
    return lambda i: pltpu.make_async_copy(
        src_ref.at[0, pl.ds(first, rows)], into.at[i], sem.at[i]
    )


def pack_kernel(first, order, slots, table_ref, src_ref, *rest):
    out_ref, sem = rest[-2:]
    copy = fetch(table_ref, src_ref, first, order, slots, out_ref, sem)

    @pl.loop(0, out_ref.shape[0])
    def _(i):
        copy(i).wait()


def pack(after, table, src, order, slots, first, rows):
    count = len(order) * slots
    return pl.pallas_call(
        functools.partial(pack_kernel, first, order, slots),
        out_shape=jax.ShapeDtypeStruct((count, rows, src.shape[2]), src.dtype),
        in_specs=in_smem() + in_hbm() + anywhere(len(after)),
        out_specs=in_vmem()[0],
        scratch_shapes=[pltpu.SemaphoreType.DMA((count,))],
        compiler_params=limits(MORE_VMEM_BYTES),
        cost_estimate=small_cost(),
    )(table, src, *after)


def add_taken_kernel(first, order, slots, parts, table_ref, src_ref, got_ref, *rest):
    mine, sem = rest[-2:]
    out_refs = rest[-2 - len(parts) : -2]
    copy = fetch(table_ref, src_ref, first, order, slots, mine, sem)
    start = 0
    for size, out_ref in zip(parts, out_refs):

        @pl.loop(0, size)
        def _(i, start=start, out_ref=out_ref):
            copy(start + i).wait()
            out_ref[i] = got_ref[start + i] + mine[start + i]

        start += size


def add_taken(after, table, src, order, slots, first, got, parts):
    count, rows, cols = got.shape
    return pl.pallas_call(
        functools.partial(add_taken_kernel, first, order, slots, parts),
        out_shape=[jax.ShapeDtypeStruct((n, rows, cols), got.dtype) for n in parts],
        in_specs=in_smem() + in_hbm() + in_vmem() + anywhere(len(after)),
        out_specs=in_vmem(len(parts)),
        scratch_shapes=[
            pltpu.VMEM(got.shape, got.dtype),
            pltpu.SemaphoreType.DMA((count,)),
        ],
        compiler_params=limits(MORE_VMEM_BYTES),
        cost_estimate=small_cost(),
    )(table, src, got, *after)


def combine_kernel(arrays, plans, *refs):
    sources = refs[:arrays]
    outs = refs[len(refs) - len(plans) :]
    for out_ref, items in zip(outs, plans):
        for i, terms in enumerate(items):
            total = sources[terms[0][0]][terms[0][1]]
            for at, item in terms[1:]:
                total = total + sources[at][item]
            out_ref[i] = total


def combine(after, *wanted):
    arrays, plans = [], []
    for items in wanted:
        plan = []
        for terms in items:
            found = []
            for array, item in terms:
                places = [i for i, a in enumerate(arrays) if a is array]
                if not places:
                    arrays.append(array)
                    places = [len(arrays) - 1]
                found.append((places[0], item))
            plan.append(tuple(found))
        plans.append(tuple(plan))
    shapes = []
    for items in wanted:
        sample = items[0][0][0]
        shapes.append(
            jax.ShapeDtypeStruct((len(items),) + sample.shape[1:], sample.dtype)
        )
    return pl.pallas_call(
        functools.partial(combine_kernel, len(arrays), tuple(plans)),
        out_shape=shapes,
        in_specs=in_vmem(len(arrays)) + anywhere(len(after)),
        out_specs=in_vmem(len(plans)),
        compiler_params=limits(),
        cost_estimate=small_cost(),
    )(*arrays, *after)


def joined(*arrays):
    return [[(array, i)] for array in arrays for i in range(array.shape[0])]


def summed(home, got, first, last):
    return [[(home, i), (got, i)] for i in range(first, last)]


def spread_kernel(plans, slots, table_ref, *refs):
    piece_refs = refs[: len(plans)]
    out_ref, sem = refs[-2:]
    for wait in (False, True):
        for p, (first, order) in enumerate(plans):
            for item, place in starts(order, slots):
                to = table_ref[place]

                @pl.when(to >= 0)
                def _(p=p, item=item, to=to, wait=wait, first=first):
                    rows = piece_refs[p].shape[1]
                    copy = pltpu.make_async_copy(
                        piece_refs[p].at[item],
                        out_ref.at[to, pl.ds(first, rows)],
                        sem.at[p, item],
                    )
                    if wait:
                        copy.wait()
                    else:
                        copy.start()


def spread(after, target, shape, table, slots, pieces):
    count = len(pieces)
    arrays = [array for array, _, _ in pieces]
    plans = tuple((first, tuple(order)) for _, first, order in pieces)
    most = max(a.shape[0] for a in arrays)
    more = [] if target is None else [target]
    after = [a for a in after if a is not target]
    return pl.pallas_call(
        functools.partial(spread_kernel, plans, slots),
        out_shape=jax.ShapeDtypeStruct(shape, arrays[0].dtype),
        in_specs=in_smem() + in_vmem(count) + anywhere(len(more) + len(after)),
        out_specs=anywhere()[0],
        scratch_shapes=[pltpu.SemaphoreType.DMA((count, most))],
        input_output_aliases={1 + count: 0} if more else {},
        compiler_params=limits(MORE_VMEM_BYTES),
        cost_estimate=small_cost(),
    )(table, *arrays, *more, *after)


def momentum_kernel(scale, sizes, held_ref, momentum_ref, *rest):
    part_refs = rest[: sum(sizes)]
    next_ref, rounded_ref, gram_ref = rest[sum(sizes) :]
    held = held_ref[pl.program_id(0)] >= 0
    first, used = 0, 0
    for size in sizes:
        total = None
        for ref in part_refs[used : used + size]:
            term = ref[0].astype(jnp.float32)
            total = term if total is None else total + term
        rows = total.shape[0]
        here = pl.ds(first, rows)
        mean = total * scale
        previous = momentum_ref[0, here]
        following = DECAY * previous + mean
        next_ref[0, here] = jnp.where(held, following, previous)
        rounded_ref[0, here] = (mean + DECAY * following).astype(jnp.bfloat16)
        first += rows
        used += size
    rounded = rounded_ref[0]
    gram_ref[0] = lax.dot_general(
        rounded, rounded, (((1,), (1,)), ((), ())), preferred_element_type=jnp.float32
    )


def momentum_step(held, momentum, parts, owner_count):
    slots, rows, cols = momentum.shape
    flat = [b for part in parts for b in part]
    return pl.pallas_call(
        functools.partial(
            momentum_kernel, 1.0 / owner_count, [len(part) for part in parts]
        ),
        grid=(slots,),
        out_shape=[
            jax.ShapeDtypeStruct((slots, rows, cols), jnp.float32),
            jax.ShapeDtypeStruct((slots, rows, cols), jnp.bfloat16),
            jax.ShapeDtypeStruct((slots, rows, rows), jnp.float32),
        ],
        in_specs=[
            pl.BlockSpec(memory_space=pltpu.SMEM),
            pl.BlockSpec((1, rows, cols), lambda s: (s, 0, 0)),
        ]
        + [
            pl.BlockSpec((1,) + b.array.shape[1:], lambda s, at=b.start: (s + at, 0, 0))
            for b in flat
        ],
        out_specs=[
            pl.BlockSpec((1, rows, cols), lambda s: (s, 0, 0)),
            pl.BlockSpec((1, rows, cols), lambda s: (s, 0, 0)),
            pl.BlockSpec((1, rows, rows), lambda s: (s, 0, 0)),
        ],
        compiler_params=limits(),
        cost_estimate=small_cost(),
    )(held, momentum, *[b.array for b in flat])


def exact(a, b):
    return jnp.dot(
        a, b, preferred_element_type=jnp.float32, precision=lax.Precision.HIGHEST
    )


def orthogonalize_kernel(factor, slots, grams, *refs):
    gram_refs = refs[:grams]
    rounded_ref = refs[grams]
    out_refs = refs[grams + 1 :]
    rows = rounded_ref.shape[1]
    row_ids = lax.broadcasted_iota(jnp.int32, (rows, rows), 0)
    col_ids = lax.broadcasted_iota(jnp.int32, (rows, rows), 1)
    diagonal = row_ids == col_ids
    held = []
    for s in range(slots):
        gram = gram_refs[0][s]
        for ref in gram_refs[1:]:
            gram = gram + ref[s]
        squares = jnp.sum(
            jnp.sum(jnp.where(diagonal, gram, 0.0), axis=0, keepdims=True),
            axis=1,
            keepdims=True,
        )
        inverse = 1.0 / (jnp.sqrt(squares) + EPSILON)
        held.append([gram * inverse * inverse, None, inverse])
    for step in range(ITERS):
        squared = [exact(h[0], h[0]) for h in held]
        factors = [
            COEF_B * h[0] + COEF_C * q + jnp.where(diagonal, COEF_A, 0.0)
            for h, q in zip(held, squared)
        ]
        for h, m in zip(held, factors):
            h[1] = m if h[1] is None else exact(m, h[1])
        if step + 1 < ITERS:
            once = [exact(m, h[0]) for h, m in zip(held, factors)]
            for h, m, o in zip(held, factors, once):
                h[0] = exact(m, o)
    for s, h in enumerate(held):
        whole = h[1] * (factor * h[2])
        high = whole.astype(jnp.bfloat16)
        low = (whole - high.astype(jnp.float32)).astype(jnp.bfloat16)
        rounded = rounded_ref[s]
        result = (
            jnp.dot(high, rounded, preferred_element_type=jnp.float32)
            + jnp.dot(low, rounded, preferred_element_type=jnp.float32)
        ).astype(jnp.bfloat16)
        first = 0
        for out_ref in out_refs:
            out_ref[s] = result[first : first + out_ref.shape[1]]
            first += out_ref.shape[1]


def orthogonalize(grams, rounded, factor, shares):
    slots, rows, cols = rounded.shape
    return pl.pallas_call(
        functools.partial(orthogonalize_kernel, factor, slots, len(grams)),
        out_shape=[
            jax.ShapeDtypeStruct((slots, share, cols), jnp.bfloat16) for share in shares
        ],
        in_specs=in_vmem(len(grams) + 1),
        out_specs=in_vmem(len(shares)),
        compiler_params=limits(),
        cost_estimate=small_cost(),
    )(*grams, rounded)


def swap(value, bit):
    count = lax.axis_size("dp")
    return lax.ppermute(value, "dp", [(i, i ^ bit) for i in range(count)])


def z_bits():
    bits, bit = [], 2 * X_BIT
    while bit < lax.axis_size("dp"):
        bits.append(bit)
        bit *= 2
    return bits


def offsets(bits):
    if not bits:
        return [0]
    rest = offsets(bits[1:])
    return [bits[0] | o for o in rest] + rest


def levels(bits):
    found = [[(0, -1)]]
    for _ in bits:
        longer = []
        for j, bit in enumerate(bits):
            longer += [(o | bit, j) for o, last in found[-1] if last < j]
        found.append(longer)
    return found


class Block:
    def __init__(self, array, start):
        self.array, self.start = array, start


def sum_to_owners(gradient, table, slots, bits, cut):
    rest = gradient.shape[1] - cut
    level = [[o for o, _ in found] for found in levels(bits)]
    last = {o: bits[j] for found in levels(bits) for o, j in found if j >= 0}
    top = len(bits)
    other_bits = bits[::-1] + [X_BIT]
    other_order = tuple(offsets(other_bits))

    def batch(k):
        order = [o | X_BIT for o in level[k]]
        return tuple(order + (level[k + 1] if k < top else []))

    batches = {k: batch(k) for k in range(top, -1, -1)}
    batches[-1] = (0,)
    merged = {k: batches[k] for k in range(top, 0, -1)}
    merged[0] = batches[0] + batches[-1]

    def send(order, first, rows, after):
        theirs = tuple(CORE_BIT | o for o in order)
        packed = pack(after, table, gradient, theirs, slots, first, rows)
        return packed, swap(packed, CORE_BIT)

    got, packed = {}, {}

    def take_off(k, after):
        packed[k], got[k] = send(merged[k], 0, cut, after)
        return [packed[k]]

    home = {}
    over_x = {}

    def take(k, after):
        order = merged[k]
        crossing = len(level[k]) * slots
        parts = (crossing,)
        if len(order) * slots > crossing:
            parts += (len(order) * slots - crossing,)
        made = add_taken(after, table, gradient, order, slots, 0, got[k], parts)
        over_x[k] = made[0]
        for n, o in enumerate(order[len(level[k]) :]):
            home[o] = Block(made[1], n * slots)
        return [made[0]]

    half = len(other_order) * slots // 2
    packed[None], other_got = send(other_order, cut, rest, [])
    after = take_off(top - 1, take_off(top, [packed[None]]))
    away, kept = add_taken(
        after, table, gradient, other_order, slots, cut, other_got, (half, half)
    )
    other_got = swap(away, other_bits[0])
    after = take(top, [away])
    x_got = swap(over_x[top], X_BIT)
    for k in range(top - 2, -1, -1):
        after = take_off(k, after)

    pending = {}
    for k in range(top, -1, -1):
        terms = {o: [] for o in level[k]}
        for n, o in enumerate(level[k]):
            terms[o].append(Block(x_got, n * slots))
        for o, value in pending.items():
            terms[o ^ last[o]].append(Block(value, 0))
        if k == 0:
            break
        if k == top:
            after = take(k - 1, after)
        wanted = []
        for o in level[k]:
            parts = [home[o]] + terms[o]
            wanted.append(
                [[(b.array, b.start + s) for b in parts] for s in range(slots)]
            )
        half //= 2
        wanted.append(summed(kept, other_got, 0, half))
        wanted.append(summed(kept, other_got, half, 2 * half))
        held_back = k == 1
        if held_back:
            wanted.append(joined(over_x[0]))
        made = list(combine(after, *wanted))
        after = [made[0]]
        if held_back:
            over_x[0] = made.pop()
        else:
            after = take(k - 2, after)
        pending = {o: swap(made[n], last[o]) for n, o in enumerate(level[k])}
        kept = made[-1]
        other_got = swap(made[-2], other_bits[top - k + 1])
        x_got = swap(over_x[k - 1], X_BIT)
    return [[home[0]] + terms[0], [Block(kept, 0), Block(other_got, 0)]]


def spread_updates(blocks, table, slots, bits, cut, shape):
    level = levels(bits)
    last = [dict(found) for found in level]
    own, cur = blocks
    top = len(bits)
    cur_order = [0]
    other_bits = [X_BIT] + bits
    front, front_order = own, [0]
    pieces = {0: own}
    after, update, waiting = [], None, []
    for k in range(top + 1):
        x_got = swap(front, X_BIT)
        longer = {}
        for j, bit in enumerate(bits):
            for o, at in level[k]:
                if at < j:
                    longer[o | bit] = swap(pieces[o], bit)
        other_got = swap(cur, other_bits[k])
        made = [(front, 0, front_order), (x_got, 0, [X_BIT | o for o in front_order])]
        if k == top:
            break
        if k == 0:
            (both,) = combine(after, joined(front, x_got))
            made = [(both, 0, front_order + [X_BIT | o for o in front_order])]
            after = [both]
        order = [o for o, _ in level[k + 1]]
        wanted = [joined(*[longer[o] for o in order]), joined(cur, other_got)]
        front, cur = combine(after, *wanted)
        after = [front]
        pieces = longer
        front_order = order
        cur_order = cur_order + [other_bits[k] | o for o in cur_order]
        if waiting:
            update = spread(after, update, shape, table, slots, waiting)
            after = [update]
        waiting = []
        for array, first, order in made:
            waiting.append((array, first, order))
            waiting.append((swap(array, CORE_BIT), first, [CORE_BIT | o for o in order]))
    update = spread(after, update, shape, table, slots, waiting)

    def with_core(array, first, order):
        return [
            (array, first, order),
            (swap(array, CORE_BIT), first, [CORE_BIT | o for o in order]),
        ]

    waiting = with_core(front, 0, front_order) + with_core(cur, cut, cur_order)
    update = spread([], update, shape, table, slots, waiting)
    waiting = with_core(x_got, 0, [X_BIT | o for o in front_order])
    waiting += with_core(other_got, cut, [other_bits[top] | o for o in cur_order])
    return spread([], update, shape, table, slots, waiting)


def per_device(grads, owner, momentum):
    owner_count = lax.axis_size("dp")
    matrices = owner.shape[0]
    slot_count = momentum.shape[1]
    head_rows, cols = grads.shape[2:]
    factor = 0.2 * math.sqrt(max(R, D))
    me = lax.axis_index("dp").astype(jnp.int32).reshape(1)
    table = build_table(me, owner, owner_count, slot_count)

    cut = head_rows * 3 // 4
    bits = z_bits()[::-1]
    parts = sum_to_owners(grads[0], table, slot_count, bits, cut)
    new_momentum, rounded, gram = momentum_step(table, momentum[0], parts, owner_count)

    width = lax.axis_size("tensor")
    grams = [gram]
    for _ in range(width - 1):
        grams.append(
            lax.ppermute(
                grams[-1], "tensor", [(i, (i + 1) % width) for i in range(width)]
            )
        )
    blocks = orthogonalize(grams, rounded, factor, [cut, head_rows - cut])
    shape = (matrices, head_rows, cols)
    update = spread_updates(blocks, table, slot_count, bits, cut, shape)
    return (update, new_momentum[None])


def solution(mesh):
    in_specs = (P("dp", None, None, "tensor"), P(), P("dp", None, None, "tensor"))
    out_specs = (P(None, None, "tensor"), P("dp", None, None, "tensor"))
    return jax.shard_map(
        per_device, mesh=mesh, in_specs=in_specs, out_specs=out_specs, check_vma=False
    )
```

time: 347 us -> 223 us (0.64)
  waiting for transfers between devices: 236 us -> 148 us
  local copies, waits for them, and re-layouts: 27.2 us -> 0.65 us
  Pallas kernels: 44.1 us -> 36.9 us
  other arithmetic: 4.26 us -> 0 us
    ppermute x42 -> x29, waiting for transfers between devices: 233 us -> 144 us  [swap(): return lax.ppermute(value, 'dp', [(i, i ^ bit) for i in range(count)])]
    unnamed x88 -> x4, local copies, waits for them, and re-layouts: 21.3 us -> 0.65 us
    pallas_call x16 -> x18, Pallas kernels: 36.7 us -> 29.7 us  [the longest x4 9.55 us: spread(): pl.pallas_call(functools.partial(spread_kernel, plans, slots), out_shape=...]
    gather x8 -> x0, local copies, waits for them, and re-layouts: 4.45 us -> none  [the longest x4 2.22 us: per_device(): to = target[me ^ places].reshape(-1)]
    ppermute x42 -> x29, starting transfers between devices: 31.5 us -> 34.5 us  [swap(): return lax.ppermute(value, 'dp', [(i, i ^ bit) for i in range(count)])]
  transfers between devices with their start and end apart: 43 -> 30, of which waited for: 14 -> 15; matrix products, arithmetic and copies ran while one was open for 2% -> 0% of each run, Pallas kernels for 9% -> 10%
where the time goes in v4:
time: 223 us; the launch traced here: 222 us
  waiting for transfers between devices  148 us (66%)
  Pallas kernels  36.9 us (17%)
  starting transfers between devices  35.7 us (16%)
    ppermute x29, waiting for transfers between devices, swap(): return lax.ppermute(value, 'dp', [(i, i ^ bit) for i in range(count)])  144 us
    ppermute x29, starting transfers between devices, swap(): return lax.ppermute(value, 'dp', [(i, i ^ bit) for i in range(count)])  34.5 us
    pallas_call x4, Pallas kernels, spread(): pl.pallas_call(functools.partial(spread_kernel, plans, slots), out_shape=...  9.55 us
    pallas_call x4, Pallas kernels, pack(): pl.pallas_call(functools.partial(pack_kernel, first, order, slots), out_s...  8.77 us
    pallas_call x4, Pallas kernels, add_taken(): pl.pallas_call(functools.partial(add_taken_kernel, first, order, slots, p...  8.76 us
  transfers between devices with their start and end apart: 30, of which 15 were waited for; matrix products, arithmetic and copies ran while one was open for 0% of the time, Pallas kernels for 10%

profile of v4, /device:TPU:0, one launch (start us, length us, event | category | flops | bytes accessed | tf_op | source)
XLA Modules:
  0.0 222.2 jit_solution(8893732739767675275)
XLA Ops:
  3.1 2.4 %shard_map.51.rest_0_ = bf16[16,32,2048]{2,1,0:T(8,128)(2,1)S(1)} custom-call(s32[32]{0:T(128)S(1)} %copy-done.1, bf16[24,128,2048]{2,1,0:T(8,128)(2,1)} %bitcast.5), custom_call_target="tpu_custom_call" | custom-call | tf_op jit(solution)/shard_map/pallas_call | solution.py:112
  7.8 2.2 shard_map.53.rest_0_
  10.4 2.3 %shard_map.54 = (bf16[8,32,2048]{2,1,0:T(8,128)(2,1)S(1)}, bf16[8,32,2048]{2,1,0:T(8,128)(2,1)S(1)}) custom-call(s32[32]{0:T(128)S(1)} %copy-done.1, bf16[24,128,2048]{2,1,0:T(8,128)(2,1)} %bitcast.8, bf16[16,32,2048]{2,1,0:T(8,128)(2,1)S(1)} %collective-permute-done.1.got_ref, bf16[6,96,2048]{2,1,0:T(8,128)(2,1)S(1)} %shard_map.53.rest_0_), custom_call_target="tpu_custom_call" | custom-call | tf_op jit(solution)/shard_map/pallas_call | solution.py:140
  14.5 2.5 %shard_map.56.rest_0_ = bf16[8,96,2048]{2,1,0:T(8,128)(2,1)S(1)} custom-call(s32[32]{0:T(128)S(1)} %copy-done.1, bf16[24,128,2048]{2,1,0:T(8,128)(2,1)} %bitcast.10, bf16[2,96,2048]{2,1,0:T(8,128)(2,1)S(1)} %shard_map.55.rest_0_), custom_call_target="tpu_custom_call" | custom-call | tf_op jit(solution)/shard_map/pallas_call | solution.py:112
  17.3 2.9 %collective-permute-start.5 = (bf16[8,32,2048]{2,1,0:T(8,128)(2,1)S(1)}, bf16[8,32,2048]{2,1,0:T(8,128)(2,1)S(1)}, u32[]{:S(2)}, u32[]{:S(2)}) collective-permute-start(bf16[8,32,2048]{2,1,0:T(8,128)(2,1)S(1)} %get-tuple-element.25.rest_0_), channel_id=1, source_target_pairs={{0,8},{2,10},{4,12},{6,14},{8,0},{10,2},{12,4},{14,6},{16,24},{18,... | collective-permute-start | bytes 3145736 | tf_op jit(solution)/shard_map/ppermute | solution.py:369
  21.6 2.2 %shard_map.57 = (bf16[4,96,2048]{2,1,0:T(8,128)(2,1)S(1)}, bf16[2,96,2048]{2,1,0:T(8,128)(2,1)S(1)}) custom-call(s32[32]{0:T(128)S(1)} %copy-done.1, bf16[24,128,2048]{2,1,0:T(8,128)(2,1)} %bitcast.11, bf16[6,96,2048]{2,1,0:T(8,128)(2,1)S(1)} %collective-permute-done.3.got_ref, bf16[8,96,2048]{2,1,0:T(8,128)(2,1)S(1)} %shard_map.56.rest_0_), custom_call_target="tpu_custom_call" | custom-call | tf_op jit(solution)/shard_map/pallas_call | solution.py:140
  24.5 16.1 %collective-permute-done.4.refs_1_ = bf16[2,96,2048]{2,1,0:T(8,128)(2,1)S(1)} collective-permute-done((bf16[2,96,2048]{2,1,0:T(8,128)(2,1)S(1)}, bf16[2,96,2048]{2,1,0:T(8,128)(2,1)S(1)}, u32[]{:S(2)}, u32[]{:S(2)}) %collective-permute-start.4) | collective-permute-done | bytes 786464 | tf_op jit(solution)/shard_map/ppermute | solution.py:369
  40.6 3.0 %collective-permute-done.5.refs_3_ = bf16[8,32,2048]{2,1,0:T(8,128)(2,1)S(1)} collective-permute-done((bf16[8,32,2048]{2,1,0:T(8,128)(2,1)S(1)}, bf16[8,32,2048]{2,1,0:T(8,128)(2,1)S(1)}, u32[]{:S(2)}, u32[]{:S(2)}) %collective-permute-start.5) | collective-permute-done | bytes 1048608 | tf_op jit(solution)/shard_map/ppermute | solution.py:369
  43.8 1.8 collective-permute-start.7
  45.6 2.7 %collective-permute-start.8 = (bf16[4,32,2048]{2,1,0:T(8,128)(2,1)S(1)}, bf16[4,32,2048]{2,1,0:T(8,128)(2,1)S(1)}, u32[]{:S(2)}, u32[]{:S(2)}) collective-permute-start(bf16[4,32,2048]{2,1,0:T(8,128)(2,1)S(1)} %get-tuple-element.32), channel_id=1, source_target_pairs={{0,16},{2,18},{4,20},{6,22},{8,24},{10,26},{12,28},{14,30},{16,0},... | collective-permute-start | bytes 1572872 | tf_op jit(solution)/shard_map/ppermute | solution.py:369
  48.3 2.5 %shard_map.59 = (bf16[2,96,2048]{2,1,0:T(8,128)(2,1)S(1)}, bf16[6,96,2048]{2,1,0:T(8,128)(2,1)S(1)}) custom-call(s32[32]{0:T(128)S(1)} %copy-done.1, bf16[24,128,2048]{2,1,0:T(8,128)(2,1)} %bitcast.12, bf16[8,96,2048]{2,1,0:T(8,128)(2,1)S(1)} %collective-permute-done.2.got_ref, bf16[2,96,2048]{2,1,0:T(8,128)(2,1)S(1)} %get-tuple-element.29.rest_0_), custom_call_target="tpu_custom_call" | custom-call | tf_op jit(solution)/shard_map/pallas_call | solution.py:140
  50.8 22.2 %collective-permute-done.8.refs_4_ = bf16[4,32,2048]{2,1,0:T(8,128)(2,1)S(1)} collective-permute-done((bf16[4,32,2048]{2,1,0:T(8,128)(2,1)S(1)}, bf16[4,32,2048]{2,1,0:T(8,128)(2,1)S(1)}, u32[]{:S(2)}, u32[]{:S(2)}) %collective-permute-start.8) | collective-permute-done | bytes 524320 | tf_op jit(solution)/shard_map/ppermute | solution.py:369
  74.4 2.4 %collective-permute-start.10 = (bf16[2,96,2048]{2,1,0:T(8,128)(2,1)S(1)}, bf16[2,96,2048]{2,1,0:T(8,128)(2,1)S(1)}, u32[]{:S(2)}, u32[]{:S(2)}) collective-permute-start(bf16[2,96,2048]{2,1,0:T(8,128)(2,1)S(1)} %get-tuple-element.35), channel_id=1, source_target_pairs={{0,16},{2,18},{4,20},{6,22},{8,24},{10,26},{12,28},{14,30},{16,0},... | collective-permute-start | bytes 2359304 | tf_op jit(solution)/shard_map/ppermute | solution.py:369
  76.8 2.0 collective-permute-start.11
  80.9 21.4 %collective-permute-done.12.rest_5_ = bf16[2,32,2048]{2,1,0:T(8,128)(2,1)S(1)} collective-permute-done((bf16[2,32,2048]{2,1,0:T(8,128)(2,1)S(1)}, bf16[2,32,2048]{2,1,0:T(8,128)(2,1)S(1)}, u32[]{:S(2)}, u32[]{:S(2)}) %collective-permute-start.12) | collective-permute-done | bytes 262176 | tf_op jit(solution)/shard_map/ppermute | solution.py:369
  102.3 8.0 %collective-permute-done.10.rest_2_ = bf16[2,96,2048]{2,1,0:T(8,128)(2,1)S(1)} collective-permute-done((bf16[2,96,2048]{2,1,0:T(8,128)(2,1)S(1)}, bf16[2,96,2048]{2,1,0:T(8,128)(2,1)S(1)}, u32[]{:S(2)}, u32[]{:S(2)}) %collective-permute-start.10) | collective-permute-done | bytes 786464 | tf_op jit(solution)/shard_map/ppermute | solution.py:369
  110.3 2.7 %shard_map.61 = (f32[2,128,2048]{2,1,0:T(8,128)}, bf16[2,128,2048]{2,1,0:T(8,128)(2,1)S(1)}, f32[2,128,128]{2,1,0:T(8,128)S(1)}) custom-call(s32[32]{0:T(128)S(1)} %copy-done.1, f32[2,128,2048]{2,1,0:T(8,128)S(1)} %bitcast.4, bf16[6,96,2048]{2,1,0:T(8,128)(2,1)S(1)} %get-tuple-element.30.refs_0_.rest_0_, ...), custom_call_target="tpu_custom_call" | custom-call | tf_op jit(solution)/shard_map/pallas_call | solution.py:272
  114.2 3.8 %collective-permute-done.13.refs_1_ = f32[2,128,128]{2,1,0:T(8,128)S(1)} collective-permute-done((f32[2,128,128]{2,1,0:T(8,128)S(1)}, f32[2,128,128]{2,1,0:T(8,128)S(1)}, u32[]{:S(2)}, u32[]{:S(2)}) %collective-permute-start.13) | collective-permute-done | bytes 131104 | tf_op jit(solution)/shard_map/ppermute | solution.py:565
  118.0 4.5 %shard_map.62 = (bf16[2,96,2048]{2,1,0:T(8,128)(2,1)S(1)}, bf16[2,32,2048]{2,1,0:T(8,128)(2,1)S(1)}) custom-call(f32[2,128,128]{2,1,0:T(8,128)S(1)} %get-tuple-element.39.refs_0_, f32[2,128,128]{2,1,0:T(8,128)S(1)} %collective-permute-done.13.refs_1_, bf16[2,128,2048]{2,1,0:T(8,128)(2,1)S(1)} %get-tuple-element.40.refs_2_), custom_call_target="tpu_custom_call" | custom-call | tf_op jit(solution)/shard_map/pallas_call | solution.py:355
  123.8 2.3 %collective-permute-start.14 = (bf16[2,96,2048]{2,1,0:T(8,128)(2,1)S(1)}, bf16[2,96,2048]{2,1,0:T(8,128)(2,1)S(1)}, u32[]{:S(2)}, u32[]{:S(2)}) collective-permute-start(bf16[2,96,2048]{2,1,0:T(8,128)(2,1)S(1)} %get-tuple-element.41.refs_0_), channel_id=1, source_target_pairs={{0,16},{2,18},{4,20},{6,22},{8,24},{10,26},{12,28},{14,30},{16,0},... | collective-permute-start | bytes 2359304 | tf_op jit(solution)/shard_map/ppermute | solution.py:369
  126.1 1.9 collective-permute-start.16
  128.8 12.8 %collective-permute-done.18.refs_1_ = bf16[2,96,2048]{2,1,0:T(8,128)(2,1)S(1)} collective-permute-done((bf16[2,96,2048]{2,1,0:T(8,128)(2,1)S(1)}, bf16[2,96,2048]{2,1,0:T(8,128)(2,1)S(1)}, u32[]{:S(2)}, u32[]{:S(2)}) %collective-permute-start.18) | collective-permute-done | bytes 786464 | tf_op jit(solution)/shard_map/ppermute | solution.py:369
  141.7 2.7 %collective-permute-done.17.refs_3_ = bf16[2,32,2048]{2,1,0:T(8,128)(2,1)S(1)} collective-permute-done((bf16[2,32,2048]{2,1,0:T(8,128)(2,1)S(1)}, bf16[2,32,2048]{2,1,0:T(8,128)(2,1)S(1)}, u32[]{:S(2)}, u32[]{:S(2)}) %collective-permute-start.17) | collective-permute-done | bytes 262176 | tf_op jit(solution)/shard_map/ppermute | solution.py:369
  144.4 13.4 %collective-permute-done.14.refs_0_ = bf16[2,96,2048]{2,1,0:T(8,128)(2,1)S(1)} collective-permute-done((bf16[2,96,2048]{2,1,0:T(8,128)(2,1)S(1)}, bf16[2,96,2048]{2,1,0:T(8,128)(2,1)S(1)}, u32[]{:S(2)}, u32[]{:S(2)}) %collective-permute-start.14) | collective-permute-done | bytes 786464 | tf_op jit(solution)/shard_map/ppermute | solution.py:369
  159.8 3.6 %collective-permute-start.19 = (bf16[4,32,2048]{2,1,0:T(8,128)(2,1)S(1)}, bf16[4,32,2048]{2,1,0:T(8,128)(2,1)S(1)}, u32[]{:S(2)}, u32[]{:S(2)}) collective-permute-start(bf16[4,32,2048]{2,1,0:T(8,128)(2,1)S(1)} %get-tuple-element.43.refs_1_), channel_id=1, source_target_pairs={{0,16},{2,18},{4,20},{6,22},{8,24},{10,26},{12,28},{14,30},{16,0},... | collective-permute-start | bytes 1572872 | tf_op jit(solution)/shard_map/ppermute | solution.py:369
  164.0 22.8 %collective-permute-done.19.refs_2_ = bf16[4,32,2048]{2,1,0:T(8,128)(2,1)S(1)} collective-permute-done((bf16[4,32,2048]{2,1,0:T(8,128)(2,1)S(1)}, bf16[4,32,2048]{2,1,0:T(8,128)(2,1)S(1)}, u32[]{:S(2)}, u32[]{:S(2)}) %collective-permute-start.19) | collective-permute-done | bytes 524320 | tf_op jit(solution)/shard_map/ppermute | solution.py:369
  187.6 3.4 %collective-permute-start.22 = (bf16[8,32,2048]{2,1,0:T(8,128)(2,1)S(1)}, bf16[8,32,2048]{2,1,0:T(8,128)(2,1)S(1)}, u32[]{:S(2)}, u32[]{:S(2)}) collective-permute-start(bf16[8,32,2048]{2,1,0:T(8,128)(2,1)S(1)} %get-tuple-element.46.refs_2_), channel_id=1, source_target_pairs={{0,8},{2,10},{4,12},{6,14},{8,0},{10,2},{12,4},{14,6},{16,24},{18,... | collective-permute-start | bytes 3145736 | tf_op jit(solution)/shard_map/ppermute | solution.py:369
  192.5 19.5 %collective-permute-done.22.refs_2_ = bf16[8,32,2048]{2,1,0:T(8,128)(2,1)S(1)} collective-permute-done((bf16[8,32,2048]{2,1,0:T(8,128)(2,1)S(1)}, bf16[8,32,2048]{2,1,0:T(8,128)(2,1)S(1)}, u32[]{:S(2)}, u32[]{:S(2)}) %collective-permute-start.22) | collective-permute-done | bytes 1048608 | tf_op jit(solution)/shard_map/ppermute | solution.py:369
  212.6 2.0 shard_map.66.refs_4_
  214.6 2.9 %shard_map.67.refs_4_ = bf16[24,128,2048]{2,1,0:T(8,128)(2,1)} custom-call(s32[32]{0:T(128)S(1)} %copy-done.1, bf16[4,96,2048]{2,1,0:T(8,128)(2,1)S(1)} %get-tuple-element.44.refs_3_.refs_0_, bf16[4,96,2048]{2,1,0:T(8,128)(2,1)S(1)} %collective-permute-done.26.refs_1_, ...), custom_call_target="tpu_custom_call", output_to_operand_aliasing={{}: (5, {})} | custom-call | tf_op jit(solution)/shard_map/pallas_call | solution.py:232
  217.5 2.4 %shard_map.68.refs_4_ = bf16[24,128,2048]{2,1,0:T(8,128)(2,1)} custom-call(s32[32]{0:T(128)S(1)} %copy-done.1, bf16[2,96,2048]{2,1,0:T(8,128)(2,1)S(1)} %get-tuple-element.45.refs_2_.refs_0_, bf16[2,96,2048]{2,1,0:T(8,128)(2,1)S(1)} %collective-permute-done.24.refs_1_, ...), custom_call_target="tpu_custom_call", output_to_operand_aliasing={{}: (5, {})} | custom-call | tf_op jit(solution)/shard_map/pallas_call | solution.py:232
  219.9 2.3 %shard_map.69 = bf16[24,128,2048]{2,1,0:T(8,128)(2,1)} custom-call(s32[32]{0:T(128)S(1)} %copy-done.1, bf16[2,96,2048]{2,1,0:T(8,128)(2,1)S(1)} %collective-permute-done.20.refs_0_, bf16[2,96,2048]{2,1,0:T(8,128)(2,1)S(1)} %collective-permute-done.21.refs_1_, ...), custom_call_target="tpu_custom_call", output_to_operand_aliasing={{}: (5, {})} | custom-call | tf_op jit(solution)/shard_map/pallas_call | solution.py:232
  (52 shorter events, 21.6 us)
Async XLA Ops:
  2.4 0.7 copy-start.1
  5.5 5.0 %collective-permute-start.1 = (bf16[16,32,2048]{2,1,0:T(8,128)(2,1)S(1)}, bf16[16,32,2048]{2,1,0:T(8,128)(2,1)S(1)}, u32[]{:S(2)}, u32[]{:S(2)}) collective-permute-start(bf16[16,32,2048]{2,1,0:T(8,128)(2,1)S(1)} %shard_map.51.rest_0_), channel_id=1, source_target_pairs={{0,2},{2,0},{4,6},{6,4},{8,10},{10,8},{12,14},{14,12},{16,18},{18,... | collective-permute-start | bytes 6291464 | tf_op jit(solution)/shard_map/ppermute | solution.py:369
  7.6 5.1 %collective-permute-start = (bf16[2,96,2048]{2,1,0:T(8,128)(2,1)S(1)}, bf16[2,96,2048]{2,1,0:T(8,128)(2,1)S(1)}, u32[]{:S(2)}, u32[]{:S(2)}) collective-permute-start(bf16[2,96,2048]{2,1,0:T(8,128)(2,1)S(1)} %shard_map.52.rest_0_), channel_id=1, source_target_pairs={{0,2},{2,0},{4,6},{6,4},{8,10},{10,8},{12,14},{14,12},{16,18},{18,... | collective-permute-start | bytes 2359304 | tf_op jit(solution)/shard_map/ppermute | solution.py:369
  10.0 11.6 %collective-permute-start.3 = (bf16[6,96,2048]{2,1,0:T(8,128)(2,1)S(1)}, bf16[6,96,2048]{2,1,0:T(8,128)(2,1)S(1)}, u32[]{:S(2)}, u32[]{:S(2)}) collective-permute-start(bf16[6,96,2048]{2,1,0:T(8,128)(2,1)S(1)} %shard_map.53.rest_0_), channel_id=1, source_target_pairs={{0,2},{2,0},{4,6},{6,4},{8,10},{10,8},{12,14},{14,12},{16,18},{18,... | collective-permute-start | bytes 7077896 | tf_op jit(solution)/shard_map/ppermute | solution.py:369
  17.0 31.3 %collective-permute-start.2 = (bf16[8,96,2048]{2,1,0:T(8,128)(2,1)S(1)}, bf16[8,96,2048]{2,1,0:T(8,128)(2,1)S(1)}, u32[]{:S(2)}, u32[]{:S(2)}) collective-permute-start(bf16[8,96,2048]{2,1,0:T(8,128)(2,1)S(1)} %shard_map.56.rest_0_), channel_id=1, source_target_pairs={{0,2},{2,0},{4,6},{6,4},{8,10},{10,8},{12,14},{14,12},{16,18},{18,... | collective-permute-start | bytes 9437192 | tf_op jit(solution)/shard_map/ppermute | solution.py:369
  17.3 26.3 %collective-permute-start.5 = (bf16[8,32,2048]{2,1,0:T(8,128)(2,1)S(1)}, bf16[8,32,2048]{2,1,0:T(8,128)(2,1)S(1)}, u32[]{:S(2)}, u32[]{:S(2)}) collective-permute-start(bf16[8,32,2048]{2,1,0:T(8,128)(2,1)S(1)} %get-tuple-element.25.rest_0_), channel_id=1, source_target_pairs={{0,8},{2,10},{4,12},{6,14},{8,0},{10,2},{12,4},{14,6},{16,24},{18,... | collective-permute-start | bytes 3145736 | tf_op jit(solution)/shard_map/ppermute | solution.py:369
  20.2 20.4 %collective-permute-start.4 = (bf16[2,96,2048]{2,1,0:T(8,128)(2,1)S(1)}, bf16[2,96,2048]{2,1,0:T(8,128)(2,1)S(1)}, u32[]{:S(2)}, u32[]{:S(2)}) collective-permute-start(bf16[2,96,2048]{2,1,0:T(8,128)(2,1)S(1)} %shard_map.55.rest_0_), channel_id=1, source_target_pairs={{0,4},{2,6},{4,0},{6,2},{8,12},{10,14},{12,8},{14,10},{16,20},{18,... | collective-permute-start | bytes 2359304 | tf_op jit(solution)/shard_map/ppermute | solution.py:369
  23.8 50.3 %collective-permute-start.6 = (bf16[4,96,2048]{2,1,0:T(8,128)(2,1)S(1)}, bf16[4,96,2048]{2,1,0:T(8,128)(2,1)S(1)}, u32[]{:S(2)}, u32[]{:S(2)}) collective-permute-start(bf16[4,96,2048]{2,1,0:T(8,128)(2,1)S(1)} %get-tuple-element.28.refs_4_), channel_id=1, source_target_pairs={{0,4},{2,6},{4,0},{6,2},{8,12},{10,14},{12,8},{14,10},{16,20},{18,... | collective-permute-start | bytes 4718600 | tf_op jit(solution)/shard_map/ppermute | solution.py:369
  43.8 30.3 %collective-permute-start.7 = (bf16[2,96,2048]{2,1,0:T(8,128)(2,1)S(1)}, bf16[2,96,2048]{2,1,0:T(8,128)(2,1)S(1)}, u32[]{:S(2)}, u32[]{:S(2)}) collective-permute-start(bf16[2,96,2048]{2,1,0:T(8,128)(2,1)S(1)} %get-tuple-element.29.rest_0_), channel_id=1, source_target_pairs={{0,8},{2,10},{4,12},{6,14},{8,0},{10,2},{12,4},{14,6},{16,24},{18,... | collective-permute-start | bytes 2359304 | tf_op jit(solution)/shard_map/ppermute | solution.py:369
  45.6 27.4 %collective-permute-start.8 = (bf16[4,32,2048]{2,1,0:T(8,128)(2,1)S(1)}, bf16[4,32,2048]{2,1,0:T(8,128)(2,1)S(1)}, u32[]{:S(2)}, u32[]{:S(2)}) collective-permute-start(bf16[4,32,2048]{2,1,0:T(8,128)(2,1)S(1)} %get-tuple-element.32), channel_id=1, source_target_pairs={{0,16},{2,18},{4,20},{6,22},{8,24},{10,26},{12,28},{14,30},{16,0},... | collective-permute-start | bytes 1572872 | tf_op jit(solution)/shard_map/ppermute | solution.py:369
  74.1 36.2 %copy-start = (f32[1,2,128,2048]{3,2,1,0:T(8,128)S(1)}, f32[1,2,128,2048]{3,2,1,0:T(8,128)}, u32[]{:S(2)}) copy-start(f32[1,2,128,2048]{3,2,1,0:T(8,128)} %param.5) | copy-start | bytes 6291460
  74.4 35.9 %collective-permute-start.10 = (bf16[2,96,2048]{2,1,0:T(8,128)(2,1)S(1)}, bf16[2,96,2048]{2,1,0:T(8,128)(2,1)S(1)}, u32[]{:S(2)}, u32[]{:S(2)}) collective-permute-start(bf16[2,96,2048]{2,1,0:T(8,128)(2,1)S(1)} %get-tuple-element.35), channel_id=1, source_target_pairs={{0,16},{2,18},{4,20},{6,22},{8,24},{10,26},{12,28},{14,30},{16,0},... | collective-permute-start | bytes 2359304 | tf_op jit(solution)/shard_map/ppermute | solution.py:369
  76.8 33.5 %collective-permute-start.11 = (bf16[2,96,2048]{2,1,0:T(8,128)(2,1)S(1)}, bf16[2,96,2048]{2,1,0:T(8,128)(2,1)S(1)}, u32[]{:S(2)}, u32[]{:S(2)}) collective-permute-start(bf16[2,96,2048]{2,1,0:T(8,128)(2,1)S(1)} %get-tuple-element.36), channel_id=1, source_target_pairs={{0,8},{2,10},{4,12},{6,14},{8,0},{10,2},{12,4},{14,6},{16,24},{18,... | collective-permute-start | bytes 2359304 | tf_op jit(solution)/shard_map/ppermute | solution.py:369
  78.8 31.5 %collective-permute-start.9 = (bf16[2,96,2048]{2,1,0:T(8,128)(2,1)S(1)}, bf16[2,96,2048]{2,1,0:T(8,128)(2,1)S(1)}, u32[]{:S(2)}, u32[]{:S(2)}) collective-permute-start(bf16[2,96,2048]{2,1,0:T(8,128)(2,1)S(1)} %get-tuple-element.34), channel_id=1, source_target_pairs={{0,4},{2,6},{4,0},{6,2},{8,12},{10,14},{12,8},{14,10},{16,20},{18,... | collective-permute-start | bytes 2359304 | tf_op jit(solution)/shard_map/ppermute | solution.py:369
  80.0 22.3 %collective-permute-start.12 = (bf16[2,32,2048]{2,1,0:T(8,128)(2,1)S(1)}, bf16[2,32,2048]{2,1,0:T(8,128)(2,1)S(1)}, u32[]{:S(2)}, u32[]{:S(2)}) collective-permute-start(bf16[2,32,2048]{2,1,0:T(8,128)(2,1)S(1)} %get-tuple-element.38), channel_id=1, source_target_pairs={{0,4},{2,6},{4,0},{6,2},{8,12},{10,14},{12,8},{14,10},{16,20},{18,... | collective-permute-start | bytes 786440 | tf_op jit(solution)/shard_map/ppermute | solution.py:369
  113.0 5.0 %collective-permute-start.13 = (f32[2,128,128]{2,1,0:T(8,128)S(1)}, f32[2,128,128]{2,1,0:T(8,128)S(1)}, u32[]{:S(2)}, u32[]{:S(2)}) collective-permute-start(f32[2,128,128]{2,1,0:T(8,128)S(1)} %get-tuple-element.39.refs_0_), channel_id=1, source_target_pairs={{0,1},{1,0},{2,3},{3,2},{4,5},{5,4},{6,7},{7,6},{8,9},{9,8},{10,11... | collective-permute-start | bytes 393224 | tf_op jit(solution)/shard_map/ppermute | solution.py:565
  122.5 19.2 %collective-permute-start.18 = (bf16[2,96,2048]{2,1,0:T(8,128)(2,1)S(1)}, bf16[2,96,2048]{2,1,0:T(8,128)(2,1)S(1)}, u32[]{:S(2)}, u32[]{:S(2)}) collective-permute-start(bf16[2,96,2048]{2,1,0:T(8,128)(2,1)S(1)} %get-tuple-element.41.refs_0_), channel_id=1, source_target_pairs={{0,4},{2,6},{4,0},{6,2},{8,12},{10,14},{12,8},{14,10},{16,20},{18,... | collective-permute-start | bytes 2359304 | tf_op jit(solution)/shard_map/ppermute | solution.py:369
  123.8 34.1 %collective-permute-start.14 = (bf16[2,96,2048]{2,1,0:T(8,128)(2,1)S(1)}, bf16[2,96,2048]{2,1,0:T(8,128)(2,1)S(1)}, u32[]{:S(2)}, u32[]{:S(2)}) collective-permute-start(bf16[2,96,2048]{2,1,0:T(8,128)(2,1)S(1)} %get-tuple-element.41.refs_0_), channel_id=1, source_target_pairs={{0,16},{2,18},{4,20},{6,22},{8,24},{10,26},{12,28},{14,30},{16,0},... | collective-permute-start | bytes 2359304 | tf_op jit(solution)/shard_map/ppermute | solution.py:369
  126.1 31.8 %collective-permute-start.16 = (bf16[2,96,2048]{2,1,0:T(8,128)(2,1)S(1)}, bf16[2,96,2048]{2,1,0:T(8,128)(2,1)S(1)}, u32[]{:S(2)}, u32[]{:S(2)}) collective-permute-start(bf16[2,96,2048]{2,1,0:T(8,128)(2,1)S(1)} %get-tuple-element.41.refs_0_), channel_id=1, source_target_pairs={{0,8},{2,10},{4,12},{6,14},{8,0},{10,2},{12,4},{14,6},{16,24},{18,... | collective-permute-start | bytes 2359304 | tf_op jit(solution)/shard_map/ppermute | solution.py:369
  128.0 16.4 %collective-permute-start.17 = (bf16[2,32,2048]{2,1,0:T(8,128)(2,1)S(1)}, bf16[2,32,2048]{2,1,0:T(8,128)(2,1)S(1)}, u32[]{:S(2)}, u32[]{:S(2)}) collective-permute-start(bf16[2,32,2048]{2,1,0:T(8,128)(2,1)S(1)} %get-tuple-element.42.refs_2_), channel_id=1, source_target_pairs={{0,4},{2,6},{4,0},{6,2},{8,12},{10,14},{12,8},{14,10},{16,20},{18,... | collective-permute-start | bytes 786440 | tf_op jit(solution)/shard_map/ppermute | solution.py:369
  158.1 33.4 %collective-permute-start.27 = (bf16[4,96,2048]{2,1,0:T(8,128)(2,1)S(1)}, bf16[4,96,2048]{2,1,0:T(8,128)(2,1)S(1)}, u32[]{:S(2)}, u32[]{:S(2)}) collective-permute-start(bf16[4,96,2048]{2,1,0:T(8,128)(2,1)S(1)} %get-tuple-element.44.refs_3_.refs_0_), channel_id=1, source_target_pairs={{0,4},{2,6},{4,0},{6,2},{8,12},{10,14},{12,8},{14,10},{16,20},{18,... | collective-permute-start | bytes 4718600 | tf_op jit(solution)/shard_map/ppermute | solution.py:369
  158.7 28.8 %collective-permute-start.15 = (bf16[2,96,2048]{2,1,0:T(8,128)(2,1)S(1)}, bf16[2,96,2048]{2,1,0:T(8,128)(2,1)S(1)}, u32[]{:S(2)}, u32[]{:S(2)}) collective-permute-start(bf16[2,96,2048]{2,1,0:T(8,128)(2,1)S(1)} %collective-permute-done.14.refs_0_), channel_id=1, source_target_pairs={{0,8},{2,10},{4,12},{6,14},{8,0},{10,2},{12,4},{14,6},{16,24},{18,... | collective-permute-start | bytes 2359304 | tf_op jit(solution)/shard_map/ppermute | solution.py:369
  159.8 26.9 %collective-permute-start.19 = (bf16[4,32,2048]{2,1,0:T(8,128)(2,1)S(1)}, bf16[4,32,2048]{2,1,0:T(8,128)(2,1)S(1)}, u32[]{:S(2)}, u32[]{:S(2)}) collective-permute-start(bf16[4,32,2048]{2,1,0:T(8,128)(2,1)S(1)} %get-tuple-element.43.refs_1_), channel_id=1, source_target_pairs={{0,16},{2,18},{4,20},{6,22},{8,24},{10,26},{12,28},{14,30},{16,0},... | collective-permute-start | bytes 1572872 | tf_op jit(solution)/shard_map/ppermute | solution.py:369
  163.5 28.8 %collective-permute-start.29 = (bf16[4,96,2048]{2,1,0:T(8,128)(2,1)S(1)}, bf16[4,96,2048]{2,1,0:T(8,128)(2,1)S(1)}, u32[]{:S(2)}, u32[]{:S(2)}) collective-permute-start(bf16[4,96,2048]{2,1,0:T(8,128)(2,1)S(1)} %shard_map.63.refs_4_.refs_0_), channel_id=1, source_target_pairs={{0,2},{2,0},{4,6},{6,4},{8,10},{10,8},{12,14},{14,12},{16,18},{18,... | collective-permute-start | bytes 4718600 | tf_op jit(solution)/shard_map/ppermute | solution.py:369
  163.5 48.5 %collective-permute-start.26 = (bf16[4,96,2048]{2,1,0:T(8,128)(2,1)S(1)}, bf16[4,96,2048]{2,1,0:T(8,128)(2,1)S(1)}, u32[]{:S(2)}, u32[]{:S(2)}) collective-permute-start(bf16[4,96,2048]{2,1,0:T(8,128)(2,1)S(1)} %get-tuple-element.44.refs_3_.refs_0_), channel_id=1, source_target_pairs={{0,2},{2,0},{4,6},{6,4},{8,10},{10,8},{12,14},{14,12},{16,18},{18,... | collective-permute-start | bytes 4718600 | tf_op jit(solution)/shard_map/ppermute | solution.py:369
  187.6 24.3 %collective-permute-start.22 = (bf16[8,32,2048]{2,1,0:T(8,128)(2,1)S(1)}, bf16[8,32,2048]{2,1,0:T(8,128)(2,1)S(1)}, u32[]{:S(2)}, u32[]{:S(2)}) collective-permute-start(bf16[8,32,2048]{2,1,0:T(8,128)(2,1)S(1)} %get-tuple-element.46.refs_2_), channel_id=1, source_target_pairs={{0,8},{2,10},{4,12},{6,14},{8,0},{10,2},{12,4},{14,6},{16,24},{18,... | collective-permute-start | bytes 3145736 | tf_op jit(solution)/shard_map/ppermute | solution.py:369
  191.5 23.0 %collective-permute-start.28 = (bf16[4,96,2048]{2,1,0:T(8,128)(2,1)S(1)}, bf16[4,96,2048]{2,1,0:T(8,128)(2,1)S(1)}, u32[]{:S(2)}, u32[]{:S(2)}) collective-permute-start(bf16[4,96,2048]{2,1,0:T(8,128)(2,1)S(1)} %collective-permute-done.27.refs_2_), channel_id=1, source_target_pairs={{0,2},{2,0},{4,6},{6,4},{8,10},{10,8},{12,14},{14,12},{16,18},{18,... | collective-permute-start | bytes 4718600 | tf_op jit(solution)/shard_map/ppermute | solution.py:369
  191.5 21.0 %collective-permute-start.20 = (bf16[2,96,2048]{2,1,0:T(8,128)(2,1)S(1)}, bf16[2,96,2048]{2,1,0:T(8,128)(2,1)S(1)}, u32[]{:S(2)}, u32[]{:S(2)}) collective-permute-start(bf16[2,96,2048]{2,1,0:T(8,128)(2,1)S(1)} %get-tuple-element.45.refs_2_.refs_0_), channel_id=1, source_target_pairs={{0,4},{2,6},{4,0},{6,2},{8,12},{10,14},{12,8},{14,10},{16,20},{18,... | collective-permute-start | bytes 2359304 | tf_op jit(solution)/shard_map/ppermute | solution.py:369
  192.2 25.2 %collective-permute-start.25 = (bf16[8,32,2048]{2,1,0:T(8,128)(2,1)S(1)}, bf16[8,32,2048]{2,1,0:T(8,128)(2,1)S(1)}, u32[]{:S(2)}, u32[]{:S(2)}) collective-permute-start(bf16[8,32,2048]{2,1,0:T(8,128)(2,1)S(1)} %get-tuple-element.46.refs_2_), channel_id=1, source_target_pairs={{0,2},{2,0},{4,6},{6,4},{8,10},{10,8},{12,14},{14,12},{16,18},{18,... | collective-permute-start | bytes 3145736 | tf_op jit(solution)/shard_map/ppermute | solution.py:369
  212.0 7.9 %collective-permute-start.23 = (bf16[8,32,2048]{2,1,0:T(8,128)(2,1)S(1)}, bf16[8,32,2048]{2,1,0:T(8,128)(2,1)S(1)}, u32[]{:S(2)}, u32[]{:S(2)}) collective-permute-start(bf16[8,32,2048]{2,1,0:T(8,128)(2,1)S(1)} %collective-permute-done.22.refs_2_), channel_id=1, source_target_pairs={{0,2},{2,0},{4,6},{6,4},{8,10},{10,8},{12,14},{14,12},{16,18},{18,... | collective-permute-start | bytes 3145736 | tf_op jit(solution)/shard_map/ppermute | solution.py:369
  212.0 5.5 %collective-permute-start.24 = (bf16[2,96,2048]{2,1,0:T(8,128)(2,1)S(1)}, bf16[2,96,2048]{2,1,0:T(8,128)(2,1)S(1)}, u32[]{:S(2)}, u32[]{:S(2)}) collective-permute-start(bf16[2,96,2048]{2,1,0:T(8,128)(2,1)S(1)} %get-tuple-element.45.refs_2_.refs_0_), channel_id=1, source_target_pairs={{0,2},{2,0},{4,6},{6,4},{8,10},{10,8},{12,14},{14,12},{16,18},{18,... | collective-permute-start | bytes 2359304 | tf_op jit(solution)/shard_map/ppermute | solution.py:369
  212.5 7.4 %collective-permute-start.21 = (bf16[2,96,2048]{2,1,0:T(8,128)(2,1)S(1)}, bf16[2,96,2048]{2,1,0:T(8,128)(2,1)S(1)}, u32[]{:S(2)}, u32[]{:S(2)}) collective-permute-start(bf16[2,96,2048]{2,1,0:T(8,128)(2,1)S(1)} %collective-permute-done.20.refs_0_), channel_id=1, source_target_pairs={{0,2},{2,0},{4,6},{6,4},{8,10},{10,8},{12,14},{14,12},{16,18},{18,... | collective-permute-start | bytes 2359304 | tf_op jit(solution)/shard_map/ppermute | solution.py:369

commit v5 on v4

--- a/solution.py
+++ b/solution.py
@@ -46,6 +46,10 @@
 
 def small_cost():
     return pl.CostEstimate(flops=0, bytes_accessed=0, transcendentals=0)
+
+
+def token():
+    return jax.ShapeDtypeStruct((8, 128), jnp.float32)
 
 
 def table_kernel(slots, me_ref, owner_ref, table_ref, used):
@@ -202,7 +206,8 @@
 
 def spread_kernel(plans, slots, table_ref, *refs):
     piece_refs = refs[: len(plans)]
-    out_ref, sem = refs[-2:]
+    out_ref, token_ref, sem = refs[-3:]
+    token_ref[...] = jnp.zeros_like(token_ref)
     for wait in (False, True):
         for p, (first, order) in enumerate(plans):
             for item, place in starts(order, slots):
@@ -228,12 +233,11 @@
     plans = tuple((first, tuple(order)) for _, first, order in pieces)
     most = max(a.shape[0] for a in arrays)
     more = [] if target is None else [target]
-    after = [a for a in after if a is not target]
     return pl.pallas_call(
         functools.partial(spread_kernel, plans, slots),
-        out_shape=jax.ShapeDtypeStruct(shape, arrays[0].dtype),
+        out_shape=[jax.ShapeDtypeStruct(shape, arrays[0].dtype), token()],
         in_specs=in_smem() + in_vmem(count) + anywhere(len(more) + len(after)),
-        out_specs=anywhere()[0],
+        out_specs=anywhere() + in_vmem(),
         scratch_shapes=[pltpu.SemaphoreType.DMA((count, most))],
         input_output_aliases={1 + count: 0} if more else {},
         compiler_params=limits(MORE_VMEM_BYTES),
@@ -241,60 +245,85 @@
     )(table, *arrays, *more, *after)
 
 
-def momentum_kernel(scale, sizes, held_ref, momentum_ref, *rest):
-    part_refs = rest[: sum(sizes)]
-    next_ref, rounded_ref, gram_ref = rest[sum(sizes) :]
-    held = held_ref[pl.program_id(0)] >= 0
+def mean_rows(scale, sizes, refs):
     first, used = 0, 0
     for size in sizes:
         total = None
-        for ref in part_refs[used : used + size]:
-            term = ref[0].astype(jnp.float32)
+        for ref, item in refs[used : used + size]:
+            term = ref[item].astype(jnp.float32)
             total = term if total is None else total + term
-        rows = total.shape[0]
-        here = pl.ds(first, rows)
-        mean = total * scale
+        yield first, total * scale
+        first += total.shape[0]
+        used += size
+
+
+def nesterov_kernel(scale, sizes, items, momentum_ref, *rest):
+    part_refs, (rounded_ref, gram_ref) = rest[: len(items)], rest[len(items) :]
+    for s in range(momentum_ref.shape[0]):
+        refs = [(ref, item + s) for ref, item in zip(part_refs, items)]
+        for first, mean in mean_rows(scale, sizes, refs):
+            here = pl.ds(first, mean.shape[0])
+            following = DECAY * momentum_ref[s, here] + mean
+            rounded_ref[s, here] = (mean + DECAY * following).astype(jnp.bfloat16)
+        rounded = rounded_ref[s]
+        gram_ref[s] = lax.dot_general(
+            rounded,
+            rounded,
+            (((1,), (1,)), ((), ())),
+            preferred_element_type=jnp.float32,
+        )
+
+
+def momentum_kernel(scale, sizes, count, table_ref, momentum_ref, *rest):
+    part_refs, (next_ref, token_ref) = rest[:count], rest[-2:]
+    token_ref[...] = jnp.zeros_like(token_ref)
+    held = table_ref[pl.program_id(0)] >= 0
+    for first, mean in mean_rows(scale, sizes, [(ref, 0) for ref in part_refs]):
+        here = pl.ds(first, mean.shape[0])
         previous = momentum_ref[0, here]
-        following = DECAY * previous + mean
-        next_ref[0, here] = jnp.where(held, following, previous)
-        rounded_ref[0, here] = (mean + DECAY * following).astype(jnp.bfloat16)
-        first += rows
-        used += size
-    rounded = rounded_ref[0]
-    gram_ref[0] = lax.dot_general(
-        rounded, rounded, (((1,), (1,)), ((), ())), preferred_element_type=jnp.float32
-    )
-
-
-def momentum_step(held, momentum, parts, owner_count):
+        next_ref[0, here] = jnp.where(held, DECAY * previous + mean, previous)
+
+
+def nesterov_step(momentum, parts, owner_count):
     slots, rows, cols = momentum.shape
     flat = [b for part in parts for b in part]
-    return pl.pallas_call(
-        functools.partial(
-            momentum_kernel, 1.0 / owner_count, [len(part) for part in parts]
-        ),
-        grid=(slots,),
+    sizes = [len(part) for part in parts]
+    items = [b.start for b in flat]
+    return pl.pallas_call(
+        functools.partial(nesterov_kernel, 1.0 / owner_count, sizes, items),
         out_shape=[
-            jax.ShapeDtypeStruct((slots, rows, cols), jnp.float32),
             jax.ShapeDtypeStruct((slots, rows, cols), jnp.bfloat16),
             jax.ShapeDtypeStruct((slots, rows, rows), jnp.float32),
         ],
-        in_specs=[
-            pl.BlockSpec(memory_space=pltpu.SMEM),
-            pl.BlockSpec((1, rows, cols), lambda s: (s, 0, 0)),
-        ]
+        in_specs=in_vmem(1 + len(flat)),
+        out_specs=in_vmem(2),
+        compiler_params=limits(),
+        cost_estimate=small_cost(),
+    )(momentum, *[b.array for b in flat])
+
+
+def momentum_step(after, table, momentum, parts, owner_count):
+    slots, rows, cols = momentum.shape
+    flat = [b for part in parts for b in part]
+    sizes = [len(part) for part in parts]
+    return pl.pallas_call(
+        functools.partial(momentum_kernel, 1.0 / owner_count, sizes, len(flat)),
+        grid=(slots,),
+        out_shape=[jax.ShapeDtypeStruct((slots, rows, cols), jnp.float32), token()],
+        in_specs=in_smem()
+        + [pl.BlockSpec((1, rows, cols), lambda s: (s, 0, 0))]
         + [
             pl.BlockSpec((1,) + b.array.shape[1:], lambda s, at=b.start: (s + at, 0, 0))
             for b in flat
-        ],
+        ]
+        + anywhere(len(after)),
         out_specs=[
             pl.BlockSpec((1, rows, cols), lambda s: (s, 0, 0)),
-            pl.BlockSpec((1, rows, cols), lambda s: (s, 0, 0)),
-            pl.BlockSpec((1, rows, rows), lambda s: (s, 0, 0)),
+            pl.BlockSpec((8, 128), lambda s: (0, 0)),
         ],
         compiler_params=limits(),
         cost_estimate=small_cost(),
-    )(held, momentum, *[b.array for b in flat])
+    )(table, momentum, *[b.array for b in flat], *after)
 
 
 def exact(a, b):
@@ -451,9 +480,6 @@
     other_got = swap(away, other_bits[0])
     after = take(top, [away])
     x_got = swap(over_x[top], X_BIT)
-    for k in range(top - 2, -1, -1):
-        after = take_off(k, after)
-
     pending = {}
     for k in range(top, -1, -1):
         terms = {o: [] for o in level[k]}
@@ -482,6 +508,9 @@
         if held_back:
             over_x[0] = made.pop()
         else:
+            if k == top:
+                for n in range(top - 2, -1, -1):
+                    after = take_off(n, after)
             after = take(k - 2, after)
         pending = {o: swap(made[n], last[o]) for n, o in enumerate(level[k])}
         kept = made[-1]
@@ -490,7 +519,7 @@
     return [[home[0]] + terms[0], [Block(kept, 0), Block(other_got, 0)]]
 
 
-def spread_updates(blocks, table, slots, bits, cut, shape):
+def spread_updates(blocks, table, slots, bits, cut, shape, early):
     level = levels(bits)
     last = [dict(found) for found in level]
     own, cur = blocks
@@ -499,7 +528,14 @@
     other_bits = [X_BIT] + bits
     front, front_order = own, [0]
     pieces = {0: own}
-    after, update, waiting = [], None, []
+    after, update = [early], None
+
+    def with_core(array, first, order):
+        return [
+            (array, first, order),
+            (swap(array, CORE_BIT), first, [CORE_BIT | o for o in order]),
+        ]
+
     for k in range(top + 1):
         x_got = swap(front, X_BIT)
         longer = {}
@@ -508,40 +544,29 @@
                 if at < j:
                     longer[o | bit] = swap(pieces[o], bit)
         other_got = swap(cur, other_bits[k])
-        made = [(front, 0, front_order), (x_got, 0, [X_BIT | o for o in front_order])]
+        crossed = (x_got, 0, [X_BIT | o for o in front_order])
+        crossed_other = (other_got, cut, [other_bits[k] | o for o in cur_order])
         if k == top:
             break
         if k == 0:
             (both,) = combine(after, joined(front, x_got))
-            made = [(both, 0, front_order + [X_BIT | o for o in front_order])]
+            waiting = with_core(both, 0, front_order + crossed[2])
             after = [both]
-        order = [o for o, _ in level[k + 1]]
-        wanted = [joined(*[longer[o] for o in order]), joined(cur, other_got)]
+        else:
+            update, ran = spread(after, update, shape, table, slots, waiting)
+            waiting = with_core(*crossed)
+            after = [ran]
+        front_order = [o for o, _ in level[k + 1]]
+        wanted = [joined(*[longer[o] for o in front_order]), joined(cur, other_got)]
         front, cur = combine(after, *wanted)
         after = [front]
         pieces = longer
-        front_order = order
-        cur_order = cur_order + [other_bits[k] | o for o in cur_order]
-        if waiting:
-            update = spread(after, update, shape, table, slots, waiting)
-            after = [update]
-        waiting = []
-        for array, first, order in made:
-            waiting.append((array, first, order))
-            waiting.append((swap(array, CORE_BIT), first, [CORE_BIT | o for o in order]))
-    update = spread(after, update, shape, table, slots, waiting)
-
-    def with_core(array, first, order):
-        return [
-            (array, first, order),
-            (swap(array, CORE_BIT), first, [CORE_BIT | o for o in order]),
-        ]
-
-    waiting = with_core(front, 0, front_order) + with_core(cur, cut, cur_order)
-    update = spread([], update, shape, table, slots, waiting)
-    waiting = with_core(x_got, 0, [X_BIT | o for o in front_order])
-    waiting += with_core(other_got, cut, [other_bits[top] | o for o in cur_order])
-    return spread([], update, shape, table, slots, waiting)
+        cur_order = cur_order + crossed_other[2]
+        waiting += with_core(front, 0, front_order)
+    waiting += with_core(cur, cut, cur_order)
+    update, _ = spread(after, update, shape, table, slots, waiting)
+    waiting = with_core(*crossed) + with_core(*crossed_other)
+    return spread([], update, shape, table, slots, waiting)[0]
 
 
 def per_device(grads, owner, momentum):
@@ -556,7 +581,7 @@
     cut = head_rows * 3 // 4
     bits = z_bits()[::-1]
     parts = sum_to_owners(grads[0], table, slot_count, bits, cut)
-    new_momentum, rounded, gram = momentum_step(table, momentum[0], parts, owner_count)
+    rounded, gram = nesterov_step(momentum[0], parts, owner_count)
 
     width = lax.axis_size("tensor")
     grams = [gram]
@@ -567,8 +592,13 @@
             )
         )
     blocks = orthogonalize(grams, rounded, factor, [cut, head_rows - cut])
+    new_momentum, early = momentum_step(
+        blocks[:1], table, momentum[0], parts, owner_count
+    )
     shape = (matrices, head_rows, cols)
-    update = spread_updates(blocks, table, slot_count, bits, cut, shape)
+    update = spread_updates(
+        blocks, table, slot_count, bits, cut, shape, early
+    )
     return (update, new_momentum[None])
 
 

time: 223 us -> 231 us (1.036)
  waiting for transfers between devices: 148 us -> 154 us
    ppermute x29, waiting for transfers between devices: 144 us -> 151 us  [swap(): return lax.ppermute(value, 'dp', [(i, i ^ bit) for i in range(count)])]
    pallas_call x4 -> x3, Pallas kernels: 9.55 us -> 9.62 us  [spread(): pl.pallas_call(functools.partial(spread_kernel, plans, slots), out_shape=...]
  transfers between devices with their start and end apart: 30 -> 30, of which waited for: 15 -> 19; matrix products, arithmetic and copies ran while one was open for 0% -> 0% of each run, Pallas kernels for 10% -> 10%
where the time goes in v5:
time: 231 us
  waiting for transfers between devices  154 us (67%)
  Pallas kernels  37.7 us (16%)
  starting transfers between devices  37.5 us (16%)
    ppermute x29, waiting for transfers between devices, swap(): return lax.ppermute(value, 'dp', [(i, i ^ bit) for i in range(count)])  151 us
    ppermute x29, starting transfers between devices, swap(): return lax.ppermute(value, 'dp', [(i, i ^ bit) for i in range(count)])  35.6 us
    pallas_call x3, Pallas kernels, spread(): pl.pallas_call(functools.partial(spread_kernel, plans, slots), out_shape=...  9.62 us
    pallas_call x4, Pallas kernels, add_taken(): pl.pallas_call(functools.partial(add_taken_kernel, first, order, slots, p...  8.94 us
    pallas_call x4, Pallas kernels, pack(): pl.pallas_call(functools.partial(pack_kernel, first, order, slots), out_s...  8.79 us
  transfers between devices with their start and end apart: 30, of which 19 were waited for; matrix products, arithmetic and copies ran while one was open for 0% of the time, Pallas kernels for 10%

profile of v5, /device:TPU:0, one launch (start us, length us, event | category | flops | bytes accessed | tf_op | source)
XLA Modules:
  0.0 231.0 jit_solution(14304558815488405950)
XLA Ops:
  3.1 2.5 %shard_map.51.rest_0_ = bf16[16,32,2048]{2,1,0:T(8,128)(2,1)S(1)} custom-call(s32[32]{0:T(128)S(1)} %copy-done.1, bf16[24,128,2048]{2,1,0:T(8,128)(2,1)} %bitcast.6), custom_call_target="tpu_custom_call" | custom-call | tf_op jit(solution)/shard_map/pallas_call | solution.py:116
  7.6 2.2 shard_map.53.rest_0_
  10.4 2.3 shard_map.54
  12.7 2.8 %collective-permute-start.4 = (bf16[8,32,2048]{2,1,0:T(8,128)(2,1)S(1)}, bf16[8,32,2048]{2,1,0:T(8,128)(2,1)S(1)}, u32[]{:S(2)}, u32[]{:S(2)}) collective-permute-start(bf16[8,32,2048]{2,1,0:T(8,128)(2,1)S(1)} %get-tuple-element.30.rest_0_), channel_id=1, source_target_pairs={{0,8},{2,10},{4,12},{6,14},{8,0},{10,2},{12,4},{14,6},{16,24},{18,... | collective-permute-start | bytes 3145736 | tf_op jit(solution)/shard_map/ppermute | solution.py:398
  17.3 2.8 %collective-permute-start.3 = (bf16[2,96,2048]{2,1,0:T(8,128)(2,1)S(1)}, bf16[2,96,2048]{2,1,0:T(8,128)(2,1)S(1)}, u32[]{:S(2)}, u32[]{:S(2)}) collective-permute-start(bf16[2,96,2048]{2,1,0:T(8,128)(2,1)S(1)} %shard_map.55.rest_0_), channel_id=1, source_target_pairs={{0,4},{2,6},{4,0},{6,2},{8,12},{10,14},{12,8},{14,10},{16,20},{18,... | collective-permute-start | bytes 2359304 | tf_op jit(solution)/shard_map/ppermute | solution.py:398
  20.1 2.4 %shard_map.56 = (bf16[4,96,2048]{2,1,0:T(8,128)(2,1)S(1)}, bf16[2,96,2048]{2,1,0:T(8,128)(2,1)S(1)}) custom-call(s32[32]{0:T(128)S(1)} %copy-done.1, bf16[24,128,2048]{2,1,0:T(8,128)(2,1)} %bitcast.11, bf16[6,96,2048]{2,1,0:T(8,128)(2,1)S(1)} %collective-permute-done.got_ref, bf16[2,96,2048]{2,1,0:T(8,128)(2,1)S(1)} %shard_map.55.rest_0_), custom_call_target="tpu_custom_call" | custom-call | tf_op jit(solution)/shard_map/pallas_call | solution.py:144
  22.6 15.6 %collective-permute-done.3.refs_1_ = bf16[2,96,2048]{2,1,0:T(8,128)(2,1)S(1)} collective-permute-done((bf16[2,96,2048]{2,1,0:T(8,128)(2,1)S(1)}, bf16[2,96,2048]{2,1,0:T(8,128)(2,1)S(1)}, u32[]{:S(2)}, u32[]{:S(2)}) %collective-permute-start.3) | collective-permute-done | bytes 786464 | tf_op jit(solution)/shard_map/ppermute | solution.py:398
  39.6 2.4 %shard_map.58.rest_0_ = bf16[8,96,2048]{2,1,0:T(8,128)(2,1)S(1)} custom-call(s32[32]{0:T(128)S(1)} %copy-done.1, bf16[24,128,2048]{2,1,0:T(8,128)(2,1)} %bitcast.12, bf16[2,96,2048]{2,1,0:T(8,128)(2,1)S(1)} %get-tuple-element.34.rest_0_), custom_call_target="tpu_custom_call" | custom-call | tf_op jit(solution)/shard_map/pallas_call | solution.py:116
  45.6 2.5 %collective-permute-start.8 = (bf16[4,32,2048]{2,1,0:T(8,128)(2,1)S(1)}, bf16[4,32,2048]{2,1,0:T(8,128)(2,1)S(1)}, u32[]{:S(2)}, u32[]{:S(2)}) collective-permute-start(bf16[4,32,2048]{2,1,0:T(8,128)(2,1)S(1)} %get-tuple-element.37), channel_id=1, source_target_pairs={{0,16},{2,18},{4,20},{6,22},{8,24},{10,26},{12,28},{14,30},{16,0},... | collective-permute-start | bytes 1572872 | tf_op jit(solution)/shard_map/ppermute | solution.py:398
  48.1 2.5 %shard_map.59 = (bf16[2,96,2048]{2,1,0:T(8,128)(2,1)S(1)}, bf16[6,96,2048]{2,1,0:T(8,128)(2,1)S(1)}) custom-call(s32[32]{0:T(128)S(1)} %copy-done.1, bf16[24,128,2048]{2,1,0:T(8,128)(2,1)} %bitcast.13, bf16[8,96,2048]{2,1,0:T(8,128)(2,1)S(1)} %collective-permute-done.5.got_ref, bf16[8,96,2048]{2,1,0:T(8,128)(2,1)S(1)} %shard_map.58.rest_0_), custom_call_target="tpu_custom_call" | custom-call | tf_op jit(solution)/shard_map/pallas_call | solution.py:144
  50.6 23.3 %collective-permute-done.8.refs_4_ = bf16[4,32,2048]{2,1,0:T(8,128)(2,1)S(1)} collective-permute-done((bf16[4,32,2048]{2,1,0:T(8,128)(2,1)S(1)}, bf16[4,32,2048]{2,1,0:T(8,128)(2,1)S(1)}, u32[]{:S(2)}, u32[]{:S(2)}) %collective-permute-start.8) | collective-permute-done | bytes 524320 | tf_op jit(solution)/shard_map/ppermute | solution.py:398
  74.9 4.1 %collective-permute-done.6.refs_1_ = bf16[4,96,2048]{2,1,0:T(8,128)(2,1)S(1)} collective-permute-done((bf16[4,96,2048]{2,1,0:T(8,128)(2,1)S(1)}, bf16[4,96,2048]{2,1,0:T(8,128)(2,1)S(1)}, u32[]{:S(2)}, u32[]{:S(2)}) %collective-permute-start.6) | collective-permute-done | bytes 1572896 | tf_op jit(solution)/shard_map/ppermute | solution.py:398
  79.3 2.8 %collective-permute-start.10 = (bf16[2,96,2048]{2,1,0:T(8,128)(2,1)S(1)}, bf16[2,96,2048]{2,1,0:T(8,128)(2,1)S(1)}, u32[]{:S(2)}, u32[]{:S(2)}) collective-permute-start(bf16[2,96,2048]{2,1,0:T(8,128)(2,1)S(1)} %get-tuple-element.40), channel_id=1, source_target_pairs={{0,16},{2,18},{4,20},{6,22},{8,24},{10,26},{12,28},{14,30},{16,0},... | collective-permute-start | bytes 2359304 | tf_op jit(solution)/shard_map/ppermute | solution.py:398
  85.9 22.1 %collective-permute-done.12.rest_5_ = bf16[2,32,2048]{2,1,0:T(8,128)(2,1)S(1)} collective-permute-done((bf16[2,32,2048]{2,1,0:T(8,128)(2,1)S(1)}, bf16[2,32,2048]{2,1,0:T(8,128)(2,1)S(1)}, u32[]{:S(2)}, u32[]{:S(2)}) %collective-permute-start.12) | collective-permute-done | bytes 262176 | tf_op jit(solution)/shard_map/ppermute | solution.py:398
  108.1 8.4 %collective-permute-done.10.rest_2_ = bf16[2,96,2048]{2,1,0:T(8,128)(2,1)S(1)} collective-permute-done((bf16[2,96,2048]{2,1,0:T(8,128)(2,1)S(1)}, bf16[2,96,2048]{2,1,0:T(8,128)(2,1)S(1)}, u32[]{:S(2)}, u32[]{:S(2)}) %collective-permute-start.10) | collective-permute-done | bytes 786464 | tf_op jit(solution)/shard_map/ppermute | solution.py:398
  117.6 1.9 collective-permute-start.13
  119.5 3.1 %collective-permute-done.13.refs_1_ = f32[2,128,128]{2,1,0:T(8,128)S(1)} collective-permute-done((f32[2,128,128]{2,1,0:T(8,128)S(1)}, f32[2,128,128]{2,1,0:T(8,128)S(1)}, u32[]{:S(2)}, u32[]{:S(2)}) %collective-permute-start.13) | collective-permute-done | bytes 131104 | tf_op jit(solution)/shard_map/ppermute | solution.py:590
  122.6 4.4 %shard_map.62 = (bf16[2,96,2048]{2,1,0:T(8,128)(2,1)S(1)}, bf16[2,32,2048]{2,1,0:T(8,128)(2,1)S(1)}) custom-call(f32[2,128,128]{2,1,0:T(8,128)S(1)} %get-tuple-element.44.refs_0_, f32[2,128,128]{2,1,0:T(8,128)S(1)} %collective-permute-done.13.refs_1_, bf16[2,128,2048]{2,1,0:T(8,128)(2,1)S(1)} %get-tuple-element.45.refs_2_), custom_call_target="tpu_custom_call" | custom-call | tf_op jit(solution)/shard_map/pallas_call | solution.py:384
  130.2 2.8 %collective-permute-start.16 = (bf16[2,96,2048]{2,1,0:T(8,128)(2,1)S(1)}, bf16[2,96,2048]{2,1,0:T(8,128)(2,1)S(1)}, u32[]{:S(2)}, u32[]{:S(2)}) collective-permute-start(bf16[2,96,2048]{2,1,0:T(8,128)(2,1)S(1)} %get-tuple-element.46.rest_6_.refs_0_), channel_id=1, source_target_pairs={{0,8},{2,10},{4,12},{6,14},{8,0},{10,2},{12,4},{14,6},{16,24},{18,... | collective-permute-start | bytes 2359304 | tf_op jit(solution)/shard_map/ppermute | solution.py:398
  133.5 2.2 shard_map.63
  135.8 11.6 %collective-permute-done.18.refs_1_ = bf16[2,96,2048]{2,1,0:T(8,128)(2,1)S(1)} collective-permute-done((bf16[2,96,2048]{2,1,0:T(8,128)(2,1)S(1)}, bf16[2,96,2048]{2,1,0:T(8,128)(2,1)S(1)}, u32[]{:S(2)}, u32[]{:S(2)}) %collective-permute-start.18) | collective-permute-done | bytes 786464 | tf_op jit(solution)/shard_map/ppermute | solution.py:398
  147.4 2.7 %collective-permute-done.17.refs_3_ = bf16[2,32,2048]{2,1,0:T(8,128)(2,1)S(1)} collective-permute-done((bf16[2,32,2048]{2,1,0:T(8,128)(2,1)S(1)}, bf16[2,32,2048]{2,1,0:T(8,128)(2,1)S(1)}, u32[]{:S(2)}, u32[]{:S(2)}) %collective-permute-start.17) | collective-permute-done | bytes 262176 | tf_op jit(solution)/shard_map/ppermute | solution.py:398
  150.1 13.4 %collective-permute-done.14.refs_0_ = bf16[2,96,2048]{2,1,0:T(8,128)(2,1)S(1)} collective-permute-done((bf16[2,96,2048]{2,1,0:T(8,128)(2,1)S(1)}, bf16[2,96,2048]{2,1,0:T(8,128)(2,1)S(1)}, u32[]{:S(2)}, u32[]{:S(2)}) %collective-permute-start.14) | collective-permute-done | bytes 786464 | tf_op jit(solution)/shard_map/ppermute | solution.py:398
  165.5 4.0 %collective-permute-start.19 = (bf16[4,32,2048]{2,1,0:T(8,128)(2,1)S(1)}, bf16[4,32,2048]{2,1,0:T(8,128)(2,1)S(1)}, u32[]{:S(2)}, u32[]{:S(2)}) collective-permute-start(bf16[4,32,2048]{2,1,0:T(8,128)(2,1)S(1)} %get-tuple-element.49.refs_1_), channel_id=1, source_target_pairs={{0,16},{2,18},{4,20},{6,22},{8,24},{10,26},{12,28},{14,30},{16,0},... | collective-permute-start | bytes 1572872 | tf_op jit(solution)/shard_map/ppermute | solution.py:398
  169.5 3.1 %shard_map.66 = (bf16[24,128,2048]{2,1,0:T(8,128)(2,1)}, f32[8,128]{1,0:T(8,128)S(1)}) custom-call(s32[32]{0:T(128)S(1)} %copy-done.1, bf16[4,96,2048]{2,1,0:T(8,128)(2,1)S(1)} %shard_map.64.refs_4_.refs_0_, bf16[4,96,2048]{2,1,0:T(8,128)(2,1)S(1)} %collective-permute-done.20.refs_1_, bf16[4,96,2048]{2,1,0:T(8,128)(2,1)S(1)} %get-tuple-element.50.refs_2_.refs_4_, ...), custom_call_target="tpu_custom_call" | custom-call | tf_op jit(solution)/shard_map/pallas_call | solution.py:236
  172.6 20.9 %collective-permute-done.19.refs_2_ = bf16[4,32,2048]{2,1,0:T(8,128)(2,1)S(1)} collective-permute-done((bf16[4,32,2048]{2,1,0:T(8,128)(2,1)S(1)}, bf16[4,32,2048]{2,1,0:T(8,128)(2,1)S(1)}, u32[]{:S(2)}, u32[]{:S(2)}) %collective-permute-start.19) | collective-permute-done | bytes 524320 | tf_op jit(solution)/shard_map/ppermute | solution.py:398
  195.5 2.9 %collective-permute-start.24 = (bf16[8,32,2048]{2,1,0:T(8,128)(2,1)S(1)}, bf16[8,32,2048]{2,1,0:T(8,128)(2,1)S(1)}, u32[]{:S(2)}, u32[]{:S(2)}) collective-permute-start(bf16[8,32,2048]{2,1,0:T(8,128)(2,1)S(1)} %get-tuple-element.53.refs_4_), channel_id=1, source_target_pairs={{0,8},{2,10},{4,12},{6,14},{8,0},{10,2},{12,4},{14,6},{16,24},{18,... | collective-permute-start | bytes 3145736 | tf_op jit(solution)/shard_map/ppermute | solution.py:398
  198.4 2.3 %collective-permute-done.26.refs_0_ = bf16[4,96,2048]{2,1,0:T(8,128)(2,1)S(1)} collective-permute-done((bf16[4,96,2048]{2,1,0:T(8,128)(2,1)S(1)}, bf16[4,96,2048]{2,1,0:T(8,128)(2,1)S(1)}, u32[]{:S(2)}, u32[]{:S(2)}) %collective-permute-start.26) | collective-permute-done | bytes 1572896 | tf_op jit(solution)/shard_map/ppermute | solution.py:398
  201.5 19.1 %collective-permute-done.24.refs_2_ = bf16[8,32,2048]{2,1,0:T(8,128)(2,1)S(1)} collective-permute-done((bf16[8,32,2048]{2,1,0:T(8,128)(2,1)S(1)}, bf16[8,32,2048]{2,1,0:T(8,128)(2,1)S(1)}, u32[]{:S(2)}, u32[]{:S(2)}) %collective-permute-start.24) | collective-permute-done | bytes 1048608 | tf_op jit(solution)/shard_map/ppermute | solution.py:398
  221.2 3.3 %collective-permute-done.28.refs_3_ = bf16[2,96,2048]{2,1,0:T(8,128)(2,1)S(1)} collective-permute-done((bf16[2,96,2048]{2,1,0:T(8,128)(2,1)S(1)}, bf16[2,96,2048]{2,1,0:T(8,128)(2,1)S(1)}, u32[]{:S(2)}, u32[]{:S(2)}) %collective-permute-start.28) | collective-permute-done | bytes 786464 | tf_op jit(solution)/shard_map/ppermute | solution.py:398
  224.4 3.6 %shard_map.68 = (bf16[24,128,2048]{2,1,0:T(8,128)(2,1)}, f32[8,128]{1,0:T(8,128)}) custom-call(s32[32]{0:T(128)S(1)} %copy-done.1, bf16[4,96,2048]{2,1,0:T(8,128)(2,1)S(1)} %collective-permute-done.26.refs_0_, bf16[4,96,2048]{2,1,0:T(8,128)(2,1)S(1)} %collective-permute-done.27.refs_1_, ...), custom_call_target="tpu_custom_call", output_to_operand_aliasing={{0}: (7, {})} | custom-call | tf_op jit(solution)/shard_map/pallas_call | solution.py:236
  228.1 2.9 %shard_map.69 = (bf16[24,128,2048]{2,1,0:T(8,128)(2,1)}, f32[8,128]{1,0:T(8,128)}) custom-call(s32[32]{0:T(128)S(1)} %copy-done.1, bf16[2,96,2048]{2,1,0:T(8,128)(2,1)S(1)} %collective-permute-done.22.refs_0_, bf16[2,96,2048]{2,1,0:T(8,128)(2,1)S(1)} %collective-permute-done.23.refs_1_, ...), custom_call_target="tpu_custom_call", output_to_operand_aliasing={{0}: (5, {})} | custom-call | tf_op jit(solution)/shard_map/pallas_call | solution.py:236
  (52 shorter events, 27.1 us)
Async XLA Ops:
  2.4 0.7 copy-start.1
  5.6 4.8 %collective-permute-start.2 = (bf16[16,32,2048]{2,1,0:T(8,128)(2,1)S(1)}, bf16[16,32,2048]{2,1,0:T(8,128)(2,1)S(1)}, u32[]{:S(2)}, u32[]{:S(2)}) collective-permute-start(bf16[16,32,2048]{2,1,0:T(8,128)(2,1)S(1)} %shard_map.51.rest_0_), channel_id=1, source_target_pairs={{0,2},{2,0},{4,6},{6,4},{8,10},{10,8},{12,14},{14,12},{16,18},{18,... | collective-permute-start | bytes 6291464 | tf_op jit(solution)/shard_map/ppermute | solution.py:398
  9.8 10.3 %collective-permute-start = (bf16[6,96,2048]{2,1,0:T(8,128)(2,1)S(1)}, bf16[6,96,2048]{2,1,0:T(8,128)(2,1)S(1)}, u32[]{:S(2)}, u32[]{:S(2)}) collective-permute-start(bf16[6,96,2048]{2,1,0:T(8,128)(2,1)S(1)} %shard_map.53.rest_0_), channel_id=1, source_target_pairs={{0,2},{2,0},{4,6},{6,4},{8,10},{10,8},{12,14},{14,12},{16,18},{18,... | collective-permute-start | bytes 7077896 | tf_op jit(solution)/shard_map/ppermute | solution.py:398
  10.3 5.3 %collective-permute-start.1 = (bf16[2,96,2048]{2,1,0:T(8,128)(2,1)S(1)}, bf16[2,96,2048]{2,1,0:T(8,128)(2,1)S(1)}, u32[]{:S(2)}, u32[]{:S(2)}) collective-permute-start(bf16[2,96,2048]{2,1,0:T(8,128)(2,1)S(1)} %shard_map.52.rest_0_), channel_id=1, source_target_pairs={{0,2},{2,0},{4,6},{6,4},{8,10},{10,8},{12,14},{14,12},{16,18},{18,... | collective-permute-start | bytes 2359304 | tf_op jit(solution)/shard_map/ppermute | solution.py:398
  12.7 26.7 %collective-permute-start.4 = (bf16[8,32,2048]{2,1,0:T(8,128)(2,1)S(1)}, bf16[8,32,2048]{2,1,0:T(8,128)(2,1)S(1)}, u32[]{:S(2)}, u32[]{:S(2)}) collective-permute-start(bf16[8,32,2048]{2,1,0:T(8,128)(2,1)S(1)} %get-tuple-element.30.rest_0_), channel_id=1, source_target_pairs={{0,8},{2,10},{4,12},{6,14},{8,0},{10,2},{12,4},{14,6},{16,24},{18,... | collective-permute-start | bytes 3145736 | tf_op jit(solution)/shard_map/ppermute | solution.py:398
  17.3 20.9 %collective-permute-start.3 = (bf16[2,96,2048]{2,1,0:T(8,128)(2,1)S(1)}, bf16[2,96,2048]{2,1,0:T(8,128)(2,1)S(1)}, u32[]{:S(2)}, u32[]{:S(2)}) collective-permute-start(bf16[2,96,2048]{2,1,0:T(8,128)(2,1)S(1)} %shard_map.55.rest_0_), channel_id=1, source_target_pairs={{0,4},{2,6},{4,0},{6,2},{8,12},{10,14},{12,8},{14,10},{16,20},{18,... | collective-permute-start | bytes 2359304 | tf_op jit(solution)/shard_map/ppermute | solution.py:398
  42.0 6.1 %collective-permute-start.5 = (bf16[8,96,2048]{2,1,0:T(8,128)(2,1)S(1)}, bf16[8,96,2048]{2,1,0:T(8,128)(2,1)S(1)}, u32[]{:S(2)}, u32[]{:S(2)}) collective-permute-start(bf16[8,96,2048]{2,1,0:T(8,128)(2,1)S(1)} %shard_map.58.rest_0_), channel_id=1, source_target_pairs={{0,2},{2,0},{4,6},{6,4},{8,10},{10,8},{12,14},{14,12},{16,18},{18,... | collective-permute-start | bytes 9437192 | tf_op jit(solution)/shard_map/ppermute | solution.py:398
  42.1 36.9 %collective-permute-start.6 = (bf16[4,96,2048]{2,1,0:T(8,128)(2,1)S(1)}, bf16[4,96,2048]{2,1,0:T(8,128)(2,1)S(1)}, u32[]{:S(2)}, u32[]{:S(2)}) collective-permute-start(bf16[4,96,2048]{2,1,0:T(8,128)(2,1)S(1)} %get-tuple-element.33.refs_4_), channel_id=1, source_target_pairs={{0,4},{2,6},{4,0},{6,2},{8,12},{10,14},{12,8},{14,10},{16,20},{18,... | collective-permute-start | bytes 4718600 | tf_op jit(solution)/shard_map/ppermute | solution.py:398
  44.0 30.8 %collective-permute-start.7 = (bf16[2,96,2048]{2,1,0:T(8,128)(2,1)S(1)}, bf16[2,96,2048]{2,1,0:T(8,128)(2,1)S(1)}, u32[]{:S(2)}, u32[]{:S(2)}) collective-permute-start(bf16[2,96,2048]{2,1,0:T(8,128)(2,1)S(1)} %get-tuple-element.34.rest_0_), channel_id=1, source_target_pairs={{0,8},{2,10},{4,12},{6,14},{8,0},{10,2},{12,4},{14,6},{16,24},{18,... | collective-permute-start | bytes 2359304 | tf_op jit(solution)/shard_map/ppermute | solution.py:398
  45.6 28.4 %collective-permute-start.8 = (bf16[4,32,2048]{2,1,0:T(8,128)(2,1)S(1)}, bf16[4,32,2048]{2,1,0:T(8,128)(2,1)S(1)}, u32[]{:S(2)}, u32[]{:S(2)}) collective-permute-start(bf16[4,32,2048]{2,1,0:T(8,128)(2,1)S(1)} %get-tuple-element.37), channel_id=1, source_target_pairs={{0,16},{2,18},{4,20},{6,22},{8,24},{10,26},{12,28},{14,30},{16,0},... | collective-permute-start | bytes 1572872 | tf_op jit(solution)/shard_map/ppermute | solution.py:398
  79.0 37.5 %copy-start = (f32[1,2,128,2048]{3,2,1,0:T(8,128)S(1)}, f32[1,2,128,2048]{3,2,1,0:T(8,128)}, u32[]{:S(2)}) copy-start(f32[1,2,128,2048]{3,2,1,0:T(8,128)} %param.5) | copy-start | bytes 6291460
  79.3 37.1 %collective-permute-start.10 = (bf16[2,96,2048]{2,1,0:T(8,128)(2,1)S(1)}, bf16[2,96,2048]{2,1,0:T(8,128)(2,1)S(1)}, u32[]{:S(2)}, u32[]{:S(2)}) collective-permute-start(bf16[2,96,2048]{2,1,0:T(8,128)(2,1)S(1)} %get-tuple-element.40), channel_id=1, source_target_pairs={{0,16},{2,18},{4,20},{6,22},{8,24},{10,26},{12,28},{14,30},{16,0},... | collective-permute-start | bytes 2359304 | tf_op jit(solution)/shard_map/ppermute | solution.py:398
  82.1 34.4 %collective-permute-start.11 = (bf16[2,96,2048]{2,1,0:T(8,128)(2,1)S(1)}, bf16[2,96,2048]{2,1,0:T(8,128)(2,1)S(1)}, u32[]{:S(2)}, u32[]{:S(2)}) collective-permute-start(bf16[2,96,2048]{2,1,0:T(8,128)(2,1)S(1)} %get-tuple-element.41), channel_id=1, source_target_pairs={{0,8},{2,10},{4,12},{6,14},{8,0},{10,2},{12,4},{14,6},{16,24},{18,... | collective-permute-start | bytes 2359304 | tf_op jit(solution)/shard_map/ppermute | solution.py:398
  83.9 32.6 %collective-permute-start.9 = (bf16[2,96,2048]{2,1,0:T(8,128)(2,1)S(1)}, bf16[2,96,2048]{2,1,0:T(8,128)(2,1)S(1)}, u32[]{:S(2)}, u32[]{:S(2)}) collective-permute-start(bf16[2,96,2048]{2,1,0:T(8,128)(2,1)S(1)} %get-tuple-element.39), channel_id=1, source_target_pairs={{0,4},{2,6},{4,0},{6,2},{8,12},{10,14},{12,8},{14,10},{16,20},{18,... | collective-permute-start | bytes 2359304 | tf_op jit(solution)/shard_map/ppermute | solution.py:398
  85.2 22.9 %collective-permute-start.12 = (bf16[2,32,2048]{2,1,0:T(8,128)(2,1)S(1)}, bf16[2,32,2048]{2,1,0:T(8,128)(2,1)S(1)}, u32[]{:S(2)}, u32[]{:S(2)}) collective-permute-start(bf16[2,32,2048]{2,1,0:T(8,128)(2,1)S(1)} %get-tuple-element.43), channel_id=1, source_target_pairs={{0,4},{2,6},{4,0},{6,2},{8,12},{10,14},{12,8},{14,10},{16,20},{18,... | collective-permute-start | bytes 786440 | tf_op jit(solution)/shard_map/ppermute | solution.py:398
  117.6 5.0 %collective-permute-start.13 = (f32[2,128,128]{2,1,0:T(8,128)S(1)}, f32[2,128,128]{2,1,0:T(8,128)S(1)}, u32[]{:S(2)}, u32[]{:S(2)}) collective-permute-start(f32[2,128,128]{2,1,0:T(8,128)S(1)} %get-tuple-element.44.refs_0_), channel_id=1, source_target_pairs={{0,1},{1,0},{2,3},{3,2},{4,5},{5,4},{6,7},{7,6},{8,9},{9,8},{10,11... | collective-permute-start | bytes 393224 | tf_op jit(solution)/shard_map/ppermute | solution.py:590
  127.1 20.3 %collective-permute-start.18 = (bf16[2,96,2048]{2,1,0:T(8,128)(2,1)S(1)}, bf16[2,96,2048]{2,1,0:T(8,128)(2,1)S(1)}, u32[]{:S(2)}, u32[]{:S(2)}) collective-permute-start(bf16[2,96,2048]{2,1,0:T(8,128)(2,1)S(1)} %get-tuple-element.46.rest_6_.refs_0_), channel_id=1, source_target_pairs={{0,4},{2,6},{4,0},{6,2},{8,12},{10,14},{12,8},{14,10},{16,20},{18,... | collective-permute-start | bytes 2359304 | tf_op jit(solution)/shard_map/ppermute | solution.py:398
  128.9 34.7 %collective-permute-start.14 = (bf16[2,96,2048]{2,1,0:T(8,128)(2,1)S(1)}, bf16[2,96,2048]{2,1,0:T(8,128)(2,1)S(1)}, u32[]{:S(2)}, u32[]{:S(2)}) collective-permute-start(bf16[2,96,2048]{2,1,0:T(8,128)(2,1)S(1)} %get-tuple-element.46.rest_6_.refs_0_), channel_id=1, source_target_pairs={{0,16},{2,18},{4,20},{6,22},{8,24},{10,26},{12,28},{14,30},{16,0},... | collective-permute-start | bytes 2359304 | tf_op jit(solution)/shard_map/ppermute | solution.py:398
  130.2 33.4 %collective-permute-start.16 = (bf16[2,96,2048]{2,1,0:T(8,128)(2,1)S(1)}, bf16[2,96,2048]{2,1,0:T(8,128)(2,1)S(1)}, u32[]{:S(2)}, u32[]{:S(2)}) collective-permute-start(bf16[2,96,2048]{2,1,0:T(8,128)(2,1)S(1)} %get-tuple-element.46.rest_6_.refs_0_), channel_id=1, source_target_pairs={{0,8},{2,10},{4,12},{6,14},{8,0},{10,2},{12,4},{14,6},{16,24},{18,... | collective-permute-start | bytes 2359304 | tf_op jit(solution)/shard_map/ppermute | solution.py:398
  133.0 17.1 %collective-permute-start.17 = (bf16[2,32,2048]{2,1,0:T(8,128)(2,1)S(1)}, bf16[2,32,2048]{2,1,0:T(8,128)(2,1)S(1)}, u32[]{:S(2)}, u32[]{:S(2)}) collective-permute-start(bf16[2,32,2048]{2,1,0:T(8,128)(2,1)S(1)} %get-tuple-element.47.refs_2_), channel_id=1, source_target_pairs={{0,4},{2,6},{4,0},{6,2},{8,12},{10,14},{12,8},{14,10},{16,20},{18,... | collective-permute-start | bytes 786440 | tf_op jit(solution)/shard_map/ppermute | solution.py:398
  163.8 5.7 %collective-permute-start.21 = (bf16[4,96,2048]{2,1,0:T(8,128)(2,1)S(1)}, bf16[4,96,2048]{2,1,0:T(8,128)(2,1)S(1)}, u32[]{:S(2)}, u32[]{:S(2)}) collective-permute-start(bf16[4,96,2048]{2,1,0:T(8,128)(2,1)S(1)} %get-tuple-element.50.refs_2_.refs_4_), channel_id=1, source_target_pairs={{0,2},{2,0},{4,6},{6,4},{8,10},{10,8},{12,14},{14,12},{16,18},{18,... | collective-permute-start | bytes 4718600 | tf_op jit(solution)/shard_map/ppermute | solution.py:398
  163.8 5.6 %collective-permute-start.20 = (bf16[4,96,2048]{2,1,0:T(8,128)(2,1)S(1)}, bf16[4,96,2048]{2,1,0:T(8,128)(2,1)S(1)}, u32[]{:S(2)}, u32[]{:S(2)}) collective-permute-start(bf16[4,96,2048]{2,1,0:T(8,128)(2,1)S(1)} %shard_map.64.refs_4_.refs_0_), channel_id=1, source_target_pairs={{0,2},{2,0},{4,6},{6,4},{8,10},{10,8},{12,14},{14,12},{16,18},{18,... | collective-permute-start | bytes 4718600 | tf_op jit(solution)/shard_map/ppermute | solution.py:398
  164.3 36.4 %collective-permute-start.26 = (bf16[4,96,2048]{2,1,0:T(8,128)(2,1)S(1)}, bf16[4,96,2048]{2,1,0:T(8,128)(2,1)S(1)}, u32[]{:S(2)}, u32[]{:S(2)}) collective-permute-start(bf16[4,96,2048]{2,1,0:T(8,128)(2,1)S(1)} %get-tuple-element.50.refs_2_.refs_4_), channel_id=1, source_target_pairs={{0,4},{2,6},{4,0},{6,2},{8,12},{10,14},{12,8},{14,10},{16,20},{18,... | collective-permute-start | bytes 4718600 | tf_op jit(solution)/shard_map/ppermute | solution.py:398
  164.9 30.5 %collective-permute-start.15 = (bf16[2,96,2048]{2,1,0:T(8,128)(2,1)S(1)}, bf16[2,96,2048]{2,1,0:T(8,128)(2,1)S(1)}, u32[]{:S(2)}, u32[]{:S(2)}) collective-permute-start(bf16[2,96,2048]{2,1,0:T(8,128)(2,1)S(1)} %collective-permute-done.14.refs_0_), channel_id=1, source_target_pairs={{0,8},{2,10},{4,12},{6,14},{8,0},{10,2},{12,4},{14,6},{16,24},{18,... | collective-permute-start | bytes 2359304 | tf_op jit(solution)/shard_map/ppermute | solution.py:398
  165.5 28.0 %collective-permute-start.19 = (bf16[4,32,2048]{2,1,0:T(8,128)(2,1)S(1)}, bf16[4,32,2048]{2,1,0:T(8,128)(2,1)S(1)}, u32[]{:S(2)}, u32[]{:S(2)}) collective-permute-start(bf16[4,32,2048]{2,1,0:T(8,128)(2,1)S(1)} %get-tuple-element.49.refs_1_), channel_id=1, source_target_pairs={{0,16},{2,18},{4,20},{6,22},{8,24},{10,26},{12,28},{14,30},{16,0},... | collective-permute-start | bytes 1572872 | tf_op jit(solution)/shard_map/ppermute | solution.py:398
  195.5 25.1 %collective-permute-start.24 = (bf16[8,32,2048]{2,1,0:T(8,128)(2,1)S(1)}, bf16[8,32,2048]{2,1,0:T(8,128)(2,1)S(1)}, u32[]{:S(2)}, u32[]{:S(2)}) collective-permute-start(bf16[8,32,2048]{2,1,0:T(8,128)(2,1)S(1)} %get-tuple-element.53.refs_4_), channel_id=1, source_target_pairs={{0,8},{2,10},{4,12},{6,14},{8,0},{10,2},{12,4},{14,6},{16,24},{18,... | collective-permute-start | bytes 3145736 | tf_op jit(solution)/shard_map/ppermute | solution.py:398
  200.7 23.7 %collective-permute-start.27 = (bf16[4,96,2048]{2,1,0:T(8,128)(2,1)S(1)}, bf16[4,96,2048]{2,1,0:T(8,128)(2,1)S(1)}, u32[]{:S(2)}, u32[]{:S(2)}) collective-permute-start(bf16[4,96,2048]{2,1,0:T(8,128)(2,1)S(1)} %collective-permute-done.26.refs_0_), channel_id=1, source_target_pairs={{0,2},{2,0},{4,6},{6,4},{8,10},{10,8},{12,14},{14,12},{16,18},{18,... | collective-permute-start | bytes 4718600 | tf_op jit(solution)/shard_map/ppermute | solution.py:398
  200.7 20.4 %collective-permute-start.22 = (bf16[2,96,2048]{2,1,0:T(8,128)(2,1)S(1)}, bf16[2,96,2048]{2,1,0:T(8,128)(2,1)S(1)}, u32[]{:S(2)}, u32[]{:S(2)}) collective-permute-start(bf16[2,96,2048]{2,1,0:T(8,128)(2,1)S(1)} %get-tuple-element.52.refs_2_.refs_7_), channel_id=1, source_target_pairs={{0,4},{2,6},{4,0},{6,2},{8,12},{10,14},{12,8},{14,10},{16,20},{18,... | collective-permute-start | bytes 2359304 | tf_op jit(solution)/shard_map/ppermute | solution.py:398
  201.3 23.1 %collective-permute-start.29 = (bf16[8,32,2048]{2,1,0:T(8,128)(2,1)S(1)}, bf16[8,32,2048]{2,1,0:T(8,128)(2,1)S(1)}, u32[]{:S(2)}, u32[]{:S(2)}) collective-permute-start(bf16[8,32,2048]{2,1,0:T(8,128)(2,1)S(1)} %get-tuple-element.53.refs_4_), channel_id=1, source_target_pairs={{0,2},{2,0},{4,6},{6,4},{8,10},{10,8},{12,14},{14,12},{16,18},{18,... | collective-permute-start | bytes 3145736 | tf_op jit(solution)/shard_map/ppermute | solution.py:398
  220.6 7.4 %collective-permute-start.25 = (bf16[8,32,2048]{2,1,0:T(8,128)(2,1)S(1)}, bf16[8,32,2048]{2,1,0:T(8,128)(2,1)S(1)}, u32[]{:S(2)}, u32[]{:S(2)}) collective-permute-start(bf16[8,32,2048]{2,1,0:T(8,128)(2,1)S(1)} %collective-permute-done.24.refs_2_), channel_id=1, source_target_pairs={{0,2},{2,0},{4,6},{6,4},{8,10},{10,8},{12,14},{14,12},{16,18},{18,... | collective-permute-start | bytes 3145736 | tf_op jit(solution)/shard_map/ppermute | solution.py:398
  220.7 3.8 %collective-permute-start.28 = (bf16[2,96,2048]{2,1,0:T(8,128)(2,1)S(1)}, bf16[2,96,2048]{2,1,0:T(8,128)(2,1)S(1)}, u32[]{:S(2)}, u32[]{:S(2)}) collective-permute-start(bf16[2,96,2048]{2,1,0:T(8,128)(2,1)S(1)} %get-tuple-element.52.refs_2_.refs_7_), channel_id=1, source_target_pairs={{0,2},{2,0},{4,6},{6,4},{8,10},{10,8},{12,14},{14,12},{16,18},{18,... | collective-permute-start | bytes 2359304 | tf_op jit(solution)/shard_map/ppermute | solution.py:398
  221.2 6.9 %collective-permute-start.23 = (bf16[2,96,2048]{2,1,0:T(8,128)(2,1)S(1)}, bf16[2,96,2048]{2,1,0:T(8,128)(2,1)S(1)}, u32[]{:S(2)}, u32[]{:S(2)}) collective-permute-start(bf16[2,96,2048]{2,1,0:T(8,128)(2,1)S(1)} %collective-permute-done.22.refs_0_), channel_id=1, source_target_pairs={{0,2},{2,0},{4,6},{6,4},{8,10},{10,8},{12,14},{14,12},{16,18},{18,... | collective-permute-start | bytes 2359304 | tf_op jit(solution)/shard_map/ppermute | solution.py:398

commit v6 on v5

--- a/solution.py
+++ b/solution.py
@@ -102,23 +102,30 @@
     )
 
 
-def pack_kernel(first, order, slots, table_ref, src_ref, *rest):
-    out_ref, sem = rest[-2:]
-    copy = fetch(table_ref, src_ref, first, order, slots, out_ref, sem)
-
-    @pl.loop(0, out_ref.shape[0])
-    def _(i):
-        copy(i).wait()
-
-
-def pack(after, table, src, order, slots, first, rows):
-    count = len(order) * slots
-    return pl.pallas_call(
-        functools.partial(pack_kernel, first, order, slots),
-        out_shape=jax.ShapeDtypeStruct((count, rows, src.shape[2]), src.dtype),
+def pack_kernel(first, orders, slots, table_ref, src_ref, *rest):
+    out_refs = rest[-2 * len(orders) : -len(orders)]
+    sems = rest[-len(orders) :]
+    copies = [
+        fetch(table_ref, src_ref, first, order, slots, out_ref, sem)
+        for order, out_ref, sem in zip(orders, out_refs, sems)
+    ]
+    for copy, out_ref in zip(copies, out_refs):
+
+        @pl.loop(0, out_ref.shape[0])
+        def _(i, copy=copy):
+            copy(i).wait()
+
+
+def pack(after, table, src, orders, slots, first, rows):
+    counts = [len(order) * slots for order in orders]
+    return pl.pallas_call(
+        functools.partial(pack_kernel, first, tuple(orders), slots),
+        out_shape=[
+            jax.ShapeDtypeStruct((n, rows, src.shape[2]), src.dtype) for n in counts
+        ],
         in_specs=in_smem() + in_hbm() + anywhere(len(after)),
-        out_specs=in_vmem()[0],
-        scratch_shapes=[pltpu.SemaphoreType.DMA((count,))],
+        out_specs=in_vmem(len(orders)),
+        scratch_shapes=[pltpu.SemaphoreType.DMA((n,)) for n in counts],
         compiler_params=limits(MORE_VMEM_BYTES),
         cost_estimate=small_cost(),
     )(table, src, *after)
@@ -440,21 +447,19 @@
         order = [o | X_BIT for o in level[k]]
         return tuple(order + (level[k + 1] if k < top else []))
 
-    batches = {k: batch(k) for k in range(top, -1, -1)}
-    batches[-1] = (0,)
-    merged = {k: batches[k] for k in range(top, 0, -1)}
-    merged[0] = batches[0] + batches[-1]
-
-    def send(order, first, rows, after):
-        theirs = tuple(CORE_BIT | o for o in order)
-        packed = pack(after, table, gradient, theirs, slots, first, rows)
-        return packed, swap(packed, CORE_BIT)
-
-    got, packed = {}, {}
-
-    def take_off(k, after):
-        packed[k], got[k] = send(merged[k], 0, cut, after)
-        return [packed[k]]
+    merged = {k: batch(k) for k in range(top, 0, -1)}
+    merged[0] = batch(0) + (0,)
+
+    def theirs(order):
+        return tuple(CORE_BIT | o for o in order)
+
+    packed = pack([], table, gradient, [theirs(other_order)], slots, cut, rest)
+    other_got = swap(packed[0], CORE_BIT)
+    falling = range(top, -1, -1)
+    orders = [theirs(merged[k]) for k in falling]
+    packed = pack(packed, table, gradient, orders, slots, 0, cut)
+    got = {k: swap(block, CORE_BIT) for k, block in zip(falling, packed)}
+    after = [packed[0]]
 
     home = {}
     over_x = {}
@@ -472,8 +477,6 @@
         return [made[0]]
 
     half = len(other_order) * slots // 2
-    packed[None], other_got = send(other_order, cut, rest, [])
-    after = take_off(top - 1, take_off(top, [packed[None]]))
     away, kept = add_taken(
         after, table, gradient, other_order, slots, cut, other_got, (half, half)
     )
@@ -508,9 +511,6 @@
         if held_back:
             over_x[0] = made.pop()
         else:
-            if k == top:
-                for n in range(top - 2, -1, -1):
-                    after = take_off(n, after)
             after = take(k - 2, after)
         pending = {o: swap(made[n], last[o]) for n, o in enumerate(level[k])}
         kept = made[-1]
@@ -537,32 +537,38 @@
         ]
 
     for k in range(top + 1):
-        x_got = swap(front, X_BIT)
         longer = {}
         for j, bit in enumerate(bits):
             for o, at in level[k]:
                 if at < j:
                     longer[o | bit] = swap(pieces[o], bit)
+        x_got = swap(front, X_BIT)
         other_got = swap(cur, other_bits[k])
         crossed = (x_got, 0, [X_BIT | o for o in front_order])
         crossed_other = (other_got, cut, [other_bits[k] | o for o in cur_order])
         if k == top:
             break
+        if k > 0:
+            update, ran = spread(after, update, shape, table, slots, waiting)
+            after = [ran]
+        waiting = []
+        order = [o for o, _ in level[k + 1]]
+        new = joined(*[longer[o] for o in order])
+        wanted = [new, joined(cur, other_got)]
         if k == 0:
-            (both,) = combine(after, joined(front, x_got))
-            waiting = with_core(both, 0, front_order + crossed[2])
-            after = [both]
+            wanted.append(joined(front, x_got))
+            more = front_order + crossed[2]
         else:
-            update, ran = spread(after, update, shape, table, slots, waiting)
-            waiting = with_core(*crossed)
-            after = [ran]
-        front_order = [o for o, _ in level[k + 1]]
-        wanted = [joined(*[longer[o] for o in front_order]), joined(cur, other_got)]
-        front, cur = combine(after, *wanted)
+            wanted.append(joined(x_got) + new)
+            more = crossed[2] + order
+        front, cur, both = combine(after, *wanted)
         after = [front]
         pieces = longer
+        front_order = order
         cur_order = cur_order + crossed_other[2]
-        waiting += with_core(front, 0, front_order)
+        waiting += with_core(both, 0, more)
+        if k == 0:
+            waiting += with_core(front, 0, front_order)
     waiting += with_core(cur, cut, cur_order)
     update, _ = spread(after, update, shape, table, slots, waiting)
     waiting = with_core(*crossed) + with_core(*crossed_other)

time: 231 us -> 231 us (level)
    pallas_call x4 -> x2, Pallas kernels: 8.79 us -> 7.4 us  [pack(): pl.pallas_call(functools.partial(pack_kernel, first, tuple(orders), slots...]
    ppermute x29 -> x28, starting transfers between devices: 35.6 us -> 36.1 us  [swap(): return lax.ppermute(value, 'dp', [(i, i ^ bit) for i in range(count)])]
    ppermute x29 -> x28, waiting for transfers between devices: 151 us -> 152 us  [swap(): return lax.ppermute(value, 'dp', [(i, i ^ bit) for i in range(count)])]
  transfers between devices with their start and end apart: 30 -> 29, of which waited for: 19 -> 16; matrix products, arithmetic and copies ran while one was open for 0% -> 0% of each run, Pallas kernels for 10% -> 10%
where the time goes in v6:
time: 231 us; the launch traced here: 230 us
  waiting for transfers between devices  155 us (67%)
  starting transfers between devices  37.7 us (16%)
  Pallas kernels  36.2 us (16%)
    ppermute x28, waiting for transfers between devices, swap(): return lax.ppermute(value, 'dp', [(i, i ^ bit) for i in range(count)])  152 us
    ppermute x28, starting transfers between devices, swap(): return lax.ppermute(value, 'dp', [(i, i ^ bit) for i in range(count)])  36.1 us
    pallas_call x3, Pallas kernels, spread(): pl.pallas_call(functools.partial(spread_kernel, plans, slots), out_shape=...  9.46 us
    pallas_call x4, Pallas kernels, add_taken(): pl.pallas_call(functools.partial(add_taken_kernel, first, order, slots, p...  8.79 us
    pallas_call x2, Pallas kernels, pack(): pl.pallas_call(functools.partial(pack_kernel, first, tuple(orders), slots...  7.4 us
  transfers between devices with their start and end apart: 29, of which 16 were waited for; matrix products, arithmetic and copies ran while one was open for 0% of the time, Pallas kernels for 10%

profile of v6, /device:TPU:0, one launch (start us, length us, event | category | flops | bytes accessed | tf_op | source)
XLA Modules:
  0.0 230.5 jit_solution(8123128754281705940)
XLA Ops:
  0.6 1.8 shard_map.50.table_ref
  3.1 2.3 shard_map.51.rest_0_
  5.9 5.1 %shard_map.52 = (bf16[2,96,2048]{2,1,0:T(8,128)(2,1)S(1)}, bf16[6,96,2048]{2,1,0:T(8,128)(2,1)S(1)}, bf16[8,96,2048]{2,1,0:T(8,128)(2,1)}) custom-call(s32[32]{0:T(128)S(1)} %copy-done.1, bf16[24,128,2048]{2,1,0:T(8,128)(2,1)} %bitcast.7, bf16[16,32,2048]{2,1,0:T(8,128)(2,1)S(1)} %shard_map.51.rest_0_), custom_call_target="tpu_custom_call" | custom-call | tf_op jit(solution)/shard_map/pallas_call | solution.py:121
  11.8 2.3 shard_map.53
  14.2 3.1 %collective-permute-start.5 = (bf16[8,32,2048]{2,1,0:T(8,128)(2,1)S(1)}, bf16[8,32,2048]{2,1,0:T(8,128)(2,1)S(1)}, u32[]{:S(2)}, u32[]{:S(2)}) collective-permute-start(bf16[8,32,2048]{2,1,0:T(8,128)(2,1)S(1)} %get-tuple-element.38.rest_0_), channel_id=1, source_target_pairs={{0,8},{2,10},{4,12},{6,14},{8,0},{10,2},{12,4},{14,6},{16,24},{18,... | collective-permute-start | bytes 3145736 | tf_op jit(solution)/shard_map/ppermute | solution.py:405
  17.2 1.8 collective-permute-done.2.got_ref
  19.0 1.7 shard_map.54.rest_0_
  20.7 4.3 %collective-permute-start.4 = (bf16[2,96,2048]{2,1,0:T(8,128)(2,1)S(1)}, bf16[2,96,2048]{2,1,0:T(8,128)(2,1)S(1)}, u32[]{:S(2)}, u32[]{:S(2)}) collective-permute-start(bf16[2,96,2048]{2,1,0:T(8,128)(2,1)S(1)} %shard_map.54.rest_0_), channel_id=1, source_target_pairs={{0,4},{2,6},{4,0},{6,2},{8,12},{10,14},{12,8},{14,10},{16,20},{18,... | collective-permute-start | bytes 2359304 | tf_op jit(solution)/shard_map/ppermute | solution.py:405
  25.0 2.2 shard_map.55
  27.5 15.9 %collective-permute-done.4.refs_1_ = bf16[2,96,2048]{2,1,0:T(8,128)(2,1)S(1)} collective-permute-done((bf16[2,96,2048]{2,1,0:T(8,128)(2,1)S(1)}, bf16[2,96,2048]{2,1,0:T(8,128)(2,1)S(1)}, u32[]{:S(2)}, u32[]{:S(2)}) %collective-permute-start.4) | collective-permute-done | bytes 786464 | tf_op jit(solution)/shard_map/ppermute | solution.py:405
  43.6 2.1 collective-permute-start.7
  45.8 2.7 %collective-permute-start.8 = (bf16[4,32,2048]{2,1,0:T(8,128)(2,1)S(1)}, bf16[4,32,2048]{2,1,0:T(8,128)(2,1)S(1)}, u32[]{:S(2)}, u32[]{:S(2)}) collective-permute-start(bf16[4,32,2048]{2,1,0:T(8,128)(2,1)S(1)} %get-tuple-element.45), channel_id=1, source_target_pairs={{0,16},{2,18},{4,20},{6,22},{8,24},{10,26},{12,28},{14,30},{16,0},... | collective-permute-start | bytes 1572872 | tf_op jit(solution)/shard_map/ppermute | solution.py:405
  48.4 2.5 %shard_map.57 = (bf16[2,96,2048]{2,1,0:T(8,128)(2,1)S(1)}, bf16[6,96,2048]{2,1,0:T(8,128)(2,1)S(1)}) custom-call(s32[32]{0:T(128)S(1)} %copy-done.1, bf16[24,128,2048]{2,1,0:T(8,128)(2,1)} %bitcast.11, bf16[8,96,2048]{2,1,0:T(8,128)(2,1)S(1)} %collective-permute-done.got_ref, bf16[2,96,2048]{2,1,0:T(8,128)(2,1)S(1)} %get-tuple-element.42.rest_0_), custom_call_target="tpu_custom_call" | custom-call | tf_op jit(solution)/shard_map/pallas_call | solution.py:151
  51.0 22.0 %collective-permute-done.8.refs_4_ = bf16[4,32,2048]{2,1,0:T(8,128)(2,1)S(1)} collective-permute-done((bf16[4,32,2048]{2,1,0:T(8,128)(2,1)S(1)}, bf16[4,32,2048]{2,1,0:T(8,128)(2,1)S(1)}, u32[]{:S(2)}, u32[]{:S(2)}) %collective-permute-start.8) | collective-permute-done | bytes 524320 | tf_op jit(solution)/shard_map/ppermute | solution.py:405
  73.8 3.0 %collective-permute-done.6.refs_1_ = bf16[4,96,2048]{2,1,0:T(8,128)(2,1)S(1)} collective-permute-done((bf16[4,96,2048]{2,1,0:T(8,128)(2,1)S(1)}, bf16[4,96,2048]{2,1,0:T(8,128)(2,1)S(1)}, u32[]{:S(2)}, u32[]{:S(2)}) %collective-permute-start.6) | collective-permute-done | bytes 1572896 | tf_op jit(solution)/shard_map/ppermute | solution.py:405
  77.1 2.9 %collective-permute-start.10 = (bf16[2,96,2048]{2,1,0:T(8,128)(2,1)S(1)}, bf16[2,96,2048]{2,1,0:T(8,128)(2,1)S(1)}, u32[]{:S(2)}, u32[]{:S(2)}) collective-permute-start(bf16[2,96,2048]{2,1,0:T(8,128)(2,1)S(1)} %get-tuple-element.48), channel_id=1, source_target_pairs={{0,16},{2,18},{4,20},{6,22},{8,24},{10,26},{12,28},{14,30},{16,0},... | collective-permute-start | bytes 2359304 | tf_op jit(solution)/shard_map/ppermute | solution.py:405
  83.7 22.0 %collective-permute-done.12.rest_5_ = bf16[2,32,2048]{2,1,0:T(8,128)(2,1)S(1)} collective-permute-done((bf16[2,32,2048]{2,1,0:T(8,128)(2,1)S(1)}, bf16[2,32,2048]{2,1,0:T(8,128)(2,1)S(1)}, u32[]{:S(2)}, u32[]{:S(2)}) %collective-permute-start.12) | collective-permute-done | bytes 262176 | tf_op jit(solution)/shard_map/ppermute | solution.py:405
  105.8 8.5 %collective-permute-done.10.rest_2_ = bf16[2,96,2048]{2,1,0:T(8,128)(2,1)S(1)} collective-permute-done((bf16[2,96,2048]{2,1,0:T(8,128)(2,1)S(1)}, bf16[2,96,2048]{2,1,0:T(8,128)(2,1)S(1)}, u32[]{:S(2)}, u32[]{:S(2)}) %collective-permute-start.10) | collective-permute-done | bytes 786464 | tf_op jit(solution)/shard_map/ppermute | solution.py:405
  117.1 3.4 %collective-permute-done.13.refs_1_ = f32[2,128,128]{2,1,0:T(8,128)S(1)} collective-permute-done((f32[2,128,128]{2,1,0:T(8,128)S(1)}, f32[2,128,128]{2,1,0:T(8,128)S(1)}, u32[]{:S(2)}, u32[]{:S(2)}) %collective-permute-start.13) | collective-permute-done | bytes 131104 | tf_op jit(solution)/shard_map/ppermute | solution.py:596
  120.6 4.4 %shard_map.60 = (bf16[2,96,2048]{2,1,0:T(8,128)(2,1)S(1)}, bf16[2,32,2048]{2,1,0:T(8,128)(2,1)S(1)}) custom-call(f32[2,128,128]{2,1,0:T(8,128)S(1)} %get-tuple-element.52.refs_0_, f32[2,128,128]{2,1,0:T(8,128)S(1)} %collective-permute-done.13.refs_1_, bf16[2,128,2048]{2,1,0:T(8,128)(2,1)S(1)} %get-tuple-element.53.refs_2_), custom_call_target="tpu_custom_call" | custom-call | tf_op jit(solution)/shard_map/pallas_call | solution.py:391
  126.5 2.9 %collective-permute-start.16 = (bf16[2,96,2048]{2,1,0:T(8,128)(2,1)S(1)}, bf16[2,96,2048]{2,1,0:T(8,128)(2,1)S(1)}, u32[]{:S(2)}, u32[]{:S(2)}) collective-permute-start(bf16[2,96,2048]{2,1,0:T(8,128)(2,1)S(1)} %get-tuple-element.54.rest_6_.refs_4_), channel_id=1, source_target_pairs={{0,8},{2,10},{4,12},{6,14},{8,0},{10,2},{12,4},{14,6},{16,24},{18,... | collective-permute-start | bytes 2359304 | tf_op jit(solution)/shard_map/ppermute | solution.py:405
  131.4 2.2 shard_map.61
  133.6 19.4 %collective-permute-done.17.refs_3_ = bf16[2,32,2048]{2,1,0:T(8,128)(2,1)S(1)} collective-permute-done((bf16[2,32,2048]{2,1,0:T(8,128)(2,1)S(1)}, bf16[2,32,2048]{2,1,0:T(8,128)(2,1)S(1)}, u32[]{:S(2)}, u32[]{:S(2)}) %collective-permute-start.17) | collective-permute-done | bytes 262176 | tf_op jit(solution)/shard_map/ppermute | solution.py:405
  153.0 6.9 %collective-permute-done.14.refs_0_ = bf16[2,96,2048]{2,1,0:T(8,128)(2,1)S(1)} collective-permute-done((bf16[2,96,2048]{2,1,0:T(8,128)(2,1)S(1)}, bf16[2,96,2048]{2,1,0:T(8,128)(2,1)S(1)}, u32[]{:S(2)}, u32[]{:S(2)}) %collective-permute-start.14) | collective-permute-done | bytes 786464 | tf_op jit(solution)/shard_map/ppermute | solution.py:405
  162.7 4.6 %collective-permute-start.19 = (bf16[4,32,2048]{2,1,0:T(8,128)(2,1)S(1)}, bf16[4,32,2048]{2,1,0:T(8,128)(2,1)S(1)}, u32[]{:S(2)}, u32[]{:S(2)}) collective-permute-start(bf16[4,32,2048]{2,1,0:T(8,128)(2,1)S(1)} %get-tuple-element.57.refs_1_), channel_id=1, source_target_pairs={{0,16},{2,18},{4,20},{6,22},{8,24},{10,26},{12,28},{14,30},{16,0},... | collective-permute-start | bytes 1572872 | tf_op jit(solution)/shard_map/ppermute | solution.py:405
  167.2 2.7 %shard_map.63 = (bf16[24,128,2048]{2,1,0:T(8,128)(2,1)}, f32[8,128]{1,0:T(8,128)S(1)}) custom-call(s32[32]{0:T(128)S(1)} %copy-done.1, bf16[4,96,2048]{2,1,0:T(8,128)(2,1)S(1)} %get-tuple-element.59.refs_0_, bf16[4,96,2048]{2,1,0:T(8,128)(2,1)S(1)} %collective-permute-done.21.refs_1_, bf16[4,96,2048]{2,1,0:T(8,128)(2,1)S(1)} %get-tuple-element.58.refs_2_.refs_4_, ...), custom_call_target="tpu_custom_call" | custom-call | tf_op jit(solution)/shard_map/pallas_call | solution.py:243
  170.0 20.7 %collective-permute-done.19.refs_2_ = bf16[4,32,2048]{2,1,0:T(8,128)(2,1)S(1)} collective-permute-done((bf16[4,32,2048]{2,1,0:T(8,128)(2,1)S(1)}, bf16[4,32,2048]{2,1,0:T(8,128)(2,1)S(1)}, u32[]{:S(2)}, u32[]{:S(2)}) %collective-permute-start.19) | collective-permute-done | bytes 524320 | tf_op jit(solution)/shard_map/ppermute | solution.py:405
  190.7 2.2 collective-permute-done.15.refs_0_
  192.9 4.4 %collective-permute-done.20.refs_3_ = bf16[4,96,2048]{2,1,0:T(8,128)(2,1)S(1)} collective-permute-done((bf16[4,96,2048]{2,1,0:T(8,128)(2,1)S(1)}, bf16[4,96,2048]{2,1,0:T(8,128)(2,1)S(1)}, u32[]{:S(2)}, u32[]{:S(2)}) %collective-permute-start.20) | collective-permute-done | bytes 1572896 | tf_op jit(solution)/shard_map/ppermute | solution.py:405
  199.5 23.7 %collective-permute-done.25.refs_2_ = bf16[8,32,2048]{2,1,0:T(8,128)(2,1)S(1)} collective-permute-done((bf16[8,32,2048]{2,1,0:T(8,128)(2,1)S(1)}, bf16[8,32,2048]{2,1,0:T(8,128)(2,1)S(1)}, u32[]{:S(2)}, u32[]{:S(2)}) %collective-permute-start.25) | collective-permute-done | bytes 1048608 | tf_op jit(solution)/shard_map/ppermute | solution.py:405
  223.7 4.0 %shard_map.65 = (bf16[24,128,2048]{2,1,0:T(8,128)(2,1)}, f32[8,128]{1,0:T(8,128)}) custom-call(s32[32]{0:T(128)S(1)} %copy-done.1, bf16[6,96,2048]{2,1,0:T(8,128)(2,1)S(1)} %get-tuple-element.63.refs_0_, bf16[6,96,2048]{2,1,0:T(8,128)(2,1)S(1)} %collective-permute-done.27.refs_1_, ...), custom_call_target="tpu_custom_call", output_to_operand_aliasing={{0}: (5, {})} | custom-call | tf_op jit(solution)/shard_map/pallas_call | solution.py:243
  227.7 2.8 %shard_map.66 = (bf16[24,128,2048]{2,1,0:T(8,128)(2,1)}, f32[8,128]{1,0:T(8,128)}) custom-call(s32[32]{0:T(128)S(1)} %copy-done.1, bf16[2,96,2048]{2,1,0:T(8,128)(2,1)S(1)} %collective-permute-done.23.refs_0_, bf16[2,96,2048]{2,1,0:T(8,128)(2,1)S(1)} %collective-permute-done.24.refs_1_, ...), custom_call_target="tpu_custom_call", output_to_operand_aliasing={{0}: (5, {})} | custom-call | tf_op jit(solution)/shard_map/pallas_call | solution.py:243
  (47 shorter events, 19.0 us)
Async XLA Ops:
  2.4 0.7 copy-start.1
  5.4 6.4 %collective-permute-start.3 = (bf16[16,32,2048]{2,1,0:T(8,128)(2,1)S(1)}, bf16[16,32,2048]{2,1,0:T(8,128)(2,1)S(1)}, u32[]{:S(2)}, u32[]{:S(2)}) collective-permute-start(bf16[16,32,2048]{2,1,0:T(8,128)(2,1)S(1)} %shard_map.51.rest_0_), channel_id=1, source_target_pairs={{0,2},{2,0},{4,6},{6,4},{8,10},{10,8},{12,14},{14,12},{16,18},{18,... | collective-permute-start | bytes 6291464 | tf_op jit(solution)/shard_map/ppermute | solution.py:405
  11.0 14.0 %collective-permute-start.1 = (bf16[6,96,2048]{2,1,0:T(8,128)(2,1)S(1)}, bf16[6,96,2048]{2,1,0:T(8,128)(2,1)S(1)}, u32[]{:S(2)}, u32[]{:S(2)}) collective-permute-start(bf16[6,96,2048]{2,1,0:T(8,128)(2,1)S(1)} %get-tuple-element.36), channel_id=1, source_target_pairs={{0,2},{2,0},{4,6},{6,4},{8,10},{10,8},{12,14},{14,12},{16,18},{18,... | collective-permute-start | bytes 7077896 | tf_op jit(solution)/shard_map/ppermute | solution.py:405
  11.3 37.1 %collective-permute-start = (bf16[8,96,2048]{2,1,0:T(8,128)(2,1)}, bf16[8,96,2048]{2,1,0:T(8,128)(2,1)S(1)}, u32[]{:S(2)}, u32[]{:S(2)}) collective-permute-start(bf16[8,96,2048]{2,1,0:T(8,128)(2,1)} %get-tuple-element.35), channel_id=1, source_target_pairs={{0,2},{2,0},{4,6},{6,4},{8,10},{10,8},{12,14},{14,12},{16,18},{18,... | collective-permute-start | bytes 9437192 | tf_op jit(solution)/shard_map/ppermute | solution.py:405
  11.6 7.4 %collective-permute-start.2 = (bf16[2,96,2048]{2,1,0:T(8,128)(2,1)S(1)}, bf16[2,96,2048]{2,1,0:T(8,128)(2,1)S(1)}, u32[]{:S(2)}, u32[]{:S(2)}) collective-permute-start(bf16[2,96,2048]{2,1,0:T(8,128)(2,1)S(1)} %get-tuple-element.37.rest_0_), channel_id=1, source_target_pairs={{0,2},{2,0},{4,6},{6,4},{8,10},{10,8},{12,14},{14,12},{16,18},{18,... | collective-permute-start | bytes 2359304 | tf_op jit(solution)/shard_map/ppermute | solution.py:405
  14.2 29.3 %collective-permute-start.5 = (bf16[8,32,2048]{2,1,0:T(8,128)(2,1)S(1)}, bf16[8,32,2048]{2,1,0:T(8,128)(2,1)S(1)}, u32[]{:S(2)}, u32[]{:S(2)}) collective-permute-start(bf16[8,32,2048]{2,1,0:T(8,128)(2,1)S(1)} %get-tuple-element.38.rest_0_), channel_id=1, source_target_pairs={{0,8},{2,10},{4,12},{6,14},{8,0},{10,2},{12,4},{14,6},{16,24},{18,... | collective-permute-start | bytes 3145736 | tf_op jit(solution)/shard_map/ppermute | solution.py:405
  20.7 22.7 %collective-permute-start.4 = (bf16[2,96,2048]{2,1,0:T(8,128)(2,1)S(1)}, bf16[2,96,2048]{2,1,0:T(8,128)(2,1)S(1)}, u32[]{:S(2)}, u32[]{:S(2)}) collective-permute-start(bf16[2,96,2048]{2,1,0:T(8,128)(2,1)S(1)} %shard_map.54.rest_0_), channel_id=1, source_target_pairs={{0,4},{2,6},{4,0},{6,2},{8,12},{10,14},{12,8},{14,10},{16,20},{18,... | collective-permute-start | bytes 2359304 | tf_op jit(solution)/shard_map/ppermute | solution.py:405
  27.3 49.5 %collective-permute-start.6 = (bf16[4,96,2048]{2,1,0:T(8,128)(2,1)S(1)}, bf16[4,96,2048]{2,1,0:T(8,128)(2,1)S(1)}, u32[]{:S(2)}, u32[]{:S(2)}) collective-permute-start(bf16[4,96,2048]{2,1,0:T(8,128)(2,1)S(1)} %get-tuple-element.41.refs_4_), channel_id=1, source_target_pairs={{0,4},{2,6},{4,0},{6,2},{8,12},{10,14},{12,8},{14,10},{16,20},{18,... | collective-permute-start | bytes 4718600 | tf_op jit(solution)/shard_map/ppermute | solution.py:405
  43.6 30.2 %collective-permute-start.7 = (bf16[2,96,2048]{2,1,0:T(8,128)(2,1)S(1)}, bf16[2,96,2048]{2,1,0:T(8,128)(2,1)S(1)}, u32[]{:S(2)}, u32[]{:S(2)}) collective-permute-start(bf16[2,96,2048]{2,1,0:T(8,128)(2,1)S(1)} %get-tuple-element.42.rest_0_), channel_id=1, source_target_pairs={{0,8},{2,10},{4,12},{6,14},{8,0},{10,2},{12,4},{14,6},{16,24},{18,... | collective-permute-start | bytes 2359304 | tf_op jit(solution)/shard_map/ppermute | solution.py:405
  45.8 27.2 %collective-permute-start.8 = (bf16[4,32,2048]{2,1,0:T(8,128)(2,1)S(1)}, bf16[4,32,2048]{2,1,0:T(8,128)(2,1)S(1)}, u32[]{:S(2)}, u32[]{:S(2)}) collective-permute-start(bf16[4,32,2048]{2,1,0:T(8,128)(2,1)S(1)} %get-tuple-element.45), channel_id=1, source_target_pairs={{0,16},{2,18},{4,20},{6,22},{8,24},{10,26},{12,28},{14,30},{16,0},... | collective-permute-start | bytes 1572872 | tf_op jit(solution)/shard_map/ppermute | solution.py:405
  76.8 37.6 %copy-start = (f32[1,2,128,2048]{3,2,1,0:T(8,128)S(1)}, f32[1,2,128,2048]{3,2,1,0:T(8,128)}, u32[]{:S(2)}) copy-start(f32[1,2,128,2048]{3,2,1,0:T(8,128)} %param.5) | copy-start | bytes 6291460
  77.1 37.2 %collective-permute-start.10 = (bf16[2,96,2048]{2,1,0:T(8,128)(2,1)S(1)}, bf16[2,96,2048]{2,1,0:T(8,128)(2,1)S(1)}, u32[]{:S(2)}, u32[]{:S(2)}) collective-permute-start(bf16[2,96,2048]{2,1,0:T(8,128)(2,1)S(1)} %get-tuple-element.48), channel_id=1, source_target_pairs={{0,16},{2,18},{4,20},{6,22},{8,24},{10,26},{12,28},{14,30},{16,0},... | collective-permute-start | bytes 2359304 | tf_op jit(solution)/shard_map/ppermute | solution.py:405
  80.0 34.4 %collective-permute-start.11 = (bf16[2,96,2048]{2,1,0:T(8,128)(2,1)S(1)}, bf16[2,96,2048]{2,1,0:T(8,128)(2,1)S(1)}, u32[]{:S(2)}, u32[]{:S(2)}) collective-permute-start(bf16[2,96,2048]{2,1,0:T(8,128)(2,1)S(1)} %get-tuple-element.49), channel_id=1, source_target_pairs={{0,8},{2,10},{4,12},{6,14},{8,0},{10,2},{12,4},{14,6},{16,24},{18,... | collective-permute-start | bytes 2359304 | tf_op jit(solution)/shard_map/ppermute | solution.py:405
  81.7 32.7 %collective-permute-start.9 = (bf16[2,96,2048]{2,1,0:T(8,128)(2,1)S(1)}, bf16[2,96,2048]{2,1,0:T(8,128)(2,1)S(1)}, u32[]{:S(2)}, u32[]{:S(2)}) collective-permute-start(bf16[2,96,2048]{2,1,0:T(8,128)(2,1)S(1)} %get-tuple-element.47), channel_id=1, source_target_pairs={{0,4},{2,6},{4,0},{6,2},{8,12},{10,14},{12,8},{14,10},{16,20},{18,... | collective-permute-start | bytes 2359304 | tf_op jit(solution)/shard_map/ppermute | solution.py:405
  83.1 22.7 %collective-permute-start.12 = (bf16[2,32,2048]{2,1,0:T(8,128)(2,1)S(1)}, bf16[2,32,2048]{2,1,0:T(8,128)(2,1)S(1)}, u32[]{:S(2)}, u32[]{:S(2)}) collective-permute-start(bf16[2,32,2048]{2,1,0:T(8,128)(2,1)S(1)} %get-tuple-element.51), channel_id=1, source_target_pairs={{0,4},{2,6},{4,0},{6,2},{8,12},{10,14},{12,8},{14,10},{16,20},{18,... | collective-permute-start | bytes 786440 | tf_op jit(solution)/shard_map/ppermute | solution.py:405
  115.5 5.0 %collective-permute-start.13 = (f32[2,128,128]{2,1,0:T(8,128)S(1)}, f32[2,128,128]{2,1,0:T(8,128)S(1)}, u32[]{:S(2)}, u32[]{:S(2)}) collective-permute-start(f32[2,128,128]{2,1,0:T(8,128)S(1)} %get-tuple-element.52.refs_0_), channel_id=1, source_target_pairs={{0,1},{1,0},{2,3},{3,2},{4,5},{5,4},{6,7},{7,6},{8,9},{9,8},{10,11... | collective-permute-start | bytes 393224 | tf_op jit(solution)/shard_map/ppermute | solution.py:596
  125.0 35.0 %collective-permute-start.14 = (bf16[2,96,2048]{2,1,0:T(8,128)(2,1)S(1)}, bf16[2,96,2048]{2,1,0:T(8,128)(2,1)S(1)}, u32[]{:S(2)}, u32[]{:S(2)}) collective-permute-start(bf16[2,96,2048]{2,1,0:T(8,128)(2,1)S(1)} %get-tuple-element.54.rest_6_.refs_4_), channel_id=1, source_target_pairs={{0,16},{2,18},{4,20},{6,22},{8,24},{10,26},{12,28},{14,30},{16,0},... | collective-permute-start | bytes 2359304 | tf_op jit(solution)/shard_map/ppermute | solution.py:405
  126.5 33.5 %collective-permute-start.16 = (bf16[2,96,2048]{2,1,0:T(8,128)(2,1)S(1)}, bf16[2,96,2048]{2,1,0:T(8,128)(2,1)S(1)}, u32[]{:S(2)}, u32[]{:S(2)}) collective-permute-start(bf16[2,96,2048]{2,1,0:T(8,128)(2,1)S(1)} %get-tuple-element.54.rest_6_.refs_4_), channel_id=1, source_target_pairs={{0,8},{2,10},{4,12},{6,14},{8,0},{10,2},{12,4},{14,6},{16,24},{18,... | collective-permute-start | bytes 2359304 | tf_op jit(solution)/shard_map/ppermute | solution.py:405
  129.4 30.7 %collective-permute-start.18 = (bf16[2,96,2048]{2,1,0:T(8,128)(2,1)S(1)}, bf16[2,96,2048]{2,1,0:T(8,128)(2,1)S(1)}, u32[]{:S(2)}, u32[]{:S(2)}) collective-permute-start(bf16[2,96,2048]{2,1,0:T(8,128)(2,1)S(1)} %get-tuple-element.54.rest_6_.refs_4_), channel_id=1, source_target_pairs={{0,4},{2,6},{4,0},{6,2},{8,12},{10,14},{12,8},{14,10},{16,20},{18,... | collective-permute-start | bytes 2359304 | tf_op jit(solution)/shard_map/ppermute | solution.py:405
  130.9 22.1 %collective-permute-start.17 = (bf16[2,32,2048]{2,1,0:T(8,128)(2,1)S(1)}, bf16[2,32,2048]{2,1,0:T(8,128)(2,1)S(1)}, u32[]{:S(2)}, u32[]{:S(2)}) collective-permute-start(bf16[2,32,2048]{2,1,0:T(8,128)(2,1)S(1)} %get-tuple-element.55.refs_2_), channel_id=1, source_target_pairs={{0,4},{2,6},{4,0},{6,2},{8,12},{10,14},{12,8},{14,10},{16,20},{18,... | collective-permute-start | bytes 786440 | tf_op jit(solution)/shard_map/ppermute | solution.py:405
  160.3 6.9 %collective-permute-start.21 = (bf16[4,96,2048]{2,1,0:T(8,128)(2,1)S(1)}, bf16[4,96,2048]{2,1,0:T(8,128)(2,1)S(1)}, u32[]{:S(2)}, u32[]{:S(2)}) collective-permute-start(bf16[4,96,2048]{2,1,0:T(8,128)(2,1)S(1)} %get-tuple-element.59.refs_0_), channel_id=1, source_target_pairs={{0,2},{2,0},{4,6},{6,4},{8,10},{10,8},{12,14},{14,12},{16,18},{18,... | collective-permute-start | bytes 4718600 | tf_op jit(solution)/shard_map/ppermute | solution.py:405
  160.4 6.9 %collective-permute-start.22 = (bf16[4,96,2048]{2,1,0:T(8,128)(2,1)S(1)}, bf16[4,96,2048]{2,1,0:T(8,128)(2,1)S(1)}, u32[]{:S(2)}, u32[]{:S(2)}) collective-permute-start(bf16[4,96,2048]{2,1,0:T(8,128)(2,1)S(1)} %get-tuple-element.58.refs_2_.refs_4_), channel_id=1, source_target_pairs={{0,2},{2,0},{4,6},{6,4},{8,10},{10,8},{12,14},{14,12},{16,18},{18,... | collective-permute-start | bytes 4718600 | tf_op jit(solution)/shard_map/ppermute | solution.py:405
  160.9 36.4 %collective-permute-start.20 = (bf16[4,96,2048]{2,1,0:T(8,128)(2,1)S(1)}, bf16[4,96,2048]{2,1,0:T(8,128)(2,1)S(1)}, u32[]{:S(2)}, u32[]{:S(2)}) collective-permute-start(bf16[4,96,2048]{2,1,0:T(8,128)(2,1)S(1)} %get-tuple-element.58.refs_2_.refs_4_), channel_id=1, source_target_pairs={{0,4},{2,6},{4,0},{6,2},{8,12},{10,14},{12,8},{14,10},{16,20},{18,... | collective-permute-start | bytes 4718600 | tf_op jit(solution)/shard_map/ppermute | solution.py:405
  162.4 30.5 %collective-permute-start.15 = (bf16[2,96,2048]{2,1,0:T(8,128)(2,1)S(1)}, bf16[2,96,2048]{2,1,0:T(8,128)(2,1)S(1)}, u32[]{:S(2)}, u32[]{:S(2)}) collective-permute-start(bf16[2,96,2048]{2,1,0:T(8,128)(2,1)S(1)} %collective-permute-done.14.refs_0_), channel_id=1, source_target_pairs={{0,8},{2,10},{4,12},{6,14},{8,0},{10,2},{12,4},{14,6},{16,24},{18,... | collective-permute-start | bytes 2359304 | tf_op jit(solution)/shard_map/ppermute | solution.py:405
  162.7 28.0 %collective-permute-start.19 = (bf16[4,32,2048]{2,1,0:T(8,128)(2,1)S(1)}, bf16[4,32,2048]{2,1,0:T(8,128)(2,1)S(1)}, u32[]{:S(2)}, u32[]{:S(2)}) collective-permute-start(bf16[4,32,2048]{2,1,0:T(8,128)(2,1)S(1)} %get-tuple-element.57.refs_1_), channel_id=1, source_target_pairs={{0,16},{2,18},{4,20},{6,22},{8,24},{10,26},{12,28},{14,30},{16,0},... | collective-permute-start | bytes 1572872 | tf_op jit(solution)/shard_map/ppermute | solution.py:405
  197.5 26.2 %collective-permute-start.27 = (bf16[6,96,2048]{2,1,0:T(8,128)(2,1)S(1)}, bf16[6,96,2048]{2,1,0:T(8,128)(2,1)S(1)}, u32[]{:S(2)}, u32[]{:S(2)}) collective-permute-start(bf16[6,96,2048]{2,1,0:T(8,128)(2,1)S(1)} %get-tuple-element.63.refs_0_), channel_id=1, source_target_pairs={{0,2},{2,0},{4,6},{6,4},{8,10},{10,8},{12,14},{14,12},{16,18},{18,... | collective-permute-start | bytes 7077896 | tf_op jit(solution)/shard_map/ppermute | solution.py:405
  197.6 25.6 %collective-permute-start.25 = (bf16[8,32,2048]{2,1,0:T(8,128)(2,1)S(1)}, bf16[8,32,2048]{2,1,0:T(8,128)(2,1)S(1)}, u32[]{:S(2)}, u32[]{:S(2)}) collective-permute-start(bf16[8,32,2048]{2,1,0:T(8,128)(2,1)S(1)} %get-tuple-element.62.refs_2_), channel_id=1, source_target_pairs={{0,8},{2,10},{4,12},{6,14},{8,0},{10,2},{12,4},{14,6},{16,24},{18,... | collective-permute-start | bytes 3145736 | tf_op jit(solution)/shard_map/ppermute | solution.py:405
  198.0 25.1 %collective-permute-start.23 = (bf16[2,96,2048]{2,1,0:T(8,128)(2,1)S(1)}, bf16[2,96,2048]{2,1,0:T(8,128)(2,1)S(1)}, u32[]{:S(2)}, u32[]{:S(2)}) collective-permute-start(bf16[2,96,2048]{2,1,0:T(8,128)(2,1)S(1)} %get-tuple-element.61.refs_5_), channel_id=1, source_target_pairs={{0,4},{2,6},{4,0},{6,2},{8,12},{10,14},{12,8},{14,10},{16,20},{18,... | collective-permute-start | bytes 2359304 | tf_op jit(solution)/shard_map/ppermute | solution.py:405
  199.5 24.2 %collective-permute-start.28 = (bf16[8,32,2048]{2,1,0:T(8,128)(2,1)S(1)}, bf16[8,32,2048]{2,1,0:T(8,128)(2,1)S(1)}, u32[]{:S(2)}, u32[]{:S(2)}) collective-permute-start(bf16[8,32,2048]{2,1,0:T(8,128)(2,1)S(1)} %get-tuple-element.62.refs_2_), channel_id=1, source_target_pairs={{0,2},{2,0},{4,6},{6,4},{8,10},{10,8},{12,14},{14,12},{16,18},{18,... | collective-permute-start | bytes 3145736 | tf_op jit(solution)/shard_map/ppermute | solution.py:405
  223.2 4.5 %collective-permute-start.26 = (bf16[8,32,2048]{2,1,0:T(8,128)(2,1)S(1)}, bf16[8,32,2048]{2,1,0:T(8,128)(2,1)S(1)}, u32[]{:S(2)}, u32[]{:S(2)}) collective-permute-start(bf16[8,32,2048]{2,1,0:T(8,128)(2,1)S(1)} %collective-permute-done.25.refs_2_), channel_id=1, source_target_pairs={{0,2},{2,0},{4,6},{6,4},{8,10},{10,8},{12,14},{14,12},{16,18},{18,... | collective-permute-start | bytes 3145736 | tf_op jit(solution)/shard_map/ppermute | solution.py:405
  223.2 4.5 %collective-permute-start.24 = (bf16[2,96,2048]{2,1,0:T(8,128)(2,1)S(1)}, bf16[2,96,2048]{2,1,0:T(8,128)(2,1)S(1)}, u32[]{:S(2)}, u32[]{:S(2)}) collective-permute-start(bf16[2,96,2048]{2,1,0:T(8,128)(2,1)S(1)} %collective-permute-done.23.refs_0_), channel_id=1, source_target_pairs={{0,2},{2,0},{4,6},{6,4},{8,10},{10,8},{12,14},{14,12},{16,18},{18,... | collective-permute-start | bytes 2359304 | tf_op jit(solution)/shard_map/ppermute | solution.py:405

commit v7 on v6

--- a/solution.py
+++ b/solution.py
@@ -71,17 +71,6 @@
         used[at] = rank + 1
 
 
-def build_table(me, owner, owners, slots):
-    return pl.pallas_call(
-        functools.partial(table_kernel, slots),
-        out_shape=jax.ShapeDtypeStruct((owners * slots,), jnp.int32),
-        in_specs=in_smem(2),
-        out_specs=in_smem()[0],
-        scratch_shapes=[pltpu.SMEM((owners,), jnp.int32)],
-        cost_estimate=small_cost(),
-    )(me, owner)
-
-
 def starts(order, slots):
     return [
         (n * slots + s, offset * slots + s)
@@ -90,24 +79,30 @@
     ]
 
 
-def fetch(table_ref, src_ref, first, order, slots, into, sem):
+def items_of(order, slots, first, rows, split=1):
+    return tuple(
+        (place, first + c * rows) for _, place in starts(order, slots) for c in range(split)
+    )
+
+
+def fetch(table_ref, src_ref, items, into, sem):
     rows = into.shape[1]
-    for item, place in starts(order, slots):
+    for item, (place, first) in enumerate(items):
         matrix = jnp.maximum(table_ref[place], 0)
         pltpu.make_async_copy(
             src_ref.at[matrix, pl.ds(first, rows)], into.at[item], sem.at[item]
         ).start()
     return lambda i: pltpu.make_async_copy(
-        src_ref.at[0, pl.ds(first, rows)], into.at[i], sem.at[i]
-    )
-
-
-def pack_kernel(first, orders, slots, table_ref, src_ref, *rest):
-    out_refs = rest[-2 * len(orders) : -len(orders)]
-    sems = rest[-len(orders) :]
+        src_ref.at[0, pl.ds(0, rows)], into.at[i], sem.at[i]
+    )
+
+
+def pack_kernel(plans, table_ref, src_ref, *rest):
+    out_refs = rest[-2 * len(plans) : -len(plans)]
+    sems = rest[-len(plans) :]
     copies = [
-        fetch(table_ref, src_ref, first, order, slots, out_ref, sem)
-        for order, out_ref, sem in zip(orders, out_refs, sems)
+        fetch(table_ref, src_ref, items, out_ref, sem)
+        for items, out_ref, sem in zip(plans, out_refs, sems)
     ]
     for copy, out_ref in zip(copies, out_refs):
 
@@ -116,25 +111,54 @@
             copy(i).wait()
 
 
-def pack(after, table, src, orders, slots, first, rows):
-    counts = [len(order) * slots for order in orders]
-    return pl.pallas_call(
-        functools.partial(pack_kernel, first, tuple(orders), slots),
+def pack(after, table, src, plans, rows):
+    return pl.pallas_call(
+        functools.partial(pack_kernel, tuple(plans)),
         out_shape=[
-            jax.ShapeDtypeStruct((n, rows, src.shape[2]), src.dtype) for n in counts
+            jax.ShapeDtypeStruct((len(items), rows, src.shape[2]), src.dtype)
+            for items in plans
         ],
         in_specs=in_smem() + in_hbm() + anywhere(len(after)),
-        out_specs=in_vmem(len(orders)),
-        scratch_shapes=[pltpu.SemaphoreType.DMA((n,)) for n in counts],
+        out_specs=in_vmem(len(plans)),
+        scratch_shapes=[pltpu.SemaphoreType.DMA((len(items),)) for items in plans],
         compiler_params=limits(MORE_VMEM_BYTES),
         cost_estimate=small_cost(),
     )(table, src, *after)
 
 
-def add_taken_kernel(first, order, slots, parts, table_ref, src_ref, got_ref, *rest):
+def first_pack_kernel(items, slots, me_ref, owner_ref, src_ref, *rest):
+    table_ref, out_ref, used, sem = rest
+    table_kernel(slots, me_ref, owner_ref, table_ref, used)
+    copy = fetch(table_ref, src_ref, items, out_ref, sem)
+
+    @pl.loop(0, out_ref.shape[0])
+    def _(i):
+        copy(i).wait()
+
+
+def first_pack(me, owner, owners, slots, src, items, rows):
+    count = len(items)
+    return pl.pallas_call(
+        functools.partial(first_pack_kernel, items, slots),
+        out_shape=[
+            jax.ShapeDtypeStruct((owners * slots,), jnp.int32),
+            jax.ShapeDtypeStruct((count, rows, src.shape[2]), src.dtype),
+        ],
+        in_specs=in_smem(2) + in_hbm(),
+        out_specs=in_smem() + in_vmem(),
+        scratch_shapes=[
+            pltpu.SMEM((owners,), jnp.int32),
+            pltpu.SemaphoreType.DMA((count,)),
+        ],
+        compiler_params=limits(MORE_VMEM_BYTES),
+        cost_estimate=small_cost(),
+    )(me, owner, src)
+
+
+def add_taken_kernel(items, parts, table_ref, src_ref, got_ref, *rest):
     mine, sem = rest[-2:]
     out_refs = rest[-2 - len(parts) : -2]
-    copy = fetch(table_ref, src_ref, first, order, slots, mine, sem)
+    copy = fetch(table_ref, src_ref, items, mine, sem)
     start = 0
     for size, out_ref in zip(parts, out_refs):
 
@@ -146,10 +170,10 @@
         start += size
 
 
-def add_taken(after, table, src, order, slots, first, got, parts):
+def add_taken(after, table, src, items, got, parts):
     count, rows, cols = got.shape
     return pl.pallas_call(
-        functools.partial(add_taken_kernel, first, order, slots, parts),
+        functools.partial(add_taken_kernel, items, parts),
         out_shape=[jax.ShapeDtypeStruct((n, rows, cols), got.dtype) for n in parts],
         in_specs=in_smem() + in_hbm() + in_vmem() + anywhere(len(after)),
         out_specs=in_vmem(len(parts)),
@@ -167,10 +191,18 @@
     outs = refs[len(refs) - len(plans) :]
     for out_ref, items in zip(outs, plans):
         for i, terms in enumerate(items):
-            total = sources[terms[0][0]][terms[0][1]]
-            for at, item in terms[1:]:
-                total = total + sources[at][item]
-            out_ref[i] = total
+            cuts = max(len(item) for _, item in terms)
+            rows = out_ref.shape[1] // cuts
+            for c in range(cuts):
+                here = pl.ds(c * rows, rows)
+                total = None
+                for at, item in terms:
+                    if len(item) == cuts:
+                        term = sources[at][item[c]]
+                    else:
+                        term = sources[at][item[0], here]
+                    total = term if total is None else total + term
+                out_ref[i, here] = total
 
 
 def combine(after, *wanted):
@@ -184,7 +216,7 @@
                 if not places:
                     arrays.append(array)
                     places = [len(arrays) - 1]
-                found.append((places[0], item))
+                found.append((places[0], item if isinstance(item, tuple) else (item,)))
             plan.append(tuple(found))
         plans.append(tuple(plan))
     shapes = []
@@ -431,11 +463,15 @@
 
 
 class Block:
-    def __init__(self, array, start):
-        self.array, self.start = array, start
-
-
-def sum_to_owners(gradient, table, slots, bits, cut):
+    def __init__(self, array, start, split=1):
+        self.array, self.start, self.split = array, start, split
+
+    def item(self, slot):
+        first = self.start + slot * self.split
+        return tuple(range(first, first + self.split))
+
+
+def sum_to_owners(gradient, me, owner, owners, slots, bits, cut):
     rest = gradient.shape[1] - cut
     level = [[o for o, _ in found] for found in levels(bits)]
     last = {o: bits[j] for found in levels(bits) for o, j in found if j >= 0}
@@ -453,11 +489,24 @@
     def theirs(order):
         return tuple(CORE_BIT | o for o in order)
 
-    packed = pack([], table, gradient, [theirs(other_order)], slots, cut, rest)
-    other_got = swap(packed[0], CORE_BIT)
-    falling = range(top, -1, -1)
-    orders = [theirs(merged[k]) for k in falling]
-    packed = pack(packed, table, gradient, orders, slots, 0, cut)
+    split = cut // rest
+    half = len(other_order) * slots // 2
+
+    def first_items(places):
+        return items_of(places(other_order), slots, cut, rest) + items_of(
+            places(merged[top]), slots, 0, rest, split
+        )
+
+    def same(order):
+        return order
+
+    table, packed = first_pack(
+        me, owner, owners, slots, gradient, first_items(theirs), rest
+    )
+    first_got = swap(packed, CORE_BIT)
+    falling = range(top - 1, -1, -1)
+    plans = [items_of(theirs(merged[k]), slots, 0, cut) for k in falling]
+    packed = pack([packed], table, gradient, plans, cut)
     got = {k: swap(block, CORE_BIT) for k, block in zip(falling, packed)}
     after = [packed[0]]
 
@@ -470,24 +519,27 @@
         parts = (crossing,)
         if len(order) * slots > crossing:
             parts += (len(order) * slots - crossing,)
-        made = add_taken(after, table, gradient, order, slots, 0, got[k], parts)
+        items = items_of(order, slots, 0, cut)
+        made = add_taken(after, table, gradient, items, got[k], parts)
         over_x[k] = made[0]
         for n, o in enumerate(order[len(level[k]) :]):
             home[o] = Block(made[1], n * slots)
         return [made[0]]
 
-    half = len(other_order) * slots // 2
-    away, kept = add_taken(
-        after, table, gradient, other_order, slots, cut, other_got, (half, half)
-    )
+    parts = (half, half, len(merged[top]) * slots * split)
+    away, kept, far = add_taken(
+        after, table, gradient, first_items(same), first_got, parts
+    )
+    after = [away]
     other_got = swap(away, other_bits[0])
-    after = take(top, [away])
-    x_got = swap(over_x[top], X_BIT)
+    x_got = swap(far, X_BIT)
+
     pending = {}
     for k in range(top, -1, -1):
         terms = {o: [] for o in level[k]}
         for n, o in enumerate(level[k]):
-            terms[o].append(Block(x_got, n * slots))
+            cuts = split if k == top else 1
+            terms[o].append(Block(x_got, n * slots * cuts, cuts))
         for o, value in pending.items():
             terms[o ^ last[o]].append(Block(value, 0))
         if k == 0:
@@ -497,9 +549,7 @@
         wanted = []
         for o in level[k]:
             parts = [home[o]] + terms[o]
-            wanted.append(
-                [[(b.array, b.start + s) for b in parts] for s in range(slots)]
-            )
+            wanted.append([[(b.array, b.item(s)) for b in parts] for s in range(slots)])
         half //= 2
         wanted.append(summed(kept, other_got, 0, half))
         wanted.append(summed(kept, other_got, half, 2 * half))
@@ -516,7 +566,8 @@
         kept = made[-1]
         other_got = swap(made[-2], other_bits[top - k + 1])
         x_got = swap(over_x[k - 1], X_BIT)
-    return [[home[0]] + terms[0], [Block(kept, 0), Block(other_got, 0)]]
+    parts = [[home[0]] + terms[0], [Block(kept, 0), Block(other_got, 0)]]
+    return table, parts
 
 
 def spread_updates(blocks, table, slots, bits, cut, shape, early):
@@ -553,25 +604,23 @@
             after = [ran]
         waiting = []
         order = [o for o, _ in level[k + 1]]
-        new = joined(*[longer[o] for o in order])
-        wanted = [new, joined(cur, other_got)]
+        wanted = [joined(*[longer[o] for o in order]), joined(cur, other_got)]
         if k == 0:
             wanted.append(joined(front, x_got))
-            more = front_order + crossed[2]
+            front, cur, both = combine(after, *wanted)
+            waiting += with_core(both, 0, front_order + crossed[2])
         else:
-            wanted.append(joined(x_got) + new)
-            more = crossed[2] + order
-        front, cur, both = combine(after, *wanted)
+            front, cur = combine(after, *wanted)
+            waiting += with_core(*crossed)
         after = [front]
         pieces = longer
         front_order = order
         cur_order = cur_order + crossed_other[2]
-        waiting += with_core(both, 0, more)
-        if k == 0:
-            waiting += with_core(front, 0, front_order)
+        last = with_core(front, 0, front_order)
+        waiting += last if k + 1 < top else last[:1]
     waiting += with_core(cur, cut, cur_order)
     update, _ = spread(after, update, shape, table, slots, waiting)
-    waiting = with_core(*crossed) + with_core(*crossed_other)
+    waiting = last[1:] + with_core(*crossed) + with_core(*crossed_other)
     return spread([], update, shape, table, slots, waiting)[0]
 
 
@@ -582,11 +631,12 @@
     head_rows, cols = grads.shape[2:]
     factor = 0.2 * math.sqrt(max(R, D))
     me = lax.axis_index("dp").astype(jnp.int32).reshape(1)
-    table = build_table(me, owner, owner_count, slot_count)
 
     cut = head_rows * 3 // 4
     bits = z_bits()[::-1]
-    parts = sum_to_owners(grads[0], table, slot_count, bits, cut)
+    table, parts = sum_to_owners(
+        grads[0], me, owner, owner_count, slot_count, bits, cut
+    )
     rounded, gram = nesterov_step(momentum[0], parts, owner_count)
 
     width = lax.axis_size("tensor")

time: 231 us -> 217 us (0.939)
  waiting for transfers between devices: 155 us -> 146 us
  starting transfers between devices: 37.7 us -> 34.3 us
    ppermute x28, waiting for transfers between devices: 152 us -> 143 us  [swap(): return lax.ppermute(value, 'dp', [(i, i ^ bit) for i in range(count)])]
    ppermute x28, starting transfers between devices: 36.1 us -> 32.7 us  [swap(): return lax.ppermute(value, 'dp', [(i, i ^ bit) for i in range(count)])]
    pallas_call x7 -> x5, Pallas kernels: 18 us -> 16.5 us  [the longest x3 7.83 us: add_taken(): pl.pallas_call(functools.partial(add_taken_kernel, items, parts), out_sha...]
  transfers between devices with their start and end apart: 29 -> 29, of which waited for: 16 -> 18; matrix products, arithmetic and copies ran while one was open for 0% -> 0% of each run, Pallas kernels for 10% -> 10%
where the time goes in v7:
time: 217 us
  waiting for transfers between devices  146 us (67%)
  Pallas kernels  34.7 us (16%)
  starting transfers between devices  34.3 us (16%)
    ppermute x28, waiting for transfers between devices, swap(): return lax.ppermute(value, 'dp', [(i, i ^ bit) for i in range(count)])  143 us
    ppermute x28, starting transfers between devices, swap(): return lax.ppermute(value, 'dp', [(i, i ^ bit) for i in range(count)])  32.7 us
    pallas_call x3, Pallas kernels, spread(): pl.pallas_call(functools.partial(spread_kernel, plans, slots), out_shape=...  9.59 us
    pallas_call x3, Pallas kernels, add_taken(): pl.pallas_call(functools.partial(add_taken_kernel, items, parts), out_sha...  7.83 us
    pallas_call x1, Pallas kernels, pack(): pl.pallas_call(functools.partial(pack_kernel, tuple(plans)), out_shape=[j...  4.87 us
    pallas_call x1, Pallas kernels, orthogonalize(): pl.pallas_call(functools.partial(orthogonalize_kernel, factor, slots, len...  4.45 us
  transfers between devices with their start and end apart: 29, of which 18 were waited for; matrix products, arithmetic and copies ran while one was open for 0% of the time, Pallas kernels for 10%

profile of v7, /device:TPU:0, one launch (start us, length us, event | category | flops | bytes accessed | tf_op | source)
XLA Modules:
  0.0 216.6 jit_solution(11543792109295764769)
XLA Ops:
  1.3 3.8 %shard_map.50 = (s32[32]{0:T(128)S(1)}, bf16[22,32,2048]{2,1,0:T(8,128)(2,1)S(1)}) custom-call(s32[1]{0:T(128)} %bitcast.me_ref, s32[24]{0:T(128)S(1)} %copy-done.1, bf16[24,128,2048]{2,1,0:T(8,128)(2,1)} %bitcast.6), custom_call_target="tpu_custom_call" | custom-call | tf_op jit(solution)/shard_map/pallas_call | solution.py:141
  5.8 4.9 %shard_map.51 = (bf16[6,96,2048]{2,1,0:T(8,128)(2,1)S(1)}, bf16[8,96,2048]{2,1,0:T(8,128)(2,1)}) custom-call(s32[32]{0:T(128)S(1)} %get-tuple-element.36.table_ref, bf16[24,128,2048]{2,1,0:T(8,128)(2,1)} %bitcast.7, bf16[22,32,2048]{2,1,0:T(8,128)(2,1)S(1)} %get-tuple-element.37.rest_0_), custom_call_target="tpu_custom_call" | custom-call | tf_op jit(solution)/shard_map/pallas_call | solution.py:115
  11.4 2.9 %shard_map.52 = (bf16[8,32,2048]{2,1,0:T(8,128)(2,1)S(1)}, bf16[8,32,2048]{2,1,0:T(8,128)(2,1)S(1)}, bf16[6,32,2048]{2,1,0:T(8,128)(2,1)S(1)}) custom-call(s32[32]{0:T(128)S(1)} %get-tuple-element.36.table_ref, bf16[24,128,2048]{2,1,0:T(8,128)(2,1)} %bitcast.8, bf16[22,32,2048]{2,1,0:T(8,128)(2,1)S(1)} %collective-permute-done.2.got_ref, ...), custom_call_target="tpu_custom_call" | custom-call | tf_op jit(solution)/shard_map/pallas_call | solution.py:175
  14.3 2.6 %collective-permute-start.4 = (bf16[8,32,2048]{2,1,0:T(8,128)(2,1)S(1)}, bf16[8,32,2048]{2,1,0:T(8,128)(2,1)S(1)}, u32[]{:S(2)}, u32[]{:S(2)}) collective-permute-start(bf16[8,32,2048]{2,1,0:T(8,128)(2,1)S(1)} %get-tuple-element.40.rest_0_), channel_id=1, source_target_pairs={{0,8},{2,10},{4,12},{6,14},{8,0},{10,2},{12,4},{14,6},{16,24},{18,... | collective-permute-start | bytes 3145736 | tf_op jit(solution)/shard_map/ppermute | solution.py:437
  16.9 1.8 collective-permute-start.3
  18.7 2.2 %shard_map.53 = (bf16[4,96,2048]{2,1,0:T(8,128)(2,1)S(1)}, bf16[2,96,2048]{2,1,0:T(8,128)(2,1)S(1)}) custom-call(s32[32]{0:T(128)S(1)} %get-tuple-element.36.table_ref, bf16[24,128,2048]{2,1,0:T(8,128)(2,1)} %bitcast.9, bf16[6,96,2048]{2,1,0:T(8,128)(2,1)S(1)} %collective-permute-done.1.got_ref, bf16[8,32,2048]{2,1,0:T(8,128)(2,1)S(1)} %get-tuple-element.40.rest_0_), custom_call_target="tpu_custom_call" | custom-call | tf_op jit(solution)/shard_map/pallas_call | solution.py:175
  20.9 1.8 collective-permute-start.5
  22.8 14.5 %collective-permute-done.3.refs_1_ = bf16[6,32,2048]{2,1,0:T(8,128)(2,1)S(1)} collective-permute-done((bf16[6,32,2048]{2,1,0:T(8,128)(2,1)S(1)}, bf16[6,32,2048]{2,1,0:T(8,128)(2,1)S(1)}, u32[]{:S(2)}, u32[]{:S(2)}) %collective-permute-start.3) | collective-permute-done | bytes 786464 | tf_op jit(solution)/shard_map/ppermute | solution.py:437
  37.3 3.0 %collective-permute-done.4.refs_3_ = bf16[8,32,2048]{2,1,0:T(8,128)(2,1)S(1)} collective-permute-done((bf16[8,32,2048]{2,1,0:T(8,128)(2,1)S(1)}, bf16[8,32,2048]{2,1,0:T(8,128)(2,1)S(1)}, u32[]{:S(2)}, u32[]{:S(2)}) %collective-permute-start.4) | collective-permute-done | bytes 1048608 | tf_op jit(solution)/shard_map/ppermute | solution.py:437
  40.6 1.8 collective-permute-start.6
  42.4 2.6 %collective-permute-start.7 = (bf16[4,32,2048]{2,1,0:T(8,128)(2,1)S(1)}, bf16[4,32,2048]{2,1,0:T(8,128)(2,1)S(1)}, u32[]{:S(2)}, u32[]{:S(2)}) collective-permute-start(bf16[4,32,2048]{2,1,0:T(8,128)(2,1)S(1)} %get-tuple-element.48), channel_id=1, source_target_pairs={{0,16},{2,18},{4,20},{6,22},{8,24},{10,26},{12,28},{14,30},{16,0},... | collective-permute-start | bytes 1572872 | tf_op jit(solution)/shard_map/ppermute | solution.py:437
  45.0 2.7 %shard_map.55 = (bf16[2,96,2048]{2,1,0:T(8,128)(2,1)S(1)}, bf16[6,96,2048]{2,1,0:T(8,128)(2,1)S(1)}) custom-call(s32[32]{0:T(128)S(1)} %get-tuple-element.36.table_ref, bf16[24,128,2048]{2,1,0:T(8,128)(2,1)} %bitcast.10, bf16[8,96,2048]{2,1,0:T(8,128)(2,1)S(1)} %collective-permute-done.got_ref, bf16[2,96,2048]{2,1,0:T(8,128)(2,1)S(1)} %get-tuple-element.45.rest_0_), custom_call_target="tpu_custom_call" | custom-call | tf_op jit(solution)/shard_map/pallas_call | solution.py:175
  47.7 22.2 %collective-permute-done.7.refs_4_ = bf16[4,32,2048]{2,1,0:T(8,128)(2,1)S(1)} collective-permute-done((bf16[4,32,2048]{2,1,0:T(8,128)(2,1)S(1)}, bf16[4,32,2048]{2,1,0:T(8,128)(2,1)S(1)}, u32[]{:S(2)}, u32[]{:S(2)}) %collective-permute-start.7) | collective-permute-done | bytes 524320 | tf_op jit(solution)/shard_map/ppermute | solution.py:437
  71.2 2.8 %collective-permute-start.10 = (bf16[2,96,2048]{2,1,0:T(8,128)(2,1)S(1)}, bf16[2,96,2048]{2,1,0:T(8,128)(2,1)S(1)}, u32[]{:S(2)}, u32[]{:S(2)}) collective-permute-start(bf16[2,96,2048]{2,1,0:T(8,128)(2,1)S(1)} %get-tuple-element.52), channel_id=1, source_target_pairs={{0,8},{2,10},{4,12},{6,14},{8,0},{10,2},{12,4},{14,6},{16,24},{18,... | collective-permute-start | bytes 2359304 | tf_op jit(solution)/shard_map/ppermute | solution.py:437
  77.3 19.8 %collective-permute-done.11.rest_5_ = bf16[2,32,2048]{2,1,0:T(8,128)(2,1)S(1)} collective-permute-done((bf16[2,32,2048]{2,1,0:T(8,128)(2,1)S(1)}, bf16[2,32,2048]{2,1,0:T(8,128)(2,1)S(1)}, u32[]{:S(2)}, u32[]{:S(2)}) %collective-permute-start.11) | collective-permute-done | bytes 262176 | tf_op jit(solution)/shard_map/ppermute | solution.py:437
  97.2 7.6 %collective-permute-done.10.rest_3_ = bf16[2,96,2048]{2,1,0:T(8,128)(2,1)S(1)} collective-permute-done((bf16[2,96,2048]{2,1,0:T(8,128)(2,1)S(1)}, bf16[2,96,2048]{2,1,0:T(8,128)(2,1)S(1)}, u32[]{:S(2)}, u32[]{:S(2)}) %collective-permute-start.10) | collective-permute-done | bytes 786464 | tf_op jit(solution)/shard_map/ppermute | solution.py:437
  104.8 5.3 %collective-permute-done.9.rest_2_ = bf16[2,96,2048]{2,1,0:T(8,128)(2,1)S(1)} collective-permute-done((bf16[2,96,2048]{2,1,0:T(8,128)(2,1)S(1)}, bf16[2,96,2048]{2,1,0:T(8,128)(2,1)S(1)}, u32[]{:S(2)}, u32[]{:S(2)}) %collective-permute-start.9) | collective-permute-done | bytes 786464 | tf_op jit(solution)/shard_map/ppermute | solution.py:437
  112.8 3.4 %collective-permute-done.12.refs_1_ = f32[2,128,128]{2,1,0:T(8,128)S(1)} collective-permute-done((f32[2,128,128]{2,1,0:T(8,128)S(1)}, f32[2,128,128]{2,1,0:T(8,128)S(1)}, u32[]{:S(2)}, u32[]{:S(2)}) %collective-permute-start.12) | collective-permute-done | bytes 131104 | tf_op jit(solution)/shard_map/ppermute | solution.py:646
  116.3 4.5 %shard_map.58 = (bf16[2,96,2048]{2,1,0:T(8,128)(2,1)S(1)}, bf16[2,32,2048]{2,1,0:T(8,128)(2,1)S(1)}) custom-call(f32[2,128,128]{2,1,0:T(8,128)S(1)} %get-tuple-element.55.refs_0_, f32[2,128,128]{2,1,0:T(8,128)S(1)} %collective-permute-done.12.refs_1_, bf16[2,128,2048]{2,1,0:T(8,128)(2,1)S(1)} %get-tuple-element.56.refs_2_), custom_call_target="tpu_custom_call" | custom-call | tf_op jit(solution)/shard_map/pallas_call | solution.py:423
  120.8 2.6 %collective-permute-start.15 = (bf16[2,96,2048]{2,1,0:T(8,128)(2,1)S(1)}, bf16[2,96,2048]{2,1,0:T(8,128)(2,1)S(1)}, u32[]{:S(2)}, u32[]{:S(2)}) collective-permute-start(bf16[2,96,2048]{2,1,0:T(8,128)(2,1)S(1)} %get-tuple-element.57.rest_6_.refs_4_), channel_id=1, source_target_pairs={{0,8},{2,10},{4,12},{6,14},{8,0},{10,2},{12,4},{14,6},{16,24},{18,... | collective-permute-start | bytes 2359304 | tf_op jit(solution)/shard_map/ppermute | solution.py:437
  125.5 2.3 %shard_map.59 = (f32[2,128,2048]{2,1,0:T(8,128)}, f32[8,128]{1,0:T(8,128)S(1)}) custom-call(s32[32]{0:T(128)S(1)} %get-tuple-element.36.table_ref, f32[2,128,2048]{2,1,0:T(8,128)S(1)} %bitcast.5, bf16[6,96,2048]{2,1,0:T(8,128)(2,1)S(1)} %get-tuple-element.46.refs_0_.rest_0_, bf16[2,96,2048]{2,1,0:T(8,128)(2,1)S(1)} %collective-permute-done.8.rest_1_, ...), custom_call_target="tpu_custom_call" | custom-call | tf_op jit(solution)/shard_map/pallas_call | solution.py:348
  127.7 14.5 %collective-permute-done.16.refs_3_ = bf16[2,32,2048]{2,1,0:T(8,128)(2,1)S(1)} collective-permute-done((bf16[2,32,2048]{2,1,0:T(8,128)(2,1)S(1)}, bf16[2,32,2048]{2,1,0:T(8,128)(2,1)S(1)}, u32[]{:S(2)}, u32[]{:S(2)}) %collective-permute-start.16) | collective-permute-done | bytes 262176 | tf_op jit(solution)/shard_map/ppermute | solution.py:437
  142.3 9.0 %collective-permute-done.13.refs_0_ = bf16[2,96,2048]{2,1,0:T(8,128)(2,1)S(1)} collective-permute-done((bf16[2,96,2048]{2,1,0:T(8,128)(2,1)S(1)}, bf16[2,96,2048]{2,1,0:T(8,128)(2,1)S(1)}, u32[]{:S(2)}, u32[]{:S(2)}) %collective-permute-start.13) | collective-permute-done | bytes 786464 | tf_op jit(solution)/shard_map/ppermute | solution.py:437
  153.0 1.8 collective-permute-start.14
  154.8 2.4 %collective-permute-start.18 = (bf16[4,32,2048]{2,1,0:T(8,128)(2,1)S(1)}, bf16[4,32,2048]{2,1,0:T(8,128)(2,1)S(1)}, u32[]{:S(2)}, u32[]{:S(2)}) collective-permute-start(bf16[4,32,2048]{2,1,0:T(8,128)(2,1)S(1)} %get-tuple-element.60.refs_1_), channel_id=1, source_target_pairs={{0,16},{2,18},{4,20},{6,22},{8,24},{10,26},{12,28},{14,30},{16,0},... | collective-permute-start | bytes 1572872 | tf_op jit(solution)/shard_map/ppermute | solution.py:437
  157.3 2.7 %shard_map.61 = (bf16[24,128,2048]{2,1,0:T(8,128)(2,1)}, f32[8,128]{1,0:T(8,128)S(1)}) custom-call(s32[32]{0:T(128)S(1)} %get-tuple-element.36.table_ref, bf16[4,96,2048]{2,1,0:T(8,128)(2,1)S(1)} %get-tuple-element.61.refs_0_, bf16[4,96,2048]{2,1,0:T(8,128)(2,1)S(1)} %collective-permute-done.19.refs_1_, ...), custom_call_target="tpu_custom_call" | custom-call | tf_op jit(solution)/shard_map/pallas_call | solution.py:275
  160.0 22.7 %collective-permute-done.18.refs_2_ = bf16[4,32,2048]{2,1,0:T(8,128)(2,1)S(1)} collective-permute-done((bf16[4,32,2048]{2,1,0:T(8,128)(2,1)S(1)}, bf16[4,32,2048]{2,1,0:T(8,128)(2,1)S(1)}, u32[]{:S(2)}, u32[]{:S(2)}) %collective-permute-start.18) | collective-permute-done | bytes 524320 | tf_op jit(solution)/shard_map/ppermute | solution.py:437
  183.7 2.5 %collective-permute-start.24 = (bf16[8,32,2048]{2,1,0:T(8,128)(2,1)S(1)}, bf16[8,32,2048]{2,1,0:T(8,128)(2,1)S(1)}, u32[]{:S(2)}, u32[]{:S(2)}) collective-permute-start(bf16[8,32,2048]{2,1,0:T(8,128)(2,1)S(1)} %get-tuple-element.65.refs_3_), channel_id=1, source_target_pairs={{0,8},{2,10},{4,12},{6,14},{8,0},{10,2},{12,4},{14,6},{16,24},{18,... | collective-permute-start | bytes 3145736 | tf_op jit(solution)/shard_map/ppermute | solution.py:437
  186.2 2.3 %collective-permute-done.26.refs_0_ = bf16[4,96,2048]{2,1,0:T(8,128)(2,1)S(1)} collective-permute-done((bf16[4,96,2048]{2,1,0:T(8,128)(2,1)S(1)}, bf16[4,96,2048]{2,1,0:T(8,128)(2,1)S(1)}, u32[]{:S(2)}, u32[]{:S(2)}) %collective-permute-start.26) | collective-permute-done | bytes 1572896 | tf_op jit(solution)/shard_map/ppermute | solution.py:437
  189.6 18.8 %collective-permute-done.24.refs_3_ = bf16[8,32,2048]{2,1,0:T(8,128)(2,1)S(1)} collective-permute-done((bf16[8,32,2048]{2,1,0:T(8,128)(2,1)S(1)}, bf16[8,32,2048]{2,1,0:T(8,128)(2,1)S(1)}, u32[]{:S(2)}, u32[]{:S(2)}) %collective-permute-start.24) | collective-permute-done | bytes 1048608 | tf_op jit(solution)/shard_map/ppermute | solution.py:437
  209.0 3.6 %shard_map.63 = (bf16[24,128,2048]{2,1,0:T(8,128)(2,1)}, f32[8,128]{1,0:T(8,128)}) custom-call(s32[32]{0:T(128)S(1)} %get-tuple-element.36.table_ref, bf16[4,96,2048]{2,1,0:T(8,128)(2,1)S(1)} %collective-permute-done.26.refs_0_, bf16[4,96,2048]{2,1,0:T(8,128)(2,1)S(1)} %collective-permute-done.27.refs_1_, ...), custom_call_target="tpu_custom_call", output_to_operand_aliasing={{0}: (6, {})} | custom-call | tf_op jit(solution)/shard_map/pallas_call | solution.py:275
  213.4 3.2 %shard_map.64 = (bf16[24,128,2048]{2,1,0:T(8,128)(2,1)}, f32[8,128]{1,0:T(8,128)}) custom-call(s32[32]{0:T(128)S(1)} %get-tuple-element.36.table_ref, bf16[2,96,2048]{2,1,0:T(8,128)(2,1)S(1)} %collective-permute-done.21.refs_0_, bf16[2,96,2048]{2,1,0:T(8,128)(2,1)S(1)} %collective-permute-done.22.refs_1_, ...), custom_call_target="tpu_custom_call", output_to_operand_aliasing={{0}: (6, {})} | custom-call | tf_op jit(solution)/shard_map/pallas_call | solution.py:275
  (45 shorter events, 16.8 us)
Async XLA Ops:
  0.6 0.7 copy-start.1
  5.1 6.3 %collective-permute-start.2 = (bf16[22,32,2048]{2,1,0:T(8,128)(2,1)S(1)}, bf16[22,32,2048]{2,1,0:T(8,128)(2,1)S(1)}, u32[]{:S(2)}, u32[]{:S(2)}) collective-permute-start(bf16[22,32,2048]{2,1,0:T(8,128)(2,1)S(1)} %get-tuple-element.37.rest_0_), channel_id=1, source_target_pairs={{0,2},{2,0},{4,6},{6,4},{8,10},{10,8},{12,14},{14,12},{16,18},{18,... | collective-permute-start | bytes 8650760 | tf_op jit(solution)/shard_map/ppermute | solution.py:437
  10.7 8.0 %collective-permute-start.1 = (bf16[6,96,2048]{2,1,0:T(8,128)(2,1)S(1)}, bf16[6,96,2048]{2,1,0:T(8,128)(2,1)S(1)}, u32[]{:S(2)}, u32[]{:S(2)}) collective-permute-start(bf16[6,96,2048]{2,1,0:T(8,128)(2,1)S(1)} %get-tuple-element.39.rest_0_), channel_id=1, source_target_pairs={{0,2},{2,0},{4,6},{6,4},{8,10},{10,8},{12,14},{14,12},{16,18},{18,... | collective-permute-start | bytes 7077896 | tf_op jit(solution)/shard_map/ppermute | solution.py:437
  11.3 33.7 %collective-permute-start = (bf16[8,96,2048]{2,1,0:T(8,128)(2,1)}, bf16[8,96,2048]{2,1,0:T(8,128)(2,1)S(1)}, u32[]{:S(2)}, u32[]{:S(2)}) collective-permute-start(bf16[8,96,2048]{2,1,0:T(8,128)(2,1)} %get-tuple-element.38), channel_id=1, source_target_pairs={{0,2},{2,0},{4,6},{6,4},{8,10},{10,8},{12,14},{14,12},{16,18},{18,... | collective-permute-start | bytes 9437192 | tf_op jit(solution)/shard_map/ppermute | solution.py:437
  14.3 26.1 %collective-permute-start.4 = (bf16[8,32,2048]{2,1,0:T(8,128)(2,1)S(1)}, bf16[8,32,2048]{2,1,0:T(8,128)(2,1)S(1)}, u32[]{:S(2)}, u32[]{:S(2)}) collective-permute-start(bf16[8,32,2048]{2,1,0:T(8,128)(2,1)S(1)} %get-tuple-element.40.rest_0_), channel_id=1, source_target_pairs={{0,8},{2,10},{4,12},{6,14},{8,0},{10,2},{12,4},{14,6},{16,24},{18,... | collective-permute-start | bytes 3145736 | tf_op jit(solution)/shard_map/ppermute | solution.py:437
  16.9 20.4 %collective-permute-start.3 = (bf16[6,32,2048]{2,1,0:T(8,128)(2,1)S(1)}, bf16[6,32,2048]{2,1,0:T(8,128)(2,1)S(1)}, u32[]{:S(2)}, u32[]{:S(2)}) collective-permute-start(bf16[6,32,2048]{2,1,0:T(8,128)(2,1)S(1)} %get-tuple-element.42), channel_id=1, source_target_pairs={{0,4},{2,6},{4,0},{6,2},{8,12},{10,14},{12,8},{14,10},{16,20},{18,... | collective-permute-start | bytes 2359304 | tf_op jit(solution)/shard_map/ppermute | solution.py:437
  20.9 49.0 %collective-permute-start.5 = (bf16[4,96,2048]{2,1,0:T(8,128)(2,1)S(1)}, bf16[4,96,2048]{2,1,0:T(8,128)(2,1)S(1)}, u32[]{:S(2)}, u32[]{:S(2)}) collective-permute-start(bf16[4,96,2048]{2,1,0:T(8,128)(2,1)S(1)} %get-tuple-element.44.refs_4_), channel_id=1, source_target_pairs={{0,4},{2,6},{4,0},{6,2},{8,12},{10,14},{12,8},{14,10},{16,20},{18,... | collective-permute-start | bytes 4718600 | tf_op jit(solution)/shard_map/ppermute | solution.py:437
  40.6 30.4 %collective-permute-start.6 = (bf16[2,96,2048]{2,1,0:T(8,128)(2,1)S(1)}, bf16[2,96,2048]{2,1,0:T(8,128)(2,1)S(1)}, u32[]{:S(2)}, u32[]{:S(2)}) collective-permute-start(bf16[2,96,2048]{2,1,0:T(8,128)(2,1)S(1)} %get-tuple-element.45.rest_0_), channel_id=1, source_target_pairs={{0,8},{2,10},{4,12},{6,14},{8,0},{10,2},{12,4},{14,6},{16,24},{18,... | collective-permute-start | bytes 2359304 | tf_op jit(solution)/shard_map/ppermute | solution.py:437
  42.4 27.5 %collective-permute-start.7 = (bf16[4,32,2048]{2,1,0:T(8,128)(2,1)S(1)}, bf16[4,32,2048]{2,1,0:T(8,128)(2,1)S(1)}, u32[]{:S(2)}, u32[]{:S(2)}) collective-permute-start(bf16[4,32,2048]{2,1,0:T(8,128)(2,1)S(1)} %get-tuple-element.48), channel_id=1, source_target_pairs={{0,16},{2,18},{4,20},{6,22},{8,24},{10,26},{12,28},{14,30},{16,0},... | collective-permute-start | bytes 1572872 | tf_op jit(solution)/shard_map/ppermute | solution.py:437
  70.9 39.2 %copy-start = (f32[1,2,128,2048]{3,2,1,0:T(8,128)S(1)}, f32[1,2,128,2048]{3,2,1,0:T(8,128)}, u32[]{:S(2)}) copy-start(f32[1,2,128,2048]{3,2,1,0:T(8,128)} %param.5) | copy-start | bytes 6291460
  71.2 33.6 %collective-permute-start.10 = (bf16[2,96,2048]{2,1,0:T(8,128)(2,1)S(1)}, bf16[2,96,2048]{2,1,0:T(8,128)(2,1)S(1)}, u32[]{:S(2)}, u32[]{:S(2)}) collective-permute-start(bf16[2,96,2048]{2,1,0:T(8,128)(2,1)S(1)} %get-tuple-element.52), channel_id=1, source_target_pairs={{0,8},{2,10},{4,12},{6,14},{8,0},{10,2},{12,4},{14,6},{16,24},{18,... | collective-permute-start | bytes 2359304 | tf_op jit(solution)/shard_map/ppermute | solution.py:437
  74.0 30.8 %collective-permute-start.8 = (bf16[2,96,2048]{2,1,0:T(8,128)(2,1)S(1)}, bf16[2,96,2048]{2,1,0:T(8,128)(2,1)S(1)}, u32[]{:S(2)}, u32[]{:S(2)}) collective-permute-start(bf16[2,96,2048]{2,1,0:T(8,128)(2,1)S(1)} %get-tuple-element.50), channel_id=1, source_target_pairs={{0,4},{2,6},{4,0},{6,2},{8,12},{10,14},{12,8},{14,10},{16,20},{18,... | collective-permute-start | bytes 2359304 | tf_op jit(solution)/shard_map/ppermute | solution.py:437
  75.1 35.1 %collective-permute-start.9 = (bf16[2,96,2048]{2,1,0:T(8,128)(2,1)S(1)}, bf16[2,96,2048]{2,1,0:T(8,128)(2,1)S(1)}, u32[]{:S(2)}, u32[]{:S(2)}) collective-permute-start(bf16[2,96,2048]{2,1,0:T(8,128)(2,1)S(1)} %get-tuple-element.51), channel_id=1, source_target_pairs={{0,16},{2,18},{4,20},{6,22},{8,24},{10,26},{12,28},{14,30},{16,0},... | collective-permute-start | bytes 2359304 | tf_op jit(solution)/shard_map/ppermute | solution.py:437
  76.8 20.4 %collective-permute-start.11 = (bf16[2,32,2048]{2,1,0:T(8,128)(2,1)S(1)}, bf16[2,32,2048]{2,1,0:T(8,128)(2,1)S(1)}, u32[]{:S(2)}, u32[]{:S(2)}) collective-permute-start(bf16[2,32,2048]{2,1,0:T(8,128)(2,1)S(1)} %get-tuple-element.54), channel_id=1, source_target_pairs={{0,4},{2,6},{4,0},{6,2},{8,12},{10,14},{12,8},{14,10},{16,20},{18,... | collective-permute-start | bytes 786440 | tf_op jit(solution)/shard_map/ppermute | solution.py:437
  111.2 5.0 %collective-permute-start.12 = (f32[2,128,128]{2,1,0:T(8,128)S(1)}, f32[2,128,128]{2,1,0:T(8,128)S(1)}, u32[]{:S(2)}, u32[]{:S(2)}) collective-permute-start(f32[2,128,128]{2,1,0:T(8,128)S(1)} %get-tuple-element.55.refs_0_), channel_id=1, source_target_pairs={{0,1},{1,0},{2,3},{3,2},{4,5},{5,4},{6,7},{7,6},{8,9},{9,8},{10,11... | collective-permute-start | bytes 393224 | tf_op jit(solution)/shard_map/ppermute | solution.py:646
  120.7 30.5 %collective-permute-start.13 = (bf16[2,96,2048]{2,1,0:T(8,128)(2,1)S(1)}, bf16[2,96,2048]{2,1,0:T(8,128)(2,1)S(1)}, u32[]{:S(2)}, u32[]{:S(2)}) collective-permute-start(bf16[2,96,2048]{2,1,0:T(8,128)(2,1)S(1)} %get-tuple-element.57.rest_6_.refs_4_), channel_id=1, source_target_pairs={{0,16},{2,18},{4,20},{6,22},{8,24},{10,26},{12,28},{14,30},{16,0},... | collective-permute-start | bytes 2359304 | tf_op jit(solution)/shard_map/ppermute | solution.py:437
  120.8 30.6 %collective-permute-start.15 = (bf16[2,96,2048]{2,1,0:T(8,128)(2,1)S(1)}, bf16[2,96,2048]{2,1,0:T(8,128)(2,1)S(1)}, u32[]{:S(2)}, u32[]{:S(2)}) collective-permute-start(bf16[2,96,2048]{2,1,0:T(8,128)(2,1)S(1)} %get-tuple-element.57.rest_6_.refs_4_), channel_id=1, source_target_pairs={{0,8},{2,10},{4,12},{6,14},{8,0},{10,2},{12,4},{14,6},{16,24},{18,... | collective-permute-start | bytes 2359304 | tf_op jit(solution)/shard_map/ppermute | solution.py:437
  123.4 27.9 %collective-permute-start.17 = (bf16[2,96,2048]{2,1,0:T(8,128)(2,1)S(1)}, bf16[2,96,2048]{2,1,0:T(8,128)(2,1)S(1)}, u32[]{:S(2)}, u32[]{:S(2)}) collective-permute-start(bf16[2,96,2048]{2,1,0:T(8,128)(2,1)S(1)} %get-tuple-element.57.rest_6_.refs_4_), channel_id=1, source_target_pairs={{0,4},{2,6},{4,0},{6,2},{8,12},{10,14},{12,8},{14,10},{16,20},{18,... | collective-permute-start | bytes 2359304 | tf_op jit(solution)/shard_map/ppermute | solution.py:437
  123.8 18.5 %collective-permute-start.16 = (bf16[2,32,2048]{2,1,0:T(8,128)(2,1)S(1)}, bf16[2,32,2048]{2,1,0:T(8,128)(2,1)S(1)}, u32[]{:S(2)}, u32[]{:S(2)}) collective-permute-start(bf16[2,32,2048]{2,1,0:T(8,128)(2,1)S(1)} %get-tuple-element.58.refs_2_), channel_id=1, source_target_pairs={{0,4},{2,6},{4,0},{6,2},{8,12},{10,14},{12,8},{14,10},{16,20},{18,... | collective-permute-start | bytes 786440 | tf_op jit(solution)/shard_map/ppermute | solution.py:437
  151.6 5.6 %collective-permute-start.19 = (bf16[4,96,2048]{2,1,0:T(8,128)(2,1)S(1)}, bf16[4,96,2048]{2,1,0:T(8,128)(2,1)S(1)}, u32[]{:S(2)}, u32[]{:S(2)}) collective-permute-start(bf16[4,96,2048]{2,1,0:T(8,128)(2,1)S(1)} %get-tuple-element.61.refs_0_), channel_id=1, source_target_pairs={{0,2},{2,0},{4,6},{6,4},{8,10},{10,8},{12,14},{14,12},{16,18},{18,... | collective-permute-start | bytes 4718600 | tf_op jit(solution)/shard_map/ppermute | solution.py:437
  151.7 5.6 %collective-permute-start.20 = (bf16[4,96,2048]{2,1,0:T(8,128)(2,1)S(1)}, bf16[4,96,2048]{2,1,0:T(8,128)(2,1)S(1)}, u32[]{:S(2)}, u32[]{:S(2)}) collective-permute-start(bf16[4,96,2048]{2,1,0:T(8,128)(2,1)S(1)} %get-tuple-element.62.refs_2_.refs_4_), channel_id=1, source_target_pairs={{0,2},{2,0},{4,6},{6,4},{8,10},{10,8},{12,14},{14,12},{16,18},{18,... | collective-permute-start | bytes 4718600 | tf_op jit(solution)/shard_map/ppermute | solution.py:437
  152.2 36.4 %collective-permute-start.26 = (bf16[4,96,2048]{2,1,0:T(8,128)(2,1)S(1)}, bf16[4,96,2048]{2,1,0:T(8,128)(2,1)S(1)}, u32[]{:S(2)}, u32[]{:S(2)}) collective-permute-start(bf16[4,96,2048]{2,1,0:T(8,128)(2,1)S(1)} %get-tuple-element.62.refs_2_.refs_4_), channel_id=1, source_target_pairs={{0,4},{2,6},{4,0},{6,2},{8,12},{10,14},{12,8},{14,10},{16,20},{18,... | collective-permute-start | bytes 4718600 | tf_op jit(solution)/shard_map/ppermute | solution.py:437
  153.0 30.5 %collective-permute-start.14 = (bf16[2,96,2048]{2,1,0:T(8,128)(2,1)S(1)}, bf16[2,96,2048]{2,1,0:T(8,128)(2,1)S(1)}, u32[]{:S(2)}, u32[]{:S(2)}) collective-permute-start(bf16[2,96,2048]{2,1,0:T(8,128)(2,1)S(1)} %collective-permute-done.13.refs_0_), channel_id=1, source_target_pairs={{0,8},{2,10},{4,12},{6,14},{8,0},{10,2},{12,4},{14,6},{16,24},{18,... | collective-permute-start | bytes 2359304 | tf_op jit(solution)/shard_map/ppermute | solution.py:437
  154.8 28.0 %collective-permute-start.18 = (bf16[4,32,2048]{2,1,0:T(8,128)(2,1)S(1)}, bf16[4,32,2048]{2,1,0:T(8,128)(2,1)S(1)}, u32[]{:S(2)}, u32[]{:S(2)}) collective-permute-start(bf16[4,32,2048]{2,1,0:T(8,128)(2,1)S(1)} %get-tuple-element.60.refs_1_), channel_id=1, source_target_pairs={{0,16},{2,18},{4,20},{6,22},{8,24},{10,26},{12,28},{14,30},{16,0},... | collective-permute-start | bytes 1572872 | tf_op jit(solution)/shard_map/ppermute | solution.py:437
  183.7 24.8 %collective-permute-start.24 = (bf16[8,32,2048]{2,1,0:T(8,128)(2,1)S(1)}, bf16[8,32,2048]{2,1,0:T(8,128)(2,1)S(1)}, u32[]{:S(2)}, u32[]{:S(2)}) collective-permute-start(bf16[8,32,2048]{2,1,0:T(8,128)(2,1)S(1)} %get-tuple-element.65.refs_3_), channel_id=1, source_target_pairs={{0,8},{2,10},{4,12},{6,14},{8,0},{10,2},{12,4},{14,6},{16,24},{18,... | collective-permute-start | bytes 3145736 | tf_op jit(solution)/shard_map/ppermute | solution.py:437
  188.5 20.4 %collective-permute-start.27 = (bf16[4,96,2048]{2,1,0:T(8,128)(2,1)S(1)}, bf16[4,96,2048]{2,1,0:T(8,128)(2,1)S(1)}, u32[]{:S(2)}, u32[]{:S(2)}) collective-permute-start(bf16[4,96,2048]{2,1,0:T(8,128)(2,1)S(1)} %collective-permute-done.26.refs_0_), channel_id=1, source_target_pairs={{0,2},{2,0},{4,6},{6,4},{8,10},{10,8},{12,14},{14,12},{16,18},{18,... | collective-permute-start | bytes 4718600 | tf_op jit(solution)/shard_map/ppermute | solution.py:437
  188.5 20.4 %collective-permute-start.22 = (bf16[2,96,2048]{2,1,0:T(8,128)(2,1)S(1)}, bf16[2,96,2048]{2,1,0:T(8,128)(2,1)S(1)}, u32[]{:S(2)}, u32[]{:S(2)}) collective-permute-start(bf16[2,96,2048]{2,1,0:T(8,128)(2,1)S(1)} %get-tuple-element.64.refs_2_.refs_6_), channel_id=1, source_target_pairs={{0,4},{2,6},{4,0},{6,2},{8,12},{10,14},{12,8},{14,10},{16,20},{18,... | collective-permute-start | bytes 2359304 | tf_op jit(solution)/shard_map/ppermute | solution.py:437
  189.4 19.6 %collective-permute-start.28 = (bf16[8,32,2048]{2,1,0:T(8,128)(2,1)S(1)}, bf16[8,32,2048]{2,1,0:T(8,128)(2,1)S(1)}, u32[]{:S(2)}, u32[]{:S(2)}) collective-permute-start(bf16[8,32,2048]{2,1,0:T(8,128)(2,1)S(1)} %get-tuple-element.65.refs_3_), channel_id=1, source_target_pairs={{0,2},{2,0},{4,6},{6,4},{8,10},{10,8},{12,14},{14,12},{16,18},{18,... | collective-permute-start | bytes 3145736 | tf_op jit(solution)/shard_map/ppermute | solution.py:437
  208.4 4.9 %collective-permute-start.25 = (bf16[8,32,2048]{2,1,0:T(8,128)(2,1)S(1)}, bf16[8,32,2048]{2,1,0:T(8,128)(2,1)S(1)}, u32[]{:S(2)}, u32[]{:S(2)}) collective-permute-start(bf16[8,32,2048]{2,1,0:T(8,128)(2,1)S(1)} %collective-permute-done.24.refs_3_), channel_id=1, source_target_pairs={{0,2},{2,0},{4,6},{6,4},{8,10},{10,8},{12,14},{14,12},{16,18},{18,... | collective-permute-start | bytes 3145736 | tf_op jit(solution)/shard_map/ppermute | solution.py:437
  208.4 4.2 %collective-permute-start.21 = (bf16[2,96,2048]{2,1,0:T(8,128)(2,1)S(1)}, bf16[2,96,2048]{2,1,0:T(8,128)(2,1)S(1)}, u32[]{:S(2)}, u32[]{:S(2)}) collective-permute-start(bf16[2,96,2048]{2,1,0:T(8,128)(2,1)S(1)} %get-tuple-element.64.refs_2_.refs_6_), channel_id=1, source_target_pairs={{0,2},{2,0},{4,6},{6,4},{8,10},{10,8},{12,14},{14,12},{16,18},{18,... | collective-permute-start | bytes 2359304 | tf_op jit(solution)/shard_map/ppermute | solution.py:437
  209.0 4.4 %collective-permute-start.23 = (bf16[2,96,2048]{2,1,0:T(8,128)(2,1)S(1)}, bf16[2,96,2048]{2,1,0:T(8,128)(2,1)S(1)}, u32[]{:S(2)}, u32[]{:S(2)}) collective-permute-start(bf16[2,96,2048]{2,1,0:T(8,128)(2,1)S(1)} %collective-permute-done.22.refs_1_), channel_id=1, source_target_pairs={{0,2},{2,0},{4,6},{6,4},{8,10},{10,8},{12,14},{14,12},{16,18},{18,... | collective-permute-start | bytes 2359304 | tf_op jit(solution)/shard_map/ppermute | solution.py:437

commit v8 on v7

--- a/solution.py
+++ b/solution.py
@@ -366,9 +366,15 @@
 
 
 def exact(a, b):
-    return jnp.dot(
-        a, b, preferred_element_type=jnp.float32, precision=lax.Precision.HIGHEST
-    )
+    def split(v):
+        high = v.astype(jnp.bfloat16)
+        return high, (v - high.astype(jnp.float32)).astype(jnp.bfloat16)
+
+    def dot(p, q):
+        return jnp.dot(p, q, preferred_element_type=jnp.float32)
+
+    (a_high, a_low), (b_high, b_low) = split(a), split(b)
+    return dot(a_high, b_high) + (dot(a_high, b_low) + dot(a_low, b_high))
 
 
 def orthogonalize_kernel(factor, slots, grams, *refs):
@@ -562,7 +568,9 @@
             over_x[0] = made.pop()
         else:
             after = take(k - 2, after)
-        pending = {o: swap(made[n], last[o]) for n, o in enumerate(level[k])}
+        pending = {
+            o: swap(made[n], last[o]) for n, o in reversed(list(enumerate(level[k])))
+        }
         kept = made[-1]
         other_got = swap(made[-2], other_bits[top - k + 1])
         x_got = swap(over_x[k - 1], X_BIT)

time: 217 us -> 218 us (level)
  starting transfers between devices: 34.3 us -> 37.3 us
    ppermute x28, starting transfers between devices: 32.7 us -> 36.2 us  [swap(): return lax.ppermute(value, 'dp', [(i, i ^ bit) for i in range(count)])]
  transfers between devices with their start and end apart: 29 -> 29, of which waited for: 18 -> 16; matrix products, arithmetic and copies ran while one was open for 0% -> 0% of each run, Pallas kernels for 10% -> 10%
where the time goes in v8:
time: 218 us
  waiting for transfers between devices  146 us (67%)
  starting transfers between devices  37.3 us (17%)
  Pallas kernels  33.7 us (15%)
    ppermute x28, waiting for transfers between devices, swap(): return lax.ppermute(value, 'dp', [(i, i ^ bit) for i in range(count)])  142 us
    ppermute x28, starting transfers between devices, swap(): return lax.ppermute(value, 'dp', [(i, i ^ bit) for i in range(count)])  36.2 us
    pallas_call x3, Pallas kernels, spread(): pl.pallas_call(functools.partial(spread_kernel, plans, slots), out_shape=...  9.6 us
    pallas_call x3, Pallas kernels, add_taken(): pl.pallas_call(functools.partial(add_taken_kernel, items, parts), out_sha...  7.79 us
    pallas_call x1, Pallas kernels, pack(): pl.pallas_call(functools.partial(pack_kernel, tuple(plans)), out_shape=[j...  4.87 us
  transfers between devices with their start and end apart: 29, of which 16 were waited for; matrix products, arithmetic and copies ran while one was open for 0% of the time, Pallas kernels for 10%

profile of v8, /device:TPU:0, one launch (start us, length us, event | category | flops | bytes accessed | tf_op | source)
XLA Modules:
  0.0 218.2 jit_solution(7277257249949462151)
XLA Ops:
  1.3 3.8 %shard_map.50 = (s32[32]{0:T(128)S(1)}, bf16[22,32,2048]{2,1,0:T(8,128)(2,1)S(1)}) custom-call(s32[1]{0:T(128)} %bitcast.me_ref, s32[24]{0:T(128)S(1)} %copy-done.1, bf16[24,128,2048]{2,1,0:T(8,128)(2,1)} %bitcast.6), custom_call_target="tpu_custom_call" | custom-call | tf_op jit(solution)/shard_map/pallas_call | solution.py:141
  5.8 4.9 %shard_map.51 = (bf16[6,96,2048]{2,1,0:T(8,128)(2,1)S(1)}, bf16[8,96,2048]{2,1,0:T(8,128)(2,1)}) custom-call(s32[32]{0:T(128)S(1)} %get-tuple-element.36.table_ref, bf16[24,128,2048]{2,1,0:T(8,128)(2,1)} %bitcast.7, bf16[22,32,2048]{2,1,0:T(8,128)(2,1)S(1)} %get-tuple-element.37.rest_0_), custom_call_target="tpu_custom_call" | custom-call | tf_op jit(solution)/shard_map/pallas_call | solution.py:115
  11.4 2.9 %shard_map.52 = (bf16[8,32,2048]{2,1,0:T(8,128)(2,1)S(1)}, bf16[8,32,2048]{2,1,0:T(8,128)(2,1)S(1)}, bf16[6,32,2048]{2,1,0:T(8,128)(2,1)S(1)}) custom-call(s32[32]{0:T(128)S(1)} %get-tuple-element.36.table_ref, bf16[24,128,2048]{2,1,0:T(8,128)(2,1)} %bitcast.8, bf16[22,32,2048]{2,1,0:T(8,128)(2,1)S(1)} %collective-permute-done.2.got_ref, ...), custom_call_target="tpu_custom_call" | custom-call | tf_op jit(solution)/shard_map/pallas_call | solution.py:175
  14.3 2.9 %collective-permute-start.4 = (bf16[8,32,2048]{2,1,0:T(8,128)(2,1)S(1)}, bf16[8,32,2048]{2,1,0:T(8,128)(2,1)S(1)}, u32[]{:S(2)}, u32[]{:S(2)}) collective-permute-start(bf16[8,32,2048]{2,1,0:T(8,128)(2,1)S(1)} %get-tuple-element.40.rest_0_), channel_id=1, source_target_pairs={{0,8},{2,10},{4,12},{6,14},{8,0},{10,2},{12,4},{14,6},{16,24},{18,... | collective-permute-start | bytes 3145736 | tf_op jit(solution)/shard_map/ppermute | solution.py:443
  17.1 1.6 collective-permute-start.3
  18.7 2.3 %shard_map.53 = (bf16[4,96,2048]{2,1,0:T(8,128)(2,1)S(1)}, bf16[2,96,2048]{2,1,0:T(8,128)(2,1)S(1)}) custom-call(s32[32]{0:T(128)S(1)} %get-tuple-element.36.table_ref, bf16[24,128,2048]{2,1,0:T(8,128)(2,1)} %bitcast.9, bf16[6,96,2048]{2,1,0:T(8,128)(2,1)S(1)} %collective-permute-done.1.got_ref, bf16[8,32,2048]{2,1,0:T(8,128)(2,1)S(1)} %get-tuple-element.40.rest_0_), custom_call_target="tpu_custom_call" | custom-call | tf_op jit(solution)/shard_map/pallas_call | solution.py:175
  21.1 2.1 collective-permute-start.5
  23.2 14.4 %collective-permute-done.3.refs_1_ = bf16[6,32,2048]{2,1,0:T(8,128)(2,1)S(1)} collective-permute-done((bf16[6,32,2048]{2,1,0:T(8,128)(2,1)S(1)}, bf16[6,32,2048]{2,1,0:T(8,128)(2,1)S(1)}, u32[]{:S(2)}, u32[]{:S(2)}) %collective-permute-start.3) | collective-permute-done | bytes 786464 | tf_op jit(solution)/shard_map/ppermute | solution.py:443
  37.6 3.1 %collective-permute-done.4.refs_3_ = bf16[8,32,2048]{2,1,0:T(8,128)(2,1)S(1)} collective-permute-done((bf16[8,32,2048]{2,1,0:T(8,128)(2,1)S(1)}, bf16[8,32,2048]{2,1,0:T(8,128)(2,1)S(1)}, u32[]{:S(2)}, u32[]{:S(2)}) %collective-permute-start.4) | collective-permute-done | bytes 1048608 | tf_op jit(solution)/shard_map/ppermute | solution.py:443
  40.8 1.8 collective-permute-start.6
  42.6 2.7 %collective-permute-start.7 = (bf16[4,32,2048]{2,1,0:T(8,128)(2,1)S(1)}, bf16[4,32,2048]{2,1,0:T(8,128)(2,1)S(1)}, u32[]{:S(2)}, u32[]{:S(2)}) collective-permute-start(bf16[4,32,2048]{2,1,0:T(8,128)(2,1)S(1)} %get-tuple-element.48), channel_id=1, source_target_pairs={{0,16},{2,18},{4,20},{6,22},{8,24},{10,26},{12,28},{14,30},{16,0},... | collective-permute-start | bytes 1572872 | tf_op jit(solution)/shard_map/ppermute | solution.py:443
  45.3 2.6 %shard_map.55 = (bf16[2,96,2048]{2,1,0:T(8,128)(2,1)S(1)}, bf16[6,96,2048]{2,1,0:T(8,128)(2,1)S(1)}) custom-call(s32[32]{0:T(128)S(1)} %get-tuple-element.36.table_ref, bf16[24,128,2048]{2,1,0:T(8,128)(2,1)} %bitcast.10, bf16[8,96,2048]{2,1,0:T(8,128)(2,1)S(1)} %collective-permute-done.got_ref, bf16[2,96,2048]{2,1,0:T(8,128)(2,1)S(1)} %get-tuple-element.45.rest_0_), custom_call_target="tpu_custom_call" | custom-call | tf_op jit(solution)/shard_map/pallas_call | solution.py:175
  47.9 22.3 %collective-permute-done.7.refs_4_ = bf16[4,32,2048]{2,1,0:T(8,128)(2,1)S(1)} collective-permute-done((bf16[4,32,2048]{2,1,0:T(8,128)(2,1)S(1)}, bf16[4,32,2048]{2,1,0:T(8,128)(2,1)S(1)}, u32[]{:S(2)}, u32[]{:S(2)}) %collective-permute-start.7) | collective-permute-done | bytes 524320 | tf_op jit(solution)/shard_map/ppermute | solution.py:443
  71.5 2.4 %collective-permute-start.10 = (bf16[2,96,2048]{2,1,0:T(8,128)(2,1)S(1)}, bf16[2,96,2048]{2,1,0:T(8,128)(2,1)S(1)}, u32[]{:S(2)}, u32[]{:S(2)}) collective-permute-start(bf16[2,96,2048]{2,1,0:T(8,128)(2,1)S(1)} %get-tuple-element.52), channel_id=1, source_target_pairs={{0,16},{2,18},{4,20},{6,22},{8,24},{10,26},{12,28},{14,30},{16,0},... | collective-permute-start | bytes 2359304 | tf_op jit(solution)/shard_map/ppermute | solution.py:443
  73.9 1.6 collective-permute-start.8
  75.5 1.6 collective-permute-start.9
  77.7 19.4 %collective-permute-done.11.rest_5_ = bf16[2,32,2048]{2,1,0:T(8,128)(2,1)S(1)} collective-permute-done((bf16[2,32,2048]{2,1,0:T(8,128)(2,1)S(1)}, bf16[2,32,2048]{2,1,0:T(8,128)(2,1)S(1)}, u32[]{:S(2)}, u32[]{:S(2)}) %collective-permute-start.11) | collective-permute-done | bytes 262176 | tf_op jit(solution)/shard_map/ppermute | solution.py:443
  97.2 10.5 %collective-permute-done.10.rest_3_ = bf16[2,96,2048]{2,1,0:T(8,128)(2,1)S(1)} collective-permute-done((bf16[2,96,2048]{2,1,0:T(8,128)(2,1)S(1)}, bf16[2,96,2048]{2,1,0:T(8,128)(2,1)S(1)}, u32[]{:S(2)}, u32[]{:S(2)}) %collective-permute-start.10) | collective-permute-done | bytes 786464 | tf_op jit(solution)/shard_map/ppermute | solution.py:443
  110.8 3.9 %collective-permute-done.12.refs_1_ = f32[2,128,128]{2,1,0:T(8,128)S(1)} collective-permute-done((f32[2,128,128]{2,1,0:T(8,128)S(1)}, f32[2,128,128]{2,1,0:T(8,128)S(1)}, u32[]{:S(2)}, u32[]{:S(2)}) %collective-permute-start.12) | collective-permute-done | bytes 131104 | tf_op jit(solution)/shard_map/ppermute | solution.py:654
  114.7 3.5 %shard_map.58 = (bf16[2,96,2048]{2,1,0:T(8,128)(2,1)S(1)}, bf16[2,32,2048]{2,1,0:T(8,128)(2,1)S(1)}) custom-call(f32[2,128,128]{2,1,0:T(8,128)S(1)} %get-tuple-element.55.refs_0_, f32[2,128,128]{2,1,0:T(8,128)S(1)} %collective-permute-done.12.refs_1_, bf16[2,128,2048]{2,1,0:T(8,128)(2,1)S(1)} %get-tuple-element.56.refs_2_), custom_call_target="tpu_custom_call" | custom-call | tf_op jit(solution)/shard_map/pallas_call | solution.py:429
  118.2 1.6 collective-permute-start.13
  119.8 2.5 %collective-permute-start.15 = (bf16[2,96,2048]{2,1,0:T(8,128)(2,1)S(1)}, bf16[2,96,2048]{2,1,0:T(8,128)(2,1)S(1)}, u32[]{:S(2)}, u32[]{:S(2)}) collective-permute-start(bf16[2,96,2048]{2,1,0:T(8,128)(2,1)S(1)} %get-tuple-element.57.rest_6_.refs_4_), channel_id=1, source_target_pairs={{0,8},{2,10},{4,12},{6,14},{8,0},{10,2},{12,4},{14,6},{16,24},{18,... | collective-permute-start | bytes 2359304 | tf_op jit(solution)/shard_map/ppermute | solution.py:443
  124.3 2.3 %shard_map.59 = (f32[2,128,2048]{2,1,0:T(8,128)}, f32[8,128]{1,0:T(8,128)S(1)}) custom-call(s32[32]{0:T(128)S(1)} %get-tuple-element.36.table_ref, f32[2,128,2048]{2,1,0:T(8,128)S(1)} %bitcast.5, bf16[6,96,2048]{2,1,0:T(8,128)(2,1)S(1)} %get-tuple-element.46.refs_0_.rest_0_, bf16[2,96,2048]{2,1,0:T(8,128)(2,1)S(1)} %collective-permute-done.8.rest_1_, ...), custom_call_target="tpu_custom_call" | custom-call | tf_op jit(solution)/shard_map/pallas_call | solution.py:348
  126.6 17.8 %collective-permute-done.16.refs_3_ = bf16[2,32,2048]{2,1,0:T(8,128)(2,1)S(1)} collective-permute-done((bf16[2,32,2048]{2,1,0:T(8,128)(2,1)S(1)}, bf16[2,32,2048]{2,1,0:T(8,128)(2,1)S(1)}, u32[]{:S(2)}, u32[]{:S(2)}) %collective-permute-start.16) | collective-permute-done | bytes 262176 | tf_op jit(solution)/shard_map/ppermute | solution.py:443
  144.4 7.7 %collective-permute-done.13.refs_0_ = bf16[2,96,2048]{2,1,0:T(8,128)(2,1)S(1)} collective-permute-done((bf16[2,96,2048]{2,1,0:T(8,128)(2,1)S(1)}, bf16[2,96,2048]{2,1,0:T(8,128)(2,1)S(1)}, u32[]{:S(2)}, u32[]{:S(2)}) %collective-permute-start.13) | collective-permute-done | bytes 786464 | tf_op jit(solution)/shard_map/ppermute | solution.py:443
  154.5 4.4 %collective-permute-start.18 = (bf16[4,32,2048]{2,1,0:T(8,128)(2,1)S(1)}, bf16[4,32,2048]{2,1,0:T(8,128)(2,1)S(1)}, u32[]{:S(2)}, u32[]{:S(2)}) collective-permute-start(bf16[4,32,2048]{2,1,0:T(8,128)(2,1)S(1)} %get-tuple-element.60.refs_1_), channel_id=1, source_target_pairs={{0,16},{2,18},{4,20},{6,22},{8,24},{10,26},{12,28},{14,30},{16,0},... | collective-permute-start | bytes 1572872 | tf_op jit(solution)/shard_map/ppermute | solution.py:443
  158.9 2.9 %shard_map.61 = (bf16[24,128,2048]{2,1,0:T(8,128)(2,1)}, f32[8,128]{1,0:T(8,128)S(1)}) custom-call(s32[32]{0:T(128)S(1)} %get-tuple-element.36.table_ref, bf16[4,96,2048]{2,1,0:T(8,128)(2,1)S(1)} %get-tuple-element.61.refs_0_, bf16[4,96,2048]{2,1,0:T(8,128)(2,1)S(1)} %collective-permute-done.19.refs_1_, ...), custom_call_target="tpu_custom_call" | custom-call | tf_op jit(solution)/shard_map/pallas_call | solution.py:275
  161.7 20.8 %collective-permute-done.18.refs_2_ = bf16[4,32,2048]{2,1,0:T(8,128)(2,1)S(1)} collective-permute-done((bf16[4,32,2048]{2,1,0:T(8,128)(2,1)S(1)}, bf16[4,32,2048]{2,1,0:T(8,128)(2,1)S(1)}, u32[]{:S(2)}, u32[]{:S(2)}) %collective-permute-start.18) | collective-permute-done | bytes 524320 | tf_op jit(solution)/shard_map/ppermute | solution.py:443
  183.9 3.9 %collective-permute-start.24 = (bf16[8,32,2048]{2,1,0:T(8,128)(2,1)S(1)}, bf16[8,32,2048]{2,1,0:T(8,128)(2,1)S(1)}, u32[]{:S(2)}, u32[]{:S(2)}) collective-permute-start(bf16[8,32,2048]{2,1,0:T(8,128)(2,1)S(1)} %get-tuple-element.65.refs_3_), channel_id=1, source_target_pairs={{0,8},{2,10},{4,12},{6,14},{8,0},{10,2},{12,4},{14,6},{16,24},{18,... | collective-permute-start | bytes 3145736 | tf_op jit(solution)/shard_map/ppermute | solution.py:443
  189.9 20.2 %collective-permute-done.24.refs_3_ = bf16[8,32,2048]{2,1,0:T(8,128)(2,1)S(1)} collective-permute-done((bf16[8,32,2048]{2,1,0:T(8,128)(2,1)S(1)}, bf16[8,32,2048]{2,1,0:T(8,128)(2,1)S(1)}, u32[]{:S(2)}, u32[]{:S(2)}) %collective-permute-start.24) | collective-permute-done | bytes 1048608 | tf_op jit(solution)/shard_map/ppermute | solution.py:443
  210.6 3.5 %shard_map.63 = (bf16[24,128,2048]{2,1,0:T(8,128)(2,1)}, f32[8,128]{1,0:T(8,128)}) custom-call(s32[32]{0:T(128)S(1)} %get-tuple-element.36.table_ref, bf16[4,96,2048]{2,1,0:T(8,128)(2,1)S(1)} %collective-permute-done.26.refs_0_, bf16[4,96,2048]{2,1,0:T(8,128)(2,1)S(1)} %collective-permute-done.27.refs_1_, ...), custom_call_target="tpu_custom_call", output_to_operand_aliasing={{0}: (6, {})} | custom-call | tf_op jit(solution)/shard_map/pallas_call | solution.py:275
  215.0 3.2 %shard_map.64 = (bf16[24,128,2048]{2,1,0:T(8,128)(2,1)}, f32[8,128]{1,0:T(8,128)}) custom-call(s32[32]{0:T(128)S(1)} %get-tuple-element.36.table_ref, bf16[2,96,2048]{2,1,0:T(8,128)(2,1)S(1)} %collective-permute-done.21.refs_0_, bf16[2,96,2048]{2,1,0:T(8,128)(2,1)S(1)} %collective-permute-done.22.refs_1_, ...), custom_call_target="tpu_custom_call", output_to_operand_aliasing={{0}: (6, {})} | custom-call | tf_op jit(solution)/shard_map/pallas_call | solution.py:275
  (45 shorter events, 16.6 us)
Async XLA Ops:
  0.6 0.7 copy-start.1
  5.1 6.3 %collective-permute-start.2 = (bf16[22,32,2048]{2,1,0:T(8,128)(2,1)S(1)}, bf16[22,32,2048]{2,1,0:T(8,128)(2,1)S(1)}, u32[]{:S(2)}, u32[]{:S(2)}) collective-permute-start(bf16[22,32,2048]{2,1,0:T(8,128)(2,1)S(1)} %get-tuple-element.37.rest_0_), channel_id=1, source_target_pairs={{0,2},{2,0},{4,6},{6,4},{8,10},{10,8},{12,14},{14,12},{16,18},{18,... | collective-permute-start | bytes 8650760 | tf_op jit(solution)/shard_map/ppermute | solution.py:443
  10.7 8.1 %collective-permute-start.1 = (bf16[6,96,2048]{2,1,0:T(8,128)(2,1)S(1)}, bf16[6,96,2048]{2,1,0:T(8,128)(2,1)S(1)}, u32[]{:S(2)}, u32[]{:S(2)}) collective-permute-start(bf16[6,96,2048]{2,1,0:T(8,128)(2,1)S(1)} %get-tuple-element.39.rest_0_), channel_id=1, source_target_pairs={{0,2},{2,0},{4,6},{6,4},{8,10},{10,8},{12,14},{14,12},{16,18},{18,... | collective-permute-start | bytes 7077896 | tf_op jit(solution)/shard_map/ppermute | solution.py:443
  11.3 34.0 %collective-permute-start = (bf16[8,96,2048]{2,1,0:T(8,128)(2,1)}, bf16[8,96,2048]{2,1,0:T(8,128)(2,1)S(1)}, u32[]{:S(2)}, u32[]{:S(2)}) collective-permute-start(bf16[8,96,2048]{2,1,0:T(8,128)(2,1)} %get-tuple-element.38), channel_id=1, source_target_pairs={{0,2},{2,0},{4,6},{6,4},{8,10},{10,8},{12,14},{14,12},{16,18},{18,... | collective-permute-start | bytes 9437192 | tf_op jit(solution)/shard_map/ppermute | solution.py:443
  14.3 26.4 %collective-permute-start.4 = (bf16[8,32,2048]{2,1,0:T(8,128)(2,1)S(1)}, bf16[8,32,2048]{2,1,0:T(8,128)(2,1)S(1)}, u32[]{:S(2)}, u32[]{:S(2)}) collective-permute-start(bf16[8,32,2048]{2,1,0:T(8,128)(2,1)S(1)} %get-tuple-element.40.rest_0_), channel_id=1, source_target_pairs={{0,8},{2,10},{4,12},{6,14},{8,0},{10,2},{12,4},{14,6},{16,24},{18,... | collective-permute-start | bytes 3145736 | tf_op jit(solution)/shard_map/ppermute | solution.py:443
  17.1 20.4 %collective-permute-start.3 = (bf16[6,32,2048]{2,1,0:T(8,128)(2,1)S(1)}, bf16[6,32,2048]{2,1,0:T(8,128)(2,1)S(1)}, u32[]{:S(2)}, u32[]{:S(2)}) collective-permute-start(bf16[6,32,2048]{2,1,0:T(8,128)(2,1)S(1)} %get-tuple-element.42), channel_id=1, source_target_pairs={{0,4},{2,6},{4,0},{6,2},{8,12},{10,14},{12,8},{14,10},{16,20},{18,... | collective-permute-start | bytes 2359304 | tf_op jit(solution)/shard_map/ppermute | solution.py:443
  21.1 49.1 %collective-permute-start.5 = (bf16[4,96,2048]{2,1,0:T(8,128)(2,1)S(1)}, bf16[4,96,2048]{2,1,0:T(8,128)(2,1)S(1)}, u32[]{:S(2)}, u32[]{:S(2)}) collective-permute-start(bf16[4,96,2048]{2,1,0:T(8,128)(2,1)S(1)} %get-tuple-element.44.refs_4_), channel_id=1, source_target_pairs={{0,4},{2,6},{4,0},{6,2},{8,12},{10,14},{12,8},{14,10},{16,20},{18,... | collective-permute-start | bytes 4718600 | tf_op jit(solution)/shard_map/ppermute | solution.py:443
  40.8 30.4 %collective-permute-start.6 = (bf16[2,96,2048]{2,1,0:T(8,128)(2,1)S(1)}, bf16[2,96,2048]{2,1,0:T(8,128)(2,1)S(1)}, u32[]{:S(2)}, u32[]{:S(2)}) collective-permute-start(bf16[2,96,2048]{2,1,0:T(8,128)(2,1)S(1)} %get-tuple-element.45.rest_0_), channel_id=1, source_target_pairs={{0,8},{2,10},{4,12},{6,14},{8,0},{10,2},{12,4},{14,6},{16,24},{18,... | collective-permute-start | bytes 2359304 | tf_op jit(solution)/shard_map/ppermute | solution.py:443
  42.6 27.5 %collective-permute-start.7 = (bf16[4,32,2048]{2,1,0:T(8,128)(2,1)S(1)}, bf16[4,32,2048]{2,1,0:T(8,128)(2,1)S(1)}, u32[]{:S(2)}, u32[]{:S(2)}) collective-permute-start(bf16[4,32,2048]{2,1,0:T(8,128)(2,1)S(1)} %get-tuple-element.48), channel_id=1, source_target_pairs={{0,16},{2,18},{4,20},{6,22},{8,24},{10,26},{12,28},{14,30},{16,0},... | collective-permute-start | bytes 1572872 | tf_op jit(solution)/shard_map/ppermute | solution.py:443
  71.2 37.3 %copy-start = (f32[1,2,128,2048]{3,2,1,0:T(8,128)S(1)}, f32[1,2,128,2048]{3,2,1,0:T(8,128)}, u32[]{:S(2)}) copy-start(f32[1,2,128,2048]{3,2,1,0:T(8,128)} %param.5) | copy-start | bytes 6291460
  71.5 36.1 %collective-permute-start.10 = (bf16[2,96,2048]{2,1,0:T(8,128)(2,1)S(1)}, bf16[2,96,2048]{2,1,0:T(8,128)(2,1)S(1)}, u32[]{:S(2)}, u32[]{:S(2)}) collective-permute-start(bf16[2,96,2048]{2,1,0:T(8,128)(2,1)S(1)} %get-tuple-element.52), channel_id=1, source_target_pairs={{0,16},{2,18},{4,20},{6,22},{8,24},{10,26},{12,28},{14,30},{16,0},... | collective-permute-start | bytes 2359304 | tf_op jit(solution)/shard_map/ppermute | solution.py:443
  73.9 33.7 %collective-permute-start.8 = (bf16[2,96,2048]{2,1,0:T(8,128)(2,1)S(1)}, bf16[2,96,2048]{2,1,0:T(8,128)(2,1)S(1)}, u32[]{:S(2)}, u32[]{:S(2)}) collective-permute-start(bf16[2,96,2048]{2,1,0:T(8,128)(2,1)S(1)} %get-tuple-element.50), channel_id=1, source_target_pairs={{0,4},{2,6},{4,0},{6,2},{8,12},{10,14},{12,8},{14,10},{16,20},{18,... | collective-permute-start | bytes 2359304 | tf_op jit(solution)/shard_map/ppermute | solution.py:443
  75.5 33.0 %collective-permute-start.9 = (bf16[2,96,2048]{2,1,0:T(8,128)(2,1)S(1)}, bf16[2,96,2048]{2,1,0:T(8,128)(2,1)S(1)}, u32[]{:S(2)}, u32[]{:S(2)}) collective-permute-start(bf16[2,96,2048]{2,1,0:T(8,128)(2,1)S(1)} %get-tuple-element.51), channel_id=1, source_target_pairs={{0,8},{2,10},{4,12},{6,14},{8,0},{10,2},{12,4},{14,6},{16,24},{18,... | collective-permute-start | bytes 2359304 | tf_op jit(solution)/shard_map/ppermute | solution.py:443
  77.1 20.0 %collective-permute-start.11 = (bf16[2,32,2048]{2,1,0:T(8,128)(2,1)S(1)}, bf16[2,32,2048]{2,1,0:T(8,128)(2,1)S(1)}, u32[]{:S(2)}, u32[]{:S(2)}) collective-permute-start(bf16[2,32,2048]{2,1,0:T(8,128)(2,1)S(1)} %get-tuple-element.54), channel_id=1, source_target_pairs={{0,4},{2,6},{4,0},{6,2},{8,12},{10,14},{12,8},{14,10},{16,20},{18,... | collective-permute-start | bytes 786440 | tf_op jit(solution)/shard_map/ppermute | solution.py:443
  109.6 5.0 %collective-permute-start.12 = (f32[2,128,128]{2,1,0:T(8,128)S(1)}, f32[2,128,128]{2,1,0:T(8,128)S(1)}, u32[]{:S(2)}, u32[]{:S(2)}) collective-permute-start(f32[2,128,128]{2,1,0:T(8,128)S(1)} %get-tuple-element.55.refs_0_), channel_id=1, source_target_pairs={{0,1},{1,0},{2,3},{3,2},{4,5},{5,4},{6,7},{7,6},{8,9},{9,8},{10,11... | collective-permute-start | bytes 393224 | tf_op jit(solution)/shard_map/ppermute | solution.py:654
  118.2 33.9 %collective-permute-start.13 = (bf16[2,96,2048]{2,1,0:T(8,128)(2,1)S(1)}, bf16[2,96,2048]{2,1,0:T(8,128)(2,1)S(1)}, u32[]{:S(2)}, u32[]{:S(2)}) collective-permute-start(bf16[2,96,2048]{2,1,0:T(8,128)(2,1)S(1)} %get-tuple-element.57.rest_6_.refs_4_), channel_id=1, source_target_pairs={{0,16},{2,18},{4,20},{6,22},{8,24},{10,26},{12,28},{14,30},{16,0},... | collective-permute-start | bytes 2359304 | tf_op jit(solution)/shard_map/ppermute | solution.py:443
  119.8 32.3 %collective-permute-start.15 = (bf16[2,96,2048]{2,1,0:T(8,128)(2,1)S(1)}, bf16[2,96,2048]{2,1,0:T(8,128)(2,1)S(1)}, u32[]{:S(2)}, u32[]{:S(2)}) collective-permute-start(bf16[2,96,2048]{2,1,0:T(8,128)(2,1)S(1)} %get-tuple-element.57.rest_6_.refs_4_), channel_id=1, source_target_pairs={{0,8},{2,10},{4,12},{6,14},{8,0},{10,2},{12,4},{14,6},{16,24},{18,... | collective-permute-start | bytes 2359304 | tf_op jit(solution)/shard_map/ppermute | solution.py:443
  122.3 29.9 %collective-permute-start.17 = (bf16[2,96,2048]{2,1,0:T(8,128)(2,1)S(1)}, bf16[2,96,2048]{2,1,0:T(8,128)(2,1)S(1)}, u32[]{:S(2)}, u32[]{:S(2)}) collective-permute-start(bf16[2,96,2048]{2,1,0:T(8,128)(2,1)S(1)} %get-tuple-element.57.rest_6_.refs_4_), channel_id=1, source_target_pairs={{0,4},{2,6},{4,0},{6,2},{8,12},{10,14},{12,8},{14,10},{16,20},{18,... | collective-permute-start | bytes 2359304 | tf_op jit(solution)/shard_map/ppermute | solution.py:443
  122.8 21.6 %collective-permute-start.16 = (bf16[2,32,2048]{2,1,0:T(8,128)(2,1)S(1)}, bf16[2,32,2048]{2,1,0:T(8,128)(2,1)S(1)}, u32[]{:S(2)}, u32[]{:S(2)}) collective-permute-start(bf16[2,32,2048]{2,1,0:T(8,128)(2,1)S(1)} %get-tuple-element.58.refs_2_), channel_id=1, source_target_pairs={{0,4},{2,6},{4,0},{6,2},{8,12},{10,14},{12,8},{14,10},{16,20},{18,... | collective-permute-start | bytes 786440 | tf_op jit(solution)/shard_map/ppermute | solution.py:443
  152.4 6.5 %collective-permute-start.19 = (bf16[4,96,2048]{2,1,0:T(8,128)(2,1)S(1)}, bf16[4,96,2048]{2,1,0:T(8,128)(2,1)S(1)}, u32[]{:S(2)}, u32[]{:S(2)}) collective-permute-start(bf16[4,96,2048]{2,1,0:T(8,128)(2,1)S(1)} %get-tuple-element.61.refs_0_), channel_id=1, source_target_pairs={{0,2},{2,0},{4,6},{6,4},{8,10},{10,8},{12,14},{14,12},{16,18},{18,... | collective-permute-start | bytes 4718600 | tf_op jit(solution)/shard_map/ppermute | solution.py:443
  152.5 6.4 %collective-permute-start.20 = (bf16[4,96,2048]{2,1,0:T(8,128)(2,1)S(1)}, bf16[4,96,2048]{2,1,0:T(8,128)(2,1)S(1)}, u32[]{:S(2)}, u32[]{:S(2)}) collective-permute-start(bf16[4,96,2048]{2,1,0:T(8,128)(2,1)S(1)} %get-tuple-element.62.refs_2_.refs_4_), channel_id=1, source_target_pairs={{0,2},{2,0},{4,6},{6,4},{8,10},{10,8},{12,14},{14,12},{16,18},{18,... | collective-permute-start | bytes 4718600 | tf_op jit(solution)/shard_map/ppermute | solution.py:443
  153.0 36.4 %collective-permute-start.26 = (bf16[4,96,2048]{2,1,0:T(8,128)(2,1)S(1)}, bf16[4,96,2048]{2,1,0:T(8,128)(2,1)S(1)}, u32[]{:S(2)}, u32[]{:S(2)}) collective-permute-start(bf16[4,96,2048]{2,1,0:T(8,128)(2,1)S(1)} %get-tuple-element.62.refs_2_.refs_4_), channel_id=1, source_target_pairs={{0,4},{2,6},{4,0},{6,2},{8,12},{10,14},{12,8},{14,10},{16,20},{18,... | collective-permute-start | bytes 4718600 | tf_op jit(solution)/shard_map/ppermute | solution.py:443
  153.3 30.5 %collective-permute-start.14 = (bf16[2,96,2048]{2,1,0:T(8,128)(2,1)S(1)}, bf16[2,96,2048]{2,1,0:T(8,128)(2,1)S(1)}, u32[]{:S(2)}, u32[]{:S(2)}) collective-permute-start(bf16[2,96,2048]{2,1,0:T(8,128)(2,1)S(1)} %collective-permute-done.13.refs_0_), channel_id=1, source_target_pairs={{0,8},{2,10},{4,12},{6,14},{8,0},{10,2},{12,4},{14,6},{16,24},{18,... | collective-permute-start | bytes 2359304 | tf_op jit(solution)/shard_map/ppermute | solution.py:443
  154.5 28.0 %collective-permute-start.18 = (bf16[4,32,2048]{2,1,0:T(8,128)(2,1)S(1)}, bf16[4,32,2048]{2,1,0:T(8,128)(2,1)S(1)}, u32[]{:S(2)}, u32[]{:S(2)}) collective-permute-start(bf16[4,32,2048]{2,1,0:T(8,128)(2,1)S(1)} %get-tuple-element.60.refs_1_), channel_id=1, source_target_pairs={{0,16},{2,18},{4,20},{6,22},{8,24},{10,26},{12,28},{14,30},{16,0},... | collective-permute-start | bytes 1572872 | tf_op jit(solution)/shard_map/ppermute | solution.py:443
  183.9 26.2 %collective-permute-start.24 = (bf16[8,32,2048]{2,1,0:T(8,128)(2,1)S(1)}, bf16[8,32,2048]{2,1,0:T(8,128)(2,1)S(1)}, u32[]{:S(2)}, u32[]{:S(2)}) collective-permute-start(bf16[8,32,2048]{2,1,0:T(8,128)(2,1)S(1)} %get-tuple-element.65.refs_3_), channel_id=1, source_target_pairs={{0,8},{2,10},{4,12},{6,14},{8,0},{10,2},{12,4},{14,6},{16,24},{18,... | collective-permute-start | bytes 3145736 | tf_op jit(solution)/shard_map/ppermute | solution.py:443
  189.4 21.2 %collective-permute-start.27 = (bf16[4,96,2048]{2,1,0:T(8,128)(2,1)S(1)}, bf16[4,96,2048]{2,1,0:T(8,128)(2,1)S(1)}, u32[]{:S(2)}, u32[]{:S(2)}) collective-permute-start(bf16[4,96,2048]{2,1,0:T(8,128)(2,1)S(1)} %collective-permute-done.26.refs_0_), channel_id=1, source_target_pairs={{0,2},{2,0},{4,6},{6,4},{8,10},{10,8},{12,14},{14,12},{16,18},{18,... | collective-permute-start | bytes 4718600 | tf_op jit(solution)/shard_map/ppermute | solution.py:443
  189.4 21.2 %collective-permute-start.22 = (bf16[2,96,2048]{2,1,0:T(8,128)(2,1)S(1)}, bf16[2,96,2048]{2,1,0:T(8,128)(2,1)S(1)}, u32[]{:S(2)}, u32[]{:S(2)}) collective-permute-start(bf16[2,96,2048]{2,1,0:T(8,128)(2,1)S(1)} %get-tuple-element.64.refs_2_.refs_6_), channel_id=1, source_target_pairs={{0,4},{2,6},{4,0},{6,2},{8,12},{10,14},{12,8},{14,10},{16,20},{18,... | collective-permute-start | bytes 2359304 | tf_op jit(solution)/shard_map/ppermute | solution.py:443
  189.7 20.9 %collective-permute-start.28 = (bf16[8,32,2048]{2,1,0:T(8,128)(2,1)S(1)}, bf16[8,32,2048]{2,1,0:T(8,128)(2,1)S(1)}, u32[]{:S(2)}, u32[]{:S(2)}) collective-permute-start(bf16[8,32,2048]{2,1,0:T(8,128)(2,1)S(1)} %get-tuple-element.65.refs_3_), channel_id=1, source_target_pairs={{0,2},{2,0},{4,6},{6,4},{8,10},{10,8},{12,14},{14,12},{16,18},{18,... | collective-permute-start | bytes 3145736 | tf_op jit(solution)/shard_map/ppermute | solution.py:443
  210.1 4.9 %collective-permute-start.25 = (bf16[8,32,2048]{2,1,0:T(8,128)(2,1)S(1)}, bf16[8,32,2048]{2,1,0:T(8,128)(2,1)S(1)}, u32[]{:S(2)}, u32[]{:S(2)}) collective-permute-start(bf16[8,32,2048]{2,1,0:T(8,128)(2,1)S(1)} %collective-permute-done.24.refs_3_), channel_id=1, source_target_pairs={{0,2},{2,0},{4,6},{6,4},{8,10},{10,8},{12,14},{14,12},{16,18},{18,... | collective-permute-start | bytes 3145736 | tf_op jit(solution)/shard_map/ppermute | solution.py:443
  210.1 4.1 %collective-permute-start.21 = (bf16[2,96,2048]{2,1,0:T(8,128)(2,1)S(1)}, bf16[2,96,2048]{2,1,0:T(8,128)(2,1)S(1)}, u32[]{:S(2)}, u32[]{:S(2)}) collective-permute-start(bf16[2,96,2048]{2,1,0:T(8,128)(2,1)S(1)} %get-tuple-element.64.refs_2_.refs_6_), channel_id=1, source_target_pairs={{0,2},{2,0},{4,6},{6,4},{8,10},{10,8},{12,14},{14,12},{16,18},{18,... | collective-permute-start | bytes 2359304 | tf_op jit(solution)/shard_map/ppermute | solution.py:443
  210.6 4.4 %collective-permute-start.23 = (bf16[2,96,2048]{2,1,0:T(8,128)(2,1)S(1)}, bf16[2,96,2048]{2,1,0:T(8,128)(2,1)S(1)}, u32[]{:S(2)}, u32[]{:S(2)}) collective-permute-start(bf16[2,96,2048]{2,1,0:T(8,128)(2,1)S(1)} %collective-permute-done.22.refs_1_), channel_id=1, source_target_pairs={{0,2},{2,0},{4,6},{6,4},{8,10},{10,8},{12,14},{14,12},{16,18},{18,... | collective-permute-start | bytes 2359304 | tf_op jit(solution)/shard_map/ppermute | solution.py:443

commit v9 on v8

--- a/solution.py
+++ b/solution.py
@@ -627,8 +627,10 @@
         last = with_core(front, 0, front_order)
         waiting += last if k + 1 < top else last[:1]
     waiting += with_core(cur, cut, cur_order)
+    crossed, crossed_other = with_core(*crossed), with_core(*crossed_other)
+    waiting += crossed[:1] + crossed_other[:1]
     update, _ = spread(after, update, shape, table, slots, waiting)
-    waiting = last[1:] + with_core(*crossed) + with_core(*crossed_other)
+    waiting = last[1:] + crossed[1:] + crossed_other[1:]
     return spread([], update, shape, table, slots, waiting)[0]
 
 

time: 218 us -> 217 us (level)
  waiting for transfers between devices: 146 us -> 143 us
    ppermute x28, waiting for transfers between devices: 142 us -> 140 us  [swap(): return lax.ppermute(value, 'dp', [(i, i ^ bit) for i in range(count)])]
where the time goes in v9:
time: 217 us
  waiting for transfers between devices  143 us (66%)
  starting transfers between devices  38.9 us (18%)
  Pallas kernels  33.6 us (15%)
    ppermute x28, waiting for transfers between devices, swap(): return lax.ppermute(value, 'dp', [(i, i ^ bit) for i in range(count)])  140 us
    ppermute x28, starting transfers between devices, swap(): return lax.ppermute(value, 'dp', [(i, i ^ bit) for i in range(count)])  37.5 us
    pallas_call x3, Pallas kernels, spread(): pl.pallas_call(functools.partial(spread_kernel, plans, slots), out_shape=...  9.56 us
    pallas_call x3, Pallas kernels, add_taken(): pl.pallas_call(functools.partial(add_taken_kernel, items, parts), out_sha...  7.69 us
    pallas_call x1, Pallas kernels, pack(): pl.pallas_call(functools.partial(pack_kernel, tuple(plans)), out_shape=[j...  4.87 us
  transfers between devices with their start and end apart: 29, of which 16 were waited for; matrix products, arithmetic and copies ran while one was open for 0% of the time, Pallas kernels for 10%

profile of v9, /device:TPU:0, one launch (start us, length us, event | category | flops | bytes accessed | tf_op | source)
XLA Modules:
  0.0 217.1 jit_solution(15134178467084235048)
XLA Ops:
  1.3 3.8 %shard_map.50 = (s32[32]{0:T(128)S(1)}, bf16[22,32,2048]{2,1,0:T(8,128)(2,1)S(1)}) custom-call(s32[1]{0:T(128)} %bitcast.me_ref, s32[24]{0:T(128)S(1)} %copy-done.1, bf16[24,128,2048]{2,1,0:T(8,128)(2,1)} %bitcast.6), custom_call_target="tpu_custom_call" | custom-call | tf_op jit(solution)/shard_map/pallas_call | solution.py:141
  5.6 4.9 %shard_map.51 = (bf16[6,96,2048]{2,1,0:T(8,128)(2,1)S(1)}, bf16[8,96,2048]{2,1,0:T(8,128)(2,1)}) custom-call(s32[32]{0:T(128)S(1)} %get-tuple-element.36.table_ref, bf16[24,128,2048]{2,1,0:T(8,128)(2,1)} %bitcast.7, bf16[22,32,2048]{2,1,0:T(8,128)(2,1)S(1)} %get-tuple-element.37.rest_0_), custom_call_target="tpu_custom_call" | custom-call | tf_op jit(solution)/shard_map/pallas_call | solution.py:115
  11.1 2.7 %shard_map.52 = (bf16[8,32,2048]{2,1,0:T(8,128)(2,1)S(1)}, bf16[8,32,2048]{2,1,0:T(8,128)(2,1)S(1)}, bf16[6,32,2048]{2,1,0:T(8,128)(2,1)S(1)}) custom-call(s32[32]{0:T(128)S(1)} %get-tuple-element.36.table_ref, bf16[24,128,2048]{2,1,0:T(8,128)(2,1)} %bitcast.8, bf16[22,32,2048]{2,1,0:T(8,128)(2,1)S(1)} %collective-permute-done.2.got_ref, ...), custom_call_target="tpu_custom_call" | custom-call | tf_op jit(solution)/shard_map/pallas_call | solution.py:175
  13.8 2.7 %collective-permute-start.4 = (bf16[8,32,2048]{2,1,0:T(8,128)(2,1)S(1)}, bf16[8,32,2048]{2,1,0:T(8,128)(2,1)S(1)}, u32[]{:S(2)}, u32[]{:S(2)}) collective-permute-start(bf16[8,32,2048]{2,1,0:T(8,128)(2,1)S(1)} %get-tuple-element.40.rest_0_), channel_id=1, source_target_pairs={{0,8},{2,10},{4,12},{6,14},{8,0},{10,2},{12,4},{14,6},{16,24},{18,... | collective-permute-start | bytes 3145736 | tf_op jit(solution)/shard_map/ppermute | solution.py:443
  16.5 1.7 collective-permute-start.3
  18.3 2.3 %shard_map.53 = (bf16[4,96,2048]{2,1,0:T(8,128)(2,1)S(1)}, bf16[2,96,2048]{2,1,0:T(8,128)(2,1)S(1)}) custom-call(s32[32]{0:T(128)S(1)} %get-tuple-element.36.table_ref, bf16[24,128,2048]{2,1,0:T(8,128)(2,1)} %bitcast.9, bf16[6,96,2048]{2,1,0:T(8,128)(2,1)S(1)} %collective-permute-done.1.got_ref, bf16[8,32,2048]{2,1,0:T(8,128)(2,1)S(1)} %get-tuple-element.40.rest_0_), custom_call_target="tpu_custom_call" | custom-call | tf_op jit(solution)/shard_map/pallas_call | solution.py:175
  20.5 2.3 %collective-permute-start.5 = (bf16[4,96,2048]{2,1,0:T(8,128)(2,1)S(1)}, bf16[4,96,2048]{2,1,0:T(8,128)(2,1)S(1)}, u32[]{:S(2)}, u32[]{:S(2)}) collective-permute-start(bf16[4,96,2048]{2,1,0:T(8,128)(2,1)S(1)} %get-tuple-element.44.refs_4_), channel_id=1, source_target_pairs={{0,4},{2,6},{4,0},{6,2},{8,12},{10,14},{12,8},{14,10},{16,20},{18,... | collective-permute-start | bytes 4718600 | tf_op jit(solution)/shard_map/ppermute | solution.py:443
  22.9 14.1 %collective-permute-done.3.refs_1_ = bf16[6,32,2048]{2,1,0:T(8,128)(2,1)S(1)} collective-permute-done((bf16[6,32,2048]{2,1,0:T(8,128)(2,1)S(1)}, bf16[6,32,2048]{2,1,0:T(8,128)(2,1)S(1)}, u32[]{:S(2)}, u32[]{:S(2)}) %collective-permute-start.3) | collective-permute-done | bytes 786464 | tf_op jit(solution)/shard_map/ppermute | solution.py:443
  36.9 3.2 %collective-permute-done.4.refs_3_ = bf16[8,32,2048]{2,1,0:T(8,128)(2,1)S(1)} collective-permute-done((bf16[8,32,2048]{2,1,0:T(8,128)(2,1)S(1)}, bf16[8,32,2048]{2,1,0:T(8,128)(2,1)S(1)}, u32[]{:S(2)}, u32[]{:S(2)}) %collective-permute-start.4) | collective-permute-done | bytes 1048608 | tf_op jit(solution)/shard_map/ppermute | solution.py:443
  40.3 1.8 collective-permute-start.6
  42.1 2.8 %collective-permute-start.7 = (bf16[4,32,2048]{2,1,0:T(8,128)(2,1)S(1)}, bf16[4,32,2048]{2,1,0:T(8,128)(2,1)S(1)}, u32[]{:S(2)}, u32[]{:S(2)}) collective-permute-start(bf16[4,32,2048]{2,1,0:T(8,128)(2,1)S(1)} %get-tuple-element.48), channel_id=1, source_target_pairs={{0,16},{2,18},{4,20},{6,22},{8,24},{10,26},{12,28},{14,30},{16,0},... | collective-permute-start | bytes 1572872 | tf_op jit(solution)/shard_map/ppermute | solution.py:443
  44.9 2.7 %shard_map.55 = (bf16[2,96,2048]{2,1,0:T(8,128)(2,1)S(1)}, bf16[6,96,2048]{2,1,0:T(8,128)(2,1)S(1)}) custom-call(s32[32]{0:T(128)S(1)} %get-tuple-element.36.table_ref, bf16[24,128,2048]{2,1,0:T(8,128)(2,1)} %bitcast.10, bf16[8,96,2048]{2,1,0:T(8,128)(2,1)S(1)} %collective-permute-done.got_ref, bf16[2,96,2048]{2,1,0:T(8,128)(2,1)S(1)} %get-tuple-element.45.rest_0_), custom_call_target="tpu_custom_call" | custom-call | tf_op jit(solution)/shard_map/pallas_call | solution.py:175
  47.6 22.2 %collective-permute-done.7.refs_4_ = bf16[4,32,2048]{2,1,0:T(8,128)(2,1)S(1)} collective-permute-done((bf16[4,32,2048]{2,1,0:T(8,128)(2,1)S(1)}, bf16[4,32,2048]{2,1,0:T(8,128)(2,1)S(1)}, u32[]{:S(2)}, u32[]{:S(2)}) %collective-permute-start.7) | collective-permute-done | bytes 524320 | tf_op jit(solution)/shard_map/ppermute | solution.py:443
  71.2 2.4 %collective-permute-start.10 = (bf16[2,96,2048]{2,1,0:T(8,128)(2,1)S(1)}, bf16[2,96,2048]{2,1,0:T(8,128)(2,1)S(1)}, u32[]{:S(2)}, u32[]{:S(2)}) collective-permute-start(bf16[2,96,2048]{2,1,0:T(8,128)(2,1)S(1)} %get-tuple-element.52), channel_id=1, source_target_pairs={{0,16},{2,18},{4,20},{6,22},{8,24},{10,26},{12,28},{14,30},{16,0},... | collective-permute-start | bytes 2359304 | tf_op jit(solution)/shard_map/ppermute | solution.py:443
  73.6 1.7 collective-permute-start.8
  75.3 1.9 collective-permute-start.9
  77.5 19.4 %collective-permute-done.11.rest_5_ = bf16[2,32,2048]{2,1,0:T(8,128)(2,1)S(1)} collective-permute-done((bf16[2,32,2048]{2,1,0:T(8,128)(2,1)S(1)}, bf16[2,32,2048]{2,1,0:T(8,128)(2,1)S(1)}, u32[]{:S(2)}, u32[]{:S(2)}) %collective-permute-start.11) | collective-permute-done | bytes 262176 | tf_op jit(solution)/shard_map/ppermute | solution.py:443
  97.0 10.6 %collective-permute-done.10.rest_3_ = bf16[2,96,2048]{2,1,0:T(8,128)(2,1)S(1)} collective-permute-done((bf16[2,96,2048]{2,1,0:T(8,128)(2,1)S(1)}, bf16[2,96,2048]{2,1,0:T(8,128)(2,1)S(1)}, u32[]{:S(2)}, u32[]{:S(2)}) %collective-permute-start.10) | collective-permute-done | bytes 786464 | tf_op jit(solution)/shard_map/ppermute | solution.py:443
  110.5 3.6 %collective-permute-done.12.refs_1_ = f32[2,128,128]{2,1,0:T(8,128)S(1)} collective-permute-done((f32[2,128,128]{2,1,0:T(8,128)S(1)}, f32[2,128,128]{2,1,0:T(8,128)S(1)}, u32[]{:S(2)}, u32[]{:S(2)}) %collective-permute-start.12) | collective-permute-done | bytes 131104 | tf_op jit(solution)/shard_map/ppermute | solution.py:656
  114.1 3.5 %shard_map.58 = (bf16[2,96,2048]{2,1,0:T(8,128)(2,1)S(1)}, bf16[2,32,2048]{2,1,0:T(8,128)(2,1)S(1)}) custom-call(f32[2,128,128]{2,1,0:T(8,128)S(1)} %get-tuple-element.55.refs_0_, f32[2,128,128]{2,1,0:T(8,128)S(1)} %collective-permute-done.12.refs_1_, bf16[2,128,2048]{2,1,0:T(8,128)(2,1)S(1)} %get-tuple-element.56.refs_2_), custom_call_target="tpu_custom_call" | custom-call | tf_op jit(solution)/shard_map/pallas_call | solution.py:429
  117.6 2.4 %collective-permute-start.13 = (bf16[2,96,2048]{2,1,0:T(8,128)(2,1)S(1)}, bf16[2,96,2048]{2,1,0:T(8,128)(2,1)S(1)}, u32[]{:S(2)}, u32[]{:S(2)}) collective-permute-start(bf16[2,96,2048]{2,1,0:T(8,128)(2,1)S(1)} %get-tuple-element.57.rest_6_.refs_4_), channel_id=1, source_target_pairs={{0,16},{2,18},{4,20},{6,22},{8,24},{10,26},{12,28},{14,30},{16,0},... | collective-permute-start | bytes 2359304 | tf_op jit(solution)/shard_map/ppermute | solution.py:443
  120.1 2.5 %collective-permute-start.15 = (bf16[2,96,2048]{2,1,0:T(8,128)(2,1)S(1)}, bf16[2,96,2048]{2,1,0:T(8,128)(2,1)S(1)}, u32[]{:S(2)}, u32[]{:S(2)}) collective-permute-start(bf16[2,96,2048]{2,1,0:T(8,128)(2,1)S(1)} %get-tuple-element.57.rest_6_.refs_4_), channel_id=1, source_target_pairs={{0,8},{2,10},{4,12},{6,14},{8,0},{10,2},{12,4},{14,6},{16,24},{18,... | collective-permute-start | bytes 2359304 | tf_op jit(solution)/shard_map/ppermute | solution.py:443
  124.6 2.3 %shard_map.59 = (f32[2,128,2048]{2,1,0:T(8,128)}, f32[8,128]{1,0:T(8,128)S(1)}) custom-call(s32[32]{0:T(128)S(1)} %get-tuple-element.36.table_ref, f32[2,128,2048]{2,1,0:T(8,128)S(1)} %bitcast.5, bf16[6,96,2048]{2,1,0:T(8,128)(2,1)S(1)} %get-tuple-element.46.refs_0_.rest_0_, bf16[2,96,2048]{2,1,0:T(8,128)(2,1)S(1)} %collective-permute-done.8.rest_1_, ...), custom_call_target="tpu_custom_call" | custom-call | tf_op jit(solution)/shard_map/pallas_call | solution.py:348
  126.8 17.2 %collective-permute-done.16.refs_3_ = bf16[2,32,2048]{2,1,0:T(8,128)(2,1)S(1)} collective-permute-done((bf16[2,32,2048]{2,1,0:T(8,128)(2,1)S(1)}, bf16[2,32,2048]{2,1,0:T(8,128)(2,1)S(1)}, u32[]{:S(2)}, u32[]{:S(2)}) %collective-permute-start.16) | collective-permute-done | bytes 262176 | tf_op jit(solution)/shard_map/ppermute | solution.py:443
  144.0 7.4 %collective-permute-done.13.refs_0_ = bf16[2,96,2048]{2,1,0:T(8,128)(2,1)S(1)} collective-permute-done((bf16[2,96,2048]{2,1,0:T(8,128)(2,1)S(1)}, bf16[2,96,2048]{2,1,0:T(8,128)(2,1)S(1)}, u32[]{:S(2)}, u32[]{:S(2)}) %collective-permute-start.13) | collective-permute-done | bytes 786464 | tf_op jit(solution)/shard_map/ppermute | solution.py:443
  155.0 3.3 %collective-permute-start.18 = (bf16[4,32,2048]{2,1,0:T(8,128)(2,1)S(1)}, bf16[4,32,2048]{2,1,0:T(8,128)(2,1)S(1)}, u32[]{:S(2)}, u32[]{:S(2)}) collective-permute-start(bf16[4,32,2048]{2,1,0:T(8,128)(2,1)S(1)} %get-tuple-element.60.refs_1_), channel_id=1, source_target_pairs={{0,16},{2,18},{4,20},{6,22},{8,24},{10,26},{12,28},{14,30},{16,0},... | collective-permute-start | bytes 1572872 | tf_op jit(solution)/shard_map/ppermute | solution.py:443
  158.3 2.9 %shard_map.61 = (bf16[24,128,2048]{2,1,0:T(8,128)(2,1)}, f32[8,128]{1,0:T(8,128)S(1)}) custom-call(s32[32]{0:T(128)S(1)} %get-tuple-element.36.table_ref, bf16[4,96,2048]{2,1,0:T(8,128)(2,1)S(1)} %get-tuple-element.61.refs_0_, bf16[4,96,2048]{2,1,0:T(8,128)(2,1)S(1)} %collective-permute-done.19.refs_1_, ...), custom_call_target="tpu_custom_call" | custom-call | tf_op jit(solution)/shard_map/pallas_call | solution.py:275
  161.2 21.9 %collective-permute-done.18.refs_2_ = bf16[4,32,2048]{2,1,0:T(8,128)(2,1)S(1)} collective-permute-done((bf16[4,32,2048]{2,1,0:T(8,128)(2,1)S(1)}, bf16[4,32,2048]{2,1,0:T(8,128)(2,1)S(1)}, u32[]{:S(2)}, u32[]{:S(2)}) %collective-permute-start.18) | collective-permute-done | bytes 524320 | tf_op jit(solution)/shard_map/ppermute | solution.py:443
  184.0 3.2 %collective-permute-start.24 = (bf16[8,32,2048]{2,1,0:T(8,128)(2,1)S(1)}, bf16[8,32,2048]{2,1,0:T(8,128)(2,1)S(1)}, u32[]{:S(2)}, u32[]{:S(2)}) collective-permute-start(bf16[8,32,2048]{2,1,0:T(8,128)(2,1)S(1)} %get-tuple-element.65.refs_3_), channel_id=1, source_target_pairs={{0,8},{2,10},{4,12},{6,14},{8,0},{10,2},{12,4},{14,6},{16,24},{18,... | collective-permute-start | bytes 3145736 | tf_op jit(solution)/shard_map/ppermute | solution.py:443
  190.0 19.5 %collective-permute-done.24.refs_6_ = bf16[8,32,2048]{2,1,0:T(8,128)(2,1)S(1)} collective-permute-done((bf16[8,32,2048]{2,1,0:T(8,128)(2,1)S(1)}, bf16[8,32,2048]{2,1,0:T(8,128)(2,1)S(1)}, u32[]{:S(2)}, u32[]{:S(2)}) %collective-permute-start.24) | collective-permute-done | bytes 1048608 | tf_op jit(solution)/shard_map/ppermute | solution.py:443
  210.1 4.1 %shard_map.63 = (bf16[24,128,2048]{2,1,0:T(8,128)(2,1)}, f32[8,128]{1,0:T(8,128)}) custom-call(s32[32]{0:T(128)S(1)} %get-tuple-element.36.table_ref, bf16[4,96,2048]{2,1,0:T(8,128)(2,1)S(1)} %collective-permute-done.26.refs_0_, bf16[4,96,2048]{2,1,0:T(8,128)(2,1)S(1)} %collective-permute-done.27.refs_1_, ...), custom_call_target="tpu_custom_call", output_to_operand_aliasing={{0}: (8, {})} | custom-call | tf_op jit(solution)/shard_map/pallas_call | solution.py:275
  214.4 2.6 %shard_map.64 = (bf16[24,128,2048]{2,1,0:T(8,128)(2,1)}, f32[8,128]{1,0:T(8,128)}) custom-call(s32[32]{0:T(128)S(1)} %get-tuple-element.36.table_ref, bf16[2,96,2048]{2,1,0:T(8,128)(2,1)S(1)} %collective-permute-done.21.refs_0_, bf16[2,96,2048]{2,1,0:T(8,128)(2,1)S(1)} %collective-permute-done.23.refs_1_, ...), custom_call_target="tpu_custom_call", output_to_operand_aliasing={{0}: (4, {})} | custom-call | tf_op jit(solution)/shard_map/pallas_call | solution.py:275
  (45 shorter events, 16.9 us)
Async XLA Ops:
  0.6 0.7 copy-start.1
  5.1 6.0 %collective-permute-start.2 = (bf16[22,32,2048]{2,1,0:T(8,128)(2,1)S(1)}, bf16[22,32,2048]{2,1,0:T(8,128)(2,1)S(1)}, u32[]{:S(2)}, u32[]{:S(2)}) collective-permute-start(bf16[22,32,2048]{2,1,0:T(8,128)(2,1)S(1)} %get-tuple-element.37.rest_0_), channel_id=1, source_target_pairs={{0,2},{2,0},{4,6},{6,4},{8,10},{10,8},{12,14},{14,12},{16,18},{18,... | collective-permute-start | bytes 8650760 | tf_op jit(solution)/shard_map/ppermute | solution.py:443
  10.5 7.8 %collective-permute-start.1 = (bf16[6,96,2048]{2,1,0:T(8,128)(2,1)S(1)}, bf16[6,96,2048]{2,1,0:T(8,128)(2,1)S(1)}, u32[]{:S(2)}, u32[]{:S(2)}) collective-permute-start(bf16[6,96,2048]{2,1,0:T(8,128)(2,1)S(1)} %get-tuple-element.39.rest_0_), channel_id=1, source_target_pairs={{0,2},{2,0},{4,6},{6,4},{8,10},{10,8},{12,14},{14,12},{16,18},{18,... | collective-permute-start | bytes 7077896 | tf_op jit(solution)/shard_map/ppermute | solution.py:443
  11.0 33.9 %collective-permute-start = (bf16[8,96,2048]{2,1,0:T(8,128)(2,1)}, bf16[8,96,2048]{2,1,0:T(8,128)(2,1)S(1)}, u32[]{:S(2)}, u32[]{:S(2)}) collective-permute-start(bf16[8,96,2048]{2,1,0:T(8,128)(2,1)} %get-tuple-element.38), channel_id=1, source_target_pairs={{0,2},{2,0},{4,6},{6,4},{8,10},{10,8},{12,14},{14,12},{16,18},{18,... | collective-permute-start | bytes 9437192 | tf_op jit(solution)/shard_map/ppermute | solution.py:443
  13.8 26.3 %collective-permute-start.4 = (bf16[8,32,2048]{2,1,0:T(8,128)(2,1)S(1)}, bf16[8,32,2048]{2,1,0:T(8,128)(2,1)S(1)}, u32[]{:S(2)}, u32[]{:S(2)}) collective-permute-start(bf16[8,32,2048]{2,1,0:T(8,128)(2,1)S(1)} %get-tuple-element.40.rest_0_), channel_id=1, source_target_pairs={{0,8},{2,10},{4,12},{6,14},{8,0},{10,2},{12,4},{14,6},{16,24},{18,... | collective-permute-start | bytes 3145736 | tf_op jit(solution)/shard_map/ppermute | solution.py:443
  16.5 20.4 %collective-permute-start.3 = (bf16[6,32,2048]{2,1,0:T(8,128)(2,1)S(1)}, bf16[6,32,2048]{2,1,0:T(8,128)(2,1)S(1)}, u32[]{:S(2)}, u32[]{:S(2)}) collective-permute-start(bf16[6,32,2048]{2,1,0:T(8,128)(2,1)S(1)} %get-tuple-element.42), channel_id=1, source_target_pairs={{0,4},{2,6},{4,0},{6,2},{8,12},{10,14},{12,8},{14,10},{16,20},{18,... | collective-permute-start | bytes 2359304 | tf_op jit(solution)/shard_map/ppermute | solution.py:443
  20.5 49.3 %collective-permute-start.5 = (bf16[4,96,2048]{2,1,0:T(8,128)(2,1)S(1)}, bf16[4,96,2048]{2,1,0:T(8,128)(2,1)S(1)}, u32[]{:S(2)}, u32[]{:S(2)}) collective-permute-start(bf16[4,96,2048]{2,1,0:T(8,128)(2,1)S(1)} %get-tuple-element.44.refs_4_), channel_id=1, source_target_pairs={{0,4},{2,6},{4,0},{6,2},{8,12},{10,14},{12,8},{14,10},{16,20},{18,... | collective-permute-start | bytes 4718600 | tf_op jit(solution)/shard_map/ppermute | solution.py:443
  40.3 30.6 %collective-permute-start.6 = (bf16[2,96,2048]{2,1,0:T(8,128)(2,1)S(1)}, bf16[2,96,2048]{2,1,0:T(8,128)(2,1)S(1)}, u32[]{:S(2)}, u32[]{:S(2)}) collective-permute-start(bf16[2,96,2048]{2,1,0:T(8,128)(2,1)S(1)} %get-tuple-element.45.rest_0_), channel_id=1, source_target_pairs={{0,8},{2,10},{4,12},{6,14},{8,0},{10,2},{12,4},{14,6},{16,24},{18,... | collective-permute-start | bytes 2359304 | tf_op jit(solution)/shard_map/ppermute | solution.py:443
  42.1 27.7 %collective-permute-start.7 = (bf16[4,32,2048]{2,1,0:T(8,128)(2,1)S(1)}, bf16[4,32,2048]{2,1,0:T(8,128)(2,1)S(1)}, u32[]{:S(2)}, u32[]{:S(2)}) collective-permute-start(bf16[4,32,2048]{2,1,0:T(8,128)(2,1)S(1)} %get-tuple-element.48), channel_id=1, source_target_pairs={{0,16},{2,18},{4,20},{6,22},{8,24},{10,26},{12,28},{14,30},{16,0},... | collective-permute-start | bytes 1572872 | tf_op jit(solution)/shard_map/ppermute | solution.py:443
  70.9 37.1 %copy-start = (f32[1,2,128,2048]{3,2,1,0:T(8,128)S(1)}, f32[1,2,128,2048]{3,2,1,0:T(8,128)}, u32[]{:S(2)}) copy-start(f32[1,2,128,2048]{3,2,1,0:T(8,128)} %param.5) | copy-start | bytes 6291460
  71.2 36.3 %collective-permute-start.10 = (bf16[2,96,2048]{2,1,0:T(8,128)(2,1)S(1)}, bf16[2,96,2048]{2,1,0:T(8,128)(2,1)S(1)}, u32[]{:S(2)}, u32[]{:S(2)}) collective-permute-start(bf16[2,96,2048]{2,1,0:T(8,128)(2,1)S(1)} %get-tuple-element.52), channel_id=1, source_target_pairs={{0,16},{2,18},{4,20},{6,22},{8,24},{10,26},{12,28},{14,30},{16,0},... | collective-permute-start | bytes 2359304 | tf_op jit(solution)/shard_map/ppermute | solution.py:443
  73.6 33.9 %collective-permute-start.8 = (bf16[2,96,2048]{2,1,0:T(8,128)(2,1)S(1)}, bf16[2,96,2048]{2,1,0:T(8,128)(2,1)S(1)}, u32[]{:S(2)}, u32[]{:S(2)}) collective-permute-start(bf16[2,96,2048]{2,1,0:T(8,128)(2,1)S(1)} %get-tuple-element.50), channel_id=1, source_target_pairs={{0,4},{2,6},{4,0},{6,2},{8,12},{10,14},{12,8},{14,10},{16,20},{18,... | collective-permute-start | bytes 2359304 | tf_op jit(solution)/shard_map/ppermute | solution.py:443
  75.3 32.7 %collective-permute-start.9 = (bf16[2,96,2048]{2,1,0:T(8,128)(2,1)S(1)}, bf16[2,96,2048]{2,1,0:T(8,128)(2,1)S(1)}, u32[]{:S(2)}, u32[]{:S(2)}) collective-permute-start(bf16[2,96,2048]{2,1,0:T(8,128)(2,1)S(1)} %get-tuple-element.51), channel_id=1, source_target_pairs={{0,8},{2,10},{4,12},{6,14},{8,0},{10,2},{12,4},{14,6},{16,24},{18,... | collective-permute-start | bytes 2359304 | tf_op jit(solution)/shard_map/ppermute | solution.py:443
  77.2 19.8 %collective-permute-start.11 = (bf16[2,32,2048]{2,1,0:T(8,128)(2,1)S(1)}, bf16[2,32,2048]{2,1,0:T(8,128)(2,1)S(1)}, u32[]{:S(2)}, u32[]{:S(2)}) collective-permute-start(bf16[2,32,2048]{2,1,0:T(8,128)(2,1)S(1)} %get-tuple-element.54), channel_id=1, source_target_pairs={{0,4},{2,6},{4,0},{6,2},{8,12},{10,14},{12,8},{14,10},{16,20},{18,... | collective-permute-start | bytes 786440 | tf_op jit(solution)/shard_map/ppermute | solution.py:443
  109.1 5.0 %collective-permute-start.12 = (f32[2,128,128]{2,1,0:T(8,128)S(1)}, f32[2,128,128]{2,1,0:T(8,128)S(1)}, u32[]{:S(2)}, u32[]{:S(2)}) collective-permute-start(f32[2,128,128]{2,1,0:T(8,128)S(1)} %get-tuple-element.55.refs_0_), channel_id=1, source_target_pairs={{0,1},{1,0},{2,3},{3,2},{4,5},{5,4},{6,7},{7,6},{8,9},{9,8},{10,11... | collective-permute-start | bytes 393224 | tf_op jit(solution)/shard_map/ppermute | solution.py:656
  117.6 33.7 %collective-permute-start.13 = (bf16[2,96,2048]{2,1,0:T(8,128)(2,1)S(1)}, bf16[2,96,2048]{2,1,0:T(8,128)(2,1)S(1)}, u32[]{:S(2)}, u32[]{:S(2)}) collective-permute-start(bf16[2,96,2048]{2,1,0:T(8,128)(2,1)S(1)} %get-tuple-element.57.rest_6_.refs_4_), channel_id=1, source_target_pairs={{0,16},{2,18},{4,20},{6,22},{8,24},{10,26},{12,28},{14,30},{16,0},... | collective-permute-start | bytes 2359304 | tf_op jit(solution)/shard_map/ppermute | solution.py:443
  120.1 31.4 %collective-permute-start.15 = (bf16[2,96,2048]{2,1,0:T(8,128)(2,1)S(1)}, bf16[2,96,2048]{2,1,0:T(8,128)(2,1)S(1)}, u32[]{:S(2)}, u32[]{:S(2)}) collective-permute-start(bf16[2,96,2048]{2,1,0:T(8,128)(2,1)S(1)} %get-tuple-element.57.rest_6_.refs_4_), channel_id=1, source_target_pairs={{0,8},{2,10},{4,12},{6,14},{8,0},{10,2},{12,4},{14,6},{16,24},{18,... | collective-permute-start | bytes 2359304 | tf_op jit(solution)/shard_map/ppermute | solution.py:443
  122.5 28.9 %collective-permute-start.17 = (bf16[2,96,2048]{2,1,0:T(8,128)(2,1)S(1)}, bf16[2,96,2048]{2,1,0:T(8,128)(2,1)S(1)}, u32[]{:S(2)}, u32[]{:S(2)}) collective-permute-start(bf16[2,96,2048]{2,1,0:T(8,128)(2,1)S(1)} %get-tuple-element.57.rest_6_.refs_4_), channel_id=1, source_target_pairs={{0,4},{2,6},{4,0},{6,2},{8,12},{10,14},{12,8},{14,10},{16,20},{18,... | collective-permute-start | bytes 2359304 | tf_op jit(solution)/shard_map/ppermute | solution.py:443
  123.2 20.8 %collective-permute-start.16 = (bf16[2,32,2048]{2,1,0:T(8,128)(2,1)S(1)}, bf16[2,32,2048]{2,1,0:T(8,128)(2,1)S(1)}, u32[]{:S(2)}, u32[]{:S(2)}) collective-permute-start(bf16[2,32,2048]{2,1,0:T(8,128)(2,1)S(1)} %get-tuple-element.58.refs_2_), channel_id=1, source_target_pairs={{0,4},{2,6},{4,0},{6,2},{8,12},{10,14},{12,8},{14,10},{16,20},{18,... | collective-permute-start | bytes 786440 | tf_op jit(solution)/shard_map/ppermute | solution.py:443
  151.7 6.6 %collective-permute-start.19 = (bf16[4,96,2048]{2,1,0:T(8,128)(2,1)S(1)}, bf16[4,96,2048]{2,1,0:T(8,128)(2,1)S(1)}, u32[]{:S(2)}, u32[]{:S(2)}) collective-permute-start(bf16[4,96,2048]{2,1,0:T(8,128)(2,1)S(1)} %get-tuple-element.61.refs_0_), channel_id=1, source_target_pairs={{0,2},{2,0},{4,6},{6,4},{8,10},{10,8},{12,14},{14,12},{16,18},{18,... | collective-permute-start | bytes 4718600 | tf_op jit(solution)/shard_map/ppermute | solution.py:443
  151.8 6.6 %collective-permute-start.20 = (bf16[4,96,2048]{2,1,0:T(8,128)(2,1)S(1)}, bf16[4,96,2048]{2,1,0:T(8,128)(2,1)S(1)}, u32[]{:S(2)}, u32[]{:S(2)}) collective-permute-start(bf16[4,96,2048]{2,1,0:T(8,128)(2,1)S(1)} %get-tuple-element.62.refs_2_.refs_4_), channel_id=1, source_target_pairs={{0,2},{2,0},{4,6},{6,4},{8,10},{10,8},{12,14},{14,12},{16,18},{18,... | collective-permute-start | bytes 4718600 | tf_op jit(solution)/shard_map/ppermute | solution.py:443
  152.3 36.4 %collective-permute-start.26 = (bf16[4,96,2048]{2,1,0:T(8,128)(2,1)S(1)}, bf16[4,96,2048]{2,1,0:T(8,128)(2,1)S(1)}, u32[]{:S(2)}, u32[]{:S(2)}) collective-permute-start(bf16[4,96,2048]{2,1,0:T(8,128)(2,1)S(1)} %get-tuple-element.62.refs_2_.refs_4_), channel_id=1, source_target_pairs={{0,4},{2,6},{4,0},{6,2},{8,12},{10,14},{12,8},{14,10},{16,20},{18,... | collective-permute-start | bytes 4718600 | tf_op jit(solution)/shard_map/ppermute | solution.py:443
  153.4 30.5 %collective-permute-start.14 = (bf16[2,96,2048]{2,1,0:T(8,128)(2,1)S(1)}, bf16[2,96,2048]{2,1,0:T(8,128)(2,1)S(1)}, u32[]{:S(2)}, u32[]{:S(2)}) collective-permute-start(bf16[2,96,2048]{2,1,0:T(8,128)(2,1)S(1)} %collective-permute-done.13.refs_0_), channel_id=1, source_target_pairs={{0,8},{2,10},{4,12},{6,14},{8,0},{10,2},{12,4},{14,6},{16,24},{18,... | collective-permute-start | bytes 2359304 | tf_op jit(solution)/shard_map/ppermute | solution.py:443
  155.0 28.0 %collective-permute-start.18 = (bf16[4,32,2048]{2,1,0:T(8,128)(2,1)S(1)}, bf16[4,32,2048]{2,1,0:T(8,128)(2,1)S(1)}, u32[]{:S(2)}, u32[]{:S(2)}) collective-permute-start(bf16[4,32,2048]{2,1,0:T(8,128)(2,1)S(1)} %get-tuple-element.60.refs_1_), channel_id=1, source_target_pairs={{0,16},{2,18},{4,20},{6,22},{8,24},{10,26},{12,28},{14,30},{16,0},... | collective-permute-start | bytes 1572872 | tf_op jit(solution)/shard_map/ppermute | solution.py:443
  184.0 25.5 %collective-permute-start.24 = (bf16[8,32,2048]{2,1,0:T(8,128)(2,1)S(1)}, bf16[8,32,2048]{2,1,0:T(8,128)(2,1)S(1)}, u32[]{:S(2)}, u32[]{:S(2)}) collective-permute-start(bf16[8,32,2048]{2,1,0:T(8,128)(2,1)S(1)} %get-tuple-element.65.refs_3_), channel_id=1, source_target_pairs={{0,8},{2,10},{4,12},{6,14},{8,0},{10,2},{12,4},{14,6},{16,24},{18,... | collective-permute-start | bytes 3145736 | tf_op jit(solution)/shard_map/ppermute | solution.py:443
  188.6 21.4 %collective-permute-start.27 = (bf16[4,96,2048]{2,1,0:T(8,128)(2,1)S(1)}, bf16[4,96,2048]{2,1,0:T(8,128)(2,1)S(1)}, u32[]{:S(2)}, u32[]{:S(2)}) collective-permute-start(bf16[4,96,2048]{2,1,0:T(8,128)(2,1)S(1)} %collective-permute-done.26.refs_0_), channel_id=1, source_target_pairs={{0,2},{2,0},{4,6},{6,4},{8,10},{10,8},{12,14},{14,12},{16,18},{18,... | collective-permute-start | bytes 4718600 | tf_op jit(solution)/shard_map/ppermute | solution.py:443
  188.6 21.4 %collective-permute-start.22 = (bf16[2,96,2048]{2,1,0:T(8,128)(2,1)S(1)}, bf16[2,96,2048]{2,1,0:T(8,128)(2,1)S(1)}, u32[]{:S(2)}, u32[]{:S(2)}) collective-permute-start(bf16[2,96,2048]{2,1,0:T(8,128)(2,1)S(1)} %get-tuple-element.64.refs_2_.refs_8_), channel_id=1, source_target_pairs={{0,4},{2,6},{4,0},{6,2},{8,12},{10,14},{12,8},{14,10},{16,20},{18,... | collective-permute-start | bytes 2359304 | tf_op jit(solution)/shard_map/ppermute | solution.py:443
  189.8 20.2 %collective-permute-start.28 = (bf16[8,32,2048]{2,1,0:T(8,128)(2,1)S(1)}, bf16[8,32,2048]{2,1,0:T(8,128)(2,1)S(1)}, u32[]{:S(2)}, u32[]{:S(2)}) collective-permute-start(bf16[8,32,2048]{2,1,0:T(8,128)(2,1)S(1)} %get-tuple-element.65.refs_3_), channel_id=1, source_target_pairs={{0,2},{2,0},{4,6},{6,4},{8,10},{10,8},{12,14},{14,12},{16,18},{18,... | collective-permute-start | bytes 3145736 | tf_op jit(solution)/shard_map/ppermute | solution.py:443
  209.5 4.9 %collective-permute-start.25 = (bf16[8,32,2048]{2,1,0:T(8,128)(2,1)S(1)}, bf16[8,32,2048]{2,1,0:T(8,128)(2,1)S(1)}, u32[]{:S(2)}, u32[]{:S(2)}) collective-permute-start(bf16[8,32,2048]{2,1,0:T(8,128)(2,1)S(1)} %collective-permute-done.24.refs_6_), channel_id=1, source_target_pairs={{0,2},{2,0},{4,6},{6,4},{8,10},{10,8},{12,14},{14,12},{16,18},{18,... | collective-permute-start | bytes 3145736 | tf_op jit(solution)/shard_map/ppermute | solution.py:443
  209.5 4.6 %collective-permute-start.21 = (bf16[2,96,2048]{2,1,0:T(8,128)(2,1)S(1)}, bf16[2,96,2048]{2,1,0:T(8,128)(2,1)S(1)}, u32[]{:S(2)}, u32[]{:S(2)}) collective-permute-start(bf16[2,96,2048]{2,1,0:T(8,128)(2,1)S(1)} %get-tuple-element.64.refs_2_.refs_8_), channel_id=1, source_target_pairs={{0,2},{2,0},{4,6},{6,4},{8,10},{10,8},{12,14},{14,12},{16,18},{18,... | collective-permute-start | bytes 2359304 | tf_op jit(solution)/shard_map/ppermute | solution.py:443
  210.0 4.4 %collective-permute-start.23 = (bf16[2,96,2048]{2,1,0:T(8,128)(2,1)S(1)}, bf16[2,96,2048]{2,1,0:T(8,128)(2,1)S(1)}, u32[]{:S(2)}, u32[]{:S(2)}) collective-permute-start(bf16[2,96,2048]{2,1,0:T(8,128)(2,1)S(1)} %collective-permute-done.22.refs_5_), channel_id=1, source_target_pairs={{0,2},{2,0},{4,6},{6,4},{8,10},{10,8},{12,14},{14,12},{16,18},{18,... | collective-permute-start | bytes 2359304 | tf_op jit(solution)/shard_map/ppermute | solution.py:443

commit v10 on v9

--- a/solution.py
+++ b/solution.py
@@ -21,7 +21,7 @@
 CORE_BIT = 1
 X_BIT = 2
 VMEM_BYTES = 24 * 1024 * 1024
-MORE_VMEM_BYTES = 44 * 1024 * 1024
+MORE_VMEM_BYTES = 41 * 1024 * 1024
 
 
 def in_vmem(count=1):
@@ -111,12 +111,12 @@
             copy(i).wait()
 
 
-def pack(after, table, src, plans, rows):
+def pack(after, table, src, plans, sizes):
     return pl.pallas_call(
         functools.partial(pack_kernel, tuple(plans)),
         out_shape=[
             jax.ShapeDtypeStruct((len(items), rows, src.shape[2]), src.dtype)
-            for items in plans
+            for items, rows in zip(plans, sizes)
         ],
         in_specs=in_smem() + in_hbm() + anywhere(len(after)),
         out_specs=in_vmem(len(plans)),
@@ -512,7 +512,8 @@
     first_got = swap(packed, CORE_BIT)
     falling = range(top - 1, -1, -1)
     plans = [items_of(theirs(merged[k]), slots, 0, cut) for k in falling]
-    packed = pack([packed], table, gradient, plans, cut)
+    plans.append(first_items(same))
+    *packed, mine = pack([packed], table, gradient, plans, [cut] * top + [rest])
     got = {k: swap(block, CORE_BIT) for k, block in zip(falling, packed)}
     after = [packed[0]]
 
@@ -532,9 +533,11 @@
             home[o] = Block(made[1], n * slots)
         return [made[0]]
 
-    parts = (half, half, len(merged[top]) * slots * split)
-    away, kept, far = add_taken(
-        after, table, gradient, first_items(same), first_got, parts
+    away, kept, far = combine(
+        after,
+        summed(mine, first_got, 0, half),
+        summed(mine, first_got, half, 2 * half),
+        summed(mine, first_got, 2 * half, mine.shape[0]),
     )
     after = [away]
     other_got = swap(away, other_bits[0])

time: 217 us -> 217 us (level)
    pallas_call x3 -> x2, Pallas kernels: 7.69 us -> 4.79 us  [add_taken(): pl.pallas_call(functools.partial(add_taken_kernel, items, parts), out_sha...]
  transfers between devices with their start and end apart: 29 -> 29, of which waited for: 16 -> 17; matrix products, arithmetic and copies ran while one was open for 0% -> 0% of each run, Pallas kernels for 10% -> 10%
where the time goes in v10:
time: 217 us; the launch traced here: 216 us
  waiting for transfers between devices  145 us (67%)
  starting transfers between devices  37.3 us (17%)
  Pallas kernels  32.4 us (15%)
    ppermute x28, waiting for transfers between devices, swap(): return lax.ppermute(value, 'dp', [(i, i ^ bit) for i in range(count)])  141 us
    ppermute x28, starting transfers between devices, swap(): return lax.ppermute(value, 'dp', [(i, i ^ bit) for i in range(count)])  35.9 us
    pallas_call x3, Pallas kernels, spread(): pl.pallas_call(functools.partial(spread_kernel, plans, slots), out_shape=...  9.55 us
    pallas_call x1, Pallas kernels, pack(): pl.pallas_call(functools.partial(pack_kernel, tuple(plans)), out_shape=[j...  6.26 us
    pallas_call x2, Pallas kernels, add_taken(): pl.pallas_call(functools.partial(add_taken_kernel, items, parts), out_sha...  4.79 us
  transfers between devices with their start and end apart: 29, of which 17 were waited for; matrix products, arithmetic and copies ran while one was open for 0% of the time, Pallas kernels for 10%

profile of v10, /device:TPU:0, one launch (start us, length us, event | category | flops | bytes accessed | tf_op | source)
XLA Modules:
  0.0 216.1 jit_solution(12150808916757111819)
XLA Ops:
  1.3 3.8 %shard_map.50 = (s32[32]{0:T(128)S(1)}, bf16[22,32,2048]{2,1,0:T(8,128)(2,1)S(1)}) custom-call(s32[1]{0:T(128)} %bitcast.me_ref, s32[24]{0:T(128)S(1)} %copy-done.1, bf16[24,128,2048]{2,1,0:T(8,128)(2,1)} %bitcast.6), custom_call_target="tpu_custom_call" | custom-call | tf_op jit(solution)/shard_map/pallas_call | solution.py:141
  5.6 6.3 %shard_map.51 = (bf16[6,96,2048]{2,1,0:T(8,128)(2,1)S(1)}, bf16[8,96,2048]{2,1,0:T(8,128)(2,1)}, bf16[22,32,2048]{2,1,0:T(8,128)(2,1)S(1)}) custom-call(s32[32]{0:T(128)S(1)} %get-tuple-element.37.table_ref, bf16[24,128,2048]{2,1,0:T(8,128)(2,1)} %bitcast.7, bf16[22,32,2048]{2,1,0:T(8,128)(2,1)S(1)} %get-tuple-element.38.rest_0_), custom_call_target="tpu_custom_call" | custom-call | tf_op jit(solution)/shard_map/pallas_call | solution.py:115
  12.7 2.6 %collective-permute-start.4 = (bf16[8,32,2048]{2,1,0:T(8,128)(2,1)S(1)}, bf16[8,32,2048]{2,1,0:T(8,128)(2,1)S(1)}, u32[]{:S(2)}, u32[]{:S(2)}) collective-permute-start(bf16[8,32,2048]{2,1,0:T(8,128)(2,1)S(1)} %get-tuple-element.42.rest_0_), channel_id=1, source_target_pairs={{0,8},{2,10},{4,12},{6,14},{8,0},{10,2},{12,4},{14,6},{16,24},{18,... | collective-permute-start | bytes 3145736 | tf_op jit(solution)/shard_map/ppermute | solution.py:443
  16.8 2.3 %collective-permute-done.1.got_ref = bf16[6,96,2048]{2,1,0:T(8,128)(2,1)S(1)} collective-permute-done((bf16[6,96,2048]{2,1,0:T(8,128)(2,1)S(1)}, bf16[6,96,2048]{2,1,0:T(8,128)(2,1)S(1)}, u32[]{:S(2)}, u32[]{:S(2)}) %collective-permute-start.1) | collective-permute-done | bytes 2359328 | tf_op jit(solution)/shard_map/ppermute | solution.py:443
  19.1 2.2 %shard_map.53 = (bf16[4,96,2048]{2,1,0:T(8,128)(2,1)S(1)}, bf16[2,96,2048]{2,1,0:T(8,128)(2,1)S(1)}) custom-call(s32[32]{0:T(128)S(1)} %get-tuple-element.37.table_ref, bf16[24,128,2048]{2,1,0:T(8,128)(2,1)} %bitcast.8, bf16[6,96,2048]{2,1,0:T(8,128)(2,1)S(1)} %collective-permute-done.1.got_ref, bf16[8,32,2048]{2,1,0:T(8,128)(2,1)S(1)} %get-tuple-element.42.rest_0_), custom_call_target="tpu_custom_call" | custom-call | tf_op jit(solution)/shard_map/pallas_call | solution.py:175
  21.3 1.8 collective-permute-start.5
  23.1 12.7 %collective-permute-done.3.refs_1_ = bf16[6,32,2048]{2,1,0:T(8,128)(2,1)S(1)} collective-permute-done((bf16[6,32,2048]{2,1,0:T(8,128)(2,1)S(1)}, bf16[6,32,2048]{2,1,0:T(8,128)(2,1)S(1)}, u32[]{:S(2)}, u32[]{:S(2)}) %collective-permute-start.3) | collective-permute-done | bytes 786464 | tf_op jit(solution)/shard_map/ppermute | solution.py:443
  35.8 3.4 %collective-permute-done.4.refs_3_ = bf16[8,32,2048]{2,1,0:T(8,128)(2,1)S(1)} collective-permute-done((bf16[8,32,2048]{2,1,0:T(8,128)(2,1)S(1)}, bf16[8,32,2048]{2,1,0:T(8,128)(2,1)S(1)}, u32[]{:S(2)}, u32[]{:S(2)}) %collective-permute-start.4) | collective-permute-done | bytes 1048608 | tf_op jit(solution)/shard_map/ppermute | solution.py:443
  39.3 1.8 collective-permute-start.6
  41.2 2.5 %collective-permute-start.7 = (bf16[4,32,2048]{2,1,0:T(8,128)(2,1)S(1)}, bf16[4,32,2048]{2,1,0:T(8,128)(2,1)S(1)}, u32[]{:S(2)}, u32[]{:S(2)}) collective-permute-start(bf16[4,32,2048]{2,1,0:T(8,128)(2,1)S(1)} %get-tuple-element.50), channel_id=1, source_target_pairs={{0,16},{2,18},{4,20},{6,22},{8,24},{10,26},{12,28},{14,30},{16,0},... | collective-permute-start | bytes 1572872 | tf_op jit(solution)/shard_map/ppermute | solution.py:443
  43.6 2.6 %shard_map.55 = (bf16[2,96,2048]{2,1,0:T(8,128)(2,1)S(1)}, bf16[6,96,2048]{2,1,0:T(8,128)(2,1)S(1)}) custom-call(s32[32]{0:T(128)S(1)} %get-tuple-element.37.table_ref, bf16[24,128,2048]{2,1,0:T(8,128)(2,1)} %bitcast.9, bf16[8,96,2048]{2,1,0:T(8,128)(2,1)S(1)} %collective-permute-done.got_ref, bf16[2,96,2048]{2,1,0:T(8,128)(2,1)S(1)} %get-tuple-element.47.rest_0_), custom_call_target="tpu_custom_call" | custom-call | tf_op jit(solution)/shard_map/pallas_call | solution.py:175
  46.2 22.8 %collective-permute-done.7.refs_4_ = bf16[4,32,2048]{2,1,0:T(8,128)(2,1)S(1)} collective-permute-done((bf16[4,32,2048]{2,1,0:T(8,128)(2,1)S(1)}, bf16[4,32,2048]{2,1,0:T(8,128)(2,1)S(1)}, u32[]{:S(2)}, u32[]{:S(2)}) %collective-permute-start.7) | collective-permute-done | bytes 524320 | tf_op jit(solution)/shard_map/ppermute | solution.py:443
  70.2 2.5 %collective-permute-start.10 = (bf16[2,96,2048]{2,1,0:T(8,128)(2,1)S(1)}, bf16[2,96,2048]{2,1,0:T(8,128)(2,1)S(1)}, u32[]{:S(2)}, u32[]{:S(2)}) collective-permute-start(bf16[2,96,2048]{2,1,0:T(8,128)(2,1)S(1)} %get-tuple-element.54), channel_id=1, source_target_pairs={{0,16},{2,18},{4,20},{6,22},{8,24},{10,26},{12,28},{14,30},{16,0},... | collective-permute-start | bytes 2359304 | tf_op jit(solution)/shard_map/ppermute | solution.py:443
  74.2 1.7 collective-permute-start.9
  76.3 20.1 %collective-permute-done.11.rest_5_ = bf16[2,32,2048]{2,1,0:T(8,128)(2,1)S(1)} collective-permute-done((bf16[2,32,2048]{2,1,0:T(8,128)(2,1)S(1)}, bf16[2,32,2048]{2,1,0:T(8,128)(2,1)S(1)}, u32[]{:S(2)}, u32[]{:S(2)}) %collective-permute-start.11) | collective-permute-done | bytes 262176 | tf_op jit(solution)/shard_map/ppermute | solution.py:443
  96.3 10.3 %collective-permute-done.10.rest_3_ = bf16[2,96,2048]{2,1,0:T(8,128)(2,1)S(1)} collective-permute-done((bf16[2,96,2048]{2,1,0:T(8,128)(2,1)S(1)}, bf16[2,96,2048]{2,1,0:T(8,128)(2,1)S(1)}, u32[]{:S(2)}, u32[]{:S(2)}) %collective-permute-start.10) | collective-permute-done | bytes 786464 | tf_op jit(solution)/shard_map/ppermute | solution.py:443
  109.2 3.7 %collective-permute-done.12.refs_1_ = f32[2,128,128]{2,1,0:T(8,128)S(1)} collective-permute-done((f32[2,128,128]{2,1,0:T(8,128)S(1)}, f32[2,128,128]{2,1,0:T(8,128)S(1)}, u32[]{:S(2)}, u32[]{:S(2)}) %collective-permute-start.12) | collective-permute-done | bytes 131104 | tf_op jit(solution)/shard_map/ppermute | solution.py:659
  112.9 3.5 %shard_map.58 = (bf16[2,96,2048]{2,1,0:T(8,128)(2,1)S(1)}, bf16[2,32,2048]{2,1,0:T(8,128)(2,1)S(1)}) custom-call(f32[2,128,128]{2,1,0:T(8,128)S(1)} %get-tuple-element.57.refs_0_, f32[2,128,128]{2,1,0:T(8,128)S(1)} %collective-permute-done.12.refs_1_, bf16[2,128,2048]{2,1,0:T(8,128)(2,1)S(1)} %get-tuple-element.58.refs_2_), custom_call_target="tpu_custom_call" | custom-call | tf_op jit(solution)/shard_map/pallas_call | solution.py:429
  116.4 2.5 %collective-permute-start.13 = (bf16[2,96,2048]{2,1,0:T(8,128)(2,1)S(1)}, bf16[2,96,2048]{2,1,0:T(8,128)(2,1)S(1)}, u32[]{:S(2)}, u32[]{:S(2)}) collective-permute-start(bf16[2,96,2048]{2,1,0:T(8,128)(2,1)S(1)} %get-tuple-element.59.rest_6_.refs_4_), channel_id=1, source_target_pairs={{0,16},{2,18},{4,20},{6,22},{8,24},{10,26},{12,28},{14,30},{16,0},... | collective-permute-start | bytes 2359304 | tf_op jit(solution)/shard_map/ppermute | solution.py:443
  118.9 2.5 %collective-permute-start.15 = (bf16[2,96,2048]{2,1,0:T(8,128)(2,1)S(1)}, bf16[2,96,2048]{2,1,0:T(8,128)(2,1)S(1)}, u32[]{:S(2)}, u32[]{:S(2)}) collective-permute-start(bf16[2,96,2048]{2,1,0:T(8,128)(2,1)S(1)} %get-tuple-element.59.rest_6_.refs_4_), channel_id=1, source_target_pairs={{0,8},{2,10},{4,12},{6,14},{8,0},{10,2},{12,4},{14,6},{16,24},{18,... | collective-permute-start | bytes 2359304 | tf_op jit(solution)/shard_map/ppermute | solution.py:443
  123.4 2.3 %shard_map.59 = (f32[2,128,2048]{2,1,0:T(8,128)}, f32[8,128]{1,0:T(8,128)S(1)}) custom-call(s32[32]{0:T(128)S(1)} %get-tuple-element.37.table_ref, f32[2,128,2048]{2,1,0:T(8,128)S(1)} %bitcast.5, bf16[6,96,2048]{2,1,0:T(8,128)(2,1)S(1)} %get-tuple-element.48.refs_0_.rest_0_, bf16[2,96,2048]{2,1,0:T(8,128)(2,1)S(1)} %collective-permute-done.8.rest_1_, ...), custom_call_target="tpu_custom_call" | custom-call | tf_op jit(solution)/shard_map/pallas_call | solution.py:348
  125.7 17.5 %collective-permute-done.16.refs_3_ = bf16[2,32,2048]{2,1,0:T(8,128)(2,1)S(1)} collective-permute-done((bf16[2,32,2048]{2,1,0:T(8,128)(2,1)S(1)}, bf16[2,32,2048]{2,1,0:T(8,128)(2,1)S(1)}, u32[]{:S(2)}, u32[]{:S(2)}) %collective-permute-start.16) | collective-permute-done | bytes 262176 | tf_op jit(solution)/shard_map/ppermute | solution.py:443
  143.2 7.3 %collective-permute-done.13.refs_0_ = bf16[2,96,2048]{2,1,0:T(8,128)(2,1)S(1)} collective-permute-done((bf16[2,96,2048]{2,1,0:T(8,128)(2,1)S(1)}, bf16[2,96,2048]{2,1,0:T(8,128)(2,1)S(1)}, u32[]{:S(2)}, u32[]{:S(2)}) %collective-permute-start.13) | collective-permute-done | bytes 786464 | tf_op jit(solution)/shard_map/ppermute | solution.py:443
  152.4 1.6 collective-permute-start.14
  154.0 3.4 %collective-permute-start.18 = (bf16[4,32,2048]{2,1,0:T(8,128)(2,1)S(1)}, bf16[4,32,2048]{2,1,0:T(8,128)(2,1)S(1)}, u32[]{:S(2)}, u32[]{:S(2)}) collective-permute-start(bf16[4,32,2048]{2,1,0:T(8,128)(2,1)S(1)} %get-tuple-element.62.refs_1_), channel_id=1, source_target_pairs={{0,16},{2,18},{4,20},{6,22},{8,24},{10,26},{12,28},{14,30},{16,0},... | collective-permute-start | bytes 1572872 | tf_op jit(solution)/shard_map/ppermute | solution.py:443
  157.5 2.9 %shard_map.61 = (bf16[24,128,2048]{2,1,0:T(8,128)(2,1)}, f32[8,128]{1,0:T(8,128)S(1)}) custom-call(s32[32]{0:T(128)S(1)} %get-tuple-element.37.table_ref, bf16[4,96,2048]{2,1,0:T(8,128)(2,1)S(1)} %get-tuple-element.63.refs_0_, bf16[4,96,2048]{2,1,0:T(8,128)(2,1)S(1)} %collective-permute-done.19.refs_1_, ...), custom_call_target="tpu_custom_call" | custom-call | tf_op jit(solution)/shard_map/pallas_call | solution.py:275
  160.3 21.7 %collective-permute-done.18.refs_2_ = bf16[4,32,2048]{2,1,0:T(8,128)(2,1)S(1)} collective-permute-done((bf16[4,32,2048]{2,1,0:T(8,128)(2,1)S(1)}, bf16[4,32,2048]{2,1,0:T(8,128)(2,1)S(1)}, u32[]{:S(2)}, u32[]{:S(2)}) %collective-permute-start.18) | collective-permute-done | bytes 524320 | tf_op jit(solution)/shard_map/ppermute | solution.py:443
  183.0 3.4 %collective-permute-start.24 = (bf16[8,32,2048]{2,1,0:T(8,128)(2,1)S(1)}, bf16[8,32,2048]{2,1,0:T(8,128)(2,1)S(1)}, u32[]{:S(2)}, u32[]{:S(2)}) collective-permute-start(bf16[8,32,2048]{2,1,0:T(8,128)(2,1)S(1)} %get-tuple-element.67.refs_3_), channel_id=1, source_target_pairs={{0,8},{2,10},{4,12},{6,14},{8,0},{10,2},{12,4},{14,6},{16,24},{18,... | collective-permute-start | bytes 3145736 | tf_op jit(solution)/shard_map/ppermute | solution.py:443
  186.4 1.4 collective-permute-done.26.refs_0_
  189.0 19.6 %collective-permute-done.24.refs_6_ = bf16[8,32,2048]{2,1,0:T(8,128)(2,1)S(1)} collective-permute-done((bf16[8,32,2048]{2,1,0:T(8,128)(2,1)S(1)}, bf16[8,32,2048]{2,1,0:T(8,128)(2,1)S(1)}, u32[]{:S(2)}, u32[]{:S(2)}) %collective-permute-start.24) | collective-permute-done | bytes 1048608 | tf_op jit(solution)/shard_map/ppermute | solution.py:443
  209.2 4.2 %shard_map.63 = (bf16[24,128,2048]{2,1,0:T(8,128)(2,1)}, f32[8,128]{1,0:T(8,128)}) custom-call(s32[32]{0:T(128)S(1)} %get-tuple-element.37.table_ref, bf16[4,96,2048]{2,1,0:T(8,128)(2,1)S(1)} %collective-permute-done.26.refs_0_, bf16[4,96,2048]{2,1,0:T(8,128)(2,1)S(1)} %collective-permute-done.27.refs_1_, ...), custom_call_target="tpu_custom_call", output_to_operand_aliasing={{0}: (8, {})} | custom-call | tf_op jit(solution)/shard_map/pallas_call | solution.py:275
  213.6 2.5 %shard_map.64 = (bf16[24,128,2048]{2,1,0:T(8,128)(2,1)}, f32[8,128]{1,0:T(8,128)}) custom-call(s32[32]{0:T(128)S(1)} %get-tuple-element.37.table_ref, bf16[2,96,2048]{2,1,0:T(8,128)(2,1)S(1)} %collective-permute-done.21.refs_0_, bf16[2,96,2048]{2,1,0:T(8,128)(2,1)S(1)} %collective-permute-done.23.refs_1_, ...), custom_call_target="tpu_custom_call", output_to_operand_aliasing={{0}: (4, {})} | custom-call | tf_op jit(solution)/shard_map/pallas_call | solution.py:275
  (45 shorter events, 16.1 us)
Async XLA Ops:
  0.6 0.7 copy-start.1
  5.1 7.4 %collective-permute-start.2 = (bf16[22,32,2048]{2,1,0:T(8,128)(2,1)S(1)}, bf16[22,32,2048]{2,1,0:T(8,128)(2,1)S(1)}, u32[]{:S(2)}, u32[]{:S(2)}) collective-permute-start(bf16[22,32,2048]{2,1,0:T(8,128)(2,1)S(1)} %get-tuple-element.38.rest_0_), channel_id=1, source_target_pairs={{0,2},{2,0},{4,6},{6,4},{8,10},{10,8},{12,14},{14,12},{16,18},{18,... | collective-permute-start | bytes 8650760 | tf_op jit(solution)/shard_map/ppermute | solution.py:443
  11.9 7.2 %collective-permute-start.1 = (bf16[6,96,2048]{2,1,0:T(8,128)(2,1)S(1)}, bf16[6,96,2048]{2,1,0:T(8,128)(2,1)S(1)}, u32[]{:S(2)}, u32[]{:S(2)}) collective-permute-start(bf16[6,96,2048]{2,1,0:T(8,128)(2,1)S(1)} %get-tuple-element.40.refs_2_), channel_id=1, source_target_pairs={{0,2},{2,0},{4,6},{6,4},{8,10},{10,8},{12,14},{14,12},{16,18},{18,... | collective-permute-start | bytes 7077896 | tf_op jit(solution)/shard_map/ppermute | solution.py:443
  12.0 31.7 %collective-permute-start = (bf16[8,96,2048]{2,1,0:T(8,128)(2,1)}, bf16[8,96,2048]{2,1,0:T(8,128)(2,1)S(1)}, u32[]{:S(2)}, u32[]{:S(2)}) collective-permute-start(bf16[8,96,2048]{2,1,0:T(8,128)(2,1)} %get-tuple-element.39), channel_id=1, source_target_pairs={{0,2},{2,0},{4,6},{6,4},{8,10},{10,8},{12,14},{14,12},{16,18},{18,... | collective-permute-start | bytes 9437192 | tf_op jit(solution)/shard_map/ppermute | solution.py:443
  12.7 26.4 %collective-permute-start.4 = (bf16[8,32,2048]{2,1,0:T(8,128)(2,1)S(1)}, bf16[8,32,2048]{2,1,0:T(8,128)(2,1)S(1)}, u32[]{:S(2)}, u32[]{:S(2)}) collective-permute-start(bf16[8,32,2048]{2,1,0:T(8,128)(2,1)S(1)} %get-tuple-element.42.rest_0_), channel_id=1, source_target_pairs={{0,8},{2,10},{4,12},{6,14},{8,0},{10,2},{12,4},{14,6},{16,24},{18,... | collective-permute-start | bytes 3145736 | tf_op jit(solution)/shard_map/ppermute | solution.py:443
  15.4 20.4 %collective-permute-start.3 = (bf16[6,32,2048]{2,1,0:T(8,128)(2,1)S(1)}, bf16[6,32,2048]{2,1,0:T(8,128)(2,1)S(1)}, u32[]{:S(2)}, u32[]{:S(2)}) collective-permute-start(bf16[6,32,2048]{2,1,0:T(8,128)(2,1)S(1)} %get-tuple-element.44), channel_id=1, source_target_pairs={{0,4},{2,6},{4,0},{6,2},{8,12},{10,14},{12,8},{14,10},{16,20},{18,... | collective-permute-start | bytes 2359304 | tf_op jit(solution)/shard_map/ppermute | solution.py:443
  21.3 47.7 %collective-permute-start.5 = (bf16[4,96,2048]{2,1,0:T(8,128)(2,1)S(1)}, bf16[4,96,2048]{2,1,0:T(8,128)(2,1)S(1)}, u32[]{:S(2)}, u32[]{:S(2)}) collective-permute-start(bf16[4,96,2048]{2,1,0:T(8,128)(2,1)S(1)} %get-tuple-element.46.refs_4_), channel_id=1, source_target_pairs={{0,4},{2,6},{4,0},{6,2},{8,12},{10,14},{12,8},{14,10},{16,20},{18,... | collective-permute-start | bytes 4718600 | tf_op jit(solution)/shard_map/ppermute | solution.py:443
  39.3 30.6 %collective-permute-start.6 = (bf16[2,96,2048]{2,1,0:T(8,128)(2,1)S(1)}, bf16[2,96,2048]{2,1,0:T(8,128)(2,1)S(1)}, u32[]{:S(2)}, u32[]{:S(2)}) collective-permute-start(bf16[2,96,2048]{2,1,0:T(8,128)(2,1)S(1)} %get-tuple-element.47.rest_0_), channel_id=1, source_target_pairs={{0,8},{2,10},{4,12},{6,14},{8,0},{10,2},{12,4},{14,6},{16,24},{18,... | collective-permute-start | bytes 2359304 | tf_op jit(solution)/shard_map/ppermute | solution.py:443
  41.2 27.9 %collective-permute-start.7 = (bf16[4,32,2048]{2,1,0:T(8,128)(2,1)S(1)}, bf16[4,32,2048]{2,1,0:T(8,128)(2,1)S(1)}, u32[]{:S(2)}, u32[]{:S(2)}) collective-permute-start(bf16[4,32,2048]{2,1,0:T(8,128)(2,1)S(1)} %get-tuple-element.50), channel_id=1, source_target_pairs={{0,16},{2,18},{4,20},{6,22},{8,24},{10,26},{12,28},{14,30},{16,0},... | collective-permute-start | bytes 1572872 | tf_op jit(solution)/shard_map/ppermute | solution.py:443
  69.9 36.9 %copy-start = (f32[1,2,128,2048]{3,2,1,0:T(8,128)S(1)}, f32[1,2,128,2048]{3,2,1,0:T(8,128)}, u32[]{:S(2)}) copy-start(f32[1,2,128,2048]{3,2,1,0:T(8,128)} %param.5) | copy-start | bytes 6291460
  70.2 36.3 %collective-permute-start.10 = (bf16[2,96,2048]{2,1,0:T(8,128)(2,1)S(1)}, bf16[2,96,2048]{2,1,0:T(8,128)(2,1)S(1)}, u32[]{:S(2)}, u32[]{:S(2)}) collective-permute-start(bf16[2,96,2048]{2,1,0:T(8,128)(2,1)S(1)} %get-tuple-element.54), channel_id=1, source_target_pairs={{0,16},{2,18},{4,20},{6,22},{8,24},{10,26},{12,28},{14,30},{16,0},... | collective-permute-start | bytes 2359304 | tf_op jit(solution)/shard_map/ppermute | solution.py:443
  72.8 33.8 %collective-permute-start.8 = (bf16[2,96,2048]{2,1,0:T(8,128)(2,1)S(1)}, bf16[2,96,2048]{2,1,0:T(8,128)(2,1)S(1)}, u32[]{:S(2)}, u32[]{:S(2)}) collective-permute-start(bf16[2,96,2048]{2,1,0:T(8,128)(2,1)S(1)} %get-tuple-element.52), channel_id=1, source_target_pairs={{0,4},{2,6},{4,0},{6,2},{8,12},{10,14},{12,8},{14,10},{16,20},{18,... | collective-permute-start | bytes 2359304 | tf_op jit(solution)/shard_map/ppermute | solution.py:443
  74.2 32.6 %collective-permute-start.9 = (bf16[2,96,2048]{2,1,0:T(8,128)(2,1)S(1)}, bf16[2,96,2048]{2,1,0:T(8,128)(2,1)S(1)}, u32[]{:S(2)}, u32[]{:S(2)}) collective-permute-start(bf16[2,96,2048]{2,1,0:T(8,128)(2,1)S(1)} %get-tuple-element.53), channel_id=1, source_target_pairs={{0,8},{2,10},{4,12},{6,14},{8,0},{10,2},{12,4},{14,6},{16,24},{18,... | collective-permute-start | bytes 2359304 | tf_op jit(solution)/shard_map/ppermute | solution.py:443
  75.9 20.5 %collective-permute-start.11 = (bf16[2,32,2048]{2,1,0:T(8,128)(2,1)S(1)}, bf16[2,32,2048]{2,1,0:T(8,128)(2,1)S(1)}, u32[]{:S(2)}, u32[]{:S(2)}) collective-permute-start(bf16[2,32,2048]{2,1,0:T(8,128)(2,1)S(1)} %get-tuple-element.56), channel_id=1, source_target_pairs={{0,4},{2,6},{4,0},{6,2},{8,12},{10,14},{12,8},{14,10},{16,20},{18,... | collective-permute-start | bytes 786440 | tf_op jit(solution)/shard_map/ppermute | solution.py:443
  107.9 5.0 %collective-permute-start.12 = (f32[2,128,128]{2,1,0:T(8,128)S(1)}, f32[2,128,128]{2,1,0:T(8,128)S(1)}, u32[]{:S(2)}, u32[]{:S(2)}) collective-permute-start(f32[2,128,128]{2,1,0:T(8,128)S(1)} %get-tuple-element.57.refs_0_), channel_id=1, source_target_pairs={{0,1},{1,0},{2,3},{3,2},{4,5},{5,4},{6,7},{7,6},{8,9},{9,8},{10,11... | collective-permute-start | bytes 393224 | tf_op jit(solution)/shard_map/ppermute | solution.py:659
  116.4 34.1 %collective-permute-start.13 = (bf16[2,96,2048]{2,1,0:T(8,128)(2,1)S(1)}, bf16[2,96,2048]{2,1,0:T(8,128)(2,1)S(1)}, u32[]{:S(2)}, u32[]{:S(2)}) collective-permute-start(bf16[2,96,2048]{2,1,0:T(8,128)(2,1)S(1)} %get-tuple-element.59.rest_6_.refs_4_), channel_id=1, source_target_pairs={{0,16},{2,18},{4,20},{6,22},{8,24},{10,26},{12,28},{14,30},{16,0},... | collective-permute-start | bytes 2359304 | tf_op jit(solution)/shard_map/ppermute | solution.py:443
  118.9 31.7 %collective-permute-start.15 = (bf16[2,96,2048]{2,1,0:T(8,128)(2,1)S(1)}, bf16[2,96,2048]{2,1,0:T(8,128)(2,1)S(1)}, u32[]{:S(2)}, u32[]{:S(2)}) collective-permute-start(bf16[2,96,2048]{2,1,0:T(8,128)(2,1)S(1)} %get-tuple-element.59.rest_6_.refs_4_), channel_id=1, source_target_pairs={{0,8},{2,10},{4,12},{6,14},{8,0},{10,2},{12,4},{14,6},{16,24},{18,... | collective-permute-start | bytes 2359304 | tf_op jit(solution)/shard_map/ppermute | solution.py:443
  121.4 29.2 %collective-permute-start.17 = (bf16[2,96,2048]{2,1,0:T(8,128)(2,1)S(1)}, bf16[2,96,2048]{2,1,0:T(8,128)(2,1)S(1)}, u32[]{:S(2)}, u32[]{:S(2)}) collective-permute-start(bf16[2,96,2048]{2,1,0:T(8,128)(2,1)S(1)} %get-tuple-element.59.rest_6_.refs_4_), channel_id=1, source_target_pairs={{0,4},{2,6},{4,0},{6,2},{8,12},{10,14},{12,8},{14,10},{16,20},{18,... | collective-permute-start | bytes 2359304 | tf_op jit(solution)/shard_map/ppermute | solution.py:443
  122.0 21.2 %collective-permute-start.16 = (bf16[2,32,2048]{2,1,0:T(8,128)(2,1)S(1)}, bf16[2,32,2048]{2,1,0:T(8,128)(2,1)S(1)}, u32[]{:S(2)}, u32[]{:S(2)}) collective-permute-start(bf16[2,32,2048]{2,1,0:T(8,128)(2,1)S(1)} %get-tuple-element.60.refs_2_), channel_id=1, source_target_pairs={{0,4},{2,6},{4,0},{6,2},{8,12},{10,14},{12,8},{14,10},{16,20},{18,... | collective-permute-start | bytes 786440 | tf_op jit(solution)/shard_map/ppermute | solution.py:443
  150.9 6.6 %collective-permute-start.19 = (bf16[4,96,2048]{2,1,0:T(8,128)(2,1)S(1)}, bf16[4,96,2048]{2,1,0:T(8,128)(2,1)S(1)}, u32[]{:S(2)}, u32[]{:S(2)}) collective-permute-start(bf16[4,96,2048]{2,1,0:T(8,128)(2,1)S(1)} %get-tuple-element.63.refs_0_), channel_id=1, source_target_pairs={{0,2},{2,0},{4,6},{6,4},{8,10},{10,8},{12,14},{14,12},{16,18},{18,... | collective-permute-start | bytes 4718600 | tf_op jit(solution)/shard_map/ppermute | solution.py:443
  150.9 6.5 %collective-permute-start.20 = (bf16[4,96,2048]{2,1,0:T(8,128)(2,1)S(1)}, bf16[4,96,2048]{2,1,0:T(8,128)(2,1)S(1)}, u32[]{:S(2)}, u32[]{:S(2)}) collective-permute-start(bf16[4,96,2048]{2,1,0:T(8,128)(2,1)S(1)} %get-tuple-element.64.refs_2_.refs_4_), channel_id=1, source_target_pairs={{0,2},{2,0},{4,6},{6,4},{8,10},{10,8},{12,14},{14,12},{16,18},{18,... | collective-permute-start | bytes 4718600 | tf_op jit(solution)/shard_map/ppermute | solution.py:443
  151.4 36.4 %collective-permute-start.26 = (bf16[4,96,2048]{2,1,0:T(8,128)(2,1)S(1)}, bf16[4,96,2048]{2,1,0:T(8,128)(2,1)S(1)}, u32[]{:S(2)}, u32[]{:S(2)}) collective-permute-start(bf16[4,96,2048]{2,1,0:T(8,128)(2,1)S(1)} %get-tuple-element.64.refs_2_.refs_4_), channel_id=1, source_target_pairs={{0,4},{2,6},{4,0},{6,2},{8,12},{10,14},{12,8},{14,10},{16,20},{18,... | collective-permute-start | bytes 4718600 | tf_op jit(solution)/shard_map/ppermute | solution.py:443
  152.4 30.5 %collective-permute-start.14 = (bf16[2,96,2048]{2,1,0:T(8,128)(2,1)S(1)}, bf16[2,96,2048]{2,1,0:T(8,128)(2,1)S(1)}, u32[]{:S(2)}, u32[]{:S(2)}) collective-permute-start(bf16[2,96,2048]{2,1,0:T(8,128)(2,1)S(1)} %collective-permute-done.13.refs_0_), channel_id=1, source_target_pairs={{0,8},{2,10},{4,12},{6,14},{8,0},{10,2},{12,4},{14,6},{16,24},{18,... | collective-permute-start | bytes 2359304 | tf_op jit(solution)/shard_map/ppermute | solution.py:443
  154.0 28.0 %collective-permute-start.18 = (bf16[4,32,2048]{2,1,0:T(8,128)(2,1)S(1)}, bf16[4,32,2048]{2,1,0:T(8,128)(2,1)S(1)}, u32[]{:S(2)}, u32[]{:S(2)}) collective-permute-start(bf16[4,32,2048]{2,1,0:T(8,128)(2,1)S(1)} %get-tuple-element.62.refs_1_), channel_id=1, source_target_pairs={{0,16},{2,18},{4,20},{6,22},{8,24},{10,26},{12,28},{14,30},{16,0},... | collective-permute-start | bytes 1572872 | tf_op jit(solution)/shard_map/ppermute | solution.py:443
  183.0 25.6 %collective-permute-start.24 = (bf16[8,32,2048]{2,1,0:T(8,128)(2,1)S(1)}, bf16[8,32,2048]{2,1,0:T(8,128)(2,1)S(1)}, u32[]{:S(2)}, u32[]{:S(2)}) collective-permute-start(bf16[8,32,2048]{2,1,0:T(8,128)(2,1)S(1)} %get-tuple-element.67.refs_3_), channel_id=1, source_target_pairs={{0,8},{2,10},{4,12},{6,14},{8,0},{10,2},{12,4},{14,6},{16,24},{18,... | collective-permute-start | bytes 3145736 | tf_op jit(solution)/shard_map/ppermute | solution.py:443
  187.8 21.4 %collective-permute-start.27 = (bf16[4,96,2048]{2,1,0:T(8,128)(2,1)S(1)}, bf16[4,96,2048]{2,1,0:T(8,128)(2,1)S(1)}, u32[]{:S(2)}, u32[]{:S(2)}) collective-permute-start(bf16[4,96,2048]{2,1,0:T(8,128)(2,1)S(1)} %collective-permute-done.26.refs_0_), channel_id=1, source_target_pairs={{0,2},{2,0},{4,6},{6,4},{8,10},{10,8},{12,14},{14,12},{16,18},{18,... | collective-permute-start | bytes 4718600 | tf_op jit(solution)/shard_map/ppermute | solution.py:443
  187.8 21.4 %collective-permute-start.22 = (bf16[2,96,2048]{2,1,0:T(8,128)(2,1)S(1)}, bf16[2,96,2048]{2,1,0:T(8,128)(2,1)S(1)}, u32[]{:S(2)}, u32[]{:S(2)}) collective-permute-start(bf16[2,96,2048]{2,1,0:T(8,128)(2,1)S(1)} %get-tuple-element.66.refs_2_.refs_8_), channel_id=1, source_target_pairs={{0,4},{2,6},{4,0},{6,2},{8,12},{10,14},{12,8},{14,10},{16,20},{18,... | collective-permute-start | bytes 2359304 | tf_op jit(solution)/shard_map/ppermute | solution.py:443
  188.8 20.4 %collective-permute-start.28 = (bf16[8,32,2048]{2,1,0:T(8,128)(2,1)S(1)}, bf16[8,32,2048]{2,1,0:T(8,128)(2,1)S(1)}, u32[]{:S(2)}, u32[]{:S(2)}) collective-permute-start(bf16[8,32,2048]{2,1,0:T(8,128)(2,1)S(1)} %get-tuple-element.67.refs_3_), channel_id=1, source_target_pairs={{0,2},{2,0},{4,6},{6,4},{8,10},{10,8},{12,14},{14,12},{16,18},{18,... | collective-permute-start | bytes 3145736 | tf_op jit(solution)/shard_map/ppermute | solution.py:443
  208.7 4.9 %collective-permute-start.25 = (bf16[8,32,2048]{2,1,0:T(8,128)(2,1)S(1)}, bf16[8,32,2048]{2,1,0:T(8,128)(2,1)S(1)}, u32[]{:S(2)}, u32[]{:S(2)}) collective-permute-start(bf16[8,32,2048]{2,1,0:T(8,128)(2,1)S(1)} %collective-permute-done.24.refs_6_), channel_id=1, source_target_pairs={{0,2},{2,0},{4,6},{6,4},{8,10},{10,8},{12,14},{14,12},{16,18},{18,... | collective-permute-start | bytes 3145736 | tf_op jit(solution)/shard_map/ppermute | solution.py:443
  208.7 4.7 %collective-permute-start.21 = (bf16[2,96,2048]{2,1,0:T(8,128)(2,1)S(1)}, bf16[2,96,2048]{2,1,0:T(8,128)(2,1)S(1)}, u32[]{:S(2)}, u32[]{:S(2)}) collective-permute-start(bf16[2,96,2048]{2,1,0:T(8,128)(2,1)S(1)} %get-tuple-element.66.refs_2_.refs_8_), channel_id=1, source_target_pairs={{0,2},{2,0},{4,6},{6,4},{8,10},{10,8},{12,14},{14,12},{16,18},{18,... | collective-permute-start | bytes 2359304 | tf_op jit(solution)/shard_map/ppermute | solution.py:443
  209.2 4.4 %collective-permute-start.23 = (bf16[2,96,2048]{2,1,0:T(8,128)(2,1)S(1)}, bf16[2,96,2048]{2,1,0:T(8,128)(2,1)S(1)}, u32[]{:S(2)}, u32[]{:S(2)}) collective-permute-start(bf16[2,96,2048]{2,1,0:T(8,128)(2,1)S(1)} %collective-permute-done.22.refs_5_), channel_id=1, source_target_pairs={{0,2},{2,0},{4,6},{6,4},{8,10},{10,8},{12,14},{14,12},{16,18},{18,... | collective-permute-start | bytes 2359304 | tf_op jit(solution)/shard_map/ppermute | solution.py:443

commit v11 on v10

--- a/solution.py
+++ b/solution.py
@@ -155,7 +155,7 @@
     )(me, owner, src)
 
 
-def add_taken_kernel(items, parts, table_ref, src_ref, got_ref, *rest):
+def add_taken_kernel(items, parts, offset, table_ref, src_ref, got_ref, *rest):
     mine, sem = rest[-2:]
     out_refs = rest[-2 - len(parts) : -2]
     copy = fetch(table_ref, src_ref, items, mine, sem)
@@ -165,20 +165,20 @@
         @pl.loop(0, size)
         def _(i, start=start, out_ref=out_ref):
             copy(start + i).wait()
-            out_ref[i] = got_ref[start + i] + mine[start + i]
+            out_ref[i] = got_ref[offset + start + i] + mine[start + i]
 
         start += size
 
 
-def add_taken(after, table, src, items, got, parts):
-    count, rows, cols = got.shape
-    return pl.pallas_call(
-        functools.partial(add_taken_kernel, items, parts),
+def add_taken(after, table, src, items, got, parts, offset=0):
+    count, (_, rows, cols) = len(items), got.shape
+    return pl.pallas_call(
+        functools.partial(add_taken_kernel, items, parts, offset),
         out_shape=[jax.ShapeDtypeStruct((n, rows, cols), got.dtype) for n in parts],
         in_specs=in_smem() + in_hbm() + in_vmem() + anywhere(len(after)),
         out_specs=in_vmem(len(parts)),
         scratch_shapes=[
-            pltpu.VMEM(got.shape, got.dtype),
+            pltpu.VMEM((count, rows, cols), got.dtype),
             pltpu.SemaphoreType.DMA((count,)),
         ],
         compiler_params=limits(MORE_VMEM_BYTES),
@@ -512,7 +512,9 @@
     first_got = swap(packed, CORE_BIT)
     falling = range(top - 1, -1, -1)
     plans = [items_of(theirs(merged[k]), slots, 0, cut) for k in falling]
-    plans.append(first_items(same))
+    staying = items_of(other_order, slots, cut, rest)[half:]
+    wanted_first = first_items(same)
+    plans.append(wanted_first[:half] + wanted_first[2 * half :])
     *packed, mine = pack([packed], table, gradient, plans, [cut] * top + [rest])
     got = {k: swap(block, CORE_BIT) for k, block in zip(falling, packed)}
     after = [packed[0]]
@@ -533,11 +535,13 @@
             home[o] = Block(made[1], n * slots)
         return [made[0]]
 
-    away, kept, far = combine(
+    away, far = combine(
         after,
         summed(mine, first_got, 0, half),
-        summed(mine, first_got, half, 2 * half),
-        summed(mine, first_got, 2 * half, mine.shape[0]),
+        [
+            [(mine, half + i), (first_got, 2 * half + i)]
+            for i in range(len(wanted_first) - 2 * half)
+        ],
     )
     after = [away]
     other_got = swap(away, other_bits[0])
@@ -555,6 +559,10 @@
             break
         if k == top:
             after = take(k - 1, after)
+            (kept,) = add_taken(
+                after, table, gradient, staying, first_got, (half,), half
+            )
+            after = [kept]
         wanted = []
         for o in level[k]:
             parts = [home[o]] + terms[o]

time: 217 us -> 214 us (0.986)
    pallas_call x1, Pallas kernels: 6.26 us -> 3.97 us  [pack(): pl.pallas_call(functools.partial(pack_kernel, tuple(plans)), out_shape=[j...]
    pallas_call x2 -> x3, Pallas kernels: 4.79 us -> 6.87 us  [add_taken(): pl.pallas_call(functools.partial(add_taken_kernel, items, parts, offset),...]
  transfers between devices with their start and end apart: 29 -> 29, of which waited for: 17 -> 16; matrix products, arithmetic and copies ran while one was open for 0% -> 0% of each run, Pallas kernels for 10% -> 10%
where the time goes in v11:
time: 214 us; the launch traced here: 213 us
  waiting for transfers between devices  144 us (67%)
  starting transfers between devices  36.2 us (17%)
  Pallas kernels  32.1 us (15%)
    ppermute x28, waiting for transfers between devices, swap(): return lax.ppermute(value, 'dp', [(i, i ^ bit) for i in range(count)])  140 us
    ppermute x28, starting transfers between devices, swap(): return lax.ppermute(value, 'dp', [(i, i ^ bit) for i in range(count)])  35.1 us
    pallas_call x3, Pallas kernels, spread(): pl.pallas_call(functools.partial(spread_kernel, plans, slots), out_shape=...  9.53 us
    pallas_call x3, Pallas kernels, add_taken(): pl.pallas_call(functools.partial(add_taken_kernel, items, parts, offset),...  6.87 us
  transfers between devices with their start and end apart: 29, of which 16 were waited for; matrix products, arithmetic and copies ran while one was open for 0% of the time, Pallas kernels for 10%

profile of v11, /device:TPU:0, one launch (start us, length us, event | category | flops | bytes accessed | tf_op | source)
XLA Modules:
  0.0 213.4 jit_solution(8299258539129740205)
XLA Ops:
  1.3 3.8 %shard_map.50 = (s32[32]{0:T(128)S(1)}, bf16[22,32,2048]{2,1,0:T(8,128)(2,1)S(1)}) custom-call(s32[1]{0:T(128)} %bitcast.me_ref, s32[24]{0:T(128)S(1)} %copy-done.1, bf16[24,128,2048]{2,1,0:T(8,128)(2,1)} %bitcast.6), custom_call_target="tpu_custom_call" | custom-call | tf_op jit(solution)/shard_map/pallas_call | solution.py:141
  5.6 4.0 %shard_map.51 = (bf16[6,96,2048]{2,1,0:T(8,128)(2,1)S(1)}, bf16[8,96,2048]{2,1,0:T(8,128)(2,1)S(1)}, bf16[14,32,2048]{2,1,0:T(8,128)(2,1)S(1)}) custom-call(s32[32]{0:T(128)S(1)} %get-tuple-element.36.table_ref, bf16[24,128,2048]{2,1,0:T(8,128)(2,1)} %bitcast.7, bf16[22,32,2048]{2,1,0:T(8,128)(2,1)S(1)} %get-tuple-element.37.rest_0_), custom_call_target="tpu_custom_call" | custom-call | tf_op jit(solution)/shard_map/pallas_call | solution.py:115
  10.7 3.0 %collective-permute-start.4 = (bf16[8,32,2048]{2,1,0:T(8,128)(2,1)S(1)}, bf16[8,32,2048]{2,1,0:T(8,128)(2,1)S(1)}, u32[]{:S(2)}, u32[]{:S(2)}) collective-permute-start(bf16[8,32,2048]{2,1,0:T(8,128)(2,1)S(1)} %get-tuple-element.41.rest_0_), channel_id=1, source_target_pairs={{0,8},{2,10},{4,12},{6,14},{8,0},{10,2},{12,4},{14,6},{16,24},{18,... | collective-permute-start | bytes 3145736 | tf_op jit(solution)/shard_map/ppermute | solution.py:443
  15.2 2.2 %shard_map.53 = (bf16[4,96,2048]{2,1,0:T(8,128)(2,1)S(1)}, bf16[2,96,2048]{2,1,0:T(8,128)(2,1)S(1)}) custom-call(s32[32]{0:T(128)S(1)} %get-tuple-element.36.table_ref, bf16[24,128,2048]{2,1,0:T(8,128)(2,1)} %bitcast.8, bf16[6,96,2048]{2,1,0:T(8,128)(2,1)S(1)} %collective-permute-done.1.got_ref, bf16[8,32,2048]{2,1,0:T(8,128)(2,1)S(1)} %get-tuple-element.41.rest_0_), custom_call_target="tpu_custom_call" | custom-call | tf_op jit(solution)/shard_map/pallas_call | solution.py:175
  17.4 1.8 collective-permute-start.5
  19.2 1.9 shard_map.54.refs_2_.refs_4_
  21.2 13.0 %collective-permute-done.3.refs_1_ = bf16[6,32,2048]{2,1,0:T(8,128)(2,1)S(1)} collective-permute-done((bf16[6,32,2048]{2,1,0:T(8,128)(2,1)S(1)}, bf16[6,32,2048]{2,1,0:T(8,128)(2,1)S(1)}, u32[]{:S(2)}, u32[]{:S(2)}) %collective-permute-start.3) | collective-permute-done | bytes 786464 | tf_op jit(solution)/shard_map/ppermute | solution.py:443
  34.2 3.0 %collective-permute-done.4.refs_3_ = bf16[8,32,2048]{2,1,0:T(8,128)(2,1)S(1)} collective-permute-done((bf16[8,32,2048]{2,1,0:T(8,128)(2,1)S(1)}, bf16[8,32,2048]{2,1,0:T(8,128)(2,1)S(1)}, u32[]{:S(2)}, u32[]{:S(2)}) %collective-permute-start.4) | collective-permute-done | bytes 1048608 | tf_op jit(solution)/shard_map/ppermute | solution.py:443
  37.4 1.8 collective-permute-start.6
  39.2 2.7 %collective-permute-start.7 = (bf16[4,32,2048]{2,1,0:T(8,128)(2,1)S(1)}, bf16[4,32,2048]{2,1,0:T(8,128)(2,1)S(1)}, u32[]{:S(2)}, u32[]{:S(2)}) collective-permute-start(bf16[4,32,2048]{2,1,0:T(8,128)(2,1)S(1)} %get-tuple-element.48), channel_id=1, source_target_pairs={{0,16},{2,18},{4,20},{6,22},{8,24},{10,26},{12,28},{14,30},{16,0},... | collective-permute-start | bytes 1572872 | tf_op jit(solution)/shard_map/ppermute | solution.py:443
  41.9 2.7 %shard_map.56 = (bf16[2,96,2048]{2,1,0:T(8,128)(2,1)S(1)}, bf16[6,96,2048]{2,1,0:T(8,128)(2,1)S(1)}) custom-call(s32[32]{0:T(128)S(1)} %get-tuple-element.36.table_ref, bf16[24,128,2048]{2,1,0:T(8,128)(2,1)} %bitcast.10, bf16[8,96,2048]{2,1,0:T(8,128)(2,1)S(1)} %collective-permute-done.got_ref, bf16[2,96,2048]{2,1,0:T(8,128)(2,1)S(1)} %get-tuple-element.45.rest_0_), custom_call_target="tpu_custom_call" | custom-call | tf_op jit(solution)/shard_map/pallas_call | solution.py:175
  44.6 22.1 %collective-permute-done.7.refs_4_ = bf16[4,32,2048]{2,1,0:T(8,128)(2,1)S(1)} collective-permute-done((bf16[4,32,2048]{2,1,0:T(8,128)(2,1)S(1)}, bf16[4,32,2048]{2,1,0:T(8,128)(2,1)S(1)}, u32[]{:S(2)}, u32[]{:S(2)}) %collective-permute-start.7) | collective-permute-done | bytes 524320 | tf_op jit(solution)/shard_map/ppermute | solution.py:443
  68.1 2.4 %collective-permute-start.10 = (bf16[2,96,2048]{2,1,0:T(8,128)(2,1)S(1)}, bf16[2,96,2048]{2,1,0:T(8,128)(2,1)S(1)}, u32[]{:S(2)}, u32[]{:S(2)}) collective-permute-start(bf16[2,96,2048]{2,1,0:T(8,128)(2,1)S(1)} %get-tuple-element.52), channel_id=1, source_target_pairs={{0,16},{2,18},{4,20},{6,22},{8,24},{10,26},{12,28},{14,30},{16,0},... | collective-permute-start | bytes 2359304 | tf_op jit(solution)/shard_map/ppermute | solution.py:443
  70.5 1.5 collective-permute-start.8
  72.0 1.7 collective-permute-start.9
  74.2 19.4 %collective-permute-done.11.rest_5_ = bf16[2,32,2048]{2,1,0:T(8,128)(2,1)S(1)} collective-permute-done((bf16[2,32,2048]{2,1,0:T(8,128)(2,1)S(1)}, bf16[2,32,2048]{2,1,0:T(8,128)(2,1)S(1)}, u32[]{:S(2)}, u32[]{:S(2)}) %collective-permute-start.11) | collective-permute-done | bytes 262176 | tf_op jit(solution)/shard_map/ppermute | solution.py:443
  93.6 10.5 %collective-permute-done.10.rest_3_ = bf16[2,96,2048]{2,1,0:T(8,128)(2,1)S(1)} collective-permute-done((bf16[2,96,2048]{2,1,0:T(8,128)(2,1)S(1)}, bf16[2,96,2048]{2,1,0:T(8,128)(2,1)S(1)}, u32[]{:S(2)}, u32[]{:S(2)}) %collective-permute-start.10) | collective-permute-done | bytes 786464 | tf_op jit(solution)/shard_map/ppermute | solution.py:443
  107.0 3.9 %collective-permute-done.12.refs_1_ = f32[2,128,128]{2,1,0:T(8,128)S(1)} collective-permute-done((f32[2,128,128]{2,1,0:T(8,128)S(1)}, f32[2,128,128]{2,1,0:T(8,128)S(1)}, u32[]{:S(2)}, u32[]{:S(2)}) %collective-permute-start.12) | collective-permute-done | bytes 131104 | tf_op jit(solution)/shard_map/ppermute | solution.py:667
  110.9 3.5 %shard_map.59 = (bf16[2,96,2048]{2,1,0:T(8,128)(2,1)S(1)}, bf16[2,32,2048]{2,1,0:T(8,128)(2,1)S(1)}) custom-call(f32[2,128,128]{2,1,0:T(8,128)S(1)} %get-tuple-element.55.refs_0_, f32[2,128,128]{2,1,0:T(8,128)S(1)} %collective-permute-done.12.refs_1_, bf16[2,128,2048]{2,1,0:T(8,128)(2,1)S(1)} %get-tuple-element.56.refs_2_), custom_call_target="tpu_custom_call" | custom-call | tf_op jit(solution)/shard_map/pallas_call | solution.py:429
  114.5 1.8 collective-permute-start.13
  116.3 2.5 %collective-permute-start.15 = (bf16[2,96,2048]{2,1,0:T(8,128)(2,1)S(1)}, bf16[2,96,2048]{2,1,0:T(8,128)(2,1)S(1)}, u32[]{:S(2)}, u32[]{:S(2)}) collective-permute-start(bf16[2,96,2048]{2,1,0:T(8,128)(2,1)S(1)} %get-tuple-element.57.rest_6_.refs_4_), channel_id=1, source_target_pairs={{0,8},{2,10},{4,12},{6,14},{8,0},{10,2},{12,4},{14,6},{16,24},{18,... | collective-permute-start | bytes 2359304 | tf_op jit(solution)/shard_map/ppermute | solution.py:443
  120.8 2.3 %shard_map.60 = (f32[2,128,2048]{2,1,0:T(8,128)}, f32[8,128]{1,0:T(8,128)S(1)}) custom-call(s32[32]{0:T(128)S(1)} %get-tuple-element.36.table_ref, f32[2,128,2048]{2,1,0:T(8,128)S(1)} %bitcast.5, bf16[6,96,2048]{2,1,0:T(8,128)(2,1)S(1)} %get-tuple-element.46.refs_0_.rest_0_, bf16[2,96,2048]{2,1,0:T(8,128)(2,1)S(1)} %collective-permute-done.8.rest_1_, ...), custom_call_target="tpu_custom_call" | custom-call | tf_op jit(solution)/shard_map/pallas_call | solution.py:348
  123.0 17.6 %collective-permute-done.16.refs_3_ = bf16[2,32,2048]{2,1,0:T(8,128)(2,1)S(1)} collective-permute-done((bf16[2,32,2048]{2,1,0:T(8,128)(2,1)S(1)}, bf16[2,32,2048]{2,1,0:T(8,128)(2,1)S(1)}, u32[]{:S(2)}, u32[]{:S(2)}) %collective-permute-start.16) | collective-permute-done | bytes 262176 | tf_op jit(solution)/shard_map/ppermute | solution.py:443
  140.6 7.7 %collective-permute-done.13.refs_0_ = bf16[2,96,2048]{2,1,0:T(8,128)(2,1)S(1)} collective-permute-done((bf16[2,96,2048]{2,1,0:T(8,128)(2,1)S(1)}, bf16[2,96,2048]{2,1,0:T(8,128)(2,1)S(1)}, u32[]{:S(2)}, u32[]{:S(2)}) %collective-permute-start.13) | collective-permute-done | bytes 786464 | tf_op jit(solution)/shard_map/ppermute | solution.py:443
  150.9 3.9 %collective-permute-start.18 = (bf16[4,32,2048]{2,1,0:T(8,128)(2,1)S(1)}, bf16[4,32,2048]{2,1,0:T(8,128)(2,1)S(1)}, u32[]{:S(2)}, u32[]{:S(2)}) collective-permute-start(bf16[4,32,2048]{2,1,0:T(8,128)(2,1)S(1)} %get-tuple-element.60.refs_1_), channel_id=1, source_target_pairs={{0,16},{2,18},{4,20},{6,22},{8,24},{10,26},{12,28},{14,30},{16,0},... | collective-permute-start | bytes 1572872 | tf_op jit(solution)/shard_map/ppermute | solution.py:443
  154.8 2.7 %shard_map.62 = (bf16[24,128,2048]{2,1,0:T(8,128)(2,1)}, f32[8,128]{1,0:T(8,128)S(1)}) custom-call(s32[32]{0:T(128)S(1)} %get-tuple-element.36.table_ref, bf16[4,96,2048]{2,1,0:T(8,128)(2,1)S(1)} %get-tuple-element.61.refs_0_, bf16[4,96,2048]{2,1,0:T(8,128)(2,1)S(1)} %collective-permute-done.19.refs_1_, ...), custom_call_target="tpu_custom_call" | custom-call | tf_op jit(solution)/shard_map/pallas_call | solution.py:275
  157.6 21.4 %collective-permute-done.18.refs_2_ = bf16[4,32,2048]{2,1,0:T(8,128)(2,1)S(1)} collective-permute-done((bf16[4,32,2048]{2,1,0:T(8,128)(2,1)S(1)}, bf16[4,32,2048]{2,1,0:T(8,128)(2,1)S(1)}, u32[]{:S(2)}, u32[]{:S(2)}) %collective-permute-start.18) | collective-permute-done | bytes 524320 | tf_op jit(solution)/shard_map/ppermute | solution.py:443
  180.5 3.3 %collective-permute-start.24 = (bf16[8,32,2048]{2,1,0:T(8,128)(2,1)S(1)}, bf16[8,32,2048]{2,1,0:T(8,128)(2,1)S(1)}, u32[]{:S(2)}, u32[]{:S(2)}) collective-permute-start(bf16[8,32,2048]{2,1,0:T(8,128)(2,1)S(1)} %get-tuple-element.65.refs_3_), channel_id=1, source_target_pairs={{0,8},{2,10},{4,12},{6,14},{8,0},{10,2},{12,4},{14,6},{16,24},{18,... | collective-permute-start | bytes 3145736 | tf_op jit(solution)/shard_map/ppermute | solution.py:443
  183.8 1.9 collective-permute-done.26.refs_0_
  186.5 19.6 %collective-permute-done.24.refs_6_ = bf16[8,32,2048]{2,1,0:T(8,128)(2,1)S(1)} collective-permute-done((bf16[8,32,2048]{2,1,0:T(8,128)(2,1)S(1)}, bf16[8,32,2048]{2,1,0:T(8,128)(2,1)S(1)}, u32[]{:S(2)}, u32[]{:S(2)}) %collective-permute-start.24) | collective-permute-done | bytes 1048608 | tf_op jit(solution)/shard_map/ppermute | solution.py:443
  206.6 4.4 %shard_map.64 = (bf16[24,128,2048]{2,1,0:T(8,128)(2,1)}, f32[8,128]{1,0:T(8,128)}) custom-call(s32[32]{0:T(128)S(1)} %get-tuple-element.36.table_ref, bf16[4,96,2048]{2,1,0:T(8,128)(2,1)S(1)} %collective-permute-done.26.refs_0_, bf16[4,96,2048]{2,1,0:T(8,128)(2,1)S(1)} %collective-permute-done.27.refs_1_, ...), custom_call_target="tpu_custom_call", output_to_operand_aliasing={{0}: (8, {})} | custom-call | tf_op jit(solution)/shard_map/pallas_call | solution.py:275
  211.0 2.4 %shard_map.65 = (bf16[24,128,2048]{2,1,0:T(8,128)(2,1)}, f32[8,128]{1,0:T(8,128)}) custom-call(s32[32]{0:T(128)S(1)} %get-tuple-element.36.table_ref, bf16[2,96,2048]{2,1,0:T(8,128)(2,1)S(1)} %collective-permute-done.21.refs_0_, bf16[2,96,2048]{2,1,0:T(8,128)(2,1)S(1)} %collective-permute-done.23.refs_1_, ...), custom_call_target="tpu_custom_call", output_to_operand_aliasing={{0}: (4, {})} | custom-call | tf_op jit(solution)/shard_map/pallas_call | solution.py:275
  (46 shorter events, 16.3 us)
Async XLA Ops:
  0.6 0.7 copy-start.1
  5.1 5.4 %collective-permute-start.2 = (bf16[22,32,2048]{2,1,0:T(8,128)(2,1)S(1)}, bf16[22,32,2048]{2,1,0:T(8,128)(2,1)S(1)}, u32[]{:S(2)}, u32[]{:S(2)}) collective-permute-start(bf16[22,32,2048]{2,1,0:T(8,128)(2,1)S(1)} %get-tuple-element.37.rest_0_), channel_id=1, source_target_pairs={{0,2},{2,0},{4,6},{6,4},{8,10},{10,8},{12,14},{14,12},{16,18},{18,... | collective-permute-start | bytes 8650760 | tf_op jit(solution)/shard_map/ppermute | solution.py:443
  9.6 5.6 %collective-permute-start.1 = (bf16[6,96,2048]{2,1,0:T(8,128)(2,1)S(1)}, bf16[6,96,2048]{2,1,0:T(8,128)(2,1)S(1)}, u32[]{:S(2)}, u32[]{:S(2)}) collective-permute-start(bf16[6,96,2048]{2,1,0:T(8,128)(2,1)S(1)} %get-tuple-element.39.refs_2_), channel_id=1, source_target_pairs={{0,2},{2,0},{4,6},{6,4},{8,10},{10,8},{12,14},{14,12},{16,18},{18,... | collective-permute-start | bytes 7077896 | tf_op jit(solution)/shard_map/ppermute | solution.py:443
  9.9 32.0 %collective-permute-start = (bf16[8,96,2048]{2,1,0:T(8,128)(2,1)S(1)}, bf16[8,96,2048]{2,1,0:T(8,128)(2,1)S(1)}, u32[]{:S(2)}, u32[]{:S(2)}) collective-permute-start(bf16[8,96,2048]{2,1,0:T(8,128)(2,1)S(1)} %get-tuple-element.38), channel_id=1, source_target_pairs={{0,2},{2,0},{4,6},{6,4},{8,10},{10,8},{12,14},{14,12},{16,18},{18,... | collective-permute-start | bytes 9437192 | tf_op jit(solution)/shard_map/ppermute | solution.py:443
  10.7 26.5 %collective-permute-start.4 = (bf16[8,32,2048]{2,1,0:T(8,128)(2,1)S(1)}, bf16[8,32,2048]{2,1,0:T(8,128)(2,1)S(1)}, u32[]{:S(2)}, u32[]{:S(2)}) collective-permute-start(bf16[8,32,2048]{2,1,0:T(8,128)(2,1)S(1)} %get-tuple-element.41.rest_0_), channel_id=1, source_target_pairs={{0,8},{2,10},{4,12},{6,14},{8,0},{10,2},{12,4},{14,6},{16,24},{18,... | collective-permute-start | bytes 3145736 | tf_op jit(solution)/shard_map/ppermute | solution.py:443
  13.7 20.4 %collective-permute-start.3 = (bf16[6,32,2048]{2,1,0:T(8,128)(2,1)S(1)}, bf16[6,32,2048]{2,1,0:T(8,128)(2,1)S(1)}, u32[]{:S(2)}, u32[]{:S(2)}) collective-permute-start(bf16[6,32,2048]{2,1,0:T(8,128)(2,1)S(1)} %get-tuple-element.43), channel_id=1, source_target_pairs={{0,4},{2,6},{4,0},{6,2},{8,12},{10,14},{12,8},{14,10},{16,20},{18,... | collective-permute-start | bytes 2359304 | tf_op jit(solution)/shard_map/ppermute | solution.py:443
  17.4 49.3 %collective-permute-start.5 = (bf16[4,96,2048]{2,1,0:T(8,128)(2,1)S(1)}, bf16[4,96,2048]{2,1,0:T(8,128)(2,1)S(1)}, u32[]{:S(2)}, u32[]{:S(2)}) collective-permute-start(bf16[4,96,2048]{2,1,0:T(8,128)(2,1)S(1)} %get-tuple-element.44.rest_0_), channel_id=1, source_target_pairs={{0,4},{2,6},{4,0},{6,2},{8,12},{10,14},{12,8},{14,10},{16,20},{18,... | collective-permute-start | bytes 4718600 | tf_op jit(solution)/shard_map/ppermute | solution.py:443
  37.4 30.4 %collective-permute-start.6 = (bf16[2,96,2048]{2,1,0:T(8,128)(2,1)S(1)}, bf16[2,96,2048]{2,1,0:T(8,128)(2,1)S(1)}, u32[]{:S(2)}, u32[]{:S(2)}) collective-permute-start(bf16[2,96,2048]{2,1,0:T(8,128)(2,1)S(1)} %get-tuple-element.45.rest_0_), channel_id=1, source_target_pairs={{0,8},{2,10},{4,12},{6,14},{8,0},{10,2},{12,4},{14,6},{16,24},{18,... | collective-permute-start | bytes 2359304 | tf_op jit(solution)/shard_map/ppermute | solution.py:443
  39.2 27.5 %collective-permute-start.7 = (bf16[4,32,2048]{2,1,0:T(8,128)(2,1)S(1)}, bf16[4,32,2048]{2,1,0:T(8,128)(2,1)S(1)}, u32[]{:S(2)}, u32[]{:S(2)}) collective-permute-start(bf16[4,32,2048]{2,1,0:T(8,128)(2,1)S(1)} %get-tuple-element.48), channel_id=1, source_target_pairs={{0,16},{2,18},{4,20},{6,22},{8,24},{10,26},{12,28},{14,30},{16,0},... | collective-permute-start | bytes 1572872 | tf_op jit(solution)/shard_map/ppermute | solution.py:443
  67.8 37.1 %copy-start = (f32[1,2,128,2048]{3,2,1,0:T(8,128)S(1)}, f32[1,2,128,2048]{3,2,1,0:T(8,128)}, u32[]{:S(2)}) copy-start(f32[1,2,128,2048]{3,2,1,0:T(8,128)} %param.5) | copy-start | bytes 6291460
  68.1 36.1 %collective-permute-start.10 = (bf16[2,96,2048]{2,1,0:T(8,128)(2,1)S(1)}, bf16[2,96,2048]{2,1,0:T(8,128)(2,1)S(1)}, u32[]{:S(2)}, u32[]{:S(2)}) collective-permute-start(bf16[2,96,2048]{2,1,0:T(8,128)(2,1)S(1)} %get-tuple-element.52), channel_id=1, source_target_pairs={{0,16},{2,18},{4,20},{6,22},{8,24},{10,26},{12,28},{14,30},{16,0},... | collective-permute-start | bytes 2359304 | tf_op jit(solution)/shard_map/ppermute | solution.py:443
  70.5 33.7 %collective-permute-start.8 = (bf16[2,96,2048]{2,1,0:T(8,128)(2,1)S(1)}, bf16[2,96,2048]{2,1,0:T(8,128)(2,1)S(1)}, u32[]{:S(2)}, u32[]{:S(2)}) collective-permute-start(bf16[2,96,2048]{2,1,0:T(8,128)(2,1)S(1)} %get-tuple-element.50), channel_id=1, source_target_pairs={{0,4},{2,6},{4,0},{6,2},{8,12},{10,14},{12,8},{14,10},{16,20},{18,... | collective-permute-start | bytes 2359304 | tf_op jit(solution)/shard_map/ppermute | solution.py:443
  72.0 32.9 %collective-permute-start.9 = (bf16[2,96,2048]{2,1,0:T(8,128)(2,1)S(1)}, bf16[2,96,2048]{2,1,0:T(8,128)(2,1)S(1)}, u32[]{:S(2)}, u32[]{:S(2)}) collective-permute-start(bf16[2,96,2048]{2,1,0:T(8,128)(2,1)S(1)} %get-tuple-element.51), channel_id=1, source_target_pairs={{0,8},{2,10},{4,12},{6,14},{8,0},{10,2},{12,4},{14,6},{16,24},{18,... | collective-permute-start | bytes 2359304 | tf_op jit(solution)/shard_map/ppermute | solution.py:443
  73.6 20.0 %collective-permute-start.11 = (bf16[2,32,2048]{2,1,0:T(8,128)(2,1)S(1)}, bf16[2,32,2048]{2,1,0:T(8,128)(2,1)S(1)}, u32[]{:S(2)}, u32[]{:S(2)}) collective-permute-start(bf16[2,32,2048]{2,1,0:T(8,128)(2,1)S(1)} %get-tuple-element.54), channel_id=1, source_target_pairs={{0,4},{2,6},{4,0},{6,2},{8,12},{10,14},{12,8},{14,10},{16,20},{18,... | collective-permute-start | bytes 786440 | tf_op jit(solution)/shard_map/ppermute | solution.py:443
  105.9 5.0 %collective-permute-start.12 = (f32[2,128,128]{2,1,0:T(8,128)S(1)}, f32[2,128,128]{2,1,0:T(8,128)S(1)}, u32[]{:S(2)}, u32[]{:S(2)}) collective-permute-start(f32[2,128,128]{2,1,0:T(8,128)S(1)} %get-tuple-element.55.refs_0_), channel_id=1, source_target_pairs={{0,1},{1,0},{2,3},{3,2},{4,5},{5,4},{6,7},{7,6},{8,9},{9,8},{10,11... | collective-permute-start | bytes 393224 | tf_op jit(solution)/shard_map/ppermute | solution.py:667
  114.5 33.9 %collective-permute-start.13 = (bf16[2,96,2048]{2,1,0:T(8,128)(2,1)S(1)}, bf16[2,96,2048]{2,1,0:T(8,128)(2,1)S(1)}, u32[]{:S(2)}, u32[]{:S(2)}) collective-permute-start(bf16[2,96,2048]{2,1,0:T(8,128)(2,1)S(1)} %get-tuple-element.57.rest_6_.refs_4_), channel_id=1, source_target_pairs={{0,16},{2,18},{4,20},{6,22},{8,24},{10,26},{12,28},{14,30},{16,0},... | collective-permute-start | bytes 2359304 | tf_op jit(solution)/shard_map/ppermute | solution.py:443
  116.3 32.1 %collective-permute-start.15 = (bf16[2,96,2048]{2,1,0:T(8,128)(2,1)S(1)}, bf16[2,96,2048]{2,1,0:T(8,128)(2,1)S(1)}, u32[]{:S(2)}, u32[]{:S(2)}) collective-permute-start(bf16[2,96,2048]{2,1,0:T(8,128)(2,1)S(1)} %get-tuple-element.57.rest_6_.refs_4_), channel_id=1, source_target_pairs={{0,8},{2,10},{4,12},{6,14},{8,0},{10,2},{12,4},{14,6},{16,24},{18,... | collective-permute-start | bytes 2359304 | tf_op jit(solution)/shard_map/ppermute | solution.py:443
  118.7 29.7 %collective-permute-start.17 = (bf16[2,96,2048]{2,1,0:T(8,128)(2,1)S(1)}, bf16[2,96,2048]{2,1,0:T(8,128)(2,1)S(1)}, u32[]{:S(2)}, u32[]{:S(2)}) collective-permute-start(bf16[2,96,2048]{2,1,0:T(8,128)(2,1)S(1)} %get-tuple-element.57.rest_6_.refs_4_), channel_id=1, source_target_pairs={{0,4},{2,6},{4,0},{6,2},{8,12},{10,14},{12,8},{14,10},{16,20},{18,... | collective-permute-start | bytes 2359304 | tf_op jit(solution)/shard_map/ppermute | solution.py:443
  119.4 21.2 %collective-permute-start.16 = (bf16[2,32,2048]{2,1,0:T(8,128)(2,1)S(1)}, bf16[2,32,2048]{2,1,0:T(8,128)(2,1)S(1)}, u32[]{:S(2)}, u32[]{:S(2)}) collective-permute-start(bf16[2,32,2048]{2,1,0:T(8,128)(2,1)S(1)} %get-tuple-element.58.refs_2_), channel_id=1, source_target_pairs={{0,4},{2,6},{4,0},{6,2},{8,12},{10,14},{12,8},{14,10},{16,20},{18,... | collective-permute-start | bytes 786440 | tf_op jit(solution)/shard_map/ppermute | solution.py:443
  148.7 6.2 %collective-permute-start.19 = (bf16[4,96,2048]{2,1,0:T(8,128)(2,1)S(1)}, bf16[4,96,2048]{2,1,0:T(8,128)(2,1)S(1)}, u32[]{:S(2)}, u32[]{:S(2)}) collective-permute-start(bf16[4,96,2048]{2,1,0:T(8,128)(2,1)S(1)} %get-tuple-element.61.refs_0_), channel_id=1, source_target_pairs={{0,2},{2,0},{4,6},{6,4},{8,10},{10,8},{12,14},{14,12},{16,18},{18,... | collective-permute-start | bytes 4718600 | tf_op jit(solution)/shard_map/ppermute | solution.py:443
  148.7 6.1 %collective-permute-start.20 = (bf16[4,96,2048]{2,1,0:T(8,128)(2,1)S(1)}, bf16[4,96,2048]{2,1,0:T(8,128)(2,1)S(1)}, u32[]{:S(2)}, u32[]{:S(2)}) collective-permute-start(bf16[4,96,2048]{2,1,0:T(8,128)(2,1)S(1)} %get-tuple-element.62.refs_2_.refs_4_), channel_id=1, source_target_pairs={{0,2},{2,0},{4,6},{6,4},{8,10},{10,8},{12,14},{14,12},{16,18},{18,... | collective-permute-start | bytes 4718600 | tf_op jit(solution)/shard_map/ppermute | solution.py:443
  149.2 36.4 %collective-permute-start.26 = (bf16[4,96,2048]{2,1,0:T(8,128)(2,1)S(1)}, bf16[4,96,2048]{2,1,0:T(8,128)(2,1)S(1)}, u32[]{:S(2)}, u32[]{:S(2)}) collective-permute-start(bf16[4,96,2048]{2,1,0:T(8,128)(2,1)S(1)} %get-tuple-element.62.refs_2_.refs_4_), channel_id=1, source_target_pairs={{0,4},{2,6},{4,0},{6,2},{8,12},{10,14},{12,8},{14,10},{16,20},{18,... | collective-permute-start | bytes 4718600 | tf_op jit(solution)/shard_map/ppermute | solution.py:443
  149.9 30.5 %collective-permute-start.14 = (bf16[2,96,2048]{2,1,0:T(8,128)(2,1)S(1)}, bf16[2,96,2048]{2,1,0:T(8,128)(2,1)S(1)}, u32[]{:S(2)}, u32[]{:S(2)}) collective-permute-start(bf16[2,96,2048]{2,1,0:T(8,128)(2,1)S(1)} %collective-permute-done.13.refs_0_), channel_id=1, source_target_pairs={{0,8},{2,10},{4,12},{6,14},{8,0},{10,2},{12,4},{14,6},{16,24},{18,... | collective-permute-start | bytes 2359304 | tf_op jit(solution)/shard_map/ppermute | solution.py:443
  150.9 28.0 %collective-permute-start.18 = (bf16[4,32,2048]{2,1,0:T(8,128)(2,1)S(1)}, bf16[4,32,2048]{2,1,0:T(8,128)(2,1)S(1)}, u32[]{:S(2)}, u32[]{:S(2)}) collective-permute-start(bf16[4,32,2048]{2,1,0:T(8,128)(2,1)S(1)} %get-tuple-element.60.refs_1_), channel_id=1, source_target_pairs={{0,16},{2,18},{4,20},{6,22},{8,24},{10,26},{12,28},{14,30},{16,0},... | collective-permute-start | bytes 1572872 | tf_op jit(solution)/shard_map/ppermute | solution.py:443
  180.5 25.6 %collective-permute-start.24 = (bf16[8,32,2048]{2,1,0:T(8,128)(2,1)S(1)}, bf16[8,32,2048]{2,1,0:T(8,128)(2,1)S(1)}, u32[]{:S(2)}, u32[]{:S(2)}) collective-permute-start(bf16[8,32,2048]{2,1,0:T(8,128)(2,1)S(1)} %get-tuple-element.65.refs_3_), channel_id=1, source_target_pairs={{0,8},{2,10},{4,12},{6,14},{8,0},{10,2},{12,4},{14,6},{16,24},{18,... | collective-permute-start | bytes 3145736 | tf_op jit(solution)/shard_map/ppermute | solution.py:443
  185.6 20.9 %collective-permute-start.27 = (bf16[4,96,2048]{2,1,0:T(8,128)(2,1)S(1)}, bf16[4,96,2048]{2,1,0:T(8,128)(2,1)S(1)}, u32[]{:S(2)}, u32[]{:S(2)}) collective-permute-start(bf16[4,96,2048]{2,1,0:T(8,128)(2,1)S(1)} %collective-permute-done.26.refs_0_), channel_id=1, source_target_pairs={{0,2},{2,0},{4,6},{6,4},{8,10},{10,8},{12,14},{14,12},{16,18},{18,... | collective-permute-start | bytes 4718600 | tf_op jit(solution)/shard_map/ppermute | solution.py:443
  185.6 20.9 %collective-permute-start.22 = (bf16[2,96,2048]{2,1,0:T(8,128)(2,1)S(1)}, bf16[2,96,2048]{2,1,0:T(8,128)(2,1)S(1)}, u32[]{:S(2)}, u32[]{:S(2)}) collective-permute-start(bf16[2,96,2048]{2,1,0:T(8,128)(2,1)S(1)} %get-tuple-element.64.refs_2_.refs_8_), channel_id=1, source_target_pairs={{0,4},{2,6},{4,0},{6,2},{8,12},{10,14},{12,8},{14,10},{16,20},{18,... | collective-permute-start | bytes 2359304 | tf_op jit(solution)/shard_map/ppermute | solution.py:443
  186.2 20.3 %collective-permute-start.28 = (bf16[8,32,2048]{2,1,0:T(8,128)(2,1)S(1)}, bf16[8,32,2048]{2,1,0:T(8,128)(2,1)S(1)}, u32[]{:S(2)}, u32[]{:S(2)}) collective-permute-start(bf16[8,32,2048]{2,1,0:T(8,128)(2,1)S(1)} %get-tuple-element.65.refs_3_), channel_id=1, source_target_pairs={{0,2},{2,0},{4,6},{6,4},{8,10},{10,8},{12,14},{14,12},{16,18},{18,... | collective-permute-start | bytes 3145736 | tf_op jit(solution)/shard_map/ppermute | solution.py:443
  206.0 5.0 %collective-permute-start.25 = (bf16[8,32,2048]{2,1,0:T(8,128)(2,1)S(1)}, bf16[8,32,2048]{2,1,0:T(8,128)(2,1)S(1)}, u32[]{:S(2)}, u32[]{:S(2)}) collective-permute-start(bf16[8,32,2048]{2,1,0:T(8,128)(2,1)S(1)} %collective-permute-done.24.refs_6_), channel_id=1, source_target_pairs={{0,2},{2,0},{4,6},{6,4},{8,10},{10,8},{12,14},{14,12},{16,18},{18,... | collective-permute-start | bytes 3145736 | tf_op jit(solution)/shard_map/ppermute | solution.py:443
  206.0 4.9 %collective-permute-start.21 = (bf16[2,96,2048]{2,1,0:T(8,128)(2,1)S(1)}, bf16[2,96,2048]{2,1,0:T(8,128)(2,1)S(1)}, u32[]{:S(2)}, u32[]{:S(2)}) collective-permute-start(bf16[2,96,2048]{2,1,0:T(8,128)(2,1)S(1)} %get-tuple-element.64.refs_2_.refs_8_), channel_id=1, source_target_pairs={{0,2},{2,0},{4,6},{6,4},{8,10},{10,8},{12,14},{14,12},{16,18},{18,... | collective-permute-start | bytes 2359304 | tf_op jit(solution)/shard_map/ppermute | solution.py:443
  206.5 4.4 %collective-permute-start.23 = (bf16[2,96,2048]{2,1,0:T(8,128)(2,1)S(1)}, bf16[2,96,2048]{2,1,0:T(8,128)(2,1)S(1)}, u32[]{:S(2)}, u32[]{:S(2)}) collective-permute-start(bf16[2,96,2048]{2,1,0:T(8,128)(2,1)S(1)} %collective-permute-done.22.refs_5_), channel_id=1, source_target_pairs={{0,2},{2,0},{4,6},{6,4},{8,10},{10,8},{12,14},{14,12},{16,18},{18,... | collective-permute-start | bytes 2359304 | tf_op jit(solution)/shard_map/ppermute | solution.py:443

commit v12 on v11

--- a/solution.py
+++ b/solution.py
@@ -55,15 +55,15 @@
 def table_kernel(slots, me_ref, owner_ref, table_ref, used):
     spots, matrices = table_ref.shape[0], owner_ref.shape[0]
 
-    @pl.loop(0, spots)
+    @pl.loop(0, spots, unroll=True)
     def _(i):
         table_ref[i] = -1
 
-    @pl.loop(0, spots // slots)
+    @pl.loop(0, spots // slots, unroll=True)
     def _(i):
         used[i] = 0
 
-    @pl.loop(0, matrices)
+    @pl.loop(0, matrices, unroll=True)
     def _(m):
         at = owner_ref[m]
         rank = used[at]

time: 214 us -> 213 us (level)
  transfers between devices with their start and end apart: 29 -> 29, of which waited for: 16 -> 17; matrix products, arithmetic and copies ran while one was open for 0% -> 0% of each run, Pallas kernels for 10% -> 10%
where the time goes in v12:
time: 213 us
  waiting for transfers between devices  144 us (68%)
  starting transfers between devices  35.8 us (17%)
  Pallas kernels  31.7 us (15%)
    ppermute x28, waiting for transfers between devices, swap(): return lax.ppermute(value, 'dp', [(i, i ^ bit) for i in range(count)])  140 us
    ppermute x28, starting transfers between devices, swap(): return lax.ppermute(value, 'dp', [(i, i ^ bit) for i in range(count)])  34.7 us
    pallas_call x3, Pallas kernels, spread(): pl.pallas_call(functools.partial(spread_kernel, plans, slots), out_shape=...  9.58 us
    pallas_call x3, Pallas kernels, add_taken(): pl.pallas_call(functools.partial(add_taken_kernel, items, parts, offset),...  6.91 us
  transfers between devices with their start and end apart: 29, of which 17 were waited for; matrix products, arithmetic and copies ran while one was open for 0% of the time, Pallas kernels for 10%

profile of v12, /device:TPU:0, one launch (start us, length us, event | category | flops | bytes accessed | tf_op | source)
XLA Modules:
  0.0 213.3 jit_solution(1532390854225542383)
XLA Ops:
  1.3 3.3 %shard_map.50 = (s32[32]{0:T(128)S(1)}, bf16[22,32,2048]{2,1,0:T(8,128)(2,1)S(1)}) custom-call(s32[1]{0:T(128)} %bitcast.me_ref, s32[24]{0:T(128)S(1)} %copy-done.1, bf16[24,128,2048]{2,1,0:T(8,128)(2,1)} %bitcast.6), custom_call_target="tpu_custom_call" | custom-call | tf_op jit(solution)/shard_map/pallas_call | solution.py:141
  5.2 4.0 %shard_map.51 = (bf16[6,96,2048]{2,1,0:T(8,128)(2,1)S(1)}, bf16[8,96,2048]{2,1,0:T(8,128)(2,1)S(1)}, bf16[14,32,2048]{2,1,0:T(8,128)(2,1)S(1)}) custom-call(s32[32]{0:T(128)S(1)} %get-tuple-element.36.table_ref, bf16[24,128,2048]{2,1,0:T(8,128)(2,1)} %bitcast.7, bf16[22,32,2048]{2,1,0:T(8,128)(2,1)S(1)} %get-tuple-element.37.rest_0_), custom_call_target="tpu_custom_call" | custom-call | tf_op jit(solution)/shard_map/pallas_call | solution.py:115
  10.3 3.0 %collective-permute-start.4 = (bf16[8,32,2048]{2,1,0:T(8,128)(2,1)S(1)}, bf16[8,32,2048]{2,1,0:T(8,128)(2,1)S(1)}, u32[]{:S(2)}, u32[]{:S(2)}) collective-permute-start(bf16[8,32,2048]{2,1,0:T(8,128)(2,1)S(1)} %get-tuple-element.41.rest_0_), channel_id=1, source_target_pairs={{0,8},{2,10},{4,12},{6,14},{8,0},{10,2},{12,4},{14,6},{16,24},{18,... | collective-permute-start | bytes 3145736 | tf_op jit(solution)/shard_map/ppermute | solution.py:443
  13.2 1.5 collective-permute-start.3
  14.7 2.5 %shard_map.53 = (bf16[4,96,2048]{2,1,0:T(8,128)(2,1)S(1)}, bf16[2,96,2048]{2,1,0:T(8,128)(2,1)S(1)}) custom-call(s32[32]{0:T(128)S(1)} %get-tuple-element.36.table_ref, bf16[24,128,2048]{2,1,0:T(8,128)(2,1)} %bitcast.8, bf16[6,96,2048]{2,1,0:T(8,128)(2,1)S(1)} %collective-permute-done.1.got_ref, bf16[8,32,2048]{2,1,0:T(8,128)(2,1)S(1)} %get-tuple-element.41.rest_0_), custom_call_target="tpu_custom_call" | custom-call | tf_op jit(solution)/shard_map/pallas_call | solution.py:175
  17.2 1.6 collective-permute-start.5
  18.8 1.9 shard_map.54.refs_2_.refs_4_
  20.7 12.9 %collective-permute-done.3.refs_1_ = bf16[6,32,2048]{2,1,0:T(8,128)(2,1)S(1)} collective-permute-done((bf16[6,32,2048]{2,1,0:T(8,128)(2,1)S(1)}, bf16[6,32,2048]{2,1,0:T(8,128)(2,1)S(1)}, u32[]{:S(2)}, u32[]{:S(2)}) %collective-permute-start.3) | collective-permute-done | bytes 786464 | tf_op jit(solution)/shard_map/ppermute | solution.py:443
  33.7 3.0 %collective-permute-done.4.refs_3_ = bf16[8,32,2048]{2,1,0:T(8,128)(2,1)S(1)} collective-permute-done((bf16[8,32,2048]{2,1,0:T(8,128)(2,1)S(1)}, bf16[8,32,2048]{2,1,0:T(8,128)(2,1)S(1)}, u32[]{:S(2)}, u32[]{:S(2)}) %collective-permute-start.4) | collective-permute-done | bytes 1048608 | tf_op jit(solution)/shard_map/ppermute | solution.py:443
  36.9 1.8 collective-permute-start.6
  38.7 2.6 %collective-permute-start.7 = (bf16[4,32,2048]{2,1,0:T(8,128)(2,1)S(1)}, bf16[4,32,2048]{2,1,0:T(8,128)(2,1)S(1)}, u32[]{:S(2)}, u32[]{:S(2)}) collective-permute-start(bf16[4,32,2048]{2,1,0:T(8,128)(2,1)S(1)} %get-tuple-element.48), channel_id=1, source_target_pairs={{0,16},{2,18},{4,20},{6,22},{8,24},{10,26},{12,28},{14,30},{16,0},... | collective-permute-start | bytes 1572872 | tf_op jit(solution)/shard_map/ppermute | solution.py:443
  41.3 2.5 %shard_map.56 = (bf16[2,96,2048]{2,1,0:T(8,128)(2,1)S(1)}, bf16[6,96,2048]{2,1,0:T(8,128)(2,1)S(1)}) custom-call(s32[32]{0:T(128)S(1)} %get-tuple-element.36.table_ref, bf16[24,128,2048]{2,1,0:T(8,128)(2,1)} %bitcast.10, bf16[8,96,2048]{2,1,0:T(8,128)(2,1)S(1)} %collective-permute-done.got_ref, bf16[2,96,2048]{2,1,0:T(8,128)(2,1)S(1)} %get-tuple-element.45.rest_0_), custom_call_target="tpu_custom_call" | custom-call | tf_op jit(solution)/shard_map/pallas_call | solution.py:175
  43.8 22.4 %collective-permute-done.7.refs_4_ = bf16[4,32,2048]{2,1,0:T(8,128)(2,1)S(1)} collective-permute-done((bf16[4,32,2048]{2,1,0:T(8,128)(2,1)S(1)}, bf16[4,32,2048]{2,1,0:T(8,128)(2,1)S(1)}, u32[]{:S(2)}, u32[]{:S(2)}) %collective-permute-start.7) | collective-permute-done | bytes 524320 | tf_op jit(solution)/shard_map/ppermute | solution.py:443
  67.6 2.4 %collective-permute-start.10 = (bf16[2,96,2048]{2,1,0:T(8,128)(2,1)S(1)}, bf16[2,96,2048]{2,1,0:T(8,128)(2,1)S(1)}, u32[]{:S(2)}, u32[]{:S(2)}) collective-permute-start(bf16[2,96,2048]{2,1,0:T(8,128)(2,1)S(1)} %get-tuple-element.52), channel_id=1, source_target_pairs={{0,16},{2,18},{4,20},{6,22},{8,24},{10,26},{12,28},{14,30},{16,0},... | collective-permute-start | bytes 2359304 | tf_op jit(solution)/shard_map/ppermute | solution.py:443
  71.5 1.7 collective-permute-start.9
  73.7 19.5 %collective-permute-done.11.rest_5_ = bf16[2,32,2048]{2,1,0:T(8,128)(2,1)S(1)} collective-permute-done((bf16[2,32,2048]{2,1,0:T(8,128)(2,1)S(1)}, bf16[2,32,2048]{2,1,0:T(8,128)(2,1)S(1)}, u32[]{:S(2)}, u32[]{:S(2)}) %collective-permute-start.11) | collective-permute-done | bytes 262176 | tf_op jit(solution)/shard_map/ppermute | solution.py:443
  93.1 10.5 %collective-permute-done.10.rest_3_ = bf16[2,96,2048]{2,1,0:T(8,128)(2,1)S(1)} collective-permute-done((bf16[2,96,2048]{2,1,0:T(8,128)(2,1)S(1)}, bf16[2,96,2048]{2,1,0:T(8,128)(2,1)S(1)}, u32[]{:S(2)}, u32[]{:S(2)}) %collective-permute-start.10) | collective-permute-done | bytes 786464 | tf_op jit(solution)/shard_map/ppermute | solution.py:443
  106.5 3.9 %collective-permute-done.12.refs_1_ = f32[2,128,128]{2,1,0:T(8,128)S(1)} collective-permute-done((f32[2,128,128]{2,1,0:T(8,128)S(1)}, f32[2,128,128]{2,1,0:T(8,128)S(1)}, u32[]{:S(2)}, u32[]{:S(2)}) %collective-permute-start.12) | collective-permute-done | bytes 131104 | tf_op jit(solution)/shard_map/ppermute | solution.py:667
  110.5 3.5 %shard_map.59 = (bf16[2,96,2048]{2,1,0:T(8,128)(2,1)S(1)}, bf16[2,32,2048]{2,1,0:T(8,128)(2,1)S(1)}) custom-call(f32[2,128,128]{2,1,0:T(8,128)S(1)} %get-tuple-element.55.refs_0_, f32[2,128,128]{2,1,0:T(8,128)S(1)} %collective-permute-done.12.refs_1_, bf16[2,128,2048]{2,1,0:T(8,128)(2,1)S(1)} %get-tuple-element.56.refs_2_), custom_call_target="tpu_custom_call" | custom-call | tf_op jit(solution)/shard_map/pallas_call | solution.py:429
  114.0 1.8 collective-permute-start.13
  115.8 2.5 %collective-permute-start.15 = (bf16[2,96,2048]{2,1,0:T(8,128)(2,1)S(1)}, bf16[2,96,2048]{2,1,0:T(8,128)(2,1)S(1)}, u32[]{:S(2)}, u32[]{:S(2)}) collective-permute-start(bf16[2,96,2048]{2,1,0:T(8,128)(2,1)S(1)} %get-tuple-element.57.rest_6_.refs_4_), channel_id=1, source_target_pairs={{0,8},{2,10},{4,12},{6,14},{8,0},{10,2},{12,4},{14,6},{16,24},{18,... | collective-permute-start | bytes 2359304 | tf_op jit(solution)/shard_map/ppermute | solution.py:443
  120.3 2.3 %shard_map.60 = (f32[2,128,2048]{2,1,0:T(8,128)}, f32[8,128]{1,0:T(8,128)S(1)}) custom-call(s32[32]{0:T(128)S(1)} %get-tuple-element.36.table_ref, f32[2,128,2048]{2,1,0:T(8,128)S(1)} %bitcast.5, bf16[6,96,2048]{2,1,0:T(8,128)(2,1)S(1)} %get-tuple-element.46.refs_0_.rest_0_, bf16[2,96,2048]{2,1,0:T(8,128)(2,1)S(1)} %collective-permute-done.8.rest_1_, ...), custom_call_target="tpu_custom_call" | custom-call | tf_op jit(solution)/shard_map/pallas_call | solution.py:348
  122.5 17.6 %collective-permute-done.16.refs_3_ = bf16[2,32,2048]{2,1,0:T(8,128)(2,1)S(1)} collective-permute-done((bf16[2,32,2048]{2,1,0:T(8,128)(2,1)S(1)}, bf16[2,32,2048]{2,1,0:T(8,128)(2,1)S(1)}, u32[]{:S(2)}, u32[]{:S(2)}) %collective-permute-start.16) | collective-permute-done | bytes 262176 | tf_op jit(solution)/shard_map/ppermute | solution.py:443
  140.1 7.7 %collective-permute-done.13.refs_0_ = bf16[2,96,2048]{2,1,0:T(8,128)(2,1)S(1)} collective-permute-done((bf16[2,96,2048]{2,1,0:T(8,128)(2,1)S(1)}, bf16[2,96,2048]{2,1,0:T(8,128)(2,1)S(1)}, u32[]{:S(2)}, u32[]{:S(2)}) %collective-permute-start.13) | collective-permute-done | bytes 786464 | tf_op jit(solution)/shard_map/ppermute | solution.py:443
  150.4 3.9 %collective-permute-start.18 = (bf16[4,32,2048]{2,1,0:T(8,128)(2,1)S(1)}, bf16[4,32,2048]{2,1,0:T(8,128)(2,1)S(1)}, u32[]{:S(2)}, u32[]{:S(2)}) collective-permute-start(bf16[4,32,2048]{2,1,0:T(8,128)(2,1)S(1)} %get-tuple-element.60.refs_1_), channel_id=1, source_target_pairs={{0,16},{2,18},{4,20},{6,22},{8,24},{10,26},{12,28},{14,30},{16,0},... | collective-permute-start | bytes 1572872 | tf_op jit(solution)/shard_map/ppermute | solution.py:443
  154.4 3.0 %shard_map.62 = (bf16[24,128,2048]{2,1,0:T(8,128)(2,1)}, f32[8,128]{1,0:T(8,128)S(1)}) custom-call(s32[32]{0:T(128)S(1)} %get-tuple-element.36.table_ref, bf16[4,96,2048]{2,1,0:T(8,128)(2,1)S(1)} %get-tuple-element.61.refs_0_, bf16[4,96,2048]{2,1,0:T(8,128)(2,1)S(1)} %collective-permute-done.19.refs_1_, ...), custom_call_target="tpu_custom_call" | custom-call | tf_op jit(solution)/shard_map/pallas_call | solution.py:275
  157.3 21.1 %collective-permute-done.18.refs_2_ = bf16[4,32,2048]{2,1,0:T(8,128)(2,1)S(1)} collective-permute-done((bf16[4,32,2048]{2,1,0:T(8,128)(2,1)S(1)}, bf16[4,32,2048]{2,1,0:T(8,128)(2,1)S(1)}, u32[]{:S(2)}, u32[]{:S(2)}) %collective-permute-start.18) | collective-permute-done | bytes 524320 | tf_op jit(solution)/shard_map/ppermute | solution.py:443
  179.8 3.5 %collective-permute-start.24 = (bf16[8,32,2048]{2,1,0:T(8,128)(2,1)S(1)}, bf16[8,32,2048]{2,1,0:T(8,128)(2,1)S(1)}, u32[]{:S(2)}, u32[]{:S(2)}) collective-permute-start(bf16[8,32,2048]{2,1,0:T(8,128)(2,1)S(1)} %get-tuple-element.65.refs_3_), channel_id=1, source_target_pairs={{0,8},{2,10},{4,12},{6,14},{8,0},{10,2},{12,4},{14,6},{16,24},{18,... | collective-permute-start | bytes 3145736 | tf_op jit(solution)/shard_map/ppermute | solution.py:443
  183.3 1.9 collective-permute-done.26.refs_0_
  185.8 19.7 %collective-permute-done.24.refs_6_ = bf16[8,32,2048]{2,1,0:T(8,128)(2,1)S(1)} collective-permute-done((bf16[8,32,2048]{2,1,0:T(8,128)(2,1)S(1)}, bf16[8,32,2048]{2,1,0:T(8,128)(2,1)S(1)}, u32[]{:S(2)}, u32[]{:S(2)}) %collective-permute-start.24) | collective-permute-done | bytes 1048608 | tf_op jit(solution)/shard_map/ppermute | solution.py:443
  206.1 3.8 %shard_map.64 = (bf16[24,128,2048]{2,1,0:T(8,128)(2,1)}, f32[8,128]{1,0:T(8,128)}) custom-call(s32[32]{0:T(128)S(1)} %get-tuple-element.36.table_ref, bf16[4,96,2048]{2,1,0:T(8,128)(2,1)S(1)} %collective-permute-done.26.refs_0_, bf16[4,96,2048]{2,1,0:T(8,128)(2,1)S(1)} %collective-permute-done.27.refs_1_, ...), custom_call_target="tpu_custom_call", output_to_operand_aliasing={{0}: (8, {})} | custom-call | tf_op jit(solution)/shard_map/pallas_call | solution.py:275
  210.5 2.8 %shard_map.65 = (bf16[24,128,2048]{2,1,0:T(8,128)(2,1)}, f32[8,128]{1,0:T(8,128)}) custom-call(s32[32]{0:T(128)S(1)} %get-tuple-element.36.table_ref, bf16[2,96,2048]{2,1,0:T(8,128)(2,1)S(1)} %collective-permute-done.21.refs_0_, bf16[2,96,2048]{2,1,0:T(8,128)(2,1)S(1)} %collective-permute-done.23.refs_1_, ...), custom_call_target="tpu_custom_call", output_to_operand_aliasing={{0}: (4, {})} | custom-call | tf_op jit(solution)/shard_map/pallas_call | solution.py:275
  (46 shorter events, 16.5 us)
Async XLA Ops:
  0.6 0.7 copy-start.1
  4.6 5.5 %collective-permute-start.2 = (bf16[22,32,2048]{2,1,0:T(8,128)(2,1)S(1)}, bf16[22,32,2048]{2,1,0:T(8,128)(2,1)S(1)}, u32[]{:S(2)}, u32[]{:S(2)}) collective-permute-start(bf16[22,32,2048]{2,1,0:T(8,128)(2,1)S(1)} %get-tuple-element.37.rest_0_), channel_id=1, source_target_pairs={{0,2},{2,0},{4,6},{6,4},{8,10},{10,8},{12,14},{14,12},{16,18},{18,... | collective-permute-start | bytes 8650760 | tf_op jit(solution)/shard_map/ppermute | solution.py:443
  9.2 5.5 %collective-permute-start.1 = (bf16[6,96,2048]{2,1,0:T(8,128)(2,1)S(1)}, bf16[6,96,2048]{2,1,0:T(8,128)(2,1)S(1)}, u32[]{:S(2)}, u32[]{:S(2)}) collective-permute-start(bf16[6,96,2048]{2,1,0:T(8,128)(2,1)S(1)} %get-tuple-element.39.refs_2_), channel_id=1, source_target_pairs={{0,2},{2,0},{4,6},{6,4},{8,10},{10,8},{12,14},{14,12},{16,18},{18,... | collective-permute-start | bytes 7077896 | tf_op jit(solution)/shard_map/ppermute | solution.py:443
  9.4 31.9 %collective-permute-start = (bf16[8,96,2048]{2,1,0:T(8,128)(2,1)S(1)}, bf16[8,96,2048]{2,1,0:T(8,128)(2,1)S(1)}, u32[]{:S(2)}, u32[]{:S(2)}) collective-permute-start(bf16[8,96,2048]{2,1,0:T(8,128)(2,1)S(1)} %get-tuple-element.38), channel_id=1, source_target_pairs={{0,2},{2,0},{4,6},{6,4},{8,10},{10,8},{12,14},{14,12},{16,18},{18,... | collective-permute-start | bytes 9437192 | tf_op jit(solution)/shard_map/ppermute | solution.py:443
  10.3 26.4 %collective-permute-start.4 = (bf16[8,32,2048]{2,1,0:T(8,128)(2,1)S(1)}, bf16[8,32,2048]{2,1,0:T(8,128)(2,1)S(1)}, u32[]{:S(2)}, u32[]{:S(2)}) collective-permute-start(bf16[8,32,2048]{2,1,0:T(8,128)(2,1)S(1)} %get-tuple-element.41.rest_0_), channel_id=1, source_target_pairs={{0,8},{2,10},{4,12},{6,14},{8,0},{10,2},{12,4},{14,6},{16,24},{18,... | collective-permute-start | bytes 3145736 | tf_op jit(solution)/shard_map/ppermute | solution.py:443
  13.2 20.4 %collective-permute-start.3 = (bf16[6,32,2048]{2,1,0:T(8,128)(2,1)S(1)}, bf16[6,32,2048]{2,1,0:T(8,128)(2,1)S(1)}, u32[]{:S(2)}, u32[]{:S(2)}) collective-permute-start(bf16[6,32,2048]{2,1,0:T(8,128)(2,1)S(1)} %get-tuple-element.43), channel_id=1, source_target_pairs={{0,4},{2,6},{4,0},{6,2},{8,12},{10,14},{12,8},{14,10},{16,20},{18,... | collective-permute-start | bytes 2359304 | tf_op jit(solution)/shard_map/ppermute | solution.py:443
  17.2 49.0 %collective-permute-start.5 = (bf16[4,96,2048]{2,1,0:T(8,128)(2,1)S(1)}, bf16[4,96,2048]{2,1,0:T(8,128)(2,1)S(1)}, u32[]{:S(2)}, u32[]{:S(2)}) collective-permute-start(bf16[4,96,2048]{2,1,0:T(8,128)(2,1)S(1)} %get-tuple-element.44.rest_0_), channel_id=1, source_target_pairs={{0,4},{2,6},{4,0},{6,2},{8,12},{10,14},{12,8},{14,10},{16,20},{18,... | collective-permute-start | bytes 4718600 | tf_op jit(solution)/shard_map/ppermute | solution.py:443
  36.9 30.4 %collective-permute-start.6 = (bf16[2,96,2048]{2,1,0:T(8,128)(2,1)S(1)}, bf16[2,96,2048]{2,1,0:T(8,128)(2,1)S(1)}, u32[]{:S(2)}, u32[]{:S(2)}) collective-permute-start(bf16[2,96,2048]{2,1,0:T(8,128)(2,1)S(1)} %get-tuple-element.45.rest_0_), channel_id=1, source_target_pairs={{0,8},{2,10},{4,12},{6,14},{8,0},{10,2},{12,4},{14,6},{16,24},{18,... | collective-permute-start | bytes 2359304 | tf_op jit(solution)/shard_map/ppermute | solution.py:443
  38.7 27.5 %collective-permute-start.7 = (bf16[4,32,2048]{2,1,0:T(8,128)(2,1)S(1)}, bf16[4,32,2048]{2,1,0:T(8,128)(2,1)S(1)}, u32[]{:S(2)}, u32[]{:S(2)}) collective-permute-start(bf16[4,32,2048]{2,1,0:T(8,128)(2,1)S(1)} %get-tuple-element.48), channel_id=1, source_target_pairs={{0,16},{2,18},{4,20},{6,22},{8,24},{10,26},{12,28},{14,30},{16,0},... | collective-permute-start | bytes 1572872 | tf_op jit(solution)/shard_map/ppermute | solution.py:443
  67.3 37.1 %copy-start = (f32[1,2,128,2048]{3,2,1,0:T(8,128)S(1)}, f32[1,2,128,2048]{3,2,1,0:T(8,128)}, u32[]{:S(2)}) copy-start(f32[1,2,128,2048]{3,2,1,0:T(8,128)} %param.5) | copy-start | bytes 6291460
  67.6 36.1 %collective-permute-start.10 = (bf16[2,96,2048]{2,1,0:T(8,128)(2,1)S(1)}, bf16[2,96,2048]{2,1,0:T(8,128)(2,1)S(1)}, u32[]{:S(2)}, u32[]{:S(2)}) collective-permute-start(bf16[2,96,2048]{2,1,0:T(8,128)(2,1)S(1)} %get-tuple-element.52), channel_id=1, source_target_pairs={{0,16},{2,18},{4,20},{6,22},{8,24},{10,26},{12,28},{14,30},{16,0},... | collective-permute-start | bytes 2359304 | tf_op jit(solution)/shard_map/ppermute | solution.py:443
  70.0 33.7 %collective-permute-start.8 = (bf16[2,96,2048]{2,1,0:T(8,128)(2,1)S(1)}, bf16[2,96,2048]{2,1,0:T(8,128)(2,1)S(1)}, u32[]{:S(2)}, u32[]{:S(2)}) collective-permute-start(bf16[2,96,2048]{2,1,0:T(8,128)(2,1)S(1)} %get-tuple-element.50), channel_id=1, source_target_pairs={{0,4},{2,6},{4,0},{6,2},{8,12},{10,14},{12,8},{14,10},{16,20},{18,... | collective-permute-start | bytes 2359304 | tf_op jit(solution)/shard_map/ppermute | solution.py:443
  71.5 32.9 %collective-permute-start.9 = (bf16[2,96,2048]{2,1,0:T(8,128)(2,1)S(1)}, bf16[2,96,2048]{2,1,0:T(8,128)(2,1)S(1)}, u32[]{:S(2)}, u32[]{:S(2)}) collective-permute-start(bf16[2,96,2048]{2,1,0:T(8,128)(2,1)S(1)} %get-tuple-element.51), channel_id=1, source_target_pairs={{0,8},{2,10},{4,12},{6,14},{8,0},{10,2},{12,4},{14,6},{16,24},{18,... | collective-permute-start | bytes 2359304 | tf_op jit(solution)/shard_map/ppermute | solution.py:443
  73.1 20.0 %collective-permute-start.11 = (bf16[2,32,2048]{2,1,0:T(8,128)(2,1)S(1)}, bf16[2,32,2048]{2,1,0:T(8,128)(2,1)S(1)}, u32[]{:S(2)}, u32[]{:S(2)}) collective-permute-start(bf16[2,32,2048]{2,1,0:T(8,128)(2,1)S(1)} %get-tuple-element.54), channel_id=1, source_target_pairs={{0,4},{2,6},{4,0},{6,2},{8,12},{10,14},{12,8},{14,10},{16,20},{18,... | collective-permute-start | bytes 786440 | tf_op jit(solution)/shard_map/ppermute | solution.py:443
  105.5 5.0 %collective-permute-start.12 = (f32[2,128,128]{2,1,0:T(8,128)S(1)}, f32[2,128,128]{2,1,0:T(8,128)S(1)}, u32[]{:S(2)}, u32[]{:S(2)}) collective-permute-start(f32[2,128,128]{2,1,0:T(8,128)S(1)} %get-tuple-element.55.refs_0_), channel_id=1, source_target_pairs={{0,1},{1,0},{2,3},{3,2},{4,5},{5,4},{6,7},{7,6},{8,9},{9,8},{10,11... | collective-permute-start | bytes 393224 | tf_op jit(solution)/shard_map/ppermute | solution.py:667
  114.0 33.9 %collective-permute-start.13 = (bf16[2,96,2048]{2,1,0:T(8,128)(2,1)S(1)}, bf16[2,96,2048]{2,1,0:T(8,128)(2,1)S(1)}, u32[]{:S(2)}, u32[]{:S(2)}) collective-permute-start(bf16[2,96,2048]{2,1,0:T(8,128)(2,1)S(1)} %get-tuple-element.57.rest_6_.refs_4_), channel_id=1, source_target_pairs={{0,16},{2,18},{4,20},{6,22},{8,24},{10,26},{12,28},{14,30},{16,0},... | collective-permute-start | bytes 2359304 | tf_op jit(solution)/shard_map/ppermute | solution.py:443
  115.8 32.2 %collective-permute-start.15 = (bf16[2,96,2048]{2,1,0:T(8,128)(2,1)S(1)}, bf16[2,96,2048]{2,1,0:T(8,128)(2,1)S(1)}, u32[]{:S(2)}, u32[]{:S(2)}) collective-permute-start(bf16[2,96,2048]{2,1,0:T(8,128)(2,1)S(1)} %get-tuple-element.57.rest_6_.refs_4_), channel_id=1, source_target_pairs={{0,8},{2,10},{4,12},{6,14},{8,0},{10,2},{12,4},{14,6},{16,24},{18,... | collective-permute-start | bytes 2359304 | tf_op jit(solution)/shard_map/ppermute | solution.py:443
  118.2 29.7 %collective-permute-start.17 = (bf16[2,96,2048]{2,1,0:T(8,128)(2,1)S(1)}, bf16[2,96,2048]{2,1,0:T(8,128)(2,1)S(1)}, u32[]{:S(2)}, u32[]{:S(2)}) collective-permute-start(bf16[2,96,2048]{2,1,0:T(8,128)(2,1)S(1)} %get-tuple-element.57.rest_6_.refs_4_), channel_id=1, source_target_pairs={{0,4},{2,6},{4,0},{6,2},{8,12},{10,14},{12,8},{14,10},{16,20},{18,... | collective-permute-start | bytes 2359304 | tf_op jit(solution)/shard_map/ppermute | solution.py:443
  118.9 21.3 %collective-permute-start.16 = (bf16[2,32,2048]{2,1,0:T(8,128)(2,1)S(1)}, bf16[2,32,2048]{2,1,0:T(8,128)(2,1)S(1)}, u32[]{:S(2)}, u32[]{:S(2)}) collective-permute-start(bf16[2,32,2048]{2,1,0:T(8,128)(2,1)S(1)} %get-tuple-element.58.refs_2_), channel_id=1, source_target_pairs={{0,4},{2,6},{4,0},{6,2},{8,12},{10,14},{12,8},{14,10},{16,20},{18,... | collective-permute-start | bytes 786440 | tf_op jit(solution)/shard_map/ppermute | solution.py:443
  148.2 6.2 %collective-permute-start.19 = (bf16[4,96,2048]{2,1,0:T(8,128)(2,1)S(1)}, bf16[4,96,2048]{2,1,0:T(8,128)(2,1)S(1)}, u32[]{:S(2)}, u32[]{:S(2)}) collective-permute-start(bf16[4,96,2048]{2,1,0:T(8,128)(2,1)S(1)} %get-tuple-element.61.refs_0_), channel_id=1, source_target_pairs={{0,2},{2,0},{4,6},{6,4},{8,10},{10,8},{12,14},{14,12},{16,18},{18,... | collective-permute-start | bytes 4718600 | tf_op jit(solution)/shard_map/ppermute | solution.py:443
  148.3 6.1 %collective-permute-start.20 = (bf16[4,96,2048]{2,1,0:T(8,128)(2,1)S(1)}, bf16[4,96,2048]{2,1,0:T(8,128)(2,1)S(1)}, u32[]{:S(2)}, u32[]{:S(2)}) collective-permute-start(bf16[4,96,2048]{2,1,0:T(8,128)(2,1)S(1)} %get-tuple-element.62.refs_2_.refs_4_), channel_id=1, source_target_pairs={{0,2},{2,0},{4,6},{6,4},{8,10},{10,8},{12,14},{14,12},{16,18},{18,... | collective-permute-start | bytes 4718600 | tf_op jit(solution)/shard_map/ppermute | solution.py:443
  148.8 36.4 %collective-permute-start.26 = (bf16[4,96,2048]{2,1,0:T(8,128)(2,1)S(1)}, bf16[4,96,2048]{2,1,0:T(8,128)(2,1)S(1)}, u32[]{:S(2)}, u32[]{:S(2)}) collective-permute-start(bf16[4,96,2048]{2,1,0:T(8,128)(2,1)S(1)} %get-tuple-element.62.refs_2_.refs_4_), channel_id=1, source_target_pairs={{0,4},{2,6},{4,0},{6,2},{8,12},{10,14},{12,8},{14,10},{16,20},{18,... | collective-permute-start | bytes 4718600 | tf_op jit(solution)/shard_map/ppermute | solution.py:443
  149.2 30.5 %collective-permute-start.14 = (bf16[2,96,2048]{2,1,0:T(8,128)(2,1)S(1)}, bf16[2,96,2048]{2,1,0:T(8,128)(2,1)S(1)}, u32[]{:S(2)}, u32[]{:S(2)}) collective-permute-start(bf16[2,96,2048]{2,1,0:T(8,128)(2,1)S(1)} %collective-permute-done.13.refs_0_), channel_id=1, source_target_pairs={{0,8},{2,10},{4,12},{6,14},{8,0},{10,2},{12,4},{14,6},{16,24},{18,... | collective-permute-start | bytes 2359304 | tf_op jit(solution)/shard_map/ppermute | solution.py:443
  150.4 28.0 %collective-permute-start.18 = (bf16[4,32,2048]{2,1,0:T(8,128)(2,1)S(1)}, bf16[4,32,2048]{2,1,0:T(8,128)(2,1)S(1)}, u32[]{:S(2)}, u32[]{:S(2)}) collective-permute-start(bf16[4,32,2048]{2,1,0:T(8,128)(2,1)S(1)} %get-tuple-element.60.refs_1_), channel_id=1, source_target_pairs={{0,16},{2,18},{4,20},{6,22},{8,24},{10,26},{12,28},{14,30},{16,0},... | collective-permute-start | bytes 1572872 | tf_op jit(solution)/shard_map/ppermute | solution.py:443
  179.8 25.7 %collective-permute-start.24 = (bf16[8,32,2048]{2,1,0:T(8,128)(2,1)S(1)}, bf16[8,32,2048]{2,1,0:T(8,128)(2,1)S(1)}, u32[]{:S(2)}, u32[]{:S(2)}) collective-permute-start(bf16[8,32,2048]{2,1,0:T(8,128)(2,1)S(1)} %get-tuple-element.65.refs_3_), channel_id=1, source_target_pairs={{0,8},{2,10},{4,12},{6,14},{8,0},{10,2},{12,4},{14,6},{16,24},{18,... | collective-permute-start | bytes 3145736 | tf_op jit(solution)/shard_map/ppermute | solution.py:443
  185.1 20.9 %collective-permute-start.27 = (bf16[4,96,2048]{2,1,0:T(8,128)(2,1)S(1)}, bf16[4,96,2048]{2,1,0:T(8,128)(2,1)S(1)}, u32[]{:S(2)}, u32[]{:S(2)}) collective-permute-start(bf16[4,96,2048]{2,1,0:T(8,128)(2,1)S(1)} %collective-permute-done.26.refs_0_), channel_id=1, source_target_pairs={{0,2},{2,0},{4,6},{6,4},{8,10},{10,8},{12,14},{14,12},{16,18},{18,... | collective-permute-start | bytes 4718600 | tf_op jit(solution)/shard_map/ppermute | solution.py:443
  185.2 20.9 %collective-permute-start.22 = (bf16[2,96,2048]{2,1,0:T(8,128)(2,1)S(1)}, bf16[2,96,2048]{2,1,0:T(8,128)(2,1)S(1)}, u32[]{:S(2)}, u32[]{:S(2)}) collective-permute-start(bf16[2,96,2048]{2,1,0:T(8,128)(2,1)S(1)} %get-tuple-element.64.refs_2_.refs_8_), channel_id=1, source_target_pairs={{0,4},{2,6},{4,0},{6,2},{8,12},{10,14},{12,8},{14,10},{16,20},{18,... | collective-permute-start | bytes 2359304 | tf_op jit(solution)/shard_map/ppermute | solution.py:443
  185.6 20.5 %collective-permute-start.28 = (bf16[8,32,2048]{2,1,0:T(8,128)(2,1)S(1)}, bf16[8,32,2048]{2,1,0:T(8,128)(2,1)S(1)}, u32[]{:S(2)}, u32[]{:S(2)}) collective-permute-start(bf16[8,32,2048]{2,1,0:T(8,128)(2,1)S(1)} %get-tuple-element.65.refs_3_), channel_id=1, source_target_pairs={{0,2},{2,0},{4,6},{6,4},{8,10},{10,8},{12,14},{14,12},{16,18},{18,... | collective-permute-start | bytes 3145736 | tf_op jit(solution)/shard_map/ppermute | solution.py:443
  205.6 4.9 %collective-permute-start.25 = (bf16[8,32,2048]{2,1,0:T(8,128)(2,1)S(1)}, bf16[8,32,2048]{2,1,0:T(8,128)(2,1)S(1)}, u32[]{:S(2)}, u32[]{:S(2)}) collective-permute-start(bf16[8,32,2048]{2,1,0:T(8,128)(2,1)S(1)} %collective-permute-done.24.refs_6_), channel_id=1, source_target_pairs={{0,2},{2,0},{4,6},{6,4},{8,10},{10,8},{12,14},{14,12},{16,18},{18,... | collective-permute-start | bytes 3145736 | tf_op jit(solution)/shard_map/ppermute | solution.py:443
  205.6 4.3 %collective-permute-start.21 = (bf16[2,96,2048]{2,1,0:T(8,128)(2,1)S(1)}, bf16[2,96,2048]{2,1,0:T(8,128)(2,1)S(1)}, u32[]{:S(2)}, u32[]{:S(2)}) collective-permute-start(bf16[2,96,2048]{2,1,0:T(8,128)(2,1)S(1)} %get-tuple-element.64.refs_2_.refs_8_), channel_id=1, source_target_pairs={{0,2},{2,0},{4,6},{6,4},{8,10},{10,8},{12,14},{14,12},{16,18},{18,... | collective-permute-start | bytes 2359304 | tf_op jit(solution)/shard_map/ppermute | solution.py:443
  206.1 4.4 %collective-permute-start.23 = (bf16[2,96,2048]{2,1,0:T(8,128)(2,1)S(1)}, bf16[2,96,2048]{2,1,0:T(8,128)(2,1)S(1)}, u32[]{:S(2)}, u32[]{:S(2)}) collective-permute-start(bf16[2,96,2048]{2,1,0:T(8,128)(2,1)S(1)} %collective-permute-done.22.refs_5_), channel_id=1, source_target_pairs={{0,2},{2,0},{4,6},{6,4},{8,10},{10,8},{12,14},{14,12},{16,18},{18,... | collective-permute-start | bytes 2359304 | tf_op jit(solution)/shard_map/ppermute | solution.py:443
